TPU v7x, 128 devices: a whole 4x4x4 slice. The times are simulated.
128 devices in a mesh: seq: 32 (over y_lo, x, z), mp: 4 (over y_hi, core).
Axes of the slice: x: 4, y: 4 (y_hi: 2, y_lo: 2; y = y_hi * 2 + y_lo), z: 4, core: 2. Of those that a mesh axis runs over, the one named last changes fastest.
Arguments:
- tokens: bfloat16 [16384, 5376], P('seq', 'mp'), may hold values from -6 to 6
- q_weight: bfloat16 [5376, 2048], P('seq', 'mp'), may hold values from -0.078125 to 0.078125
- key_matrix: bfloat16 [5376, 1024], P('seq', 'mp'), may hold values from -0.078125 to 0.078125
- value_matrix: bfloat16 [5376, 1024], P('seq', 'mp'), may hold values from -0.078125 to 0.078125
- o_weight: bfloat16 [2048, 5376], P('mp', 'seq'), may hold values from -0.79549513 to 0.79549513
- pre_gain: float32 [5376], replicated, may hold values from 0.1 to 1.9
- post_gain: float32 [5376], P('mp'), may hold values from 0.1 to 1.9
- q_gain: float32 [128], replicated, may hold values from 0.1 to 1.9
- k_gain: float32 [128], replicated, may hold values from 0.1 to 1.9
Outputs:
- layer_out: bfloat16 [16384, 5376], P('seq', 'mp')
All inputs are finite; a program needn't handle non-finite values.
Results may differ from a plain program's by a relative error of at most 0.015.
Values may be sent and summed in bfloat16 or wider, within the bound.
No kernel may reach another device: no remote copies, remote signals or barrier semaphores. Data moves between devices by JAX's collectives and lax.ppermute only.
A program may use at most 128 MiB of HBM per device.

v0:
```python
import math

import jax
import jax.numpy as jnp
from jax import lax
from jax.sharding import PartitionSpec as P

MODEL_WIDTH = 5376
HEAD_SIZE = 128
WINDOW_LENGTH = 1024


score_scale = 168.0 ** (-0.5)
epsilon = 1e-06


def from_behind(value, axis, steps):
    count = lax.axis_size(axis)
    initial, last = (max(0, -steps), min(count, count - steps))
    return lax.ppermute(value, axis, [(source, source + steps) for source in range(initial, last)])


def rms_heads(raw, gain, positions):
    normal = raw * lax.rsqrt(jnp.mean(raw * raw, axis=-1, keepdims=True) + epsilon) * gain
    half = raw.shape[-1] // 2
    freq = 10000.0 ** (-(jnp.arange(half, dtype=jnp.float32) * 2.0) / raw.shape[-1])
    angle = positions.astype(jnp.float32)[:, None] * freq[None, :]
    cosine = jnp.cos(angle)[:, None, :]
    sine = jnp.sin(angle)[:, None, :]
    first = normal[..., :half]
    second = normal[..., half:]
    return jnp.concatenate(
        [first * cosine - second * sine, second * cosine + first * sine], axis=-1
    )


def local(
    tokens, q_weight, key_matrix, value_matrix, o_weight, pre_gain, post_gain, q_gain, k_gain
):
    rows = tokens.shape[0]
    seq_index = lax.axis_index("seq")
    hops = max(1, WINDOW_LENGTH // rows)
    whole = lax.all_gather(tokens, "mp", axis=1, tiled=True)
    wide = whole.astype(jnp.float32)
    normed_input = (
        wide * lax.rsqrt(jnp.mean(wide * wide, axis=1, keepdims=True) + epsilon) * pre_gain
    ).astype(jnp.bfloat16)
    q_cols = q_weight.shape[1]
    kv_cols = key_matrix.shape[1]
    q_sum = jnp.dot(
        normed_input,
        lax.all_gather(q_weight, "seq", axis=0, tiled=True),
        preferred_element_type=jnp.float32,
    )
    k_sum = jnp.dot(
        normed_input,
        lax.all_gather(key_matrix, "seq", axis=0, tiled=True),
        preferred_element_type=jnp.float32,
    )
    v_sum = jnp.dot(
        normed_input,
        lax.all_gather(value_matrix, "seq", axis=0, tiled=True),
        preferred_element_type=jnp.float32,
    )
    base = seq_index * rows
    query_pos_all = base + jnp.arange(rows, dtype=jnp.int32)
    key_pos_all = base + jnp.arange(rows, dtype=jnp.int32)
    local_kv = kv_cols // HEAD_SIZE
    query_vectors = rms_heads(
        q_sum.reshape(rows, q_cols // HEAD_SIZE, HEAD_SIZE), q_gain, query_pos_all
    ).astype(jnp.bfloat16)
    keys_own = rms_heads(k_sum.reshape(rows, local_kv, HEAD_SIZE), k_gain, key_pos_all).astype(
        jnp.bfloat16
    )
    values_own = v_sum.astype(jnp.bfloat16)
    stacked = jnp.stack([keys_own.reshape(rows, kv_cols), values_own], axis=0)
    received = []
    for hop in range(hops, 0, -1):
        received.append(from_behind(stacked, "seq", hop))
    joined = jnp.concatenate(received + [stacked], axis=1)
    key_vectors = joined[0].reshape(WINDOW_LENGTH + rows, local_kv, HEAD_SIZE)
    value_vectors = joined[1].reshape(WINDOW_LENGTH + rows, local_kv, HEAD_SIZE)
    head_group = q_cols // HEAD_SIZE // local_kv
    grouped_queries = query_vectors.reshape(rows, local_kv, head_group, HEAD_SIZE)
    block = math.gcd(rows, 512)
    blocks = rows // block

    def attend(index):
        start = index * block
        scores = (
            jnp.einsum(
                "qkgd,skd->kgqs", grouped_queries, key_vectors, preferred_element_type=jnp.float32
            )
            * score_scale
        )
        query_pos = base + start + jnp.arange(block, dtype=jnp.int32)
        key_pos = base - WINDOW_LENGTH + start + jnp.arange(block + WINDOW_LENGTH, dtype=jnp.int32)
        distance = query_pos[:, None] - key_pos[None, :]
        allowed = (distance >= 0) & (distance < WINDOW_LENGTH) & (key_pos >= 0)[None, :]
        weights = jnp.where(allowed[None, None], jnp.exp(scores), 0.0)
        denominator = jnp.sum(weights, axis=-1)
        mixed = jnp.einsum(
            "kgqs,skd->qkgd",
            weights.astype(jnp.bfloat16),
            value_vectors,
            preferred_element_type=jnp.float32,
        )
        mixed = mixed / jnp.transpose(denominator, (2, 0, 1))[..., None]
        return mixed.astype(jnp.bfloat16).reshape(block, q_cols)

    context = lax.map(attend, jnp.arange(blocks, dtype=jnp.int32)).reshape(rows, q_cols)
    terms = jnp.dot(
        context,
        lax.all_gather(o_weight, "seq", axis=1, tiled=True),
        preferred_element_type=jnp.float32,
    )
    share = lax.psum_scatter(
        terms.astype(jnp.bfloat16), "mp", scatter_dimension=1, tiled=True
    ).astype(jnp.float32)
    total = lax.psum(jnp.sum(share * share, axis=1), "mp")
    scale_rows = lax.rsqrt(total / MODEL_WIDTH + epsilon)
    return (tokens.astype(jnp.float32) + share * scale_rows[:, None] * post_gain).astype(
        jnp.bfloat16
    )


def solution(mesh):
    return jax.shard_map(
        local,
        mesh=mesh,
        in_specs=(
            P("seq", "mp"),
            P("seq", "mp"),
            P("seq", "mp"),
            P("seq", "mp"),
            P("mp", "seq"),
            P(),
            P("mp"),
            P(),
            P(),
        ),
        out_specs=P("seq", "mp"),
        check_vma=False,
    )
```

profile of v0, /device:TPU:40, one launch (start us, length us, event | category | flops | bytes accessed | tf_op | source)
XLA Modules:
  0.0 785.7 jit_solution(1481580721408870141)
XLA Ops:
  6.5 0.0 copy-start.4
  6.5 0.0 all-gather.6.cloned.1.call-start
  6.5 0.7 all-gather.6.cloned.1.call-update
  7.3 0.0 all-gather.8.cloned.1.call-start
  7.3 0.7 all-gather.8.cloned.1.call-update
  8.0 0.0 all-gather.10.cloned.1.call-start
  8.1 0.7 all-gather.10.cloned.1.call-update
  8.7 0.0 all-gather.12.cloned.1.call-start
  8.8 0.5 all-gather.12.cloned.1.call-update
  9.3 0.0 all-gather.14.cloned.1.call-start
  9.4 0.5 all-gather.14.cloned.1.call-update
  9.9 0.0 reduce-scatter.2.cloned.1.call-start
  10.0 0.5 multiply_cosine_fusion
  10.5 45.5 %all-gather.6.cloned.1.call-done = bf16[512,5376]{0,1:T(8,128)(2,1)} async-done(((bf16[512,1344]{0,1:T(8,128)(2,1)}), bf16[512,5376]{0,1:T(8,128)(2,1)}) %all-gather.6.cloned.1.call-update) | async-done | bytes 5505040 | tf_op jit(solution)/shard_map/all_gather | solution.py:43
  56.1 3.8 fusion
  59.8 0.0 copy-start.2
  59.8 151.9 %all-gather.8.cloned.1.call-done = bf16[5376,256]{1,0:T(8,128)(2,1)} async-done(((bf16[168,256]{1,0:T(8,128)(2,1)}), bf16[5376,256]{1,0:T(8,128)(2,1)}) %all-gather.8.cloned.1.call-update) | async-done | bytes 2752528 | tf_op jit(solution)/shard_map/all_gather | solution.py:57
  211.8 0.0 copy-done.4
  211.8 5.4 multiply_reduce_fusion.1
  217.2 0.0 copy-done.2
  217.3 0.1 multiply_multiply_fusion.1
  217.4 0.1 subtract_convert_fusion.1
  217.5 0.1 copy.19
  217.6 153.0 %all-gather.10.cloned.1.call-done = bf16[5376,256]{1,0:T(8,128)(2,1)} async-done(((bf16[168,256]{1,0:T(8,128)(2,1)}), bf16[5376,256]{1,0:T(8,128)(2,1)}) %all-gather.10.cloned.1.call-update) | async-done | bytes 2752528 | tf_op jit(solution)/shard_map/all_gather | solution.py:62
  370.7 5.9 fusion.19
  376.6 0.1 pad_maximum_fusion
  376.6 2.1 collective-permute-start
  378.8 2.1 collective-permute-start.1
  380.9 1.2 fusion.11
  382.1 15.2 %collective-permute-done = bf16[2,512,256]{2,1,0:T(8,128)(2,1)S(1)} collective-permute-done((bf16[2,512,256]{2,1,0:T(8,128)(2,1)S(1)}, bf16[2,512,256]{2,1,0:T(8,128)(2,1)S(1)}, u32[]{:S(2)}, u32[]{:S(2)}) %collective-permute-start) | collective-permute-done | bytes 524320 | tf_op jit(solution)/shard_map/ppermute | solution.py:20
  397.3 0.0 collective-permute-done.1
  397.3 0.1 maximum_maximum_fusion
  397.4 0.1 fusion.36
  397.5 0.2 reshape_squeeze.7
  397.7 0.3 copy.20
  398.0 0.0 copy-start.3
  398.0 136.7 %all-gather.12.cloned.1.call-done = bf16[5376,512]{1,0:T(8,128)(2,1)} async-done(((bf16[168,512]{1,0:T(8,128)(2,1)}), bf16[5376,512]{1,0:T(8,128)(2,1)}) %all-gather.12.cloned.1.call-update) | async-done | bytes 5505040 | tf_op jit(solution)/shard_map/all_gather | solution.py:52
  534.7 7.6 multiply_reduce_fusion
  542.3 0.0 copy-done.3
  542.3 0.2 multiply_multiply_fusion
  542.5 0.2 subtract_convert_fusion
  542.7 1.0 copy.11
  543.7 0.3 copy.12
  544.0 4.7 fusion.3
  548.7 2.7 divide_convert_fusion
  551.4 146.7 %all-gather.14.cloned.1.call-done = bf16[512,5376]{0,1:T(8,128)(2,1)} async-done(((bf16[512,168]{0,1:T(8,128)(2,1)}), bf16[512,5376]{0,1:T(8,128)(2,1)}) %all-gather.14.cloned.1.call-update) | async-done | bytes 5505040 | tf_op jit(solution)/shard_map/all_gather | solution.py:114
  698.1 7.3 convolution_convert_fusion
  705.4 0.0 copy-start
  705.4 0.0 copy-start.1
  705.4 0.0 reduce-scatter.2.cloned.1.call-update
  705.4 60.4 %reduce-scatter.2.cloned.1.call-done = bf16[512,1344]{0,1:T(8,128)(2,1)} async-done(((bf16[512,5376]{0,1:T(8,128)(2,1)}), bf16[512,1344]{0,1:T(8,128)(2,1)}) %reduce-scatter.2.cloned.1.call-update) | async-done | bytes 1376272 | tf_op jit(solution)/shard_map/reduce_scatter | solution.py:117
  765.9 1.7 fusion.12
  767.6 8.3 %psum.7 = f32[512]{0:T(512)S(1)} all-reduce(f32[512]{0:T(512)S(1)} %fusion.12), channel_id=1, replica_groups=mesh['seq'=32,'mp'=4] {'mp'}, use_global_device_ids=true, to_apply=%region_6.7 | all-reduce | flops 512 | bytes 4096 | tf_op jit(solution)/shard_map/psum | solution.py:120
  775.9 0.0 copy-done
  775.9 0.0 copy-done.1
  775.9 2.9 fusion.15
  (9 shorter events, 0.1 us)
Async XLA Ops:
  6.5 205.2 %copy-start.4 = (f32[5376]{0:T(1024)S(1)}, f32[5376]{0:T(1024)}, u32[]{:S(2)}) copy-start(f32[5376]{0:T(1024)} %param.14) | copy-start | bytes 64516
  6.5 49.5 %all-gather.6.cloned.1.call-start = ((), (), s32[]{:S(2)}) async-start(), calls=%async_computation.1 | async-start | bytes 6881280 | tf_op jit(solution)/shard_map/all_gather | solution.py:43
  7.3 204.5 %all-gather.8.cloned.1.call-start = ((), (), s32[]{:S(2)}) async-start(), calls=%async_computation.2 | async-start | bytes 2838528 | tf_op jit(solution)/shard_map/all_gather | solution.py:57
  8.0 362.7 %all-gather.10.cloned.1.call-start = ((), (), s32[]{:S(2)}) async-start(), calls=%async_computation.3 | async-start | bytes 2838528 | tf_op jit(solution)/shard_map/all_gather | solution.py:62
  8.7 526.0 %all-gather.12.cloned.1.call-start = ((), (), s32[]{:S(2)}) async-start(), calls=%async_computation.4 | async-start | bytes 5677056 | tf_op jit(solution)/shard_map/all_gather | solution.py:52
  9.3 688.8 %all-gather.14.cloned.1.call-start = ((), (), s32[]{:S(2)}) async-start(), calls=%async_computation.5 | async-start | bytes 5677056 | tf_op jit(solution)/shard_map/all_gather | solution.py:114
  9.9 756.0 %reduce-scatter.2.cloned.1.call-start = ((), (), s32[]{:S(2)}) async-start(), calls=%async_computation.6 | async-start | bytes 6881280 | tf_op jit(solution)/shard_map/reduce_scatter | solution.py:117
  59.8 157.4 %copy-start.2 = (f32[128]{0:T(128)S(1)}, f32[128]{0:T(128)}, u32[]{:S(2)}) copy-start(f32[128]{0:T(128)} %param.17) | copy-start | bytes 1540
  376.6 20.7 %collective-permute-start = (bf16[2,512,256]{2,1,0:T(8,128)(2,1)S(1)}, bf16[2,512,256]{2,1,0:T(8,128)(2,1)S(1)}, u32[]{:S(2)}, u32[]{:S(2)}) collective-permute-start(bf16[2,512,256]{2,1,0:T(8,128)(2,1)S(1)} %pad_maximum_fusion), channel_id=1, source_target_pairs={{0,8},{4,12},{8,16},{12,20},{16,24},{20,28},{24,32},{28,36},{32,40... | collective-permute-start | bytes 1572872 | tf_op jit(solution)/shard_map/ppermute | solution.py:20
  378.8 18.5 %collective-permute-start.1 = (bf16[2,512,256]{2,1,0:T(8,128)(2,1)S(1)}, bf16[2,512,256]{2,1,0:T(8,128)(2,1)S(1)}, u32[]{:S(2)}, u32[]{:S(2)}) collective-permute-start(bf16[2,512,256]{2,1,0:T(8,128)(2,1)S(1)} %pad_maximum_fusion), channel_id=1, source_target_pairs={{0,4},{4,8},{8,12},{12,16},{16,20},{20,24},{24,28},{28,32},{32,36}... | collective-permute-start | bytes 1572872 | tf_op jit(solution)/shard_map/ppermute | solution.py:20
  398.0 144.4 %copy-start.3 = (f32[128]{0:T(128)S(1)}, f32[128]{0:T(128)}, u32[]{:S(2)}) copy-start(f32[128]{0:T(128)} %param.16) | copy-start | bytes 1540
  705.4 70.5 %copy-start = (bf16[512,1344]{0,1:T(8,128)(2,1)S(1)}, bf16[512,1344]{0,1:T(8,128)(2,1)}, u32[]{:S(2)}) copy-start(bf16[512,1344]{0,1:T(8,128)(2,1)} %param.9) | copy-start | bytes 4128772
  705.4 70.5 %copy-start.1 = (f32[1344]{0:T(1024)S(1)}, f32[1344]{0:T(1024)}, u32[]{:S(2)}) copy-start(f32[1344]{0:T(1024)} %param.15) | copy-start | bytes 16132
Sparse Core Ops, SparseCore 0:
  9.0 46.9 all-gather.5
  57.7 154.0 all-gather.7
  213.4 157.2 all-gather.9
  372.2 162.4 all-gather.11
  536.2 161.8 all-gather.13
  705.6 60.2 reduce-scatter.1
where the time goes:
time: 787 us; the launch traced here: 786 us
  waiting for transfers between devices  713 us (91%)
  matrix products  33.6 us (4%)
  between operations  13.7 us (2%)
  other arithmetic  10.9 us (1%)
  blocking collectives  8.31 us (1%)
    all_gather x1, waiting for transfers between devices, local(): lax.all_gather(value_matrix, 'seq', axis=0, tiled=True)  153 us
    all_gather x1, waiting for transfers between devices, local(): lax.all_gather(key_matrix, 'seq', axis=0, tiled=True)  152 us
    all_gather x1, waiting for transfers between devices, local(): lax.all_gather(o_weight, 'seq', axis=1, tiled=True)  147 us
    all_gather x1, waiting for transfers between devices, local(): lax.all_gather(q_weight, 'seq', axis=0, tiled=True)  137 us
    reduce_scatter x1, waiting for transfers between devices, local(): lax.psum_scatter(terms.astype(jnp.bfloat16), 'mp', scatter_dimension=1, t...  60.4 us
    all_gather x1, waiting for transfers between devices, local(): whole = lax.all_gather(tokens, 'mp', axis=1, tiled=True)  45.5 us
  transfers between devices with their start and end apart: 8, of which 7 were waited for; matrix products, arithmetic and copies ran while one was open for 4% of the time, Pallas kernels for 0%

commit v1 on v0

v1 whole, which is shorter than its diff:
```python
import math

import jax
import jax.numpy as jnp
import numpy as np
from jax import lax
from jax.sharding import Mesh, PartitionSpec as P

MODEL_WIDTH = 5376
HEAD_SIZE = 128
WINDOW_LENGTH = 1024

score_scale = 168.0 ** (-0.5)
epsilon = 1e-06
SEQ = ("yl", "x", "z")
MP = ("yh", "c")


def shift(value, axis, step):
    count = lax.axis_size(axis)
    return lax.ppermute(value, axis, [(i, (i + step) % count) for i in range(count)])


def from_behind(value, steps):
    count = 32
    return lax.ppermute(value, SEQ, [(source, source + steps) for source in range(count - steps)])


def rms_heads(raw, gain, positions):
    normal = raw * lax.rsqrt(jnp.mean(raw * raw, axis=-1, keepdims=True) + epsilon) * gain
    half = raw.shape[-1] // 2
    freq = 10000.0 ** (-(jnp.arange(half, dtype=jnp.float32) * 2.0) / raw.shape[-1])
    angle = positions.astype(jnp.float32)[:, None] * freq[None, :]
    cosine = jnp.cos(angle)[:, None, :]
    sine = jnp.sin(angle)[:, None, :]
    first = normal[..., :half]
    second = normal[..., half:]
    return jnp.concatenate(
        [first * cosine - second * sine, second * cosine + first * sine], axis=-1
    )


def place(buffer, piece, index, axis):
    return lax.dynamic_update_index_in_dim(buffer, piece, index, axis)


def gather_two(own, first, second):
    at = lax.axis_index(first)
    line = jnp.zeros((4,) + own.shape, own.dtype)
    line = place(line, own, at, 0)
    for step in (1, 3, 2):
        line = place(line, shift(own, first, step), (at - step) % 4, 0)
    there = lax.axis_index(second)
    ahead = shift(line, second, 1)
    behind = shift(line, second, 3)
    far_low = shift(ahead[:2], second, 1)
    far_high = shift(behind[2:], second, 3)
    whole = jnp.zeros((4, 4) + own.shape, own.dtype)
    whole = place(whole, line, there, 1)
    whole = place(whole, ahead, (there - 1) % 4, 1)
    whole = place(whole, behind, (there + 1) % 4, 1)
    far = jnp.concatenate([far_low, far_high], axis=0)
    return place(whole, far, (there + 2) % 4, 1)


def local(
    tokens, q_weight, key_matrix, value_matrix, o_weight, pre_gain, post_gain, q_gain, k_gain
):
    rows = tokens.shape[0]
    yl, x, z, yh, c = (lax.axis_index(name) for name in ("yl", "x", "z", "yh", "c"))
    seq_index = (yl * 4 + x) * 4 + z
    whole = lax.all_gather(tokens, MP, axis=1, tiled=True)

    own = jnp.concatenate([q_weight, key_matrix, value_matrix], axis=1)
    other = shift(own, "yl", 1)
    near_weights = gather_two(own, "x", "z")
    far_weights = jnp.swapaxes(gather_two(other, "z", "x"), 0, 1)
    span = 16 * own.shape[0]
    near_weights = near_weights.reshape(span, own.shape[1])
    far_weights = far_weights.reshape(span, own.shape[1])

    turned = o_weight.T
    y = yh * 2 + yl
    flat = lambda p: (p % 2) * 2 + p // 2
    one = lax.ppermute(turned, ("yl", "yh"), [(flat(a), flat(b)) for a, b in ((0, 1), (2, 0), (1, 3), (3, 2))])
    two = lax.ppermute(turned, ("yl", "yh"), [(flat(a), flat(b)) for a, b in ((1, 2), (2, 1))])
    outer = (y == 0) | (y == 3)
    pair = jnp.concatenate([jnp.where(outer, turned, one), jnp.where(outer, one, two)], axis=1)
    out_all = lax.all_gather(pair, ("x", "z"), axis=0, tiled=True)
    half_rows = out_all.shape[0] // 2
    out_mine = lax.dynamic_slice_in_dim(out_all, c * half_rows, half_rows, 0)
    out_theirs = shift(lax.dynamic_slice_in_dim(out_all, (1 - c) * half_rows, half_rows, 0), "c", 1)

    wide = whole.astype(jnp.float32)
    normed = (
        wide * lax.rsqrt(jnp.mean(wide * wide, axis=1, keepdims=True) + epsilon) * pre_gain
    ).astype(jnp.bfloat16)
    near = lax.dynamic_slice_in_dim(normed, yl * span, span, 1)
    far = lax.dynamic_slice_in_dim(normed, (1 - yl) * span, span, 1)
    qkv = jnp.dot(near, near_weights, preferred_element_type=jnp.float32) + jnp.dot(
        far, far_weights, preferred_element_type=jnp.float32
    )
    q_cols = q_weight.shape[1]
    kv_cols = key_matrix.shape[1]
    q_sum = qkv[:, :q_cols]
    k_sum = qkv[:, q_cols : q_cols + kv_cols]
    v_sum = qkv[:, q_cols + kv_cols :]
    base = seq_index * rows
    positions = base + jnp.arange(rows, dtype=jnp.int32)
    local_kv = kv_cols // HEAD_SIZE
    keys_own = rms_heads(k_sum.reshape(rows, local_kv, HEAD_SIZE), k_gain, positions).astype(
        jnp.bfloat16
    )
    values_own = v_sum.astype(jnp.bfloat16)
    stacked = jnp.stack([keys_own.reshape(rows, kv_cols), values_own], axis=0)
    received = [from_behind(stacked, 2), from_behind(stacked, 1)]
    query_vectors = rms_heads(
        q_sum.reshape(rows, q_cols // HEAD_SIZE, HEAD_SIZE), q_gain, positions
    ).astype(jnp.bfloat16)
    joined = jnp.concatenate(received + [stacked], axis=1)
    key_vectors = joined[0].reshape(WINDOW_LENGTH + rows, local_kv, HEAD_SIZE)
    value_vectors = joined[1].reshape(WINDOW_LENGTH + rows, local_kv, HEAD_SIZE)
    head_group = q_cols // HEAD_SIZE // local_kv
    grouped_queries = query_vectors.reshape(rows, local_kv, head_group, HEAD_SIZE)
    scores = (
        jnp.einsum("qkgd,skd->kgqs", grouped_queries, key_vectors, preferred_element_type=jnp.float32)
        * score_scale
    )
    key_pos = base - WINDOW_LENGTH + jnp.arange(rows + WINDOW_LENGTH, dtype=jnp.int32)
    distance = positions[:, None] - key_pos[None, :]
    allowed = (distance >= 0) & (distance < WINDOW_LENGTH) & (key_pos >= 0)[None, :]
    weights = jnp.where(allowed[None, None], jnp.exp(scores), 0.0)
    denominator = jnp.sum(weights, axis=-1)
    mixed = jnp.einsum(
        "kgqs,skd->qkgd",
        weights.astype(jnp.bfloat16),
        value_vectors,
        preferred_element_type=jnp.float32,
    )
    mixed = mixed / jnp.transpose(denominator, (2, 0, 1))[..., None]
    context = mixed.astype(jnp.bfloat16).reshape(rows, q_cols)

    across = shift(context, "yh", 1)
    mine = jnp.concatenate([context, across], axis=1)
    theirs = shift(mine, "c", 1)
    share = lax.dot_general(
        mine, out_mine, (((1,), (1,)), ((), ())), preferred_element_type=jnp.float32
    ) + lax.dot_general(
        theirs, out_theirs, (((1,), (1,)), ((), ())), preferred_element_type=jnp.float32
    )
    total = lax.psum(jnp.sum(share * share, axis=1), MP)
    scale_rows = lax.rsqrt(total / MODEL_WIDTH + epsilon)
    return (tokens.astype(jnp.float32) + share * scale_rows[:, None] * post_gain).astype(
        jnp.bfloat16
    )


def solution(mesh):
    fine = Mesh(np.asarray(mesh.devices).reshape(2, 4, 4, 2, 2), SEQ + MP)
    return jax.shard_map(
        local,
        mesh=fine,
        in_specs=(
            P(SEQ, MP),
            P(SEQ, MP),
            P(SEQ, MP),
            P(SEQ, MP),
            P(MP, SEQ),
            P(),
            P(MP),
            P(),
            P(),
        ),
        out_specs=P(SEQ, MP),
        check_vma=False,
    )
```

time: 787 us -> 274 us (0.35)
  the two profiles are of different devices: /device:TPU:40 before, /device:TPU:6 now
where the time goes in v1:
time: 274 us; the launch traced here: 273 us
  waiting for transfers between devices  137 us (50%)
  starting transfers between devices  41.7 us (15%)
  matrix products  28.9 us (11%)
  other arithmetic  22.1 us (8%)
  local copies, waits for them, and re-layouts  18.9 us (7%)
  between operations  14.2 us (5%)
  blocking collectives  10.1 us (4%)
    ppermute x18, waiting for transfers between devices, shift(): lax.ppermute(value, axis, [(i, (i + step) % count) for i in range(count)])  127 us
    ppermute x18, starting transfers between devices, shift(): lax.ppermute(value, axis, [(i, (i + step) % count) for i in range(count)])  30.4 us
    psum x1, blocking collectives, local(): total = lax.psum(jnp.sum(share * share, axis=1), MP)  10.1 us
    ppermute x2, starting transfers between devices, from_behind(): lax.ppermute(value, SEQ, [(source, source + steps) for source in range(co...  8.35 us
    ppermute x2, waiting for transfers between devices, from_behind(): lax.ppermute(value, SEQ, [(source, source + steps) for source in range(co...  7.94 us
    dot_general x1, matrix products, local(): jnp.einsum('kgqs,skd->qkgd', weights.astype(jnp.bfloat16), value_vectors,...  7.51 us
    dot_general x1, matrix products, local(): jnp.einsum('qkgd,skd->kgqs', grouped_queries, key_vectors, preferred_elem...  6.23 us
  transfers between devices with their start and end apart: 24, of which 12 were waited for; matrix products, arithmetic and copies ran while one was open for 20% of the time, Pallas kernels for 0%

profile of v1, /device:TPU:6, one launch (start us, length us, event | category | flops | bytes accessed | tf_op | source)
XLA Modules:
  0.0 273.3 jit_solution(7486310524891646623)
XLA Ops:
  6.5 0.7 all-gather.3.cloned.1.call-update
  7.3 0.9 constant_dynamic-update-slice_fusion.2
  8.2 0.9 constant_dynamic-update-slice_fusion.1
  9.1 0.9 constant_dynamic-update-slice_fusion
  10.4 1.6 collective-permute-start.1
  12.1 1.4 collective-permute-start.2
  13.5 1.6 collective-permute-start.18
  15.1 1.3 collective-permute-start.19
  16.4 2.0 fusion.11
  18.8 1.8 collective-permute-done.18
  20.6 1.2 collective-permute-start.7
  21.9 0.8 pad_maximum_fusion.2
  22.7 13.0 %collective-permute-done.7 = bf16[168,1024]{1,0:T(8,128)(2,1)S(1)} collective-permute-done((bf16[168,1024]{1,0:T(8,128)(2,1)S(1)}, bf16[168,1024]{1,0:T(8,128)(2,1)S(1)}, u32[]{:S(2)}, u32[]{:S(2)}) %collective-permute-start.7) | collective-permute-done | bytes 344096 | tf_op jit(solution)/shard_map/ppermute | solution.py:21
  35.7 2.3 collective-permute-start.8
  38.1 2.1 collective-permute-start.3
  40.2 1.2 collective-permute-start.4
  41.4 1.1 collective-permute-start.9
  42.5 1.8 collective-permute-start.10
  44.5 4.7 %collective-permute-done.8 = bf16[168,1024]{1,0:T(8,128)(2,1)S(1)} collective-permute-done((bf16[168,1024]{1,0:T(8,128)(2,1)S(1)}, bf16[168,1024]{1,0:T(8,128)(2,1)S(1)}, u32[]{:S(2)}, u32[]{:S(2)}) %collective-permute-start.8) | collective-permute-done | bytes 344096 | tf_op jit(solution)/shard_map/ppermute | solution.py:21
  49.2 31.2 %collective-permute-done.9 = bf16[168,1024]{1,0:T(8,128)(2,1)S(1)} collective-permute-done((bf16[168,1024]{1,0:T(8,128)(2,1)S(1)}, bf16[168,1024]{1,0:T(8,128)(2,1)S(1)}, u32[]{:S(2)}, u32[]{:S(2)}) %collective-permute-start.9) | collective-permute-done | bytes 344096 | tf_op jit(solution)/shard_map/ppermute | solution.py:21
  80.4 6.3 %collective-permute-done.10 = bf16[168,1024]{1,0:T(8,128)(2,1)S(1)} collective-permute-done((bf16[168,1024]{1,0:T(8,128)(2,1)S(1)}, bf16[168,1024]{1,0:T(8,128)(2,1)S(1)}, u32[]{:S(2)}, u32[]{:S(2)}) %collective-permute-start.10) | collective-permute-done | bytes 344096 | tf_op jit(solution)/shard_map/ppermute | solution.py:21
  86.7 5.0 %collective-permute-start.11 = (bf16[4,168,1024]{2,1,0:T(8,128)(2,1)S(1)}, bf16[4,168,1024]{2,1,0:T(8,128)(2,1)S(1)}, u32[]{:S(2)}, u32[]{:S(2)}) collective-permute-start(bf16[4,168,1024]{2,1,0:T(8,128)(2,1)S(1)} %bitcast_dynamic-update-slice_fusion.6), channel_id=1, source_target_pairs={{0,16},{16,32},{32,48},{48,0},{1,17},{17,33},{33,49},{49,1},{2,18}... | collective-permute-start | bytes 4128776 | tf_op jit(solution)/shard_map/ppermute | solution.py:21
  91.7 1.0 multiply_cosine_fusion
  92.7 0.7 broadcast.165.clone.1
  93.6 0.7 broadcast.165.clone
  94.5 2.2 collective-permute-start.5
  96.7 1.4 collective-permute-start.6
  98.5 44.6 %collective-permute-done.11 = bf16[4,168,1024]{2,1,0:T(8,128)(2,1)S(1)} collective-permute-done((bf16[4,168,1024]{2,1,0:T(8,128)(2,1)S(1)}, bf16[4,168,1024]{2,1,0:T(8,128)(2,1)S(1)}, u32[]{:S(2)}, u32[]{:S(2)}) %collective-permute-start.11) | collective-permute-done | bytes 1376288 | tf_op jit(solution)/shard_map/ppermute | solution.py:21
  143.2 3.8 %collective-permute-start.13 = (bf16[2,168,1024]{2,1,0:T(8,128)(2,1)S(1)}, bf16[2,168,1024]{2,1,0:T(8,128)(2,1)S(1)}, u32[]{:S(2)}, u32[]{:S(2)}) collective-permute-start(bf16[2,168,1024]{2,1,0:T(8,128)(2,1)S(1)} %slice.55), channel_id=1, source_target_pairs={{0,16},{16,32},{32,48},{48,0},{1,17},{17,33},{33,49},{49,1},{2,18}... | collective-permute-start | bytes 2064392 | tf_op jit(solution)/shard_map/ppermute | solution.py:21
  147.8 7.6 %collective-permute-done.13 = bf16[2,168,1024]{2,1,0:T(8,128)(2,1)S(1)} collective-permute-done((bf16[2,168,1024]{2,1,0:T(8,128)(2,1)S(1)}, bf16[2,168,1024]{2,1,0:T(8,128)(2,1)S(1)}, u32[]{:S(2)}, u32[]{:S(2)}) %collective-permute-start.13) | collective-permute-done | bytes 688160 | tf_op jit(solution)/shard_map/ppermute | solution.py:21
  155.4 4.0 %collective-permute-done.14 = bf16[2,168,1024]{2,1,0:T(8,128)(2,1)S(1)} collective-permute-done((bf16[2,168,1024]{2,1,0:T(8,128)(2,1)S(1)}, bf16[2,168,1024]{2,1,0:T(8,128)(2,1)S(1)}, u32[]{:S(2)}, u32[]{:S(2)}) %collective-permute-start.14) | collective-permute-done | bytes 688160 | tf_op jit(solution)/shard_map/ppermute | solution.py:21
  159.6 3.1 %copy.62 = bf16[4,4,168,1024]{3,2,1,0:T(8,128)(2,1)} copy(bf16[4,4,168,1024]{3,2,0,1:T(8,128)(2,1)S(1)} %bitcast.87) | data formatting | bytes 11010048 | tf_op jit(solution)/shard_map/transpose | solution.py:77
  162.6 3.9 %fusion = f32[512]{0:T(512)S(1)} fusion(bf16[512,5376]{0,1:T(8,128)(2,1)} %all-gather.3.cloned.1.call-done), kind=kLoop, calls=%fused_computation.3 | loop fusion | flops 8257024 | bytes 5507072 | tf_op jit(solution)/shard_map/reduce_sum | solution.py:96
  166.8 2.4 fusion.2
  169.2 3.2 %fusion.13 = f32[512,1024]{1,0:T(8,128)S(1)} fusion(bf16[2688,1024]{1,0:T(8,128)(2,1)S(1)} %bitcast.90, bf16[512,5376]{0,1:T(8,128)(2,1)S(1)} %fusion.2, s32[]{:T(128)S(6)} %select_n.132), kind=kOutput, calls=%fused_computation.20 | convolution fusion | flops 2818572288 | bytes 10354692 | tf_op jit(solution)/shard_map/dot_general | solution.py:100
  172.4 3.2 %fusion.17 = f32[512,1024]{1,0:T(8,128)S(1)} fusion(f32[512,1024]{1,0:T(8,128)S(1)} %fusion.13, bf16[2688,1024]{1,0:T(8,128)(2,1)S(1)} %bitcast.93, bf16[512,5376]{0,1:T(8,128)(2,1)S(1)} %fusion.2, s32[]{:T(128)S(6)} %select_n.117), kind=kOutput, calls=%fused_computation.25 | convolution fusion | flops 2819096576 | bytes 12451844 | tf_op jit(solution)/shard_map/dot_general | solution.py:100
  175.8 1.3 copy-done.3
  178.0 0.7 multiply_multiply_fusion.1
  178.7 0.8 subtract_convert_fusion.1
  179.6 0.7 pad_maximum_fusion.3
  180.5 1.1 fusion.32
  181.6 0.8 pad_maximum_fusion.1
  182.4 1.9 collective-permute-start.15
  184.3 6.4 %collective-permute-start.16 = (bf16[2,512,256]{2,1,0:T(8,128)(2,1)}, bf16[2,512,256]{2,1,0:T(8,128)(2,1)}, u32[]{:S(2)}, u32[]{:S(2)}) collective-permute-start(bf16[2,512,256]{2,1,0:T(8,128)(2,1)} %pad_maximum_fusion.1), channel_id=1, source_target_pairs={{0,4},{4,8},{8,12},{12,16},{16,20},{20,24},{24,28},{28,32},{32,36}... | collective-permute-start | bytes 1572872 | tf_op jit(solution)/shard_map/ppermute | solution.py:26
  191.8 0.7 multiply_multiply_fusion
  192.5 0.8 subtract_convert_fusion
  193.4 0.9 copy.67
  194.2 0.9 copy.68
  195.1 1.1 collective-permute-done.15
  196.3 6.8 %collective-permute-done.16 = bf16[2,512,256]{2,1,0:T(8,128)(2,1)} collective-permute-done((bf16[2,512,256]{2,1,0:T(8,128)(2,1)}, bf16[2,512,256]{2,1,0:T(8,128)(2,1)}, u32[]{:S(2)}, u32[]{:S(2)}) %collective-permute-start.16) | collective-permute-done | bytes 524320 | tf_op jit(solution)/shard_map/ppermute | solution.py:26
  203.1 1.3 maximum_maximum_fusion
  204.5 1.1 reshape_squeeze.7
  205.6 2.2 constant_dynamic-slice_fusion
  208.0 6.2 %fusion.3 = (f32[2,2,512]{2,1,0:T(2,128)S(1)}, f32[2,1536,512,2]{2,1,3,0:T(8,128)}) fusion(pred[512,1536]{0,1:T(8,128)(4,1)S(1)} %copy-done.4, bf16[512,2,2,64]{3,0,2,1:T(8,128)(2,1)S(1)} %bitcast.97, bf16[512,2,2,64]{3,0,2,1:T(8,128)(2,1)S(1)} %bitcast.96, bf16[1536,2,128,1]{2,1,0,3:T(2,128)(2,1)S(1)} %bitcast.94), kind=kOutput, calls=%fused_computation.6 | convolution fusion | flops 815790080 | bytes 14688256 | tf_op jit(solution)/shard_map/qkgd,skd->kgqs/dot_general | solution.py:126
  214.3 1.2 copy.75
  215.4 7.5 %divide_convert_fusion = bf16[512,2,2,128]{0,3,2,1:T(8,128)(2,1)S(1)} fusion(bf16[1536,2,128,1]{0,2,3,1:T(8,128)(2,1)} %bitcast.95, f32[2,1536,512,2]{2,1,3,0:T(8,128)} %get-tuple-element.16, pred[512,1536]{0,1:T(8,128)(4,1)} %fusion.11, f32[512,2,2]{0,2,1:T(2,128)S(1)} %bitcast.103), kind=kOutput, calls=%fused_computation.38 | convolution fusion | flops 815267840 | bytes 14688256 | tf_op jit(solution)/shard_map/kgqs,skd->qkgd/dot_general | solution.py:134
  223.0 4.6 %collective-permute-start.17 = (bf16[512,512]{0,1:T(8,128)(2,1)S(1)}, bf16[512,512]{0,1:T(8,128)(2,1)S(1)}, u32[]{:S(2)}, u32[]{:S(2)}) collective-permute-start(bf16[512,512]{0,1:T(8,128)(2,1)S(1)} %bitcast.98), channel_id=1, source_target_pairs={{0,2},{2,0},{1,3},{3,1},{4,6},{6,4},{5,7},{7,5},{8,10},{10,8},{9,1... | collective-permute-start | bytes 1572872 | tf_op jit(solution)/shard_map/ppermute | solution.py:21
  227.5 12.4 %collective-permute-done.17 = bf16[512,512]{0,1:T(8,128)(2,1)S(1)} collective-permute-done((bf16[512,512]{0,1:T(8,128)(2,1)S(1)}, bf16[512,512]{0,1:T(8,128)(2,1)S(1)}, u32[]{:S(2)}, u32[]{:S(2)}) %collective-permute-start.17) | collective-permute-done | bytes 524320 | tf_op jit(solution)/shard_map/ppermute | solution.py:21
  239.9 1.1 pad_maximum_fusion
  241.1 3.0 %collective-permute-done.20 = bf16[512,1024]{0,1:T(8,128)(2,1)} collective-permute-done((bf16[512,1024]{0,1:T(8,128)(2,1)}, bf16[512,1024]{0,1:T(8,128)(2,1)}, u32[]{:S(2)}, u32[]{:S(2)}) %collective-permute-start.20) | collective-permute-done | bytes 1048608 | tf_op jit(solution)/shard_map/ppermute | solution.py:21
  244.1 3.7 %fusion.41 = f32[512,1344]{0,1:T(8,128)S(1)} fusion(bf16[1344,1024]{1,0:T(8,128)(2,1)} %collective-permute-done.21, bf16[512,1024]{0,1:T(8,128)(2,1)} %collective-permute-done.20), kind=kOutput, calls=%fused_computation.89 | convolution fusion | flops 1409286144 | bytes 6553600 | tf_op jit(solution)/shard_map/dot_general | solution.py:148
  247.8 5.2 %multiply_reduce_fusion = (f32[512]{0:T(512)S(1)}, f32[512,1344]{0,1:T(8,128)}) fusion(f32[512,1344]{0,1:T(8,128)S(1)} %fusion.41, bf16[512,512]{0,1:T(8,128)(2,1)S(1)} %copy-done.11, bf16[512,512]{0,1:T(8,128)(2,1)S(1)} %bitcast.100, bf16[2688,1024]{1,0:T(8,128)(2,1)} %all-gather.5.cloned.1.call-done, s32[]{:T(128)S(6)} %select_n.145), kind=kOutput, calls=%fused_computation.18 | convolution fusion | flops 1413447168 | bytes 9308164 | tf_op jit(solution)/shard_map/dot_general | solution.py:146
  253.0 10.1 %psum.7 = f32[512]{0:T(512)S(1)} all-reduce(f32[512]{0:T(512)S(1)} %get-tuple-element.17), channel_id=1, replica_groups=mesh['yl'=2,'x'=4,'z'=4,'yh'=2,'c'=2] {'yh','c'}, use_global_device_ids=true, to_apply=%region_5.6 | all-reduce | flops 512 | bytes 4096 | tf_op jit(solution)/shard_map/psum | solution.py:151
  263.1 3.3 %add_convert_fusion = bf16[512,1344]{0,1:T(8,128)(2,1)} fusion(f32[512,1344]{0,1:T(8,128)} %get-tuple-element.18, bf16[512,1344]{0,1:T(8,128)(2,1)S(1)} %copy-done.2, f32[1344]{0:T(1024)S(1)} %copy-done.14, f32[512]{0:T(512)S(1)} %add_rsqrt_fusion.2), kind=kLoop, calls=%fused_computation.17 | loop fusion | flops 3440640 | bytes 5512448 | tf_op jit(solution)/shard_map/convert_element_type | solution.py:153
  (102 shorter events, 5.8 us)
Async XLA Ops:
  6.5 15.3 %copy-start.12 = (bf16[512,168]{0,1:T(8,128)(2,1)S(1)}, bf16[512,168]{0,1:T(8,128)(2,1)}, u32[]{:S(2)}) copy-start(bf16[512,168]{0,1:T(8,128)(2,1)} %param.13) | copy-start | bytes 516100
  6.5 156.1 %all-gather.3.cloned.1.call-start = ((), (), s32[]{:S(2)}) async-start(), calls=%async_computation | async-start | bytes 6881280 | tf_op jit(solution)/shard_map/all_gather | solution.py:72
  7.3 198.3 %all-gather.5.cloned.1.call-start = ((), (), s32[]{:S(2)}) async-start(), calls=%async_computation.1 | async-start | bytes 5849088 | tf_op jit(solution)/shard_map/all_gather | solution.py:89
  10.0 27.9 %collective-permute-start = (bf16[168,1024]{1,0:T(8,128)(2,1)S(1)}, bf16[168,1024]{1,0:T(8,128)(2,1)S(1)}, u32[]{:S(2)}, u32[]{:S(2)}) collective-permute-start(bf16[168,1024]{1,0:T(8,128)(2,1)S(1)} %constant_dynamic-update-slice_fusion), channel_id=1, source_target_pairs={{0,16},{16,32},{32,48},{48,0},{1,17},{17,33},{33,49},{49,1},{2,18}... | collective-permute-start | bytes 1032200 | tf_op jit(solution)/shard_map/ppermute | solution.py:21
  10.4 27.5 %collective-permute-start.1 = (bf16[168,1024]{1,0:T(8,128)(2,1)S(1)}, bf16[168,1024]{1,0:T(8,128)(2,1)S(1)}, u32[]{:S(2)}, u32[]{:S(2)}) collective-permute-start(bf16[168,1024]{1,0:T(8,128)(2,1)S(1)} %constant_dynamic-update-slice_fusion), channel_id=1, source_target_pairs={{0,48},{16,0},{32,16},{48,32},{1,49},{17,1},{33,17},{49,33},{2,50}... | collective-permute-start | bytes 1032200 | tf_op jit(solution)/shard_map/ppermute | solution.py:21
  12.1 26.0 %collective-permute-start.2 = (bf16[168,1024]{1,0:T(8,128)(2,1)S(1)}, bf16[168,1024]{1,0:T(8,128)(2,1)S(1)}, u32[]{:S(2)}, u32[]{:S(2)}) collective-permute-start(bf16[168,1024]{1,0:T(8,128)(2,1)S(1)} %constant_dynamic-update-slice_fusion), channel_id=1, source_target_pairs={{0,32},{16,48},{32,0},{48,16},{1,33},{17,49},{33,1},{49,17},{2,34}... | collective-permute-start | bytes 1032200 | tf_op jit(solution)/shard_map/ppermute | solution.py:21
  13.5 7.1 %collective-permute-start.18 = (bf16[168,512]{1,0:T(8,128)(2,1)}, bf16[168,512]{1,0:T(8,128)(2,1)S(1)}, u32[]{:S(2)}, u32[]{:S(2)}) collective-permute-start(bf16[168,512]{1,0:T(8,128)(2,1)} %bitcast.101), channel_id=1, source_target_pairs={{0,64},{2,0},{64,66},{66,2},{1,65},{3,1},{65,67},{67,3},{4,68},{6,... | collective-permute-start | bytes 516104 | tf_op jit(solution)/shard_map/ppermute | solution.py:85
  15.1 6.8 %collective-permute-start.19 = (bf16[168,512]{1,0:T(8,128)(2,1)}, bf16[168,512]{1,0:T(8,128)(2,1)}, u32[]{:S(2)}, u32[]{:S(2)}) collective-permute-start(bf16[168,512]{1,0:T(8,128)(2,1)} %bitcast.102), channel_id=1, source_target_pairs={{64,2},{2,64},{65,3},{3,65},{68,6},{6,68},{69,7},{7,69},{72,10},{1... | collective-permute-start | bytes 516104 | tf_op jit(solution)/shard_map/ppermute | solution.py:86
  20.6 15.1 %collective-permute-start.7 = (bf16[168,1024]{1,0:T(8,128)(2,1)S(1)}, bf16[168,1024]{1,0:T(8,128)(2,1)S(1)}, u32[]{:S(2)}, u32[]{:S(2)}) collective-permute-start(bf16[168,1024]{1,0:T(8,128)(2,1)S(1)} %constant_dynamic-update-slice_fusion), channel_id=1, source_target_pairs={{0,64},{64,0},{1,65},{65,1},{2,66},{66,2},{3,67},{67,3},{4,68},{68... | collective-permute-start | bytes 1032200 | tf_op jit(solution)/shard_map/ppermute | solution.py:21
  35.7 13.5 %collective-permute-start.8 = (bf16[168,1024]{1,0:T(8,128)(2,1)S(1)}, bf16[168,1024]{1,0:T(8,128)(2,1)S(1)}, u32[]{:S(2)}, u32[]{:S(2)}) collective-permute-start(bf16[168,1024]{1,0:T(8,128)(2,1)S(1)} %collective-permute-done.7), channel_id=1, source_target_pairs={{0,4},{4,8},{8,12},{12,0},{1,5},{5,9},{9,13},{13,1},{2,6},{6,10},{... | collective-permute-start | bytes 1032200 | tf_op jit(solution)/shard_map/ppermute | solution.py:21
  38.1 56.4 %collective-permute-start.3 = (bf16[4,168,1024]{2,1,0:T(8,128)(2,1)S(1)}, bf16[4,168,1024]{2,1,0:T(8,128)(2,1)S(1)}, u32[]{:S(2)}, u32[]{:S(2)}) collective-permute-start(bf16[4,168,1024]{2,1,0:T(8,128)(2,1)S(1)} %bitcast_dynamic-update-slice_fusion.10), channel_id=1, source_target_pairs={{0,4},{4,8},{8,12},{12,0},{1,5},{5,9},{9,13},{13,1},{2,6},{6,10},{... | collective-permute-start | bytes 4128776 | tf_op jit(solution)/shard_map/ppermute | solution.py:21
  40.2 56.5 %collective-permute-start.4 = (bf16[4,168,1024]{2,1,0:T(8,128)(2,1)S(1)}, bf16[4,168,1024]{2,1,0:T(8,128)(2,1)S(1)}, u32[]{:S(2)}, u32[]{:S(2)}) collective-permute-start(bf16[4,168,1024]{2,1,0:T(8,128)(2,1)S(1)} %bitcast_dynamic-update-slice_fusion.10), channel_id=1, source_target_pairs={{0,12},{4,0},{8,4},{12,8},{1,13},{5,1},{9,5},{13,9},{2,14},{6,2},{... | collective-permute-start | bytes 4128776 | tf_op jit(solution)/shard_map/ppermute | solution.py:21
  41.4 39.0 %collective-permute-start.9 = (bf16[168,1024]{1,0:T(8,128)(2,1)S(1)}, bf16[168,1024]{1,0:T(8,128)(2,1)S(1)}, u32[]{:S(2)}, u32[]{:S(2)}) collective-permute-start(bf16[168,1024]{1,0:T(8,128)(2,1)S(1)} %collective-permute-done.7), channel_id=1, source_target_pairs={{0,12},{4,0},{8,4},{12,8},{1,13},{5,1},{9,5},{13,9},{2,14},{6,2},{... | collective-permute-start | bytes 1032200 | tf_op jit(solution)/shard_map/ppermute | solution.py:21
  42.5 44.2 %collective-permute-start.10 = (bf16[168,1024]{1,0:T(8,128)(2,1)S(1)}, bf16[168,1024]{1,0:T(8,128)(2,1)S(1)}, u32[]{:S(2)}, u32[]{:S(2)}) collective-permute-start(bf16[168,1024]{1,0:T(8,128)(2,1)S(1)} %collective-permute-done.7), channel_id=1, source_target_pairs={{0,8},{4,12},{8,0},{12,4},{1,9},{5,13},{9,1},{13,5},{2,10},{6,14},... | collective-permute-start | bytes 1032200 | tf_op jit(solution)/shard_map/ppermute | solution.py:21
  86.7 56.4 %collective-permute-start.11 = (bf16[4,168,1024]{2,1,0:T(8,128)(2,1)S(1)}, bf16[4,168,1024]{2,1,0:T(8,128)(2,1)S(1)}, u32[]{:S(2)}, u32[]{:S(2)}) collective-permute-start(bf16[4,168,1024]{2,1,0:T(8,128)(2,1)S(1)} %bitcast_dynamic-update-slice_fusion.6), channel_id=1, source_target_pairs={{0,16},{16,32},{32,48},{48,0},{1,17},{17,33},{33,49},{49,1},{2,18}... | collective-permute-start | bytes 4128776 | tf_op jit(solution)/shard_map/ppermute | solution.py:21
  91.7 55.2 %collective-permute-start.12 = (bf16[4,168,1024]{2,1,0:T(8,128)(2,1)S(1)}, bf16[4,168,1024]{2,1,0:T(8,128)(2,1)S(1)}, u32[]{:S(2)}, u32[]{:S(2)}) collective-permute-start(bf16[4,168,1024]{2,1,0:T(8,128)(2,1)S(1)} %bitcast_dynamic-update-slice_fusion.6), channel_id=1, source_target_pairs={{0,48},{16,0},{32,16},{48,32},{1,49},{17,1},{33,17},{49,33},{2,50}... | collective-permute-start | bytes 4128776 | tf_op jit(solution)/shard_map/ppermute | solution.py:21
  94.5 53.1 %collective-permute-start.5 = (bf16[2,168,1024]{2,1,0:T(8,128)(2,1)S(1)}, bf16[2,168,1024]{2,1,0:T(8,128)(2,1)S(1)}, u32[]{:S(2)}, u32[]{:S(2)}) collective-permute-start(bf16[2,168,1024]{2,1,0:T(8,128)(2,1)S(1)} %slice.53), channel_id=1, source_target_pairs={{0,4},{4,8},{8,12},{12,0},{1,5},{5,9},{9,13},{13,1},{2,6},{6,10},{... | collective-permute-start | bytes 2064392 | tf_op jit(solution)/shard_map/ppermute | solution.py:21
  96.7 50.8 %collective-permute-start.6 = (bf16[2,168,1024]{2,1,0:T(8,128)(2,1)S(1)}, bf16[2,168,1024]{2,1,0:T(8,128)(2,1)S(1)}, u32[]{:S(2)}, u32[]{:S(2)}) collective-permute-start(bf16[2,168,1024]{2,1,0:T(8,128)(2,1)S(1)} %slice.54), channel_id=1, source_target_pairs={{0,12},{4,0},{8,4},{12,8},{1,13},{5,1},{9,5},{13,9},{2,14},{6,2},{... | collective-permute-start | bytes 2064392 | tf_op jit(solution)/shard_map/ppermute | solution.py:21
  143.2 12.2 %collective-permute-start.13 = (bf16[2,168,1024]{2,1,0:T(8,128)(2,1)S(1)}, bf16[2,168,1024]{2,1,0:T(8,128)(2,1)S(1)}, u32[]{:S(2)}, u32[]{:S(2)}) collective-permute-start(bf16[2,168,1024]{2,1,0:T(8,128)(2,1)S(1)} %slice.55), channel_id=1, source_target_pairs={{0,16},{16,32},{32,48},{48,0},{1,17},{17,33},{33,49},{49,1},{2,18}... | collective-permute-start | bytes 2064392 | tf_op jit(solution)/shard_map/ppermute | solution.py:21
  147.0 12.4 %collective-permute-start.14 = (bf16[2,168,1024]{2,1,0:T(8,128)(2,1)S(1)}, bf16[2,168,1024]{2,1,0:T(8,128)(2,1)S(1)}, u32[]{:S(2)}, u32[]{:S(2)}) collective-permute-start(bf16[2,168,1024]{2,1,0:T(8,128)(2,1)S(1)} %slice.56), channel_id=1, source_target_pairs={{0,48},{16,0},{32,16},{48,32},{1,49},{17,1},{33,17},{49,33},{2,50}... | collective-permute-start | bytes 2064392 | tf_op jit(solution)/shard_map/ppermute | solution.py:21
  147.7 11.8 %copy-start.1 = (bf16[4,4,168,1024]{3,2,1,0:T(8,128)(2,1)}, bf16[4,4,168,1024]{3,2,1,0:T(8,128)(2,1)S(1)}, u32[]{:S(2)}) copy-start(bf16[4,4,168,1024]{3,2,1,0:T(8,128)(2,1)S(1)} %fusion.20) | copy-start | bytes 16515076
  159.5 7.0 %copy-start.13 = (f32[5376]{0:T(1024)S(1)}, f32[5376]{0:T(1024)}, u32[]{:S(2)}) copy-start(f32[5376]{0:T(1024)} %param.14) | copy-start | bytes 64516
  162.6 4.2 %copy-start = (bf16[512,5376]{0,1:T(8,128)(2,1)S(1)}, bf16[512,5376]{0,1:T(8,128)(2,1)}, u32[]{:S(2)}) copy-start(bf16[512,5376]{0,1:T(8,128)(2,1)} %all-gather.3.cloned.1.call-done) | copy-start | bytes 16515076
  162.6 6.6 %slice-start = ((s8[5505024]{0:T(1024)(128)(4,1)}), s8[4194304]{0:T(1024)(128)(4,1)S(1)}, s32[]{:S(2)}) async-start(s8[5505024]{0:T(1024)(128)(4,1)} %bitcast.88), calls=%async_computation.2 | async-start | bytes 8388608
  166.8 2.4 slice-start.1
  166.8 5.6 %slice-start.2 = ((s8[5505024]{0:T(1024)(128)(4,1)}), s8[4194304]{0:T(1024)(128)(4,1)S(1)}, s32[]{:S(2)}) async-start(s8[5505024]{0:T(1024)(128)(4,1)} %bitcast.91), calls=%async_computation.4 | async-start | bytes 8388608
  169.2 3.2 %slice-start.3 = ((s8[5505024]{0:T(1024)(128)(4,1)}), s8[1310720]{0:T(1024)(128)(4,1)S(1)}, s32[]{:S(2)}) async-start(s8[5505024]{0:T(1024)(128)(4,1)} %bitcast.91), calls=%async_computation.5 | async-start | bytes 2621440
  175.6 1.4 copy-start.3
  175.7 2.4 copy-start.15
  180.5 11.3 %copy-start.16 = (f32[128]{0:T(128)S(1)}, f32[128]{0:T(128)}, u32[]{:S(2)}) copy-start(f32[128]{0:T(128)} %param.16) | copy-start | bytes 1540
  182.4 13.9 %collective-permute-start.15 = (bf16[2,512,256]{2,1,0:T(8,128)(2,1)}, bf16[2,512,256]{2,1,0:T(8,128)(2,1)}, u32[]{:S(2)}, u32[]{:S(2)}) collective-permute-start(bf16[2,512,256]{2,1,0:T(8,128)(2,1)} %pad_maximum_fusion.1), channel_id=1, source_target_pairs={{0,8},{4,12},{8,16},{12,20},{16,24},{20,28},{24,32},{28,36},{32,40... | collective-permute-start | bytes 1572872 | tf_op jit(solution)/shard_map/ppermute | solution.py:26
  184.3 18.8 %collective-permute-start.16 = (bf16[2,512,256]{2,1,0:T(8,128)(2,1)}, bf16[2,512,256]{2,1,0:T(8,128)(2,1)}, u32[]{:S(2)}, u32[]{:S(2)}) collective-permute-start(bf16[2,512,256]{2,1,0:T(8,128)(2,1)} %pad_maximum_fusion.1), channel_id=1, source_target_pairs={{0,4},{4,8},{8,12},{12,16},{16,20},{20,24},{24,28},{28,32},{32,36}... | collective-permute-start | bytes 1572872 | tf_op jit(solution)/shard_map/ppermute | solution.py:26
  205.5 2.3 copy-start.4
  205.5 2.3 copy-start.5
  205.5 2.3 copy-start.6
  205.6 2.5 copy-start.7
  207.8 36.3 %collective-permute-start.21 = (bf16[1344,1024]{1,0:T(8,128)(2,1)S(1)}, bf16[1344,1024]{1,0:T(8,128)(2,1)}, u32[]{:S(2)}, u32[]{:S(2)}) collective-permute-start(bf16[1344,1024]{1,0:T(8,128)(2,1)S(1)} %constant_dynamic-slice_fusion), channel_id=1, source_target_pairs={{0,1},{1,0},{2,3},{3,2},{4,5},{5,4},{6,7},{7,6},{8,9},{9,8},{10,11... | collective-permute-start | bytes 8257544 | tf_op jit(solution)/shard_map/ppermute | solution.py:21
  222.9 17.0 %copy-start.8 = (bf16[512,2,2,128]{0,3,2,1:T(8,128)(2,1)}, bf16[512,2,2,128]{0,3,2,1:T(8,128)(2,1)S(1)}, u32[]{:S(2)}) copy-start(bf16[512,2,2,128]{0,3,2,1:T(8,128)(2,1)S(1)} %divide_convert_fusion) | copy-start | bytes 1572868
  223.0 17.0 %collective-permute-start.17 = (bf16[512,512]{0,1:T(8,128)(2,1)S(1)}, bf16[512,512]{0,1:T(8,128)(2,1)S(1)}, u32[]{:S(2)}, u32[]{:S(2)}) collective-permute-start(bf16[512,512]{0,1:T(8,128)(2,1)S(1)} %bitcast.98), channel_id=1, source_target_pairs={{0,2},{2,0},{1,3},{3,1},{4,6},{6,4},{5,7},{7,5},{8,10},{10,8},{9,1... | collective-permute-start | bytes 1572872 | tf_op jit(solution)/shard_map/ppermute | solution.py:21
  239.9 1.2 copy-start.10
  241.1 3.0 %collective-permute-start.20 = (bf16[512,1024]{0,1:T(8,128)(2,1)}, bf16[512,1024]{0,1:T(8,128)(2,1)}, u32[]{:S(2)}, u32[]{:S(2)}) collective-permute-start(bf16[512,1024]{0,1:T(8,128)(2,1)} %pad_maximum_fusion), channel_id=1, source_target_pairs={{0,1},{1,0},{2,3},{3,2},{4,5},{5,4},{6,7},{7,6},{8,9},{9,8},{10,11... | collective-permute-start | bytes 3145736 | tf_op jit(solution)/shard_map/ppermute | solution.py:21
  241.1 6.7 %copy-start.9 = (bf16[512,2,2,128]{0,3,2,1:T(8,128)(2,1)S(1)}, bf16[512,2,2,128]{0,3,2,1:T(8,128)(2,1)}, u32[]{:S(2)}) copy-start(bf16[512,2,2,128]{0,3,2,1:T(8,128)(2,1)} %copy-done.8) | copy-start | bytes 1572868
  241.1 6.7 %copy-start.11 = (bf16[512,512]{0,1:T(8,128)(2,1)S(1)}, bf16[512,512]{0,1:T(8,128)(2,1)}, u32[]{:S(2)}) copy-start(bf16[512,512]{0,1:T(8,128)(2,1)} %copy-done.10) | copy-start | bytes 1572868
  247.8 15.3 %copy-start.2 = (bf16[512,1344]{0,1:T(8,128)(2,1)S(1)}, bf16[512,1344]{0,1:T(8,128)(2,1)}, u32[]{:S(2)}) copy-start(bf16[512,1344]{0,1:T(8,128)(2,1)} %param.9) | copy-start | bytes 4128772
  247.8 15.3 %copy-start.14 = (f32[1344]{0:T(1024)S(1)}, f32[1344]{0:T(1024)}, u32[]{:S(2)}) copy-start(f32[1344]{0:T(1024)} %param.15) | copy-start | bytes 16132
Sparse Core Ops, SparseCore 0:
  9.0 52.9 all-gather.2
  64.2 78.8 all-gather.4

commit v2 on v1

v2 whole, which is shorter than its diff:
```python
import functools

import jax
import jax.numpy as jnp
import numpy as np
from jax import lax
from jax.experimental import pallas as pl
from jax.experimental.pallas import tpu as pltpu
from jax.sharding import Mesh, PartitionSpec as P

MODEL_WIDTH = 5376
HEAD_SIZE = 128
WINDOW_LENGTH = 1024
SHARD = MODEL_WIDTH // 32

score_scale = 168.0 ** (-0.5)
epsilon = 1e-06
SEQ = ("yl", "x", "z")
MP = ("yh", "c")


def shift(value, axis, step):
    count = lax.axis_size(axis)
    return lax.ppermute(value, axis, [(i, (i + step) % count) for i in range(count)])


def from_behind(value, steps):
    count = 32
    return lax.ppermute(value, SEQ, [(source, source + steps) for source in range(count - steps)])


def later(values, done):
    return lax.optimization_barrier((values, done))[0]


def place(buffer, piece, index):
    return lax.dynamic_update_index_in_dim(buffer, piece, index, 0)


def in_line(pieces, at):
    line = jnp.zeros((4,) + pieces[0].shape, pieces[0].dtype)
    for piece, offset in zip(pieces, (0, -1, 1, 2)):
        line = place(line, piece, (at + offset) % 4)
    return line.reshape(4 * pieces[0].shape[0], -1)


def norm_kernel(side, own_ref, other_ref, own_gain, other_gain, near_ref, far_ref):
    own = own_ref[0].astype(jnp.float32)
    other = other_ref[0].astype(jnp.float32)
    total = jnp.sum(own * own, axis=-1, keepdims=True) + jnp.sum(other * other, axis=-1, keepdims=True)
    scale = lax.rsqrt((total[0] + total[1]) / MODEL_WIDTH + epsilon)
    own = (own * scale[None] * own_gain[0]).astype(jnp.bfloat16)
    other = (other * scale[None] * other_gain[0]).astype(jnp.bfloat16)
    for i in range(4):
        for j in range(4):
            start = ((j % 2) * 4 + i) * SHARD
            near_ref[i, :, j * SHARD : (j + 1) * SHARD] = own[j // 2][:, start : start + SHARD]
        far_ref[i] = other[i // 2][:, (i % 2) * 4 * SHARD : ((i % 2) * 4 + 4) * SHARD]


def norm_parts(pieces, gain, side):
    rows = pieces.shape[1]
    width = pieces.shape[2]
    step = 64
    pieces = pieces.reshape(2, 2, rows, width)
    gain = gain.reshape(2, 2, 1, width)
    half = lambda flip: pl.BlockSpec((1, 2, step, width), lambda i, s: (s[flip], 0, i, 0))
    gains = lambda flip: pl.BlockSpec((1, 2, 1, width), lambda i, s: (s[flip], 0, 0, 0))
    out = pl.BlockSpec((4, step, 4 * SHARD), lambda i, s: (0, i, 0))
    shape = jax.ShapeDtypeStruct((4, rows, 4 * SHARD), jnp.bfloat16)
    return pl.pallas_call(
        norm_kernel,
        grid_spec=pltpu.PrefetchScalarGridSpec(
            num_scalar_prefetch=1,
            grid=(rows // step,),
            in_specs=[half(0), half(1), gains(0), gains(1)],
            out_specs=[out, out],
        ),
        out_shape=[shape, shape],
        compiler_params=pltpu.CompilerParams(vmem_limit_bytes=40 << 20),
        cost_estimate=pl.CostEstimate(flops=20_000_000, bytes_accessed=12_000_000, transcendentals=0),
    )(jnp.stack([side, 1 - side]), pieces, pieces, gain, gain)


def accumulate(index, near_ref, far_ref, weights, w_buf, t_buf, sems, total, n_near):
    copies = []
    for k, weight in enumerate(weights):
        source = near_ref if k < n_near else far_ref
        copies.append(
            (
                pltpu.make_async_copy(source.at[index[k]], t_buf.at[k], sems.at[0, k]),
                pltpu.make_async_copy(weight, w_buf.at[k], sems.at[1, k]),
            )
        )
    for pair in copies:
        for copy in pair:
            copy.start()
    rows = total.shape[0]
    for k, pair in enumerate(copies):
        for copy in pair:
            copy.wait()

        @pl.loop(0, rows // 128)
        def _(i):
            at = pl.ds(pl.multiple_of(i * 128, 128), 128)
            part = jnp.dot(t_buf[k, at, :], w_buf[k], preferred_element_type=jnp.float32)
            total[at, :] = part if (k == 0 and n_near == 3) else total[at, :] + part


def early_kernel(index, near_ref, far_ref, *refs):
    weights, (total, w_buf, t_buf, sems) = refs[:6], refs[6:]
    accumulate(index, near_ref, far_ref, weights, w_buf, t_buf, sems, total, 3)


def early_product(index, near, far, weights):
    rows, depth, columns = near.shape[1], near.shape[2], weights[0].shape[1]
    anywhere = pl.BlockSpec(memory_space=pl.ANY)
    count = len(weights)
    return pl.pallas_call(
        early_kernel,
        grid_spec=pltpu.PrefetchScalarGridSpec(
            num_scalar_prefetch=1,
            grid=(1,),
            in_specs=[anywhere] * (2 + count),
            out_specs=pl.BlockSpec((rows, columns), lambda i, s: (0, 0)),
            scratch_shapes=[
                pltpu.VMEM((count, depth, columns), jnp.bfloat16),
                pltpu.VMEM((count, rows, depth), jnp.bfloat16),
                pltpu.SemaphoreType.DMA((2, count)),
            ],
        ),
        out_shape=jax.ShapeDtypeStruct((rows, columns), jnp.float32),
        compiler_params=pltpu.CompilerParams(vmem_limit_bytes=48 << 20),
        cost_estimate=pl.CostEstimate(
            flops=2 * rows * depth * columns * count, bytes_accessed=16_000_000, transcendentals=0
        ),
    )(index, near, far, *weights)


def turned_heads(raw, gain, cosine, sine):
    normal = raw * lax.rsqrt(jnp.mean(raw * raw, axis=-1, keepdims=True) + epsilon) * gain
    return normal * cosine + pltpu.roll(normal, HEAD_SIZE // 2, 1) * sine


def late_kernel(heads, index, near_ref, far_ref, w_near, w_far, before, gain, cosine, sine, out_ref, total, w_buf, t_buf, sems):
    total[...] = before[...]
    accumulate(index, near_ref, far_ref, (w_near, w_far), w_buf, t_buf, sems, total, 1)

    @pl.loop(0, total.shape[0] // 128)
    def _(i):
        at = pl.ds(pl.multiple_of(i * 128, 128), 128)
        for h in range(total.shape[1] // HEAD_SIZE):
            lanes = slice(h * HEAD_SIZE, (h + 1) * HEAD_SIZE)
            raw = total[at, lanes]
            if h < heads:
                raw = turned_heads(raw, gain[...], cosine[at, :], sine[at, :])
            out_ref[at, lanes] = raw.astype(jnp.bfloat16)


def late_product(heads, column, index, near, far, w_near, w_far, before, gain, cosine, sine):
    rows, depth = near.shape[1:]
    columns = w_near.shape[1]
    anywhere = pl.BlockSpec(memory_space=pl.ANY)
    table = pl.BlockSpec((rows, HEAD_SIZE), lambda i, s: (0, 0))
    return pl.pallas_call(
        functools.partial(late_kernel, heads),
        grid_spec=pltpu.PrefetchScalarGridSpec(
            num_scalar_prefetch=1,
            grid=(1,),
            in_specs=[anywhere] * 4
            + [
                pl.BlockSpec((rows, columns), lambda i, s: (0, column)),
                pl.BlockSpec((1, HEAD_SIZE), lambda i, s: (0, 0)),
                table,
                table,
            ],
            out_specs=pl.BlockSpec((rows, columns), lambda i, s: (0, 0)),
            scratch_shapes=[
                pltpu.VMEM((rows, columns), jnp.float32),
                pltpu.VMEM((2, depth, columns), jnp.bfloat16),
                pltpu.VMEM((2, rows, depth), jnp.bfloat16),
                pltpu.SemaphoreType.DMA((2, 2)),
            ],
        ),
        out_shape=jax.ShapeDtypeStruct((rows, columns), jnp.bfloat16),
        compiler_params=pltpu.CompilerParams(vmem_limit_bytes=40 << 20),
        cost_estimate=pl.CostEstimate(
            flops=4 * rows * depth * columns, bytes_accessed=6_000_000, transcendentals=0
        ),
    )(index, near, far, w_near, w_far, before, gain, cosine, sine)


def scores_of(queries, keys):
    score = lax.dot_general(
        queries, keys, (((1,), (1,)), ((), ())), preferred_element_type=jnp.float32
    )
    return jnp.exp(score * score_scale)


def lane_sums(weights):
    parts = [weights[:, i : i + HEAD_SIZE] for i in range(0, weights.shape[1], HEAD_SIZE)]
    return functools.reduce(lambda a, b: a + b, parts)


def both_heads(ref, at):
    return jnp.concatenate([ref[at, :HEAD_SIZE], ref[at, HEAD_SIZE:]], axis=0)


def own_kernel(q_ref, k_ref, v_ref, sum_ref, weight_ref):
    for r in range(q_ref.shape[0] // 128):
        at = slice(r * 128, (r + 1) * 128)
        seen = (r + 1) * 128
        e = scores_of(both_heads(q_ref, at), k_ref[:seen])
        i = lax.broadcasted_iota(jnp.int32, e.shape, 0) % 128
        j = lax.broadcasted_iota(jnp.int32, e.shape, 1)
        e = jnp.where(j <= i + r * 128, e, 0.0)
        mixed = jnp.dot(e.astype(jnp.bfloat16), v_ref[:seen], preferred_element_type=jnp.float32)
        weight = lane_sums(e)
        for h in range(2):
            lanes = slice(h * HEAD_SIZE, (h + 1) * HEAD_SIZE)
            sum_ref[at, lanes] = mixed[h * 128 : (h + 1) * 128]
            weight_ref[at, lanes] = weight[h * 128 : (h + 1) * 128]


def behind_kernel(valid, q_ref, k1_ref, v1_ref, k2_ref, v2_ref, sum_ref, weight_ref, out_ref):
    has_one = valid[0].astype(jnp.float32)
    has_two = valid[1].astype(jnp.float32)
    rows = q_ref.shape[0]
    for r in range(rows // 128):
        at = slice(r * 128, (r + 1) * 128)
        q = both_heads(q_ref, at)
        one = scores_of(q, k1_ref[...])
        two = scores_of(q, k2_ref[r * 128 :])
        i = lax.broadcasted_iota(jnp.int32, two.shape, 0) % 128
        j = lax.broadcasted_iota(jnp.int32, two.shape, 1)
        two = jnp.where(j > i, two, 0.0)
        mixed = has_one * jnp.dot(
            one.astype(jnp.bfloat16), v1_ref[...], preferred_element_type=jnp.float32
        ) + has_two * jnp.dot(
            two.astype(jnp.bfloat16), v2_ref[r * 128 :], preferred_element_type=jnp.float32
        )
        weight = has_one * lane_sums(one) + has_two * lane_sums(two)
        for h in range(2):
            lanes = slice(h * HEAD_SIZE, (h + 1) * HEAD_SIZE)
            top = sum_ref[at, lanes] + mixed[h * 128 : (h + 1) * 128]
            low = jnp.sum(weight_ref[at, lanes] + weight[h * 128 : (h + 1) * 128], axis=-1, keepdims=True)
            out_ref[at, lanes] = (top / low).astype(jnp.bfloat16)


def attend_own(queries, keyed):
    rows, columns = queries.shape
    groups = columns // (2 * HEAD_SIZE)
    pair = pl.BlockSpec((rows, 2 * HEAD_SIZE), lambda g: (0, g))
    shape = jax.ShapeDtypeStruct((rows, columns), jnp.float32)
    return pl.pallas_call(
        own_kernel,
        grid=(groups,),
        in_specs=[
            pair,
            pl.BlockSpec((rows, HEAD_SIZE), lambda g: (0, g)),
            pl.BlockSpec((rows, HEAD_SIZE), lambda g: (0, groups + g)),
        ],
        out_specs=[pair, pair],
        out_shape=[shape, shape],
        compiler_params=pltpu.CompilerParams(vmem_limit_bytes=32 << 20),
        cost_estimate=pl.CostEstimate(
            flops=4 * rows * rows * columns, bytes_accessed=3_000_000, transcendentals=rows * rows * 4
        ),
    )(queries, keyed, keyed)


def attend_behind(valid, queries, one, two, sums, weights):
    rows, columns = queries.shape
    groups = columns // (2 * HEAD_SIZE)
    pair = pl.BlockSpec((rows, 2 * HEAD_SIZE), lambda g, s: (0, g))
    keys = pl.BlockSpec((rows, HEAD_SIZE), lambda g, s: (0, g))
    values = pl.BlockSpec((rows, HEAD_SIZE), lambda g, s: (0, groups + g))
    return pl.pallas_call(
        behind_kernel,
        grid_spec=pltpu.PrefetchScalarGridSpec(
            num_scalar_prefetch=1,
            grid=(groups,),
            in_specs=[pair, keys, values, keys, values, pair, pair],
            out_specs=pair,
        ),
        out_shape=jax.ShapeDtypeStruct((rows, columns), jnp.bfloat16),
        compiler_params=pltpu.CompilerParams(vmem_limit_bytes=32 << 20),
        cost_estimate=pl.CostEstimate(
            flops=8 * rows * rows * columns, bytes_accessed=4_000_000, transcendentals=rows * rows * 8
        ),
    )(valid, queries, one, one, two, two, sums, weights)


def local(
    tokens, q_weight, key_matrix, value_matrix, o_weight, pre_gain, post_gain, q_gain, k_gain
):
    rows = tokens.shape[0]
    q_cols = q_weight.shape[1]
    yl, x, z, yh, c = (lax.axis_index(name) for name in ("yl", "x", "z", "yh", "c"))
    seq_index = (yl * 4 + x) * 4 + z
    whole = lax.all_gather(tokens, MP, axis=0)

    own = jnp.concatenate([q_weight, key_matrix, value_matrix], axis=1)
    other = shift(own, "yl", 1)
    own_line = in_line([own] + [shift(own, "x", step) for step in (1, 3, 2)], x)
    other_line = in_line([other] + [shift(other, "z", step) for step in (1, 3, 2)], z)
    own_line, other_line = lax.optimization_barrier((own_line, other_line))
    own_ahead, own_behind = shift(own_line, "z", 1), shift(own_line, "z", 3)
    other_ahead, other_behind = shift(other_line, "x", 1), shift(other_line, "x", 3)
    own_ahead, own_behind, other_ahead, other_behind = lax.optimization_barrier(
        (own_ahead, own_behind, other_ahead, other_behind)
    )
    own_far_q = shift(own_ahead[:, :q_cols], "z", 1)
    own_far_kv = shift(own_behind[:, q_cols:], "z", 3)
    other_far_q = shift(other_ahead[:, :q_cols], "x", 1)
    other_far_kv = shift(other_behind[:, q_cols:], "x", 3)

    turned = o_weight.T
    y = yh * 2 + yl
    flat = lambda p: (p % 2) * 2 + p // 2
    one = lax.ppermute(turned, ("yl", "yh"), [(flat(a), flat(b)) for a, b in ((0, 1), (2, 0), (1, 3), (3, 2))])
    two = lax.ppermute(turned, ("yl", "yh"), [(flat(a), flat(b)) for a, b in ((1, 2), (2, 1))])
    outer = (y == 0) | (y == 3)
    pair = jnp.concatenate([jnp.where(outer, turned, one), jnp.where(outer, one, two)], axis=1)
    out_all = lax.all_gather(pair, ("x", "z"), axis=0, tiled=True)
    half_rows = out_all.shape[0] // 2
    out_mine = lax.dynamic_slice_in_dim(out_all, c * half_rows, half_rows, 0)
    out_theirs = shift(lax.dynamic_slice_in_dim(out_all, (1 - c) * half_rows, half_rows, 0), "c", 1)

    positions = seq_index * rows + jnp.arange(rows, dtype=jnp.int32)
    half = HEAD_SIZE // 2
    freq = 10000.0 ** (-(jnp.arange(half, dtype=jnp.float32) * 2.0) / HEAD_SIZE)
    angle = positions.astype(jnp.float32)[:, None] * freq[None, :]
    cosine = jnp.cos(angle)
    sine = jnp.sin(angle)
    cosine = jnp.concatenate([cosine, cosine], axis=1)
    sine = jnp.concatenate([-sine, sine], axis=1)

    near, far = norm_parts(whole, pre_gain, yl)
    index = jnp.stack([z, (z + 3) % 4, (z + 1) % 4, x, (x + 3) % 4, (x + 1) % 4])
    total = early_product(
        index, near, far, (own_line, own_ahead, own_behind, other_line, other_ahead, other_behind)
    )
    last = jnp.stack([(z + 2) % 4, (x + 2) % 4])
    keyed = late_product(
        2, 1, last, near, far, own_far_kv, other_far_kv, total, k_gain[None], cosine, sine
    )
    behind_one = from_behind(keyed, 1)
    behind_two = from_behind(keyed, 2)
    queries = late_product(
        4, 0, last, near, far, own_far_q, other_far_q, total, q_gain[None], cosine, sine
    )
    sums, weights = attend_own(queries, keyed)
    valid = jnp.stack([seq_index >= 1, seq_index >= 2]).astype(jnp.int32)
    context = attend_behind(valid, queries, behind_one, behind_two, sums, weights)

    across = shift(context, "yh", 1)
    theirs = shift(context, "c", 1)
    product = lambda a, b: lax.dot_general(
        a, b, (((1,), (1,)), ((), ())), preferred_element_type=jnp.float32
    )
    share = product(context, out_mine[:, :q_cols]) + product(theirs, out_theirs[:, :q_cols])
    theirs_across = shift(across, "c", 1)
    share = share + product(across, out_mine[:, q_cols:]) + product(theirs_across, out_theirs[:, q_cols:])
    total = lax.psum(jnp.sum(share * share, axis=1), MP)
    scale_rows = lax.rsqrt(total / MODEL_WIDTH + epsilon)
    return (tokens.astype(jnp.float32) + share * scale_rows[:, None] * post_gain).astype(
        jnp.bfloat16
    )


def solution(mesh):
    fine = Mesh(np.asarray(mesh.devices).reshape(2, 4, 4, 2, 2), SEQ + MP)
    return jax.shard_map(
        local,
        mesh=fine,
        in_specs=(
            P(SEQ, MP),
            P(SEQ, MP),
            P(SEQ, MP),
            P(SEQ, MP),
            P(MP, SEQ),
            P(),
            P(MP),
            P(),
            P(),
        ),
        out_specs=P(SEQ, MP),
        check_vma=False,
    )
```

time: 274 us -> 276 us (level)
  the two profiles are of different devices: /device:TPU:6 before, /device:TPU:40 now
where the time goes in v2:
time: 276 us; the launch traced here: 275 us
  waiting for transfers between devices  131 us (47%)
  local copies, waits for them, and re-layouts  36.3 us (13%)
  Pallas kernels  36 us (13%)
  starting transfers between devices  32.6 us (12%)
  between operations  14 us (5%)
  matrix products  9.12 us (3%)
  blocking collectives  8.66 us (3%)
  other arithmetic  6.73 us (2%)
    all_gather x1, waiting for transfers between devices, local(): out_all = lax.all_gather(pair, ('x', 'z'), axis=0, tiled=True)  48.1 us
    ppermute x19, waiting for transfers between devices, shift(): lax.ppermute(value, axis, [(i, (i + step) % count) for i in range(count)])  31.5 us
    all_gather x1, waiting for transfers between devices, local(): whole = lax.all_gather(tokens, MP, axis=0)  27.4 us
    ppermute x19, starting transfers between devices, shift(): lax.ppermute(value, axis, [(i, (i + step) % count) for i in range(count)])  21.1 us
    ppermute x2, waiting for transfers between devices, from_behind(): lax.ppermute(value, SEQ, [(source, source + steps) for source in range(co...  17.5 us
    pallas_call x1, Pallas kernels, early_product(): pl.pallas_call(early_kernel, grid_spec=pltpu.PrefetchScalarGridSpec(num_s...  12.4 us
    unnamed x42, local copies, waits for them, and re-layouts  12 us
    pallas_call x2, Pallas kernels, late_product(): pl.pallas_call(functools.partial(late_kernel, heads), grid_spec=pltpu.Pre...  10.8 us
  transfers between devices with their start and end apart: 25, of which 11 were waited for; matrix products, arithmetic and copies ran while one was open for 12% of the time, Pallas kernels for 13%

profile of v2, /device:TPU:40, one launch (start us, length us, event | category | flops | bytes accessed | tf_op | source)
XLA Modules:
  0.0 274.7 jit_solution(7746521281418798492)
XLA Ops:
  6.5 2.3 collective-permute-start.17
  8.8 1.9 collective-permute-start.18
  10.8 2.1 collective-permute-done.17
  12.9 3.9 %collective-permute-done.18 = bf16[168,512]{1,0:T(8,128)(2,1)S(1)} collective-permute-done((bf16[168,512]{1,0:T(8,128)(2,1)}, bf16[168,512]{1,0:T(8,128)(2,1)S(1)}, u32[]{:S(2)}, u32[]{:S(2)}) %collective-permute-start.18) | collective-permute-done | bytes 172064 | tf_op jit(solution)/shard_map/ppermute | solution.py:322
  16.8 1.0 broadcast_select_fusion.1
  17.8 0.8 pad_maximum_fusion
  18.6 0.7 all-gather.6.cloned.1.call-update
  19.5 1.6 collective-permute-start
  21.0 1.7 collective-permute-start.1
  22.8 1.8 collective-permute-start.2
  24.6 0.2 broadcast.33.clone
  24.9 3.2 %collective-permute-done.3 = bf16[168,1024]{1,0:T(8,128)(2,1)S(1)} collective-permute-done((bf16[168,1024]{1,0:T(8,128)(2,1)S(1)}, bf16[168,1024]{1,0:T(8,128)(2,1)S(1)}, u32[]{:S(2)}, u32[]{:S(2)}) %collective-permute-start.3) | collective-permute-done | bytes 344096 | tf_op jit(solution)/shard_map/ppermute | solution.py:24
  28.1 1.9 collective-permute-start.4
  30.1 0.2 broadcast.33.clone.1
  30.3 0.6 collective-permute-done
  30.9 3.0 %collective-permute-start.6 = (bf16[168,1024]{1,0:T(8,128)(2,1)S(1)}, bf16[168,1024]{1,0:T(8,128)(2,1)S(1)}, u32[]{:S(2)}, u32[]{:S(2)}) collective-permute-start(bf16[168,1024]{1,0:T(8,128)(2,1)S(1)} %collective-permute-done.3), channel_id=1, source_target_pairs={{0,8},{4,12},{8,0},{12,4},{1,9},{5,13},{9,1},{13,5},{2,10},{6,14},... | collective-permute-start | bytes 1032200 | tf_op jit(solution)/shard_map/ppermute | solution.py:24
  33.8 1.0 bitcast_dynamic-update-slice_fusion.6
  34.9 1.0 bitcast_dynamic-update-slice_fusion.5
  35.9 5.7 %collective-permute-done.2 = bf16[168,1024]{1,0:T(8,128)(2,1)} collective-permute-done((bf16[168,1024]{1,0:T(8,128)(2,1)S(1)}, bf16[168,1024]{1,0:T(8,128)(2,1)}, u32[]{:S(2)}, u32[]{:S(2)}) %collective-permute-start.2) | collective-permute-done | bytes 344096 | tf_op jit(solution)/shard_map/ppermute | solution.py:24
  41.6 1.0 bitcast_dynamic-update-slice_fusion.4
  42.6 5.6 %collective-permute-done.4 = bf16[168,1024]{1,0:T(8,128)(2,1)S(1)} collective-permute-done((bf16[168,1024]{1,0:T(8,128)(2,1)S(1)}, bf16[168,1024]{1,0:T(8,128)(2,1)S(1)}, u32[]{:S(2)}, u32[]{:S(2)}) %collective-permute-start.4) | collective-permute-done | bytes 344096 | tf_op jit(solution)/shard_map/ppermute | solution.py:24
  48.3 3.1 %collective-permute-done.6 = bf16[168,1024]{1,0:T(8,128)(2,1)S(1)} collective-permute-done((bf16[168,1024]{1,0:T(8,128)(2,1)S(1)}, bf16[168,1024]{1,0:T(8,128)(2,1)S(1)}, u32[]{:S(2)}, u32[]{:S(2)}) %collective-permute-start.6) | collective-permute-done | bytes 344096 | tf_op jit(solution)/shard_map/ppermute | solution.py:24
  51.6 2.0 collective-permute-start.8
  53.6 1.5 collective-permute-start.9
  55.1 1.7 collective-permute-start.10
  56.8 48.1 %all-gather.4.cloned.1.call-done = bf16[2688,1024]{1,0:T(8,128)(2,1)} async-done(((bf16[168,1024]{1,0:T(8,128)(2,1)}), bf16[2688,1024]{1,0:T(8,128)(2,1)}) %all-gather.4.cloned.1.call-update) | async-done | bytes 5505040 | tf_op jit(solution)/shard_map/all_gather | solution.py:325
  105.0 3.6 %constant_dynamic-slice_fusion = bf16[1344,1024]{1,0:T(8,128)(2,1)} fusion(bf16[2688,1024]{1,0:T(8,128)(2,1)} %all-gather.4.cloned.1.call-done, s32[]{:T(128)S(6)} %select_n.116), kind=kLoop, calls=%fused_computation.31 | loop fusion | bytes 5505028 | tf_op jit(solution)/shard_map/dynamic_slice | solution.py:328
  108.6 1.0 fusion.7
  109.7 2.0 slice.26
  111.7 1.2 collective-permute-start.13
  112.9 2.0 slice.27
  114.9 1.8 collective-permute-start.14
  116.8 0.8 reshape.27.own_gain.other_gain
  117.8 0.9 pad_maximum_fusion.1
  118.7 2.1 slice.24
  120.8 0.7 collective-permute-start.11
  121.5 2.0 slice.25
  123.5 0.3 collective-permute-start.12
  123.8 27.4 %all-gather.6.cloned.1.call-done = bf16[2048,1344]{0,1:T(8,128)(2,1)} async-done(((bf16[512,1344]{0,1:T(8,128)(2,1)}), bf16[2048,1344]{0,1:T(8,128)(2,1)}) %all-gather.6.cloned.1.call-update) | async-done | bytes 5505040 | tf_op jit(solution)/shard_map/all_gather | solution.py:301
  151.2 8.2 %copy.10 = bf16[2048,1344]{1,0:T(8,128)(2,1)} copy(bf16[2048,1344]{0,1:T(8,128)(2,1)} %all-gather.6.cloned.1.call-done) | data formatting | bytes 11010048 | tf_op jit(solution)/shard_map/all_gather | solution.py:301
  159.4 2.6 copy-done
  162.0 5.6 %shard_map.91 = (bf16[4,512,672]{2,1,0:T(8,128)(2,1)S(1)}, bf16[4,512,672]{2,1,0:T(8,128)(2,1)S(1)}) custom-call(s32[2]{0:T(128)S(1)} %pad_add_fusion.1.side, bf16[2,2,512,1344]{3,2,1,0:T(8,128)(2,1)S(1)} %bitcast.39, bf16[2,2,512,1344]{3,2,1,0:T(8,128)(2,1)S(1)} %bitcast.40, f32[2,2,1,1344]{3,2,1,0:T(1,128)S(1)} %reshape.27.own_gain.other_gain, ...), custom_call_target="tpu_custom_call" | custom-call | flops 20000000 | bytes 12000000 | tf_op jit(solution)/shard_map/pallas_call | solution.py:71
  167.7 1.7 copy-done.1
  169.3 1.6 copy-done.3
  171.0 12.4 %shard_map.92.before = f32[512,1024]{1,0:T(8,128)} custom-call(s32[6]{0:T(128)S(1)} %stack.63.index, bf16[4,512,672]{2,1,0:T(8,128)(2,1)} %copy-done.1, bf16[4,512,672]{2,1,0:T(8,128)(2,1)} %copy-done.3, bf16[672,1024]{1,0:T(8,128)(2,1)S(1)} %bitcast.46, bf16[672,1024]{1,0:T(8,128)(2,1)} %collective-permute-done.7.refs_1_, ...), custom_call_target="tpu_custom_call" | custom-call | flops 4227858432 | bytes 16000000 | tf_op jit(solution)/shard_map/pallas_call | solution.py:119
  183.5 1.6 copy-done.6
  185.0 5.5 %shard_map.94.k_ref.v_ref = bf16[512,512]{1,0:T(8,128)(2,1)} custom-call(s32[2]{0:T(128)S(1)} %pad_add_fusion.index, bf16[4,512,672]{2,1,0:T(8,128)(2,1)S(1)} %copy-done.2, bf16[4,512,672]{2,1,0:T(8,128)(2,1)S(1)} %copy-done.4, bf16[672,512]{1,0:T(8,128)(2,1)} %collective-permute-done.13.w_near, bf16[672,512]{1,0:T(8,128)(2,1)} %collective-permute-done.14.w_far, ...), custom_call_target="tpu_custom_call" | custom-call | flops 704643072 | bytes 6000000 | tf_op jit(solution)/shard_map/pallas_call | solution.py:165
  190.6 3.5 %collective-permute-start.15 = (bf16[512,512]{1,0:T(8,128)(2,1)}, bf16[512,512]{1,0:T(8,128)(2,1)}, u32[]{:S(2)}, u32[]{:S(2)}) collective-permute-start(bf16[512,512]{1,0:T(8,128)(2,1)} %shard_map.94.k_ref.v_ref), channel_id=1, source_target_pairs={{0,4},{4,8},{8,12},{12,16},{16,20},{20,24},{24,28},{28,32},{32,36}... | collective-permute-start | bytes 1572872 | tf_op jit(solution)/shard_map/ppermute | solution.py:29
  194.1 3.8 %collective-permute-start.16 = (bf16[512,512]{1,0:T(8,128)(2,1)}, bf16[512,512]{1,0:T(8,128)(2,1)}, u32[]{:S(2)}, u32[]{:S(2)}) collective-permute-start(bf16[512,512]{1,0:T(8,128)(2,1)} %shard_map.94.k_ref.v_ref), channel_id=1, source_target_pairs={{0,8},{4,12},{8,16},{12,20},{16,24},{20,28},{24,32},{28,36},{32,40... | collective-permute-start | bytes 1572872 | tf_op jit(solution)/shard_map/ppermute | solution.py:29
  198.0 1.9 copy-done.5
  199.8 1.6 copy-done.7
  201.4 0.9 copy-done.13
  202.4 5.3 %shard_map.93.q_ref = bf16[512,512]{1,0:T(8,128)(2,1)S(1)} custom-call(s32[2]{0:T(128)S(1)} %pad_add_fusion.index, bf16[4,512,672]{2,1,0:T(8,128)(2,1)S(1)} %copy-done.2, bf16[4,512,672]{2,1,0:T(8,128)(2,1)S(1)} %copy-done.5, bf16[672,512]{1,0:T(8,128)(2,1)} %collective-permute-done.11.w_near, bf16[672,512]{1,0:T(8,128)(2,1)} %collective-permute-done.12.w_far, ...), custom_call_target="tpu_custom_call" | custom-call | flops 704643072 | bytes 6000000 | tf_op jit(solution)/shard_map/pallas_call | solution.py:165
  207.7 2.9 %shard_map.95 = (f32[512,512]{1,0:T(8,128)S(1)}, f32[512,512]{1,0:T(8,128)S(1)}) custom-call(bf16[512,512]{1,0:T(8,128)(2,1)S(1)} %shard_map.93.q_ref, bf16[512,512]{1,0:T(8,128)(2,1)} %shard_map.94.k_ref.v_ref, bf16[512,512]{1,0:T(8,128)(2,1)} %shard_map.94.k_ref.v_ref), custom_call_target="tpu_custom_call" | custom-call | flops 536870912 | bytes 3000000 | tf_op jit(solution)/shard_map/pallas_call | solution.py:255
  210.6 17.5 %collective-permute-done.16.k2_ref.v2_ref = bf16[512,512]{1,0:T(8,128)(2,1)} collective-permute-done((bf16[512,512]{1,0:T(8,128)(2,1)}, bf16[512,512]{1,0:T(8,128)(2,1)}, u32[]{:S(2)}, u32[]{:S(2)}) %collective-permute-start.16) | collective-permute-done | bytes 524320 | tf_op jit(solution)/shard_map/ppermute | solution.py:29
  228.1 4.2 %shard_map.96 = bf16[512,512]{1,0:T(8,128)(2,1)S(1)} custom-call(s32[2]{0:T(128)S(1)} %add_convert_fusion.2.valid, bf16[512,512]{1,0:T(8,128)(2,1)S(1)} %shard_map.93.q_ref, bf16[512,512]{1,0:T(8,128)(2,1)} %collective-permute-done.15.k1_ref.v1_ref, bf16[512,512]{1,0:T(8,128)(2,1)} %collective-permute-done.15.k1_ref.v1_ref, ...), custom_call_target="tpu_custom_call" | custom-call | flops 1073741824 | bytes 4000000 | tf_op jit(solution)/shard_map/pallas_call | solution.py:278
  232.4 1.5 collective-permute-start.21
  233.9 13.3 %collective-permute-done.21 = bf16[512,512]{1,0:T(8,128)(2,1)S(1)} collective-permute-done((bf16[512,512]{1,0:T(8,128)(2,1)S(1)}, bf16[512,512]{1,0:T(8,128)(2,1)S(1)}, u32[]{:S(2)}, u32[]{:S(2)}) %collective-permute-start.21) | collective-permute-done | bytes 524320 | tf_op jit(solution)/shard_map/ppermute | solution.py:24
  247.1 2.3 fusion.2
  249.4 2.3 fusion.4
  251.7 2.3 fusion
  254.0 2.3 multiply_reduce_fusion
  256.3 8.7 %psum.7 = f32[512]{0:T(512)S(1)} all-reduce(f32[512]{0:T(512)S(1)} %get-tuple-element.30), channel_id=1, replica_groups=mesh['yl'=2,'x'=4,'z'=4,'yh'=2,'c'=2] {'yh','c'}, use_global_device_ids=true, to_apply=%region_1.2 | all-reduce | flops 512 | bytes 4096 | tf_op jit(solution)/shard_map/psum | solution.py:365
  265.0 2.9 %add_convert_fusion = bf16[512,1344]{0,1:T(8,128)(2,1)} fusion(f32[512,1344]{0,1:T(8,128)S(1)} %get-tuple-element.31, bf16[512,1344]{0,1:T(8,128)(2,1)} %param.9, f32[1344]{0:T(1024)S(1)} %copy-done.19, f32[512]{0:T(512)S(1)} %add_rsqrt_fusion), kind=kLoop, calls=%fused_computation.3 | loop fusion | flops 3440640 | bytes 5512448 | tf_op jit(solution)/shard_map/convert_element_type | solution.py:367
  (71 shorter events, 1.0 us)
Async XLA Ops:
  6.5 98.5 %all-gather.4.cloned.1.call-start = ((), (), s32[]{:S(2)}) async-start(), calls=%async_computation | async-start | bytes 5849088 | tf_op jit(solution)/shard_map/all_gather | solution.py:325
  6.5 6.3 %collective-permute-start.17 = (bf16[168,512]{1,0:T(8,128)(2,1)}, bf16[168,512]{1,0:T(8,128)(2,1)S(1)}, u32[]{:S(2)}, u32[]{:S(2)}) collective-permute-start(bf16[168,512]{1,0:T(8,128)(2,1)} %bitcast.49), channel_id=1, source_target_pairs={{0,64},{2,0},{64,66},{66,2},{1,65},{3,1},{65,67},{67,3},{4,68},{6,... | collective-permute-start | bytes 516104 | tf_op jit(solution)/shard_map/ppermute | solution.py:321
  8.8 7.9 %collective-permute-start.18 = (bf16[168,512]{1,0:T(8,128)(2,1)}, bf16[168,512]{1,0:T(8,128)(2,1)S(1)}, u32[]{:S(2)}, u32[]{:S(2)}) collective-permute-start(bf16[168,512]{1,0:T(8,128)(2,1)} %bitcast.50), channel_id=1, source_target_pairs={{64,2},{2,64},{65,3},{3,65},{68,6},{6,68},{69,7},{7,69},{72,10},{1... | collective-permute-start | bytes 516104 | tf_op jit(solution)/shard_map/ppermute | solution.py:322
  17.7 1.6 copy-start.16
  17.7 1.6 copy-start.17
  17.7 1.6 copy-start.18
  18.5 132.6 %all-gather.6.cloned.1.call-start = ((), (), s32[]{:S(2)}) async-start(), calls=%async_computation.1 | async-start | bytes 6881280 | tf_op jit(solution)/shard_map/all_gather | solution.py:301
  19.4 8.7 %collective-permute-start.3 = (bf16[168,1024]{1,0:T(8,128)(2,1)S(1)}, bf16[168,1024]{1,0:T(8,128)(2,1)S(1)}, u32[]{:S(2)}, u32[]{:S(2)}) collective-permute-start(bf16[168,1024]{1,0:T(8,128)(2,1)S(1)} %constant_dynamic-update-slice_fusion), channel_id=1, source_target_pairs={{0,64},{64,0},{1,65},{65,1},{2,66},{66,2},{3,67},{67,3},{4,68},{68... | collective-permute-start | bytes 1032200 | tf_op jit(solution)/shard_map/ppermute | solution.py:24
  19.5 11.4 %collective-permute-start = (bf16[168,1024]{1,0:T(8,128)(2,1)S(1)}, bf16[168,1024]{1,0:T(8,128)(2,1)}, u32[]{:S(2)}, u32[]{:S(2)}) collective-permute-start(bf16[168,1024]{1,0:T(8,128)(2,1)S(1)} %constant_dynamic-update-slice_fusion), channel_id=1, source_target_pairs={{0,16},{16,32},{32,48},{48,0},{1,17},{17,33},{33,49},{49,1},{2,18}... | collective-permute-start | bytes 1032200 | tf_op jit(solution)/shard_map/ppermute | solution.py:24
  21.0 13.8 %collective-permute-start.1 = (bf16[168,1024]{1,0:T(8,128)(2,1)S(1)}, bf16[168,1024]{1,0:T(8,128)(2,1)}, u32[]{:S(2)}, u32[]{:S(2)}) collective-permute-start(bf16[168,1024]{1,0:T(8,128)(2,1)S(1)} %constant_dynamic-update-slice_fusion), channel_id=1, source_target_pairs={{0,48},{16,0},{32,16},{48,32},{1,49},{17,1},{33,17},{49,33},{2,50}... | collective-permute-start | bytes 1032200 | tf_op jit(solution)/shard_map/ppermute | solution.py:24
  22.8 18.8 %collective-permute-start.2 = (bf16[168,1024]{1,0:T(8,128)(2,1)S(1)}, bf16[168,1024]{1,0:T(8,128)(2,1)}, u32[]{:S(2)}, u32[]{:S(2)}) collective-permute-start(bf16[168,1024]{1,0:T(8,128)(2,1)S(1)} %constant_dynamic-update-slice_fusion), channel_id=1, source_target_pairs={{0,32},{16,48},{32,0},{48,16},{1,33},{17,49},{33,1},{49,17},{2,34}... | collective-permute-start | bytes 1032200 | tf_op jit(solution)/shard_map/ppermute | solution.py:24
  28.1 20.2 %collective-permute-start.4 = (bf16[168,1024]{1,0:T(8,128)(2,1)S(1)}, bf16[168,1024]{1,0:T(8,128)(2,1)S(1)}, u32[]{:S(2)}, u32[]{:S(2)}) collective-permute-start(bf16[168,1024]{1,0:T(8,128)(2,1)S(1)} %collective-permute-done.3), channel_id=1, source_target_pairs={{0,4},{4,8},{8,12},{12,0},{1,5},{5,9},{9,13},{13,1},{2,6},{6,10},{... | collective-permute-start | bytes 1032200 | tf_op jit(solution)/shard_map/ppermute | solution.py:24
  30.0 18.3 %collective-permute-start.5 = (bf16[168,1024]{1,0:T(8,128)(2,1)S(1)}, bf16[168,1024]{1,0:T(8,128)(2,1)S(1)}, u32[]{:S(2)}, u32[]{:S(2)}) collective-permute-start(bf16[168,1024]{1,0:T(8,128)(2,1)S(1)} %collective-permute-done.3), channel_id=1, source_target_pairs={{0,12},{4,0},{8,4},{12,8},{1,13},{5,1},{9,5},{13,9},{2,14},{6,2},{... | collective-permute-start | bytes 1032200 | tf_op jit(solution)/shard_map/ppermute | solution.py:24
  30.9 20.6 %collective-permute-start.6 = (bf16[168,1024]{1,0:T(8,128)(2,1)S(1)}, bf16[168,1024]{1,0:T(8,128)(2,1)S(1)}, u32[]{:S(2)}, u32[]{:S(2)}) collective-permute-start(bf16[168,1024]{1,0:T(8,128)(2,1)S(1)} %collective-permute-done.3), channel_id=1, source_target_pairs={{0,8},{4,12},{8,0},{12,4},{1,9},{5,13},{9,1},{13,5},{2,10},{6,14},... | collective-permute-start | bytes 1032200 | tf_op jit(solution)/shard_map/ppermute | solution.py:24
  42.6 66.0 %copy-start.10 = (bf16[4,168,1024]{2,1,0:T(8,128)(2,1)}, bf16[4,168,1024]{2,1,0:T(8,128)(2,1)S(1)}, u32[]{:S(2)}) copy-start(bf16[4,168,1024]{2,1,0:T(8,128)(2,1)S(1)} %bitcast_dynamic-update-slice_fusion.4) | copy-start | bytes 4128772
  51.5 57.1 %copy-start.8 = (bf16[4,168,1024]{2,1,0:T(8,128)(2,1)}, bf16[4,168,1024]{2,1,0:T(8,128)(2,1)S(1)}, u32[]{:S(2)}) copy-start(bf16[4,168,1024]{2,1,0:T(8,128)(2,1)S(1)} %bitcast_dynamic-update-slice_fusion) | copy-start | bytes 4128772
  51.5 58.1 %collective-permute-start.7 = (bf16[672,1024]{1,0:T(8,128)(2,1)S(1)}, bf16[672,1024]{1,0:T(8,128)(2,1)}, u32[]{:S(2)}, u32[]{:S(2)}) collective-permute-start(bf16[672,1024]{1,0:T(8,128)(2,1)S(1)} %bitcast.44), channel_id=1, source_target_pairs={{0,4},{4,8},{8,12},{12,0},{1,5},{5,9},{9,13},{13,1},{2,6},{6,10},{... | collective-permute-start | bytes 4128776 | tf_op jit(solution)/shard_map/ppermute | solution.py:24
  51.6 58.1 %collective-permute-start.8 = (bf16[672,1024]{1,0:T(8,128)(2,1)S(1)}, bf16[672,1024]{1,0:T(8,128)(2,1)}, u32[]{:S(2)}, u32[]{:S(2)}) collective-permute-start(bf16[672,1024]{1,0:T(8,128)(2,1)S(1)} %bitcast.45), channel_id=1, source_target_pairs={{0,12},{4,0},{8,4},{12,8},{1,13},{5,1},{9,5},{13,9},{2,14},{6,2},{... | collective-permute-start | bytes 4128776 | tf_op jit(solution)/shard_map/ppermute | solution.py:24
  53.6 56.1 %collective-permute-start.9 = (bf16[672,1024]{1,0:T(8,128)(2,1)S(1)}, bf16[672,1024]{1,0:T(8,128)(2,1)}, u32[]{:S(2)}, u32[]{:S(2)}) collective-permute-start(bf16[672,1024]{1,0:T(8,128)(2,1)S(1)} %bitcast.41), channel_id=1, source_target_pairs={{0,16},{16,32},{32,48},{48,0},{1,17},{17,33},{33,49},{49,1},{2,18}... | collective-permute-start | bytes 4128776 | tf_op jit(solution)/shard_map/ppermute | solution.py:24
  55.1 54.6 %collective-permute-start.10 = (bf16[672,1024]{1,0:T(8,128)(2,1)S(1)}, bf16[672,1024]{1,0:T(8,128)(2,1)}, u32[]{:S(2)}, u32[]{:S(2)}) collective-permute-start(bf16[672,1024]{1,0:T(8,128)(2,1)S(1)} %bitcast.42), channel_id=1, source_target_pairs={{0,48},{16,0},{32,16},{48,32},{1,49},{17,1},{33,17},{49,33},{2,50}... | collective-permute-start | bytes 4128776 | tf_op jit(solution)/shard_map/ppermute | solution.py:24
  108.6 140.9 %collective-permute-start.20 = (bf16[1344,1024]{1,0:T(8,128)(2,1)}, bf16[1344,1024]{1,0:T(8,128)(2,1)}, u32[]{:S(2)}, u32[]{:S(2)}) collective-permute-start(bf16[1344,1024]{1,0:T(8,128)(2,1)} %constant_dynamic-slice_fusion), channel_id=1, source_target_pairs={{0,1},{1,0},{2,3},{3,2},{4,5},{5,4},{6,7},{7,6},{8,9},{9,8},{10,11... | collective-permute-start | bytes 8257544 | tf_op jit(solution)/shard_map/ppermute | solution.py:24
  111.7 71.7 %collective-permute-start.13 = (bf16[672,512]{1,0:T(8,128)(2,1)}, bf16[672,512]{1,0:T(8,128)(2,1)}, u32[]{:S(2)}, u32[]{:S(2)}) collective-permute-start(bf16[672,512]{1,0:T(8,128)(2,1)} %slice.26), channel_id=1, source_target_pairs={{0,12},{4,0},{8,4},{12,8},{1,13},{5,1},{9,5},{13,9},{2,14},{6,2},{... | collective-permute-start | bytes 2064392 | tf_op jit(solution)/shard_map/ppermute | solution.py:24
  114.9 68.5 %collective-permute-start.14 = (bf16[672,512]{1,0:T(8,128)(2,1)}, bf16[672,512]{1,0:T(8,128)(2,1)}, u32[]{:S(2)}, u32[]{:S(2)}) collective-permute-start(bf16[672,512]{1,0:T(8,128)(2,1)} %slice.27), channel_id=1, source_target_pairs={{0,48},{16,0},{32,16},{48,32},{1,49},{17,1},{33,17},{49,33},{2,50}... | collective-permute-start | bytes 2064392 | tf_op jit(solution)/shard_map/ppermute | solution.py:24
  120.8 77.2 %collective-permute-start.11 = (bf16[672,512]{1,0:T(8,128)(2,1)}, bf16[672,512]{1,0:T(8,128)(2,1)}, u32[]{:S(2)}, u32[]{:S(2)}) collective-permute-start(bf16[672,512]{1,0:T(8,128)(2,1)} %slice.24), channel_id=1, source_target_pairs={{0,4},{4,8},{8,12},{12,0},{1,5},{5,9},{9,13},{13,1},{2,6},{6,10},{... | collective-permute-start | bytes 2064392 | tf_op jit(solution)/shard_map/ppermute | solution.py:24
  123.5 74.5 %collective-permute-start.12 = (bf16[672,512]{1,0:T(8,128)(2,1)}, bf16[672,512]{1,0:T(8,128)(2,1)}, u32[]{:S(2)}, u32[]{:S(2)}) collective-permute-start(bf16[672,512]{1,0:T(8,128)(2,1)} %slice.25), channel_id=1, source_target_pairs={{0,16},{16,32},{32,48},{48,0},{1,17},{17,33},{33,49},{49,1},{2,18}... | collective-permute-start | bytes 2064392 | tf_op jit(solution)/shard_map/ppermute | solution.py:24
  159.4 2.6 copy-start
  162.0 8.9 %copy-start.9 = (bf16[4,168,1024]{2,1,0:T(8,128)(2,1)S(1)}, bf16[4,168,1024]{2,1,0:T(8,128)(2,1)}, u32[]{:S(2)}) copy-start(bf16[4,168,1024]{2,1,0:T(8,128)(2,1)} %copy-done.8) | copy-start | bytes 4128772
  162.0 8.9 %copy-start.11 = (bf16[4,168,1024]{2,1,0:T(8,128)(2,1)S(1)}, bf16[4,168,1024]{2,1,0:T(8,128)(2,1)}, u32[]{:S(2)}) copy-start(bf16[4,168,1024]{2,1,0:T(8,128)(2,1)} %copy-done.10) | copy-start | bytes 4128772
  167.7 1.7 copy-start.1
  169.3 1.6 copy-start.3
  171.0 12.4 %copy-start.2 = (bf16[4,512,672]{2,1,0:T(8,128)(2,1)S(1)}, bf16[4,512,672]{2,1,0:T(8,128)(2,1)}, u32[]{:S(2)}) copy-start(bf16[4,512,672]{2,1,0:T(8,128)(2,1)} %copy-done.1) | copy-start | bytes 8257540
  171.0 12.5 %copy-start.4 = (bf16[4,512,672]{2,1,0:T(8,128)(2,1)S(1)}, bf16[4,512,672]{2,1,0:T(8,128)(2,1)}, u32[]{:S(2)}) copy-start(bf16[4,512,672]{2,1,0:T(8,128)(2,1)} %copy-done.3) | copy-start | bytes 8257540
  171.0 12.5 %copy-start.12 = (f32[512,128]{1,0:T(8,128)S(1)}, f32[512,128]{1,0:T(8,128)}, u32[]{:S(2)}) copy-start(f32[512,128]{1,0:T(8,128)} %get-tuple-element.33.sine) | copy-start | bytes 786436
  171.0 12.5 %copy-start.14 = (f32[128]{0:T(128)S(1)}, f32[128]{0:T(128)}, u32[]{:S(2)}) copy-start(f32[128]{0:T(128)} %param.17) | copy-start | bytes 1540
  183.5 1.6 copy-start.6
  185.0 12.9 %copy-start.15 = (f32[128]{0:T(128)S(1)}, f32[128]{0:T(128)}, u32[]{:S(2)}) copy-start(f32[128]{0:T(128)} %param.16) | copy-start | bytes 1540
  190.6 20.0 %collective-permute-start.15 = (bf16[512,512]{1,0:T(8,128)(2,1)}, bf16[512,512]{1,0:T(8,128)(2,1)}, u32[]{:S(2)}, u32[]{:S(2)}) collective-permute-start(bf16[512,512]{1,0:T(8,128)(2,1)} %shard_map.94.k_ref.v_ref), channel_id=1, source_target_pairs={{0,4},{4,8},{8,12},{12,16},{16,20},{20,24},{24,28},{28,32},{32,36}... | collective-permute-start | bytes 1572872 | tf_op jit(solution)/shard_map/ppermute | solution.py:29
  194.1 34.0 %collective-permute-start.16 = (bf16[512,512]{1,0:T(8,128)(2,1)}, bf16[512,512]{1,0:T(8,128)(2,1)}, u32[]{:S(2)}, u32[]{:S(2)}) collective-permute-start(bf16[512,512]{1,0:T(8,128)(2,1)} %shard_map.94.k_ref.v_ref), channel_id=1, source_target_pairs={{0,8},{4,12},{8,16},{12,20},{16,24},{20,28},{24,32},{28,36},{32,40... | collective-permute-start | bytes 1572872 | tf_op jit(solution)/shard_map/ppermute | solution.py:29
  197.9 1.9 copy-start.5
  199.8 1.6 copy-start.7
  201.4 0.9 copy-start.13
  232.4 14.8 %collective-permute-start.21 = (bf16[512,512]{1,0:T(8,128)(2,1)S(1)}, bf16[512,512]{1,0:T(8,128)(2,1)S(1)}, u32[]{:S(2)}, u32[]{:S(2)}) collective-permute-start(bf16[512,512]{1,0:T(8,128)(2,1)S(1)} %shard_map.96), channel_id=1, source_target_pairs={{0,2},{2,0},{1,3},{3,1},{4,6},{6,4},{5,7},{7,5},{8,10},{10,8},{9,1... | collective-permute-start | bytes 1572872 | tf_op jit(solution)/shard_map/ppermute | solution.py:24
  233.9 15.6 %collective-permute-start.19 = (bf16[512,512]{1,0:T(8,128)(2,1)S(1)}, bf16[512,512]{1,0:T(8,128)(2,1)S(1)}, u32[]{:S(2)}, u32[]{:S(2)}) collective-permute-start(bf16[512,512]{1,0:T(8,128)(2,1)S(1)} %shard_map.96), channel_id=1, source_target_pairs={{0,1},{1,0},{2,3},{3,2},{4,5},{5,4},{6,7},{7,6},{8,9},{9,8},{10,11... | collective-permute-start | bytes 1572872 | tf_op jit(solution)/shard_map/ppermute | solution.py:24
  247.1 6.9 %collective-permute-start.22 = (bf16[512,512]{1,0:T(8,128)(2,1)S(1)}, bf16[512,512]{1,0:T(8,128)(2,1)S(1)}, u32[]{:S(2)}, u32[]{:S(2)}) collective-permute-start(bf16[512,512]{1,0:T(8,128)(2,1)S(1)} %collective-permute-done.21), channel_id=1, source_target_pairs={{0,1},{1,0},{2,3},{3,2},{4,5},{5,4},{6,7},{7,6},{8,9},{9,8},{10,11... | collective-permute-start | bytes 1572872 | tf_op jit(solution)/shard_map/ppermute | solution.py:24
  254.0 11.0 %copy-start.19 = (f32[1344]{0:T(1024)S(1)}, f32[1344]{0:T(1024)}, u32[]{:S(2)}) copy-start(f32[1344]{0:T(1024)} %param.15) | copy-start | bytes 16132
Sparse Core Ops, SparseCore 0:
  18.7 86.2 all-gather.3
  106.7 44.4 all-gather.5

commit v3 on v2

--- a/solution.py
+++ b/solution.py
@@ -12,6 +12,7 @@
 HEAD_SIZE = 128
 WINDOW_LENGTH = 1024
 SHARD = MODEL_WIDTH // 32
+VMEM = 56 << 20
 
 score_scale = 168.0 ** (-0.5)
 epsilon = 1e-06
@@ -33,39 +34,68 @@
     return lax.optimization_barrier((values, done))[0]
 
 
-def place(buffer, piece, index):
-    return lax.dynamic_update_index_in_dim(buffer, piece, index, 0)
-
-
-def in_line(pieces, at):
-    line = jnp.zeros((4,) + pieces[0].shape, pieces[0].dtype)
-    for piece, offset in zip(pieces, (0, -1, 1, 2)):
-        line = place(line, piece, (at + offset) % 4)
-    return line.reshape(4 * pieces[0].shape[0], -1)
-
-
-def norm_kernel(side, own_ref, other_ref, own_gain, other_gain, near_ref, far_ref):
+def line_kernel(at, *refs):
+    pieces, (first, second), sems = refs[:4], refs[4:6], refs[6]
+    cut = first.shape[2]
+    copies = []
+    for k, (piece, offset) in enumerate(zip(pieces, (0, 3, 1, 2))):
+        slot = lax.rem(at[0] + offset, 4)
+        copies.append(pltpu.make_async_copy(piece.at[:, :cut], first.at[slot], sems.at[0, k]))
+        copies.append(pltpu.make_async_copy(piece.at[:, cut:], second.at[slot], sems.at[1, k]))
+    for copy in copies:
+        copy.start()
+    for copy in copies:
+        copy.wait()
+
+
+def in_line(pieces, at, cut):
+    depth, columns = pieces[0].shape
+    anywhere = pl.BlockSpec(memory_space=pl.ANY)
+    shapes = [
+        jax.ShapeDtypeStruct((4, depth, cut), jnp.bfloat16),
+        jax.ShapeDtypeStruct((4, depth, columns - cut), jnp.bfloat16),
+    ]
+    first, second = pl.pallas_call(
+        line_kernel,
+        grid_spec=pltpu.PrefetchScalarGridSpec(
+            num_scalar_prefetch=1,
+            grid=(1,),
+            in_specs=[anywhere] * 4,
+            out_specs=[anywhere] * 2,
+            scratch_shapes=[pltpu.SemaphoreType.DMA((2, 4))],
+        ),
+        out_shape=shapes,
+        compiler_params=pltpu.CompilerParams(vmem_limit_bytes=VMEM),
+        cost_estimate=pl.CostEstimate(flops=0, bytes_accessed=3_000_000, transcendentals=0),
+    )(at[None], *pieces)
+    return first.reshape(4 * depth, cut), second.reshape(4 * depth, columns - cut)
+
+
+def norm_kernel(side, own_ref, other_ref, near_gain, far_gain, near_ref, far_ref):
     own = own_ref[0].astype(jnp.float32)
     other = other_ref[0].astype(jnp.float32)
-    total = jnp.sum(own * own, axis=-1, keepdims=True) + jnp.sum(other * other, axis=-1, keepdims=True)
-    scale = lax.rsqrt((total[0] + total[1]) / MODEL_WIDTH + epsilon)
-    own = (own * scale[None] * own_gain[0]).astype(jnp.bfloat16)
-    other = (other * scale[None] * other_gain[0]).astype(jnp.bfloat16)
+    total = jnp.sum(own * own, axis=(0, 1)) + jnp.sum(other * other, axis=(0, 1))
+    scale = lax.rsqrt(total / MODEL_WIDTH + epsilon)[None, None]
+    own = own * scale
+    other = other * scale
     for i in range(4):
-        for j in range(4):
-            start = ((j % 2) * 4 + i) * SHARD
-            near_ref[i, :, j * SHARD : (j + 1) * SHARD] = own[j // 2][:, start : start + SHARD]
-        far_ref[i] = other[i // 2][:, (i % 2) * 4 * SHARD : ((i % 2) * 4 + 4) * SHARD]
+        starts = [(j // 2, ((j % 2) * 4 + i) * SHARD) for j in range(4)]
+        part = jnp.concatenate([own[k, s : s + SHARD] for k, s in starts], axis=0)
+        near_ref[i] = (part.T * near_gain[0, i]).astype(jnp.bfloat16)
+        start = (i % 2) * 4 * SHARD
+        part = other[i // 2, start : start + 4 * SHARD]
+        far_ref[i] = (part.T * far_gain[0, i]).astype(jnp.bfloat16)
 
 
 def norm_parts(pieces, gain, side):
-    rows = pieces.shape[1]
-    width = pieces.shape[2]
-    step = 64
-    pieces = pieces.reshape(2, 2, rows, width)
-    gain = gain.reshape(2, 2, 1, width)
-    half = lambda flip: pl.BlockSpec((1, 2, step, width), lambda i, s: (s[flip], 0, i, 0))
-    gains = lambda flip: pl.BlockSpec((1, 2, 1, width), lambda i, s: (s[flip], 0, 0, 0))
+    width, rows = pieces.shape[1:]
+    step = 128
+    pieces = pieces.reshape(2, 2, width, rows)
+    far_gain = gain.reshape(2, 4, 4, SHARD)
+    near_gain = jnp.swapaxes(far_gain, 1, 2).reshape(2, 4, 1, 4 * SHARD)
+    far_gain = far_gain.reshape(2, 4, 1, 4 * SHARD)
+    half = lambda flip: pl.BlockSpec((1, 2, width, step), lambda i, s: (s[flip], 0, 0, i))
+    gains = lambda flip: pl.BlockSpec((1, 4, 1, 4 * SHARD), lambda i, s: (s[flip], 0, 0, 0))
     out = pl.BlockSpec((4, step, 4 * SHARD), lambda i, s: (0, i, 0))
     shape = jax.ShapeDtypeStruct((4, rows, 4 * SHARD), jnp.bfloat16)
     return pl.pallas_call(
@@ -77,9 +107,9 @@
             out_specs=[out, out],
         ),
         out_shape=[shape, shape],
-        compiler_params=pltpu.CompilerParams(vmem_limit_bytes=40 << 20),
+        compiler_params=pltpu.CompilerParams(vmem_limit_bytes=VMEM),
         cost_estimate=pl.CostEstimate(flops=20_000_000, bytes_accessed=12_000_000, transcendentals=0),
-    )(jnp.stack([side, 1 - side]), pieces, pieces, gain, gain)
+    )(jnp.stack([side, 1 - side]), pieces, pieces, near_gain, far_gain)
 
 
 def accumulate(index, near_ref, far_ref, weights, w_buf, t_buf, sems, total, n_near):
@@ -95,16 +125,15 @@
     for pair in copies:
         for copy in pair:
             copy.start()
-    rows = total.shape[0]
     for k, pair in enumerate(copies):
         for copy in pair:
             copy.wait()
 
-        @pl.loop(0, rows // 128)
+        @pl.loop(0, total.shape[1] // 256)
         def _(i):
-            at = pl.ds(pl.multiple_of(i * 128, 128), 128)
-            part = jnp.dot(t_buf[k, at, :], w_buf[k], preferred_element_type=jnp.float32)
-            total[at, :] = part if (k == 0 and n_near == 3) else total[at, :] + part
+            at = pl.ds(pl.multiple_of(i * 256, 256), 256)
+            part = jnp.dot(t_buf[k], w_buf[k, :, at], preferred_element_type=jnp.float32)
+            total[:, at] = part if (k == 0 and n_near == 3) else total[:, at] + part
 
 
 def early_kernel(index, near_ref, far_ref, *refs):
@@ -130,9 +159,9 @@
             ],
         ),
         out_shape=jax.ShapeDtypeStruct((rows, columns), jnp.float32),
-        compiler_params=pltpu.CompilerParams(vmem_limit_bytes=48 << 20),
-        cost_estimate=pl.CostEstimate(
-            flops=2 * rows * depth * columns * count, bytes_accessed=16_000_000, transcendentals=0
+        compiler_params=pltpu.CompilerParams(vmem_limit_bytes=VMEM),
+        cost_estimate=pl.CostEstimate(
+            flops=2 * rows * depth * columns * count, bytes_accessed=10_000_000, transcendentals=0
         ),
     )(index, near, far, *weights)
 
@@ -157,7 +186,7 @@
             out_ref[at, lanes] = raw.astype(jnp.bfloat16)
 
 
-def late_product(heads, column, index, near, far, w_near, w_far, before, gain, cosine, sine):
+def late_product(heads, index, near, far, w_near, w_far, before, gain, cosine, sine):
     rows, depth = near.shape[1:]
     columns = w_near.shape[1]
     anywhere = pl.BlockSpec(memory_space=pl.ANY)
@@ -169,7 +198,7 @@
             grid=(1,),
             in_specs=[anywhere] * 4
             + [
-                pl.BlockSpec((rows, columns), lambda i, s: (0, column)),
+                pl.BlockSpec((rows, columns), lambda i, s: (0, 0)),
                 pl.BlockSpec((1, HEAD_SIZE), lambda i, s: (0, 0)),
                 table,
                 table,
@@ -183,7 +212,7 @@
             ],
         ),
         out_shape=jax.ShapeDtypeStruct((rows, columns), jnp.bfloat16),
-        compiler_params=pltpu.CompilerParams(vmem_limit_bytes=40 << 20),
+        compiler_params=pltpu.CompilerParams(vmem_limit_bytes=VMEM),
         cost_estimate=pl.CostEstimate(
             flops=4 * rows * depth * columns, bytes_accessed=6_000_000, transcendentals=0
         ),
@@ -262,7 +291,7 @@
         ],
         out_specs=[pair, pair],
         out_shape=[shape, shape],
-        compiler_params=pltpu.CompilerParams(vmem_limit_bytes=32 << 20),
+        compiler_params=pltpu.CompilerParams(vmem_limit_bytes=VMEM),
         cost_estimate=pl.CostEstimate(
             flops=4 * rows * rows * columns, bytes_accessed=3_000_000, transcendentals=rows * rows * 4
         ),
@@ -284,11 +313,71 @@
             out_specs=pair,
         ),
         out_shape=jax.ShapeDtypeStruct((rows, columns), jnp.bfloat16),
-        compiler_params=pltpu.CompilerParams(vmem_limit_bytes=32 << 20),
+        compiler_params=pltpu.CompilerParams(vmem_limit_bytes=VMEM),
         cost_estimate=pl.CostEstimate(
             flops=8 * rows * rows * columns, bytes_accessed=4_000_000, transcendentals=rows * rows * 8
         ),
     )(valid, queries, one, one, two, two, sums, weights)
+
+
+def first_kernel(w_ref, c_ref, out_ref):
+    out_ref[...] = lax.dot_general(
+        w_ref[...], c_ref[...], (((1,), (1,)), ((), ())), preferred_element_type=jnp.float32
+    )
+
+
+def second_kernel(half, w_ref, c_ref, before_ref, out_ref):
+    out_ref[...] = (
+        before_ref[...]
+        + lax.dot_general(
+            w_ref[...], c_ref[...], (((1,), (1,)), ((), ())), preferred_element_type=jnp.float32
+        )
+    ).astype(out_ref.dtype)
+
+
+def out_first(weight, context):
+    rows, depth = context.shape
+    columns = weight.shape[0]
+    tile = 672
+    return pl.pallas_call(
+        first_kernel,
+        grid=(columns // tile,),
+        in_specs=[
+            pl.BlockSpec((tile, depth), lambda i: (i, 0)),
+            pl.BlockSpec((rows, depth), lambda i: (0, 0)),
+        ],
+        out_specs=pl.BlockSpec((tile, rows), lambda i: (i, 0)),
+        out_shape=jax.ShapeDtypeStruct((columns, rows), jnp.float32),
+        compiler_params=pltpu.CompilerParams(vmem_limit_bytes=VMEM),
+        cost_estimate=pl.CostEstimate(
+            flops=2 * rows * depth * columns, bytes_accessed=9_000_000, transcendentals=0
+        ),
+    )(weight, context)
+
+
+def out_second(half, weight, context, before, dtype):
+    rows, depth = context.shape
+    columns = weight.shape[0] // 2
+    tile = 672
+    steps = columns // tile
+    return pl.pallas_call(
+        second_kernel,
+        grid_spec=pltpu.PrefetchScalarGridSpec(
+            num_scalar_prefetch=1,
+            grid=(steps,),
+            in_specs=[
+                pl.BlockSpec((tile, depth), lambda i, s: (s[0] * steps + i, 1)),
+                pl.BlockSpec((rows, depth), lambda i, s: (0, 0)),
+                pl.BlockSpec((tile, rows), lambda i, s: (s[0] * steps + i, 0)),
+            ],
+            out_specs=pl.BlockSpec((tile, rows), lambda i, s: (i, 0)),
+        ),
+        out_shape=jax.ShapeDtypeStruct((columns, rows), dtype),
+        compiler_params=pltpu.CompilerParams(vmem_limit_bytes=VMEM),
+        cost_estimate=pl.CostEstimate(
+            flops=2 * rows * depth * columns, bytes_accessed=6_000_000, transcendentals=0
+        ),
+    )(half[None], weight, context, before)
 
 
 def local(
@@ -298,34 +387,37 @@
     q_cols = q_weight.shape[1]
     yl, x, z, yh, c = (lax.axis_index(name) for name in ("yl", "x", "z", "yh", "c"))
     seq_index = (yl * 4 + x) * 4 + z
-    whole = lax.all_gather(tokens, MP, axis=0)
+    whole = lax.all_gather(tokens.T, MP, axis=0)
 
     own = jnp.concatenate([q_weight, key_matrix, value_matrix], axis=1)
     other = shift(own, "yl", 1)
-    own_line = in_line([own] + [shift(own, "x", step) for step in (1, 3, 2)], x)
-    other_line = in_line([other] + [shift(other, "z", step) for step in (1, 3, 2)], z)
-    own_line, other_line = lax.optimization_barrier((own_line, other_line))
-    own_ahead, own_behind = shift(own_line, "z", 1), shift(own_line, "z", 3)
-    other_ahead, other_behind = shift(other_line, "x", 1), shift(other_line, "x", 3)
-    own_ahead, own_behind, other_ahead, other_behind = lax.optimization_barrier(
-        (own_ahead, own_behind, other_ahead, other_behind)
-    )
-    own_far_q = shift(own_ahead[:, :q_cols], "z", 1)
-    own_far_kv = shift(own_behind[:, q_cols:], "z", 3)
-    other_far_q = shift(other_ahead[:, :q_cols], "x", 1)
-    other_far_kv = shift(other_behind[:, q_cols:], "x", 3)
-
-    turned = o_weight.T
+    own_pieces = [own] + [shift(own, "x", step) for step in (1, 3, 2)]
+    other_pieces = [other] + [shift(other, "z", step) for step in (1, 3, 2)]
+    own_q, own_kv = in_line(own_pieces, x, q_cols)
+    other_q, other_kv = in_line(other_pieces, z, q_cols)
+    own_q, own_kv, other_q, other_kv, turned = lax.optimization_barrier(
+        (own_q, own_kv, other_q, other_kv, o_weight.T)
+    )
+    own_ahead_q, own_behind_kv = shift(own_q, "z", 1), shift(own_kv, "z", 3)
+    other_ahead_q, other_behind_kv = shift(other_q, "x", 1), shift(other_kv, "x", 3)
+    own_ahead_kv, own_behind_q = shift(own_kv, "z", 1), shift(own_q, "z", 3)
+    other_ahead_kv, other_behind_q = shift(other_kv, "x", 1), shift(other_q, "x", 3)
+    own_ahead_q, own_behind_kv, other_ahead_q, other_behind_kv, whole = lax.optimization_barrier(
+        (own_ahead_q, own_behind_kv, other_ahead_q, other_behind_kv, whole)
+    )
+    own_far_kv = shift(own_behind_kv, "z", 3)
+    other_far_kv = shift(other_behind_kv, "x", 3)
+    own_far_q = shift(own_ahead_q, "z", 1)
+    other_far_q = shift(other_ahead_q, "x", 1)
+
     y = yh * 2 + yl
     flat = lambda p: (p % 2) * 2 + p // 2
     one = lax.ppermute(turned, ("yl", "yh"), [(flat(a), flat(b)) for a, b in ((0, 1), (2, 0), (1, 3), (3, 2))])
     two = lax.ppermute(turned, ("yl", "yh"), [(flat(a), flat(b)) for a, b in ((1, 2), (2, 1))])
     outer = (y == 0) | (y == 3)
     pair = jnp.concatenate([jnp.where(outer, turned, one), jnp.where(outer, one, two)], axis=1)
+    pair, whole = lax.optimization_barrier((pair, whole))
     out_all = lax.all_gather(pair, ("x", "z"), axis=0, tiled=True)
-    half_rows = out_all.shape[0] // 2
-    out_mine = lax.dynamic_slice_in_dim(out_all, c * half_rows, half_rows, 0)
-    out_theirs = shift(lax.dynamic_slice_in_dim(out_all, (1 - c) * half_rows, half_rows, 0), "c", 1)
 
     positions = seq_index * rows + jnp.arange(rows, dtype=jnp.int32)
     half = HEAD_SIZE // 2
@@ -338,30 +430,33 @@
 
     near, far = norm_parts(whole, pre_gain, yl)
     index = jnp.stack([z, (z + 3) % 4, (z + 1) % 4, x, (x + 3) % 4, (x + 1) % 4])
-    total = early_product(
-        index, near, far, (own_line, own_ahead, own_behind, other_line, other_ahead, other_behind)
+    early_kv = early_product(
+        index, near, far, (own_kv, own_ahead_kv, own_behind_kv, other_kv, other_ahead_kv, other_behind_kv)
+    )
+    early_q = early_product(
+        index, near, far, (own_q, own_ahead_q, own_behind_q, other_q, other_ahead_q, other_behind_q)
     )
     last = jnp.stack([(z + 2) % 4, (x + 2) % 4])
     keyed = late_product(
-        2, 1, last, near, far, own_far_kv, other_far_kv, total, k_gain[None], cosine, sine
+        2, last, near, far, own_far_kv, other_far_kv, early_kv, k_gain[None], cosine, sine
     )
     behind_one = from_behind(keyed, 1)
     behind_two = from_behind(keyed, 2)
     queries = late_product(
-        4, 0, last, near, far, own_far_q, other_far_q, total, q_gain[None], cosine, sine
+        4, last, near, far, own_far_q, other_far_q, early_q, q_gain[None], cosine, sine
     )
     sums, weights = attend_own(queries, keyed)
     valid = jnp.stack([seq_index >= 1, seq_index >= 2]).astype(jnp.int32)
     context = attend_behind(valid, queries, behind_one, behind_two, sums, weights)
 
     across = shift(context, "yh", 1)
-    theirs = shift(context, "c", 1)
-    product = lambda a, b: lax.dot_general(
-        a, b, (((1,), (1,)), ((), ())), preferred_element_type=jnp.float32
-    )
-    share = product(context, out_mine[:, :q_cols]) + product(theirs, out_theirs[:, :q_cols])
-    theirs_across = shift(across, "c", 1)
-    share = share + product(across, out_mine[:, q_cols:]) + product(theirs_across, out_theirs[:, q_cols:])
+    out_all, context = lax.optimization_barrier((out_all, context))
+    before = out_first(out_all, context)
+    across, before = lax.optimization_barrier((across, before))
+    sent = out_second(1 - c, out_all, across, before, jnp.bfloat16)
+    received = shift(sent, "c", 1)
+    kept = out_second(c, out_all, across, before, jnp.float32)
+    share = (kept + received.astype(jnp.float32)).T
     total = lax.psum(jnp.sum(share * share, axis=1), MP)
     scale_rows = lax.rsqrt(total / MODEL_WIDTH + epsilon)
     return (tokens.astype(jnp.float32) + share * scale_rows[:, None] * post_gain).astype(

time: 276 us -> 277 us (level)
  Pallas kernels: 36 us -> 146 us
  waiting for transfers between devices: 131 us -> 46.3 us
  local copies, waits for them, and re-layouts: 36.3 us -> 9.2 us
  starting transfers between devices: 32.6 us -> 41.8 us
  matrix products: 9.12 us -> 0 us
  other arithmetic: 6.73 us -> 10.6 us
    pallas_call x0 -> x5, Pallas kernels: none -> 99.2 us  [the longest x2 85.7 us: in_line(): pl.pallas_call(line_kernel, grid_spec=pltpu.PrefetchScalarGridSpec(num_sc...]
    all_gather x1, waiting for transfers between devices: 48.1 us -> 0.01 us  [local(): out_all = lax.all_gather(pair, ('x', 'z'), axis=0, tiled=True)]
    all_gather x1, waiting for transfers between devices: 27.4 us -> 0.01 us  [local(): whole = lax.all_gather(tokens.T, MP, axis=0)]
    ppermute x2, waiting for transfers between devices: 17.5 us -> 6.78 us  [from_behind(): lax.ppermute(value, SEQ, [(source, source + steps) for source in range(co...]
    dot_general x4 -> x0, matrix products: 9.12 us -> none  [local(): lax.dot_general(a, b, (((1,), (1,)), ((), ())), preferred_element_type=jn...]
    all_gather x1 -> x0, local copies, waits for them, and re-layouts: 8.24 us -> none  [local(): whole = lax.all_gather(tokens, MP, axis=0)]
    slice x4 -> x0, local copies, waits for them, and re-layouts: 8.09 us -> none  [the longest x1 2.09 us: local(): own_far_q = shift(own_ahead[:, :q_cols], 'z', 1)]
    unnamed x42, local copies, waits for them, and re-layouts: 12 us -> 6.15 us
  transfers between devices with their start and end apart: 25 -> 27, of which waited for: 11 -> 12; matrix products, arithmetic and copies ran while one was open for 12% -> 3% of each run, Pallas kernels for 13% -> 52%
where the time goes in v3:
time: 277 us; the launch traced here: 276 us
  Pallas kernels  146 us (53%)
  waiting for transfers between devices  46.3 us (17%)
  starting transfers between devices  41.8 us (15%)
  between operations  13.7 us (5%)
  other arithmetic  10.6 us (4%)
  local copies, waits for them, and re-layouts  9.2 us (3%)
  blocking collectives  8.11 us (3%)
    pallas_call x2, Pallas kernels, in_line(): pl.pallas_call(line_kernel, grid_spec=pltpu.PrefetchScalarGridSpec(num_sc...  85.7 us
    ppermute x21, waiting for transfers between devices, shift(): lax.ppermute(value, axis, [(i, (i + step) % count) for i in range(count)])  33.9 us
    ppermute x21, starting transfers between devices, shift(): lax.ppermute(value, axis, [(i, (i + step) % count) for i in range(count)])  26.6 us
    pallas_call x2, Pallas kernels, early_product(): pl.pallas_call(early_kernel, grid_spec=pltpu.PrefetchScalarGridSpec(num_s...  15.2 us
    pallas_call x2, Pallas kernels, late_product(): pl.pallas_call(functools.partial(late_kernel, heads), grid_spec=pltpu.Pre...  13.6 us
    ppermute x2, starting transfers between devices, from_behind(): lax.ppermute(value, SEQ, [(source, source + steps) for source in range(co...  10.2 us
    pallas_call x1, Pallas kernels, norm_parts(): pl.pallas_call(norm_kernel, grid_spec=pltpu.PrefetchScalarGridSpec(num_sc...  9.2 us
    psum x1, blocking collectives, local(): total = lax.psum(jnp.sum(share * share, axis=1), MP)  8.11 us
  transfers between devices with their start and end apart: 27, of which 12 were waited for; matrix products, arithmetic and copies ran while one was open for 3% of the time, Pallas kernels for 52%

profile of v3, /device:TPU:40, one launch (start us, length us, event | category | flops | bytes accessed | tf_op | source)
XLA Modules:
  0.0 276.1 jit_solution(13955047105783160455)
XLA Ops:
  6.5 0.7 all-gather.6.cloned.1.call-update
  7.3 0.9 constant_dynamic-update-slice_fusion.2
  8.2 0.9 constant_dynamic-update-slice_fusion.1
  9.1 0.9 constant_dynamic-update-slice_fusion.refs_0_
  10.0 0.5 collective-permute-start.3
  10.6 1.5 collective-permute-start
  12.1 1.7 collective-permute-start.1
  13.8 1.8 collective-permute-start.2
  15.6 4.3 %collective-permute-done.3.refs_0_ = bf16[168,1024]{1,0:T(8,128)(2,1)S(1)} collective-permute-done((bf16[168,1024]{1,0:T(8,128)(2,1)S(1)}, bf16[168,1024]{1,0:T(8,128)(2,1)S(1)}, u32[]{:S(2)}, u32[]{:S(2)}) %collective-permute-start.3) | collective-permute-done | bytes 344096 | tf_op jit(solution)/shard_map/ppermute | solution.py:25
  19.9 1.9 collective-permute-start.4
  22.0 3.0 %collective-permute-start.6 = (bf16[168,1024]{1,0:T(8,128)(2,1)S(1)}, bf16[168,1024]{1,0:T(8,128)(2,1)S(1)}, u32[]{:S(2)}, u32[]{:S(2)}) collective-permute-start(bf16[168,1024]{1,0:T(8,128)(2,1)S(1)} %collective-permute-done.3.refs_0_), channel_id=1, source_target_pairs={{0,8},{4,12},{8,0},{12,4},{1,9},{5,13},{9,1},{13,5},{2,10},{6,14},... | collective-permute-start | bytes 1032200 | tf_op jit(solution)/shard_map/ppermute | solution.py:25
  24.9 3.0 %collective-permute-done.1.refs_2_ = bf16[168,1024]{1,0:T(8,128)(2,1)S(1)} collective-permute-done((bf16[168,1024]{1,0:T(8,128)(2,1)S(1)}, bf16[168,1024]{1,0:T(8,128)(2,1)S(1)}, u32[]{:S(2)}, u32[]{:S(2)}) %collective-permute-start.1) | collective-permute-done | bytes 344096 | tf_op jit(solution)/shard_map/ppermute | solution.py:25
  28.0 1.7 collective-permute-done.2.refs_3_
  29.7 0.7 copy-done.15
  30.4 42.9 %shard_map.91 = (bf16[4,168,512]{2,1,0:T(8,128)(2,1)}, bf16[4,168,512]{2,1,0:T(8,128)(2,1)}) custom-call(s32[1]{0:T(128)} %bitcast.1.at, bf16[168,1024]{1,0:T(8,128)(2,1)} %copy-done.5, bf16[168,1024]{1,0:T(8,128)(2,1)} %copy-done.12, bf16[168,1024]{1,0:T(8,128)(2,1)} %copy-done.14, bf16[168,1024]{1,0:T(8,128)(2,1)} %copy-done.15), custom_call_target="tpu_custom_call" | custom-call | bytes 3000000 | tf_op jit(solution)/shard_map/pallas_call | solution.py:58
  73.4 0.7 copy-done.11
  74.0 0.1 copy-done.13
  74.2 42.9 %shard_map.92 = (bf16[4,168,512]{2,1,0:T(8,128)(2,1)}, bf16[4,168,512]{2,1,0:T(8,128)(2,1)}) custom-call(s32[1]{0:T(128)} %bitcast.4.at, bf16[168,1024]{1,0:T(8,128)(2,1)} %copy-done.10, bf16[168,1024]{1,0:T(8,128)(2,1)} %copy-done.11, bf16[168,1024]{1,0:T(8,128)(2,1)} %copy-done.13, bf16[168,1024]{1,0:T(8,128)(2,1)} %copy-done.16), custom_call_target="tpu_custom_call" | custom-call | bytes 3000000 | tf_op jit(solution)/shard_map/pallas_call | solution.py:58
  117.1 2.7 collective-permute-start.7
  119.8 0.1 collective-permute-start.10
  119.9 1.1 collective-permute-start.11
  121.0 2.1 collective-permute-start.12
  123.1 1.9 collective-permute-start.9
  125.1 2.3 collective-permute-start.8
  127.4 4.9 %collective-permute-done.8 = bf16[168,512]{1,0:T(8,128)(2,1)S(1)} collective-permute-done((bf16[168,512]{1,0:T(8,128)(2,1)S(1)}, bf16[168,512]{1,0:T(8,128)(2,1)S(1)}, u32[]{:S(2)}, u32[]{:S(2)}) %collective-permute-start.8) | collective-permute-done | bytes 172064 | tf_op jit(solution)/shard_map/ppermute | solution.py:416
  132.4 0.8 pad_maximum_fusion
  133.2 2.9 %collective-permute-done.10.refs_2_ = bf16[672,512]{1,0:T(8,128)(2,1)} collective-permute-done((bf16[672,512]{1,0:T(8,128)(2,1)}, bf16[672,512]{1,0:T(8,128)(2,1)}, u32[]{:S(2)}, u32[]{:S(2)}) %collective-permute-start.10) | collective-permute-done | bytes 688160 | tf_op jit(solution)/shard_map/ppermute | solution.py:25
  136.1 0.9 collective-permute-done.11.refs_4_
  137.0 3.6 %collective-permute-done.9.refs_1_ = bf16[672,512]{1,0:T(8,128)(2,1)S(1)} collective-permute-done((bf16[672,512]{1,0:T(8,128)(2,1)}, bf16[672,512]{1,0:T(8,128)(2,1)S(1)}, u32[]{:S(2)}, u32[]{:S(2)}) %collective-permute-start.9) | collective-permute-done | bytes 688160 | tf_op jit(solution)/shard_map/ppermute | solution.py:25
  140.8 3.0 %collective-permute-start.17 = (bf16[672,512]{1,0:T(8,128)(2,1)}, bf16[672,512]{1,0:T(8,128)(2,1)}, u32[]{:S(2)}, u32[]{:S(2)}) collective-permute-start(bf16[672,512]{1,0:T(8,128)(2,1)} %collective-permute-done.10.refs_2_), channel_id=1, source_target_pairs={{0,12},{4,0},{8,4},{12,8},{1,13},{5,1},{9,5},{13,9},{2,14},{6,2},{... | collective-permute-start | bytes 2064392 | tf_op jit(solution)/shard_map/ppermute | solution.py:25
  143.9 3.1 %collective-permute-start.15 = (bf16[672,512]{1,0:T(8,128)(2,1)S(1)}, bf16[672,512]{1,0:T(8,128)(2,1)}, u32[]{:S(2)}, u32[]{:S(2)}) collective-permute-start(bf16[672,512]{1,0:T(8,128)(2,1)S(1)} %bitcast.34), channel_id=1, source_target_pairs={{0,12},{4,0},{8,4},{12,8},{1,13},{5,1},{9,5},{13,9},{2,14},{6,2},{... | collective-permute-start | bytes 2064392 | tf_op jit(solution)/shard_map/ppermute | solution.py:25
  147.0 3.2 %collective-permute-start.18 = (bf16[672,512]{1,0:T(8,128)(2,1)}, bf16[672,512]{1,0:T(8,128)(2,1)}, u32[]{:S(2)}, u32[]{:S(2)}) collective-permute-start(bf16[672,512]{1,0:T(8,128)(2,1)} %collective-permute-done.12.refs_5_), channel_id=1, source_target_pairs={{0,48},{16,0},{32,16},{48,32},{1,49},{17,1},{33,17},{49,33},{2,50}... | collective-permute-start | bytes 2064392 | tf_op jit(solution)/shard_map/ppermute | solution.py:25
  150.2 1.0 fusion.1
  151.3 1.0 pad_maximum_fusion.1
  152.3 9.2 %collective-permute-done.19.refs_1_ = bf16[672,512]{1,0:T(8,128)(2,1)} collective-permute-done((bf16[672,512]{1,0:T(8,128)(2,1)}, bf16[672,512]{1,0:T(8,128)(2,1)}, u32[]{:S(2)}, u32[]{:S(2)}) %collective-permute-start.19) | collective-permute-done | bytes 688160 | tf_op jit(solution)/shard_map/ppermute | solution.py:25
  161.5 0.7 pad_add_fusion.1.side
  162.2 1.2 collective-permute-done.20.refs_4_
  163.4 2.1 collective-permute-done.17.w_near
  165.6 0.6 pad_add_fusion.index
  166.3 0.7 reshape_reshape.3.far_gain
  167.0 0.7 reshape.41.near_gain
  167.7 0.6 stack.57.index
  168.3 9.2 %shard_map.93 = (bf16[4,512,672]{2,1,0:T(8,128)(2,1)}, bf16[4,512,672]{2,1,0:T(8,128)(2,1)}) custom-call(s32[2]{0:T(128)} %pad_add_fusion.1.side, bf16[2,2,1344,512]{3,2,1,0:T(8,128)(2,1)} %bitcast.29, bf16[2,2,1344,512]{3,2,1,0:T(8,128)(2,1)} %bitcast.30, f32[2,4,1,672]{3,2,1,0:T(1,128)} %reshape.41.near_gain, f32[2,4,1,672]{3,2,1,0:T(1,128)} %reshape_reshape.3.far_gain), custom_call_target="tpu_custom_call" | custom-call | flops 20000000 | bytes 12000000 | tf_op jit(solution)/shard_map/pallas_call | solution.py:101
  177.5 7.6 %shard_map.96.before = f32[512,512]{1,0:T(8,128)} custom-call(s32[6]{0:T(128)} %stack.57.index, bf16[4,512,672]{2,1,0:T(8,128)(2,1)} %get-tuple-element.41.near_ref, bf16[4,512,672]{2,1,0:T(8,128)(2,1)} %get-tuple-element.42.far_ref, bf16[672,512]{1,0:T(8,128)(2,1)} %bitcast.3.refs_0_, bf16[672,512]{1,0:T(8,128)(2,1)} %collective-permute-done.19.refs_1_, ...), custom_call_target="tpu_custom_call" | custom-call | flops 2113929216 | bytes 10000000 | tf_op jit(solution)/shard_map/pallas_call | solution.py:148
  185.2 6.5 %shard_map.97.k_ref.v_ref = bf16[512,512]{1,0:T(8,128)(2,1)} custom-call(s32[2]{0:T(128)} %pad_add_fusion.index, bf16[4,512,672]{2,1,0:T(8,128)(2,1)} %get-tuple-element.41.near_ref, bf16[4,512,672]{2,1,0:T(8,128)(2,1)} %get-tuple-element.42.far_ref, bf16[672,512]{1,0:T(8,128)(2,1)} %collective-permute-done.17.w_near, ...), custom_call_target="tpu_custom_call" | custom-call | flops 704643072 | bytes 6000000 | tf_op jit(solution)/shard_map/pallas_call | solution.py:194
  191.7 5.7 %collective-permute-start.21 = (bf16[512,512]{1,0:T(8,128)(2,1)}, bf16[512,512]{1,0:T(8,128)(2,1)S(1)}, u32[]{:S(2)}, u32[]{:S(2)}) collective-permute-start(bf16[512,512]{1,0:T(8,128)(2,1)} %shard_map.97.k_ref.v_ref), channel_id=1, source_target_pairs={{0,4},{4,8},{8,12},{12,16},{16,20},{20,24},{24,28},{28,32},{32,36}... | collective-permute-start | bytes 1572872 | tf_op jit(solution)/shard_map/ppermute | solution.py:30
  197.4 4.5 %collective-permute-start.22 = (bf16[512,512]{1,0:T(8,128)(2,1)}, bf16[512,512]{1,0:T(8,128)(2,1)S(1)}, u32[]{:S(2)}, u32[]{:S(2)}) collective-permute-start(bf16[512,512]{1,0:T(8,128)(2,1)} %shard_map.97.k_ref.v_ref), channel_id=1, source_target_pairs={{0,8},{4,12},{8,16},{12,20},{16,24},{20,28},{24,32},{28,36},{32,40... | collective-permute-start | bytes 1572872 | tf_op jit(solution)/shard_map/ppermute | solution.py:30
  201.9 0.6 add_convert_fusion.1.valid
  202.5 7.6 %shard_map.94.before = f32[512,512]{1,0:T(8,128)} custom-call(s32[6]{0:T(128)} %stack.57.index, bf16[4,512,672]{2,1,0:T(8,128)(2,1)} %get-tuple-element.41.near_ref, bf16[4,512,672]{2,1,0:T(8,128)(2,1)} %get-tuple-element.42.far_ref, bf16[672,512]{1,0:T(8,128)(2,1)} %bitcast.33, bf16[672,512]{1,0:T(8,128)(2,1)} %copy-done.9, ...), custom_call_target="tpu_custom_call" | custom-call | flops 2113929216 | bytes 10000000 | tf_op jit(solution)/shard_map/pallas_call | solution.py:148
  210.1 7.1 %shard_map.95.q_ref = bf16[512,512]{1,0:T(8,128)(2,1)} custom-call(s32[2]{0:T(128)} %pad_add_fusion.index, bf16[4,512,672]{2,1,0:T(8,128)(2,1)} %get-tuple-element.41.near_ref, bf16[4,512,672]{2,1,0:T(8,128)(2,1)} %get-tuple-element.42.far_ref, bf16[672,512]{1,0:T(8,128)(2,1)} %collective-permute-done.13.w_near, ...), custom_call_target="tpu_custom_call" | custom-call | flops 704643072 | bytes 6000000 | tf_op jit(solution)/shard_map/pallas_call | solution.py:194
  217.2 3.7 %shard_map.98 = (f32[512,512]{1,0:T(8,128)}, f32[512,512]{1,0:T(8,128)}) custom-call(bf16[512,512]{1,0:T(8,128)(2,1)} %shard_map.95.q_ref, bf16[512,512]{1,0:T(8,128)(2,1)} %shard_map.97.k_ref.v_ref, bf16[512,512]{1,0:T(8,128)(2,1)} %shard_map.97.k_ref.v_ref), custom_call_target="tpu_custom_call" | custom-call | flops 536870912 | bytes 3000000 | tf_op jit(solution)/shard_map/pallas_call | solution.py:284
  220.9 6.8 %collective-permute-done.22.k2_ref.v2_ref = bf16[512,512]{1,0:T(8,128)(2,1)S(1)} collective-permute-done((bf16[512,512]{1,0:T(8,128)(2,1)}, bf16[512,512]{1,0:T(8,128)(2,1)S(1)}, u32[]{:S(2)}, u32[]{:S(2)}) %collective-permute-start.22) | collective-permute-done | bytes 524320 | tf_op jit(solution)/shard_map/ppermute | solution.py:30
  227.7 0.8 copy-done.4
  228.5 5.4 %shard_map.99.c_ref = bf16[512,512]{1,0:T(8,128)(2,1)} custom-call(s32[2]{0:T(128)} %add_convert_fusion.1.valid, bf16[512,512]{1,0:T(8,128)(2,1)} %shard_map.95.q_ref, bf16[512,512]{1,0:T(8,128)(2,1)} %copy-done.3, bf16[512,512]{1,0:T(8,128)(2,1)} %copy-done.3, bf16[512,512]{1,0:T(8,128)(2,1)} %copy-done.4, bf16[512,512]{1,0:T(8,128)(2,1)} %copy-done.4, ...), custom_call_target="tpu_custom_call" | custom-call | flops 1073741824 | bytes 4000000 | tf_op jit(solution)/shard_map/pallas_call | solution.py:307
  233.9 1.2 collective-permute-start.23
  235.1 5.8 %shard_map.100.before_ref = f32[2688,512]{1,0:T(8,128)} custom-call(bf16[2688,1024]{1,0:T(8,128)(2,1)} %all-gather.4.cloned.1.call-done.w_ref, bf16[512,512]{1,0:T(8,128)(2,1)} %shard_map.99.c_ref), custom_call_target="tpu_custom_call" | custom-call | flops 1409286144 | bytes 9000000 | tf_op jit(solution)/shard_map/pallas_call | solution.py:342
  240.8 4.7 %collective-permute-done.23.c_ref = bf16[512,512]{1,0:T(8,128)(2,1)S(1)} collective-permute-done((bf16[512,512]{1,0:T(8,128)(2,1)}, bf16[512,512]{1,0:T(8,128)(2,1)S(1)}, u32[]{:S(2)}, u32[]{:S(2)}) %collective-permute-start.23) | collective-permute-done | bytes 524320 | tf_op jit(solution)/shard_map/ppermute | solution.py:25
  245.6 0.8 copy-done.2
  246.4 3.7 %shard_map.102 = bf16[1344,512]{1,0:T(8,128)(2,1)} custom-call(s32[1]{0:T(128)} %bitcast.24.half, bf16[2688,1024]{1,0:T(8,128)(2,1)} %all-gather.4.cloned.1.call-done.w_ref, bf16[512,512]{1,0:T(8,128)(2,1)} %copy-done.2, f32[2688,512]{1,0:T(8,128)} %shard_map.100.before_ref), custom_call_target="tpu_custom_call" | custom-call | flops 704643072 | bytes 6000000 | tf_op jit(solution)/shard_map/pallas_call | solution.py:363
  250.1 4.0 %shard_map.101 = f32[1344,512]{1,0:T(8,128)} custom-call(s32[1]{0:T(128)} %bitcast.half, bf16[2688,1024]{1,0:T(8,128)(2,1)} %all-gather.4.cloned.1.call-done.w_ref, bf16[512,512]{1,0:T(8,128)(2,1)} %copy-done.2, f32[2688,512]{1,0:T(8,128)} %shard_map.100.before_ref), custom_call_target="tpu_custom_call" | custom-call | flops 704643072 | bytes 6000000 | tf_op jit(solution)/shard_map/pallas_call | solution.py:363
  254.2 1.1 copy-done.1
  255.2 2.5 multiply_reduce_fusion
  257.7 8.1 %psum.7 = f32[512]{0:T(512)S(1)} all-reduce(f32[512]{0:T(512)S(1)} %multiply_reduce_fusion), channel_id=1, replica_groups=mesh['yl'=2,'x'=4,'z'=4,'yh'=2,'c'=2] {'yh','c'}, use_global_device_ids=true, to_apply=%region_1.2 | all-reduce | flops 512 | bytes 4096 | tf_op jit(solution)/shard_map/psum | solution.py:460
  265.8 3.4 %fusion = bf16[512,1344]{0,1:T(8,128)(2,1)} fusion(bf16[512,1344]{0,1:T(8,128)(2,1)} %param.9, f32[1344,512]{1,0:T(8,128)S(1)} %copy-done, bf16[1344,512]{1,0:T(8,128)(2,1)} %copy-done.1, f32[1344]{0:T(1024)S(1)} %copy-done.19, f32[512]{0:T(512)S(1)} %add_rsqrt_fusion), kind=kLoop, calls=%fused_computation.1 | loop fusion | flops 4816896 | bytes 6888704 | tf_op jit(solution)/shard_map/convert_element_type | solution.py:462
  (65 shorter events, 0.7 us)
Async XLA Ops:
  6.5 110.6 %copy-start.17 = (bf16[512,168]{0,1:T(8,128)(2,1)S(1)}, bf16[512,168]{0,1:T(8,128)(2,1)}, u32[]{:S(2)}) copy-start(bf16[512,168]{0,1:T(8,128)(2,1)} %param.13) | copy-start | bytes 516100
  6.5 134.1 %all-gather.6.cloned.1.call-start = ((), (), s32[]{:S(2)}) async-start(), calls=%async_computation.1 | async-start | bytes 6881280 | tf_op jit(solution)/shard_map/all_gather | solution.py:390
  7.3 227.8 %all-gather.4.cloned.1.call-start = ((), (), s32[]{:S(2)}) async-start(), calls=%async_computation | async-start | bytes 5849088 | tf_op jit(solution)/shard_map/all_gather | solution.py:420
  10.0 19.6 %copy-start.5 = (bf16[168,1024]{1,0:T(8,128)(2,1)}, bf16[168,1024]{1,0:T(8,128)(2,1)S(1)}, u32[]{:S(2)}) copy-start(bf16[168,1024]{1,0:T(8,128)(2,1)S(1)} %constant_dynamic-update-slice_fusion.refs_0_) | copy-start | bytes 1032196
  10.0 9.9 %collective-permute-start.3 = (bf16[168,1024]{1,0:T(8,128)(2,1)S(1)}, bf16[168,1024]{1,0:T(8,128)(2,1)S(1)}, u32[]{:S(2)}, u32[]{:S(2)}) collective-permute-start(bf16[168,1024]{1,0:T(8,128)(2,1)S(1)} %constant_dynamic-update-slice_fusion.refs_0_), channel_id=1, source_target_pairs={{0,64},{64,0},{1,65},{65,1},{2,66},{66,2},{3,67},{67,3},{4,68},{68... | collective-permute-start | bytes 1032200 | tf_op jit(solution)/shard_map/ppermute | solution.py:25
  10.6 11.4 %collective-permute-start = (bf16[168,1024]{1,0:T(8,128)(2,1)S(1)}, bf16[168,1024]{1,0:T(8,128)(2,1)S(1)}, u32[]{:S(2)}, u32[]{:S(2)}) collective-permute-start(bf16[168,1024]{1,0:T(8,128)(2,1)S(1)} %constant_dynamic-update-slice_fusion.refs_0_), channel_id=1, source_target_pairs={{0,16},{16,32},{32,48},{48,0},{1,17},{17,33},{33,49},{49,1},{2,18}... | collective-permute-start | bytes 1032200 | tf_op jit(solution)/shard_map/ppermute | solution.py:25
  12.1 15.9 %collective-permute-start.1 = (bf16[168,1024]{1,0:T(8,128)(2,1)S(1)}, bf16[168,1024]{1,0:T(8,128)(2,1)S(1)}, u32[]{:S(2)}, u32[]{:S(2)}) collective-permute-start(bf16[168,1024]{1,0:T(8,128)(2,1)S(1)} %constant_dynamic-update-slice_fusion.refs_0_), channel_id=1, source_target_pairs={{0,48},{16,0},{32,16},{48,32},{1,49},{17,1},{33,17},{49,33},{2,50}... | collective-permute-start | bytes 1032200 | tf_op jit(solution)/shard_map/ppermute | solution.py:25
  13.8 15.9 %collective-permute-start.2 = (bf16[168,1024]{1,0:T(8,128)(2,1)S(1)}, bf16[168,1024]{1,0:T(8,128)(2,1)S(1)}, u32[]{:S(2)}, u32[]{:S(2)}) collective-permute-start(bf16[168,1024]{1,0:T(8,128)(2,1)S(1)} %constant_dynamic-update-slice_fusion.refs_0_), channel_id=1, source_target_pairs={{0,32},{16,48},{32,0},{48,16},{1,33},{17,49},{33,1},{49,17},{2,34}... | collective-permute-start | bytes 1032200 | tf_op jit(solution)/shard_map/ppermute | solution.py:25
  19.9 53.4 %copy-start.10 = (bf16[168,1024]{1,0:T(8,128)(2,1)}, bf16[168,1024]{1,0:T(8,128)(2,1)S(1)}, u32[]{:S(2)}) copy-start(bf16[168,1024]{1,0:T(8,128)(2,1)S(1)} %collective-permute-done.3.refs_0_) | copy-start | bytes 1032196
  19.9 53.4 %collective-permute-start.4 = (bf16[168,1024]{1,0:T(8,128)(2,1)S(1)}, bf16[168,1024]{1,0:T(8,128)(2,1)S(1)}, u32[]{:S(2)}, u32[]{:S(2)}) collective-permute-start(bf16[168,1024]{1,0:T(8,128)(2,1)S(1)} %collective-permute-done.3.refs_0_), channel_id=1, source_target_pairs={{0,4},{4,8},{8,12},{12,0},{1,5},{5,9},{9,13},{13,1},{2,6},{6,10},{... | collective-permute-start | bytes 1032200 | tf_op jit(solution)/shard_map/ppermute | solution.py:25
  21.8 51.5 %collective-permute-start.5 = (bf16[168,1024]{1,0:T(8,128)(2,1)S(1)}, bf16[168,1024]{1,0:T(8,128)(2,1)S(1)}, u32[]{:S(2)}, u32[]{:S(2)}) collective-permute-start(bf16[168,1024]{1,0:T(8,128)(2,1)S(1)} %collective-permute-done.3.refs_0_), channel_id=1, source_target_pairs={{0,12},{4,0},{8,4},{12,8},{1,13},{5,1},{9,5},{13,9},{2,14},{6,2},{... | collective-permute-start | bytes 1032200 | tf_op jit(solution)/shard_map/ppermute | solution.py:25
  21.9 7.7 %copy-start.12 = (bf16[168,1024]{1,0:T(8,128)(2,1)}, bf16[168,1024]{1,0:T(8,128)(2,1)S(1)}, u32[]{:S(2)}) copy-start(bf16[168,1024]{1,0:T(8,128)(2,1)S(1)} %collective-permute-done.refs_1_) | copy-start | bytes 1032196
  22.0 51.4 %collective-permute-start.6 = (bf16[168,1024]{1,0:T(8,128)(2,1)S(1)}, bf16[168,1024]{1,0:T(8,128)(2,1)S(1)}, u32[]{:S(2)}, u32[]{:S(2)}) collective-permute-start(bf16[168,1024]{1,0:T(8,128)(2,1)S(1)} %collective-permute-done.3.refs_0_), channel_id=1, source_target_pairs={{0,8},{4,12},{8,0},{12,4},{1,9},{5,13},{9,1},{13,5},{2,10},{6,14},... | collective-permute-start | bytes 1032200 | tf_op jit(solution)/shard_map/ppermute | solution.py:25
  28.0 1.7 copy-start.14
  29.7 0.7 copy-start.15
  73.3 70.6 %copy-start.6 = (bf16[4,168,512]{2,1,0:T(8,128)(2,1)S(1)}, bf16[4,168,512]{2,1,0:T(8,128)(2,1)}, u32[]{:S(2)}) copy-start(bf16[4,168,512]{2,1,0:T(8,128)(2,1)} %get-tuple-element.29) | copy-start | bytes 2064388
  73.3 92.9 %copy-start.18 = (f32[5376]{0:T(1024)S(1)}, f32[5376]{0:T(1024)}, u32[]{:S(2)}) copy-start(f32[5376]{0:T(1024)} %param.14) | copy-start | bytes 64516
  73.3 0.7 copy-start.11
  73.3 0.8 copy-start.13
  73.3 0.9 copy-start.16
  117.1 44.4 %copy-start.7 = (bf16[4,168,512]{2,1,0:T(8,128)(2,1)S(1)}, bf16[4,168,512]{2,1,0:T(8,128)(2,1)}, u32[]{:S(2)}) copy-start(bf16[4,168,512]{2,1,0:T(8,128)(2,1)} %get-tuple-element.31) | copy-start | bytes 2064388
  117.1 7.9 %collective-permute-start.7 = (bf16[168,512]{1,0:T(8,128)(2,1)S(1)}, bf16[168,512]{1,0:T(8,128)(2,1)S(1)}, u32[]{:S(2)}, u32[]{:S(2)}) collective-permute-start(bf16[168,512]{1,0:T(8,128)(2,1)S(1)} %bitcast.41), channel_id=1, source_target_pairs={{0,64},{2,0},{64,66},{66,2},{1,65},{3,1},{65,67},{67,3},{4,68},{6,... | collective-permute-start | bytes 516104 | tf_op jit(solution)/shard_map/ppermute | solution.py:415
  119.8 16.3 %collective-permute-start.10 = (bf16[672,512]{1,0:T(8,128)(2,1)}, bf16[672,512]{1,0:T(8,128)(2,1)}, u32[]{:S(2)}, u32[]{:S(2)}) collective-permute-start(bf16[672,512]{1,0:T(8,128)(2,1)} %bitcast.3.refs_0_), channel_id=1, source_target_pairs={{0,12},{4,0},{8,4},{12,8},{1,13},{5,1},{9,5},{13,9},{2,14},{6,2},{... | collective-permute-start | bytes 2064392 | tf_op jit(solution)/shard_map/ppermute | solution.py:25
  119.9 17.1 %collective-permute-start.11 = (bf16[672,512]{1,0:T(8,128)(2,1)}, bf16[672,512]{1,0:T(8,128)(2,1)S(1)}, u32[]{:S(2)}, u32[]{:S(2)}) collective-permute-start(bf16[672,512]{1,0:T(8,128)(2,1)} %bitcast.35), channel_id=1, source_target_pairs={{0,16},{16,32},{32,48},{48,0},{1,17},{17,33},{33,49},{49,1},{2,18}... | collective-permute-start | bytes 2064392 | tf_op jit(solution)/shard_map/ppermute | solution.py:25
  121.0 16.0 %collective-permute-start.12 = (bf16[672,512]{1,0:T(8,128)(2,1)}, bf16[672,512]{1,0:T(8,128)(2,1)}, u32[]{:S(2)}, u32[]{:S(2)}) collective-permute-start(bf16[672,512]{1,0:T(8,128)(2,1)} %bitcast.38), channel_id=1, source_target_pairs={{0,48},{16,0},{32,16},{48,32},{1,49},{17,1},{33,17},{49,33},{2,50}... | collective-permute-start | bytes 2064392 | tf_op jit(solution)/shard_map/ppermute | solution.py:25
  123.1 17.5 %collective-permute-start.9 = (bf16[672,512]{1,0:T(8,128)(2,1)}, bf16[672,512]{1,0:T(8,128)(2,1)S(1)}, u32[]{:S(2)}, u32[]{:S(2)}) collective-permute-start(bf16[672,512]{1,0:T(8,128)(2,1)} %bitcast.32), channel_id=1, source_target_pairs={{0,4},{4,8},{8,12},{12,0},{1,5},{5,9},{9,13},{13,1},{2,6},{6,10},{... | collective-permute-start | bytes 2064392 | tf_op jit(solution)/shard_map/ppermute | solution.py:25
  125.1 7.3 %collective-permute-start.8 = (bf16[168,512]{1,0:T(8,128)(2,1)S(1)}, bf16[168,512]{1,0:T(8,128)(2,1)S(1)}, u32[]{:S(2)}, u32[]{:S(2)}) collective-permute-start(bf16[168,512]{1,0:T(8,128)(2,1)S(1)} %bitcast.42), channel_id=1, source_target_pairs={{64,2},{2,64},{65,3},{3,65},{68,6},{6,68},{69,7},{7,69},{72,10},{1... | collective-permute-start | bytes 516104 | tf_op jit(solution)/shard_map/ppermute | solution.py:416
  137.0 40.5 %copy-start.8 = (bf16[672,512]{1,0:T(8,128)(2,1)}, bf16[672,512]{1,0:T(8,128)(2,1)S(1)}, u32[]{:S(2)}) copy-start(bf16[672,512]{1,0:T(8,128)(2,1)S(1)} %collective-permute-done.11.refs_4_) | copy-start | bytes 2064388
  140.6 6.4 %copy-start.9 = (bf16[672,512]{1,0:T(8,128)(2,1)}, bf16[672,512]{1,0:T(8,128)(2,1)S(1)}, u32[]{:S(2)}) copy-start(bf16[672,512]{1,0:T(8,128)(2,1)S(1)} %collective-permute-done.9.refs_1_) | copy-start | bytes 2064388
  140.6 20.9 %collective-permute-start.19 = (bf16[672,512]{1,0:T(8,128)(2,1)}, bf16[672,512]{1,0:T(8,128)(2,1)}, u32[]{:S(2)}, u32[]{:S(2)}) collective-permute-start(bf16[672,512]{1,0:T(8,128)(2,1)} %bitcast.3.refs_0_), channel_id=1, source_target_pairs={{0,4},{4,8},{8,12},{12,0},{1,5},{5,9},{9,13},{13,1},{2,6},{6,10},{... | collective-permute-start | bytes 2064392 | tf_op jit(solution)/shard_map/ppermute | solution.py:25
  140.7 22.7 %collective-permute-start.20 = (bf16[672,512]{1,0:T(8,128)(2,1)}, bf16[672,512]{1,0:T(8,128)(2,1)}, u32[]{:S(2)}, u32[]{:S(2)}) collective-permute-start(bf16[672,512]{1,0:T(8,128)(2,1)} %bitcast.39), channel_id=1, source_target_pairs={{0,16},{16,32},{32,48},{48,0},{1,17},{17,33},{33,49},{49,1},{2,18}... | collective-permute-start | bytes 2064392 | tf_op jit(solution)/shard_map/ppermute | solution.py:25
  140.8 24.8 %collective-permute-start.17 = (bf16[672,512]{1,0:T(8,128)(2,1)}, bf16[672,512]{1,0:T(8,128)(2,1)}, u32[]{:S(2)}, u32[]{:S(2)}) collective-permute-start(bf16[672,512]{1,0:T(8,128)(2,1)} %collective-permute-done.10.refs_2_), channel_id=1, source_target_pairs={{0,12},{4,0},{8,4},{12,8},{1,13},{5,1},{9,5},{13,9},{2,14},{6,2},{... | collective-permute-start | bytes 2064392 | tf_op jit(solution)/shard_map/ppermute | solution.py:25
  143.9 53.5 %collective-permute-start.15 = (bf16[672,512]{1,0:T(8,128)(2,1)S(1)}, bf16[672,512]{1,0:T(8,128)(2,1)}, u32[]{:S(2)}, u32[]{:S(2)}) collective-permute-start(bf16[672,512]{1,0:T(8,128)(2,1)S(1)} %bitcast.34), channel_id=1, source_target_pairs={{0,12},{4,0},{8,4},{12,8},{1,13},{5,1},{9,5},{13,9},{2,14},{6,2},{... | collective-permute-start | bytes 2064392 | tf_op jit(solution)/shard_map/ppermute | solution.py:25
  147.0 38.2 %collective-permute-start.18 = (bf16[672,512]{1,0:T(8,128)(2,1)}, bf16[672,512]{1,0:T(8,128)(2,1)}, u32[]{:S(2)}, u32[]{:S(2)}) collective-permute-start(bf16[672,512]{1,0:T(8,128)(2,1)} %collective-permute-done.12.refs_5_), channel_id=1, source_target_pairs={{0,48},{16,0},{32,16},{48,32},{1,49},{17,1},{33,17},{49,33},{2,50}... | collective-permute-start | bytes 2064392 | tf_op jit(solution)/shard_map/ppermute | solution.py:25
  161.5 41.0 %collective-permute-start.16 = (bf16[672,512]{1,0:T(8,128)(2,1)S(1)}, bf16[672,512]{1,0:T(8,128)(2,1)}, u32[]{:S(2)}, u32[]{:S(2)}) collective-permute-start(bf16[672,512]{1,0:T(8,128)(2,1)S(1)} %bitcast.37), channel_id=1, source_target_pairs={{0,48},{16,0},{32,16},{48,32},{1,49},{17,1},{33,17},{49,33},{2,50}... | collective-permute-start | bytes 2064392 | tf_op jit(solution)/shard_map/ppermute | solution.py:25
  163.4 46.7 %collective-permute-start.13 = (bf16[672,512]{1,0:T(8,128)(2,1)}, bf16[672,512]{1,0:T(8,128)(2,1)}, u32[]{:S(2)}, u32[]{:S(2)}) collective-permute-start(bf16[672,512]{1,0:T(8,128)(2,1)} %copy-done.9), channel_id=1, source_target_pairs={{0,4},{4,8},{8,12},{12,0},{1,5},{5,9},{9,13},{13,1},{2,6},{6,10},{... | collective-permute-start | bytes 2064392 | tf_op jit(solution)/shard_map/ppermute | solution.py:25
  165.6 44.5 %collective-permute-start.14 = (bf16[672,512]{1,0:T(8,128)(2,1)S(1)}, bf16[672,512]{1,0:T(8,128)(2,1)}, u32[]{:S(2)}, u32[]{:S(2)}) collective-permute-start(bf16[672,512]{1,0:T(8,128)(2,1)S(1)} %collective-permute-done.11.refs_4_), channel_id=1, source_target_pairs={{0,16},{16,32},{32,48},{48,0},{1,17},{17,33},{33,49},{49,1},{2,18}... | collective-permute-start | bytes 2064392 | tf_op jit(solution)/shard_map/ppermute | solution.py:25
  191.7 29.2 %collective-permute-start.21 = (bf16[512,512]{1,0:T(8,128)(2,1)}, bf16[512,512]{1,0:T(8,128)(2,1)S(1)}, u32[]{:S(2)}, u32[]{:S(2)}) collective-permute-start(bf16[512,512]{1,0:T(8,128)(2,1)} %shard_map.97.k_ref.v_ref), channel_id=1, source_target_pairs={{0,4},{4,8},{8,12},{12,16},{16,20},{20,24},{24,28},{28,32},{32,36}... | collective-permute-start | bytes 1572872 | tf_op jit(solution)/shard_map/ppermute | solution.py:30
  197.4 30.3 %collective-permute-start.22 = (bf16[512,512]{1,0:T(8,128)(2,1)}, bf16[512,512]{1,0:T(8,128)(2,1)S(1)}, u32[]{:S(2)}, u32[]{:S(2)}) collective-permute-start(bf16[512,512]{1,0:T(8,128)(2,1)} %shard_map.97.k_ref.v_ref), channel_id=1, source_target_pairs={{0,8},{4,12},{8,16},{12,20},{16,24},{20,28},{24,32},{28,36},{32,40... | collective-permute-start | bytes 1572872 | tf_op jit(solution)/shard_map/ppermute | solution.py:30
  220.9 6.8 %copy-start.3 = (bf16[512,512]{1,0:T(8,128)(2,1)}, bf16[512,512]{1,0:T(8,128)(2,1)S(1)}, u32[]{:S(2)}) copy-start(bf16[512,512]{1,0:T(8,128)(2,1)S(1)} %collective-permute-done.21.k1_ref.v1_ref) | copy-start | bytes 1572868
  227.7 0.8 copy-start.4
  233.9 11.7 %collective-permute-start.23 = (bf16[512,512]{1,0:T(8,128)(2,1)}, bf16[512,512]{1,0:T(8,128)(2,1)S(1)}, u32[]{:S(2)}, u32[]{:S(2)}) collective-permute-start(bf16[512,512]{1,0:T(8,128)(2,1)} %shard_map.99.c_ref), channel_id=1, source_target_pairs={{0,2},{2,0},{1,3},{3,1},{4,6},{6,4},{5,7},{7,5},{8,10},{10,8},{9,1... | collective-permute-start | bytes 1572872 | tf_op jit(solution)/shard_map/ppermute | solution.py:25
  245.6 0.8 copy-start.2
  250.1 4.0 %collective-permute-start.24 = (bf16[1344,512]{1,0:T(8,128)(2,1)}, bf16[1344,512]{1,0:T(8,128)(2,1)S(1)}, u32[]{:S(2)}, u32[]{:S(2)}) collective-permute-start(bf16[1344,512]{1,0:T(8,128)(2,1)} %shard_map.102), channel_id=1, source_target_pairs={{0,1},{1,0},{2,3},{3,2},{4,5},{5,4},{6,7},{7,6},{8,9},{9,8},{10,11... | collective-permute-start | bytes 4128776 | tf_op jit(solution)/shard_map/ppermute | solution.py:25
  254.1 11.7 %copy-start = (f32[1344,512]{1,0:T(8,128)S(1)}, f32[1344,512]{1,0:T(8,128)}, u32[]{:S(2)}) copy-start(f32[1344,512]{1,0:T(8,128)} %shard_map.101) | copy-start | bytes 8257540
  254.1 11.7 %copy-start.19 = (f32[1344]{0:T(1024)S(1)}, f32[1344]{0:T(1024)}, u32[]{:S(2)}) copy-start(f32[1344]{0:T(1024)} %param.15) | copy-start | bytes 16132
  254.1 1.1 copy-start.1
Sparse Core Ops, SparseCore 0:
  9.0 46.9 all-gather.5
  140.8 65.8 all-gather.3

commit v4 on v3

v4 whole, which is shorter than its diff:
```python
import functools

import jax
import jax.numpy as jnp
import numpy as np
from jax import lax
from jax.experimental import pallas as pl
from jax.experimental.pallas import tpu as pltpu
from jax.sharding import Mesh, PartitionSpec as P

MODEL_WIDTH = 5376
HEAD_SIZE = 128
WINDOW_LENGTH = 1024
SHARD = MODEL_WIDTH // 32
VMEM = 40 << 20
SMALL = 16 << 20

score_scale = 168.0 ** (-0.5)
epsilon = 1e-06
SEQ = ("yl", "x", "z")
MP = ("yh", "c")


def shift(value, axis, step):
    count = lax.axis_size(axis)
    return lax.ppermute(value, axis, [(i, (i + step) % count) for i in range(count)])


def from_behind(value, steps):
    count = 32
    return lax.ppermute(value, SEQ, [(source, source + steps) for source in range(count - steps)])


def later(values, done):
    return lax.optimization_barrier((values, done))[0]


def line_kernel(slots, *refs):
    pieces, (first, second) = refs[:4], refs[4:]
    cut = first.shape[2]
    for k, piece in enumerate(pieces):

        @pl.when(pl.program_id(0) == k)
        def _():
            first[0] = piece[:, :cut]
            second[0] = piece[:, cut:]


def in_line(pieces, at, cut):
    depth, columns = pieces[0].shape
    out = lambda wide: pl.BlockSpec((1, depth, wide), lambda i, s: (s[i], 0, 0))
    first, second = pl.pallas_call(
        line_kernel,
        grid_spec=pltpu.PrefetchScalarGridSpec(
            num_scalar_prefetch=1,
            grid=(4,),
            in_specs=[pl.BlockSpec((depth, columns), lambda i, s: (0, 0))] * 4,
            out_specs=[out(cut), out(columns - cut)],
        ),
        out_shape=[
            jax.ShapeDtypeStruct((4, depth, cut), jnp.bfloat16),
            jax.ShapeDtypeStruct((4, depth, columns - cut), jnp.bfloat16),
        ],
        compiler_params=pltpu.CompilerParams(vmem_limit_bytes=VMEM),
        cost_estimate=pl.CostEstimate(flops=0, bytes_accessed=3_000_000, transcendentals=0),
    )((at + jnp.array([0, 3, 1, 2], jnp.int32)) % 4, *pieces)
    return first.reshape(4 * depth, cut), second.reshape(4 * depth, columns - cut)


def norm_kernel(side, own_ref, other_ref, near_gain, far_gain, near_ref, far_ref):
    own = own_ref[0].astype(jnp.float32)
    other = other_ref[0].astype(jnp.float32)
    total = jnp.sum(own * own, axis=(0, 1)) + jnp.sum(other * other, axis=(0, 1))
    scale = lax.rsqrt(total / MODEL_WIDTH + epsilon)[None, None]
    own = own * scale
    other = other * scale
    for i in range(4):
        starts = [(j // 2, ((j % 2) * 4 + i) * SHARD) for j in range(4)]
        part = jnp.concatenate([own[k, s : s + SHARD] for k, s in starts], axis=0)
        near_ref[i] = (part.T * near_gain[0, i]).astype(jnp.bfloat16)
        start = (i % 2) * 4 * SHARD
        part = other[i // 2, start : start + 4 * SHARD]
        far_ref[i] = (part.T * far_gain[0, i]).astype(jnp.bfloat16)


def norm_parts(pieces, gain, side):
    width, rows = pieces.shape[1:]
    step = 128
    pieces = pieces.reshape(2, 2, width, rows)
    far_gain = gain.reshape(2, 4, 4, SHARD)
    near_gain = jnp.swapaxes(far_gain, 1, 2).reshape(2, 4, 1, 4 * SHARD)
    far_gain = far_gain.reshape(2, 4, 1, 4 * SHARD)
    half = lambda flip: pl.BlockSpec((1, 2, width, step), lambda i, s: (s[flip], 0, 0, i))
    gains = lambda flip: pl.BlockSpec((1, 4, 1, 4 * SHARD), lambda i, s: (s[flip], 0, 0, 0))
    out = pl.BlockSpec((4, step, 4 * SHARD), lambda i, s: (0, i, 0))
    shape = jax.ShapeDtypeStruct((4, rows, 4 * SHARD), jnp.bfloat16)
    return pl.pallas_call(
        norm_kernel,
        grid_spec=pltpu.PrefetchScalarGridSpec(
            num_scalar_prefetch=1,
            grid=(rows // step,),
            in_specs=[half(0), half(1), gains(0), gains(1)],
            out_specs=[out, out],
        ),
        out_shape=[shape, shape],
        compiler_params=pltpu.CompilerParams(vmem_limit_bytes=VMEM),
        cost_estimate=pl.CostEstimate(flops=20_000_000, bytes_accessed=12_000_000, transcendentals=0),
    )(jnp.stack([side, 1 - side]), pieces, pieces, near_gain, far_gain)


def pick(parts, at):
    return lax.dynamic_index_in_dim(parts, at % 4, 0, keepdims=False)


def product(left, right):
    return jnp.dot(left, right, preferred_element_type=jnp.float32)


def turned_heads(raw, gain, cosine, sine):
    normal = raw * lax.rsqrt(jnp.mean(raw * raw, axis=-1, keepdims=True) + epsilon) * gain
    return normal * cosine + pltpu.roll(normal, HEAD_SIZE // 2, 1) * sine


def heads_kernel(heads, raw_ref, gain, cosine, sine, out_ref):
    for h in range(raw_ref.shape[1] // HEAD_SIZE):
        lanes = slice(h * HEAD_SIZE, (h + 1) * HEAD_SIZE)
        raw = raw_ref[:, lanes]
        if h < heads:
            raw = turned_heads(raw, gain[...], cosine[...], sine[...])
        out_ref[:, lanes] = raw.astype(jnp.bfloat16)


def finish_heads(heads, raw, gain, cosine, sine):
    rows, columns = raw.shape
    step = 256
    block = pl.BlockSpec((step, columns), lambda i: (i, 0))
    table = pl.BlockSpec((step, HEAD_SIZE), lambda i: (i, 0))
    return pl.pallas_call(
        functools.partial(heads_kernel, heads),
        grid=(rows // step,),
        in_specs=[block, pl.BlockSpec((1, HEAD_SIZE), lambda i: (0, 0)), table, table],
        out_specs=block,
        out_shape=jax.ShapeDtypeStruct((rows, columns), jnp.bfloat16),
        compiler_params=pltpu.CompilerParams(vmem_limit_bytes=SMALL),
        cost_estimate=pl.CostEstimate(flops=5_000_000, bytes_accessed=3_000_000, transcendentals=0),
    )(raw, gain, cosine, sine)


def scores_of(queries, keys):
    score = lax.dot_general(
        queries, keys, (((1,), (1,)), ((), ())), preferred_element_type=jnp.float32
    )
    return jnp.exp(score * score_scale)


def lane_sums(weights):
    parts = [weights[:, i : i + HEAD_SIZE] for i in range(0, weights.shape[1], HEAD_SIZE)]
    return functools.reduce(lambda a, b: a + b, parts)


def both_heads(ref, at):
    return jnp.concatenate([ref[at, :HEAD_SIZE], ref[at, HEAD_SIZE:]], axis=0)


def own_kernel(q_ref, k_ref, v_ref, sum_ref, weight_ref):
    for r in range(q_ref.shape[0] // 128):
        at = slice(r * 128, (r + 1) * 128)
        seen = (r + 1) * 128
        e = scores_of(both_heads(q_ref, at), k_ref[:seen])
        i = lax.broadcasted_iota(jnp.int32, e.shape, 0) % 128
        j = lax.broadcasted_iota(jnp.int32, e.shape, 1)
        e = jnp.where(j <= i + r * 128, e, 0.0)
        mixed = jnp.dot(e.astype(jnp.bfloat16), v_ref[:seen], preferred_element_type=jnp.float32)
        weight = lane_sums(e)
        for h in range(2):
            lanes = slice(h * HEAD_SIZE, (h + 1) * HEAD_SIZE)
            sum_ref[at, lanes] = mixed[h * 128 : (h + 1) * 128]
            weight_ref[at, lanes] = weight[h * 128 : (h + 1) * 128]


def behind_kernel(valid, q_ref, k1_ref, v1_ref, k2_ref, v2_ref, sum_ref, weight_ref, out_ref):
    has_one = valid[0].astype(jnp.float32)
    has_two = valid[1].astype(jnp.float32)
    rows = q_ref.shape[0]
    for r in range(rows // 128):
        at = slice(r * 128, (r + 1) * 128)
        q = both_heads(q_ref, at)
        one = scores_of(q, k1_ref[...])
        two = scores_of(q, k2_ref[r * 128 :])
        i = lax.broadcasted_iota(jnp.int32, two.shape, 0) % 128
        j = lax.broadcasted_iota(jnp.int32, two.shape, 1)
        two = jnp.where(j > i, two, 0.0)
        mixed = has_one * jnp.dot(
            one.astype(jnp.bfloat16), v1_ref[...], preferred_element_type=jnp.float32
        ) + has_two * jnp.dot(
            two.astype(jnp.bfloat16), v2_ref[r * 128 :], preferred_element_type=jnp.float32
        )
        weight = has_one * lane_sums(one) + has_two * lane_sums(two)
        for h in range(2):
            lanes = slice(h * HEAD_SIZE, (h + 1) * HEAD_SIZE)
            top = sum_ref[at, lanes] + mixed[h * 128 : (h + 1) * 128]
            low = jnp.sum(weight_ref[at, lanes] + weight[h * 128 : (h + 1) * 128], axis=-1, keepdims=True)
            out_ref[at, lanes] = (top / low).astype(jnp.bfloat16)


def attend_own(queries, keyed):
    rows, columns = queries.shape
    groups = columns // (2 * HEAD_SIZE)
    pair = pl.BlockSpec((rows, 2 * HEAD_SIZE), lambda g: (0, g))
    shape = jax.ShapeDtypeStruct((rows, columns), jnp.float32)
    return pl.pallas_call(
        own_kernel,
        grid=(groups,),
        in_specs=[
            pair,
            pl.BlockSpec((rows, HEAD_SIZE), lambda g: (0, g)),
            pl.BlockSpec((rows, HEAD_SIZE), lambda g: (0, groups + g)),
        ],
        out_specs=[pair, pair],
        out_shape=[shape, shape],
        compiler_params=pltpu.CompilerParams(vmem_limit_bytes=SMALL),
        cost_estimate=pl.CostEstimate(
            flops=4 * rows * rows * columns, bytes_accessed=3_000_000, transcendentals=rows * rows * 4
        ),
    )(queries, keyed, keyed)


def attend_behind(valid, queries, one, two, sums, weights):
    rows, columns = queries.shape
    groups = columns // (2 * HEAD_SIZE)
    pair = pl.BlockSpec((rows, 2 * HEAD_SIZE), lambda g, s: (0, g))
    keys = pl.BlockSpec((rows, HEAD_SIZE), lambda g, s: (0, g))
    values = pl.BlockSpec((rows, HEAD_SIZE), lambda g, s: (0, groups + g))
    return pl.pallas_call(
        behind_kernel,
        grid_spec=pltpu.PrefetchScalarGridSpec(
            num_scalar_prefetch=1,
            grid=(groups,),
            in_specs=[pair, keys, values, keys, values, pair, pair],
            out_specs=pair,
        ),
        out_shape=jax.ShapeDtypeStruct((rows, columns), jnp.bfloat16),
        compiler_params=pltpu.CompilerParams(vmem_limit_bytes=SMALL),
        cost_estimate=pl.CostEstimate(
            flops=8 * rows * rows * columns, bytes_accessed=4_000_000, transcendentals=rows * rows * 8
        ),
    )(valid, queries, one, one, two, two, sums, weights)


def gather_out(own, first, second):
    depth, columns = own.shape
    at = lax.axis_index(first)
    line = jnp.zeros((4, depth, columns), own.dtype)
    for step in (0, 1, 3, 2):
        piece = own if step == 0 else shift(own, first, step)
        line = lax.dynamic_update_index_in_dim(line, piece, (at - step) % 4, 0)
    ahead, behind = shift(line, second, 1), shift(line, second, 3)
    low, high = shift(ahead[:2], second, 1), shift(behind[2:], second, 3)
    there = lax.axis_index(second)
    whole = jnp.zeros((4, 4, depth, columns), own.dtype)
    for piece, offset, start in ((line, 0, 0), (ahead, 3, 0), (behind, 1, 0), (low, 2, 0), (high, 2, 2)):
        place = (there + offset) % 4
        if first == "x":
            whole = lax.dynamic_update_slice(whole, piece[:, None], (start, place, 0, 0))
        else:
            whole = lax.dynamic_update_slice(whole, piece[None], (place, start, 0, 0))
    return whole.reshape(16 * depth, columns)


def local(
    tokens, q_weight, key_matrix, value_matrix, o_weight, pre_gain, post_gain, q_gain, k_gain
):
    rows = tokens.shape[0]
    q_cols = q_weight.shape[1]
    yl, x, z, yh, c = (lax.axis_index(name) for name in ("yl", "x", "z", "yh", "c"))
    seq_index = (yl * 4 + x) * 4 + z
    whole = lax.all_gather(tokens.T, MP, axis=0)

    own = jnp.concatenate([q_weight, key_matrix, value_matrix], axis=1)
    other = shift(own, "yl", 1)
    own_pieces = [own] + [shift(own, "x", step) for step in (1, 3, 2)]
    other_pieces = [other] + [shift(other, "z", step) for step in (1, 3, 2)]
    own_q, own_kv = in_line(own_pieces, x, q_cols)
    other_q, other_kv = in_line(other_pieces, z, q_cols)
    own_ahead_q, own_behind_kv = shift(own_q, "z", 1), shift(own_kv, "z", 3)
    other_ahead_q, other_behind_kv = shift(other_q, "x", 1), shift(other_kv, "x", 3)
    own_ahead_kv, own_behind_q = shift(own_kv, "z", 1), shift(own_q, "z", 3)
    other_ahead_kv, other_behind_q = shift(other_kv, "x", 1), shift(other_q, "x", 3)
    own_ahead_q, own_behind_kv, other_ahead_q, other_behind_kv, whole, turned = lax.optimization_barrier(
        (own_ahead_q, own_behind_kv, other_ahead_q, other_behind_kv, whole, o_weight.T)
    )
    own_far_kv = shift(own_behind_kv, "z", 3)
    other_far_kv = shift(other_behind_kv, "x", 3)
    own_far_q = shift(own_ahead_q, "z", 1)
    other_far_q = shift(other_ahead_q, "x", 1)
    near, far = norm_parts(whole, pre_gain, yl)
    part_kv = product(pick(near, z), own_kv) + product(pick(far, x), other_kv)
    part_q = product(pick(near, z), own_q) + product(pick(far, x), other_q)
    part_kv = part_kv + product(pick(near, z + 3), own_ahead_kv) + product(pick(near, z + 1), own_behind_kv)
    part_kv = part_kv + product(pick(far, x + 3), other_ahead_kv) + product(pick(far, x + 1), other_behind_kv)

    y = yh * 2 + yl
    flat = lambda p: (p % 2) * 2 + p // 2
    one = lax.ppermute(turned, ("yl", "yh"), [(flat(a), flat(b)) for a, b in ((0, 1), (2, 0), (1, 3), (3, 2))])
    two = lax.ppermute(turned, ("yl", "yh"), [(flat(a), flat(b)) for a, b in ((1, 2), (2, 1))])
    outer = (y == 0) | (y == 3)
    out_same, out_other = jnp.where(outer, turned, one), jnp.where(outer, one, two)
    out_same, out_other, own_far_kv, other_far_kv = lax.optimization_barrier(
        (out_same, out_other, own_far_kv, other_far_kv)
    )
    out_same = gather_out(out_same, "x", "z")
    out_other = gather_out(out_other, "z", "x")

    positions = seq_index * rows + jnp.arange(rows, dtype=jnp.int32)
    half = HEAD_SIZE // 2
    freq = 10000.0 ** (-(jnp.arange(half, dtype=jnp.float32) * 2.0) / HEAD_SIZE)
    angle = positions.astype(jnp.float32)[:, None] * freq[None, :]
    cosine = jnp.cos(angle)
    sine = jnp.sin(angle)
    cosine = jnp.concatenate([cosine, cosine], axis=1)
    sine = jnp.concatenate([-sine, sine], axis=1)

    part_kv = part_kv + product(pick(near, z + 2), own_far_kv) + product(pick(far, x + 2), other_far_kv)
    keyed = finish_heads(2, part_kv, k_gain[None], cosine, sine)
    behind_one = from_behind(keyed, 1)
    behind_two = from_behind(keyed, 2)
    part_q = part_q + product(pick(near, z + 3), own_ahead_q) + product(pick(near, z + 1), own_behind_q)
    part_q = part_q + product(pick(far, x + 3), other_ahead_q) + product(pick(far, x + 1), other_behind_q)
    part_q = part_q + product(pick(near, z + 2), own_far_q) + product(pick(far, x + 2), other_far_q)
    queries = finish_heads(4, part_q, q_gain[None], cosine, sine)
    sums, weights = attend_own(queries, keyed)
    valid = jnp.stack([seq_index >= 1, seq_index >= 2]).astype(jnp.int32)
    context = attend_behind(valid, queries, behind_one, behind_two, sums, weights)

    across = shift(context, "yh", 1)
    summed = lambda weight, value: lax.dot_general(
        weight, value, (((1,), (1,)), ((), ())), preferred_element_type=jnp.float32
    )
    before = summed(out_same, context)
    across, before = lax.optimization_barrier((across, before))
    columns = out_same.shape[0] // 2

    def half_of(core):
        weight = lax.dynamic_slice_in_dim(out_other, core * columns, columns, 0)
        return lax.dynamic_slice_in_dim(before, core * columns, columns, 0) + summed(weight, across)

    received = shift(half_of(1 - c).astype(jnp.bfloat16), "c", 1)
    share = (half_of(c) + received.astype(jnp.float32)).T
    total = lax.psum(jnp.sum(share * share, axis=1), MP)
    scale_rows = lax.rsqrt(total / MODEL_WIDTH + epsilon)
    return (tokens.astype(jnp.float32) + share * scale_rows[:, None] * post_gain).astype(
        jnp.bfloat16
    )


def solution(mesh):
    fine = Mesh(np.asarray(mesh.devices).reshape(2, 4, 4, 2, 2), SEQ + MP)
    return jax.shard_map(
        local,
        mesh=fine,
        in_specs=(
            P(SEQ, MP),
            P(SEQ, MP),
            P(SEQ, MP),
            P(SEQ, MP),
            P(MP, SEQ),
            P(),
            P(MP),
            P(),
            P(),
        ),
        out_specs=P(SEQ, MP),
        check_vma=False,
    )
```

time: 277 us -> 200 us (0.72)
  the two profiles are of different devices: /device:TPU:40 before, /device:TPU:30 now
where the time goes in v4:
time: 200 us; the launch traced here: 199 us
  waiting for transfers between devices  68.2 us (34%)
  starting transfers between devices  51.8 us (26%)
  matrix products  21.7 us (11%)
  Pallas kernels  17.3 us (9%)
  between operations  14.3 us (7%)
  local copies, waits for them, and re-layouts  10.6 us (5%)
  blocking collectives  9.8 us (5%)
  other arithmetic  5.81 us (3%)
    ppermute x35, waiting for transfers between devices, shift(): lax.ppermute(value, axis, [(i, (i + step) % count) for i in range(count)])  47.6 us
    ppermute x35, starting transfers between devices, shift(): lax.ppermute(value, axis, [(i, (i + step) % count) for i in range(count)])  44.6 us
    ppermute x2, waiting for transfers between devices, from_behind(): lax.ppermute(value, SEQ, [(source, source + steps) for source in range(co...  17.1 us
    dot_general x16, matrix products, product(): return jnp.dot(left, right, preferred_element_type=jnp.float32)  15.2 us
    psum x1, blocking collectives, local(): total = lax.psum(jnp.sum(share * share, axis=1), MP)  9.8 us
    pallas_call x1, Pallas kernels, norm_parts(): pl.pallas_call(norm_kernel, grid_spec=pltpu.PrefetchScalarGridSpec(num_sc...  7.04 us
    unnamed x36, local copies, waits for them, and re-layouts  6.7 us
    dot_general x3, matrix products, local(): lax.dot_general(weight, value, (((1,), (1,)), ((), ())), preferred_elemen...  6.49 us
  transfers between devices with their start and end apart: 40, of which 18 were waited for; matrix products, arithmetic and copies ran while one was open for 12% of the time, Pallas kernels for 9%

profile of v4, /device:TPU:30, one launch (start us, length us, event | category | flops | bytes accessed | tf_op | source)
XLA Modules:
  0.0 199.5 jit_solution(9482546553732847794)
XLA Ops:
  7.3 0.9 constant_dynamic-update-slice_fusion.2
  8.2 0.9 constant_dynamic-update-slice_fusion.1
  9.1 0.9 constant_dynamic-update-slice_fusion.refs_0_
  11.2 1.5 collective-permute-start.1
  12.8 1.4 collective-permute-start.2
  14.2 0.8 reshape.46
  15.0 0.8 reshape_reshape.3.far_gain
  15.9 3.9 %collective-permute-done.5.refs_0_ = bf16[168,1024]{1,0:T(8,128)(2,1)S(1)} collective-permute-done((bf16[168,1024]{1,0:T(8,128)(2,1)S(1)}, bf16[168,1024]{1,0:T(8,128)(2,1)S(1)}, u32[]{:S(2)}, u32[]{:S(2)}) %collective-permute-start.5) | collective-permute-done | bytes 344096 | tf_op jit(solution)/shard_map/ppermute | solution.py:26
  19.8 1.9 collective-permute-start.6
  21.7 2.1 %collective-permute-start.7 = (bf16[168,1024]{1,0:T(8,128)(2,1)S(1)}, bf16[168,1024]{1,0:T(8,128)(2,1)}, u32[]{:S(2)}, u32[]{:S(2)}) collective-permute-start(bf16[168,1024]{1,0:T(8,128)(2,1)S(1)} %collective-permute-done.5.refs_0_), channel_id=1, source_target_pairs={{0,12},{4,0},{8,4},{12,8},{1,13},{5,1},{9,5},{13,9},{2,14},{6,2},{... | collective-permute-start | bytes 1032200 | tf_op jit(solution)/shard_map/ppermute | solution.py:26
  23.8 1.9 collective-permute-start.8
  26.0 3.1 %collective-permute-done.1.refs_2_ = bf16[168,1024]{1,0:T(8,128)(2,1)S(1)} collective-permute-done((bf16[168,1024]{1,0:T(8,128)(2,1)S(1)}, bf16[168,1024]{1,0:T(8,128)(2,1)S(1)}, u32[]{:S(2)}, u32[]{:S(2)}) %collective-permute-start.1) | collective-permute-done | bytes 344096 | tf_op jit(solution)/shard_map/ppermute | solution.py:26
  29.8 2.0 collective-permute-start.3
  31.8 2.2 %collective-permute-start.4 = (bf16[672,512]{1,0:T(8,128)(2,1)S(1)}, bf16[672,512]{1,0:T(8,128)(2,1)S(1)}, u32[]{:S(2)}, u32[]{:S(2)}) collective-permute-start(bf16[672,512]{1,0:T(8,128)(2,1)S(1)} %bitcast.129), channel_id=1, source_target_pairs={{0,12},{4,0},{8,4},{12,8},{1,13},{5,1},{9,5},{13,9},{2,14},{6,2},{... | collective-permute-start | bytes 2064392 | tf_op jit(solution)/shard_map/ppermute | solution.py:26
  34.0 2.9 %collective-permute-done.7.refs_2_ = bf16[168,1024]{1,0:T(8,128)(2,1)} collective-permute-done((bf16[168,1024]{1,0:T(8,128)(2,1)S(1)}, bf16[168,1024]{1,0:T(8,128)(2,1)}, u32[]{:S(2)}, u32[]{:S(2)}) %collective-permute-start.7) | collective-permute-done | bytes 344096 | tf_op jit(solution)/shard_map/ppermute | solution.py:26
  36.9 4.9 %collective-permute-done.8.refs_3_ = bf16[168,1024]{1,0:T(8,128)(2,1)} collective-permute-done((bf16[168,1024]{1,0:T(8,128)(2,1)S(1)}, bf16[168,1024]{1,0:T(8,128)(2,1)}, u32[]{:S(2)}, u32[]{:S(2)}) %collective-permute-start.8) | collective-permute-done | bytes 344096 | tf_op jit(solution)/shard_map/ppermute | solution.py:26
  41.8 1.0 copy-done.2
  42.8 2.0 %shard_map.110 = (bf16[4,168,512]{2,1,0:T(8,128)(2,1)S(1)}, bf16[4,168,512]{2,1,0:T(8,128)(2,1)S(1)}) custom-call(s32[4]{0:T(128)S(1)} %get-tuple-element.50.slots, bf16[168,1024]{1,0:T(8,128)(2,1)S(1)} %copy-done.2, bf16[168,1024]{1,0:T(8,128)(2,1)} %collective-permute-done.6.refs_1_, bf16[168,1024]{1,0:T(8,128)(2,1)} %collective-permute-done.7.refs_2_, ...), custom_call_target="tpu_custom_call" | custom-call | bytes 3000000 | tf_op jit(solution)/shard_map/pallas_call | solution.py:52
  45.4 1.6 collective-permute-start.10
  47.1 1.0 fusion.65
  48.3 1.1 collective-permute-start.11
  49.4 4.3 %collective-permute-done.3 = bf16[672,512]{1,0:T(8,128)(2,1)S(1)} collective-permute-done((bf16[672,512]{1,0:T(8,128)(2,1)S(1)}, bf16[672,512]{1,0:T(8,128)(2,1)S(1)}, u32[]{:S(2)}, u32[]{:S(2)}) %collective-permute-start.3) | collective-permute-done | bytes 688160 | tf_op jit(solution)/shard_map/ppermute | solution.py:26
  53.7 1.2 collective-permute-done.4
  54.9 0.8 collective-permute-start.12
  55.7 4.0 %collective-permute-done.9 = bf16[672,512]{1,0:T(8,128)(2,1)S(1)} collective-permute-done((bf16[672,512]{1,0:T(8,128)(2,1)S(1)}, bf16[672,512]{1,0:T(8,128)(2,1)S(1)}, u32[]{:S(2)}, u32[]{:S(2)}) %collective-permute-start.9) | collective-permute-done | bytes 688160 | tf_op jit(solution)/shard_map/ppermute | solution.py:26
  60.5 1.7 collective-permute-done.10
  62.3 2.6 %copy-done = bf16[5376,512]{1,0:T(8,128)(2,1)S(1)} copy-done((bf16[5376,512]{1,0:T(8,128)(2,1)S(1)}, bf16[5376,512]{1,0:T(8,128)(2,1)}, u32[]{:S(2)}) %copy-start) | copy-done | bytes 5505048
  64.8 7.0 %shard_map.111 = (bf16[4,512,672]{2,1,0:T(8,128)(2,1)S(1)}, bf16[4,512,672]{2,1,0:T(8,128)(2,1)S(1)}) custom-call(s32[2]{0:T(128)S(1)} %pad_add_fusion.side, bf16[2,2,1344,512]{3,2,1,0:T(8,128)(2,1)S(1)} %bitcast.127, bf16[2,2,1344,512]{3,2,1,0:T(8,128)(2,1)S(1)} %bitcast.128, f32[2,4,1,672]{3,2,1,0:T(1,128)S(1)} %reshape.47.near_gain, ...), custom_call_target="tpu_custom_call" | custom-call | flops 20000000 | bytes 12000000 | tf_op jit(solution)/shard_map/pallas_call | solution.py:97
  74.3 1.7 fusion.27
  76.7 1.7 fusion.29
  78.4 2.2 %collective-permute-start.20 = (bf16[672,512]{1,0:T(8,128)(2,1)}, bf16[672,512]{1,0:T(8,128)(2,1)S(1)}, u32[]{:S(2)}, u32[]{:S(2)}) collective-permute-start(bf16[672,512]{1,0:T(8,128)(2,1)} %collective-permute-done.10), channel_id=1, source_target_pairs={{0,48},{16,0},{32,16},{48,32},{1,49},{17,1},{33,17},{49,33},{2,50}... | collective-permute-start | bytes 2064392 | tf_op jit(solution)/shard_map/ppermute | solution.py:26
  80.6 1.7 fusion.37
  82.5 1.7 fusion.31
  84.9 1.7 fusion.39
  86.6 2.7 %collective-permute-done.17 = bf16[168,512]{1,0:T(8,128)(2,1)S(1)} collective-permute-done((bf16[168,512]{1,0:T(8,128)(2,1)S(1)}, bf16[168,512]{1,0:T(8,128)(2,1)S(1)}, u32[]{:S(2)}, u32[]{:S(2)}) %collective-permute-start.17) | collective-permute-done | bytes 172064 | tf_op jit(solution)/shard_map/ppermute | solution.py:304
  89.3 2.0 %collective-permute-start.13 = (bf16[672,512]{1,0:T(8,128)(2,1)S(1)}, bf16[672,512]{1,0:T(8,128)(2,1)S(1)}, u32[]{:S(2)}, u32[]{:S(2)}) collective-permute-start(bf16[672,512]{1,0:T(8,128)(2,1)S(1)} %copy-done.9), channel_id=1, source_target_pairs={{0,4},{4,8},{8,12},{12,0},{1,5},{5,9},{9,13},{13,1},{2,6},{6,10},{... | collective-permute-start | bytes 2064392 | tf_op jit(solution)/shard_map/ppermute | solution.py:26
  91.3 3.2 %collective-permute-done.20 = bf16[672,512]{1,0:T(8,128)(2,1)S(1)} collective-permute-done((bf16[672,512]{1,0:T(8,128)(2,1)}, bf16[672,512]{1,0:T(8,128)(2,1)S(1)}, u32[]{:S(2)}, u32[]{:S(2)}) %collective-permute-start.20) | collective-permute-done | bytes 688160 | tf_op jit(solution)/shard_map/ppermute | solution.py:26
  94.9 1.7 collective-permute-start.25
  98.1 0.9 fusion.17.raw_ref
  99.8 4.2 %collective-permute-start.31 = (bf16[168,512]{1,0:T(8,128)(2,1)S(1)}, bf16[168,512]{1,0:T(8,128)(2,1)S(1)}, u32[]{:S(2)}, u32[]{:S(2)}) collective-permute-start(bf16[168,512]{1,0:T(8,128)(2,1)S(1)} %get-tuple-element.43), channel_id=1, source_target_pairs={{0,4},{4,8},{8,12},{12,0},{1,5},{5,9},{9,13},{13,1},{2,6},{6,10},{... | collective-permute-start | bytes 516104 | tf_op jit(solution)/shard_map/ppermute | solution.py:26
  104.6 7.4 %collective-permute-done.13 = bf16[672,512]{1,0:T(8,128)(2,1)S(1)} collective-permute-done((bf16[672,512]{1,0:T(8,128)(2,1)S(1)}, bf16[672,512]{1,0:T(8,128)(2,1)S(1)}, u32[]{:S(2)}, u32[]{:S(2)}) %collective-permute-start.13) | collective-permute-done | bytes 688160 | tf_op jit(solution)/shard_map/ppermute | solution.py:26
  112.8 3.9 %collective-permute-start.21 = (bf16[512,512]{1,0:T(8,128)(2,1)S(1)}, bf16[512,512]{1,0:T(8,128)(2,1)S(1)}, u32[]{:S(2)}, u32[]{:S(2)}) collective-permute-start(bf16[512,512]{1,0:T(8,128)(2,1)S(1)} %shard_map.113.k_ref.v_ref), channel_id=1, source_target_pairs={{0,4},{4,8},{8,12},{12,16},{16,20},{20,24},{24,28},{28,32},{32,36}... | collective-permute-start | bytes 1572872 | tf_op jit(solution)/shard_map/ppermute | solution.py:31
  116.8 1.5 collective-permute-start.27
  118.3 1.8 collective-permute-start.28
  120.1 1.5 collective-permute-done.33
  121.8 2.0 %collective-permute-start.35 = (bf16[4,168,512]{2,1,0:T(8,128)(2,1)S(1)}, bf16[4,168,512]{2,1,0:T(8,128)(2,1)S(1)}, u32[]{:S(2)}, u32[]{:S(2)}) collective-permute-start(bf16[4,168,512]{2,1,0:T(8,128)(2,1)S(1)} %bitcast_dynamic-update-slice_fusion.10), channel_id=1, source_target_pairs={{0,48},{16,0},{32,16},{48,32},{1,49},{17,1},{33,17},{49,33},{2,50}... | collective-permute-start | bytes 2064392 | tf_op jit(solution)/shard_map/ppermute | solution.py:26
  124.6 1.2 shard_map.112.q_ref
  125.9 6.5 %collective-permute-done.21.k1_ref.v1_ref = bf16[512,512]{1,0:T(8,128)(2,1)S(1)} collective-permute-done((bf16[512,512]{1,0:T(8,128)(2,1)S(1)}, bf16[512,512]{1,0:T(8,128)(2,1)S(1)}, u32[]{:S(2)}, u32[]{:S(2)}) %collective-permute-start.21) | collective-permute-done | bytes 524320 | tf_op jit(solution)/shard_map/ppermute | solution.py:31
  132.4 2.3 %collective-permute-start.22 = (bf16[512,512]{1,0:T(8,128)(2,1)S(1)}, bf16[512,512]{1,0:T(8,128)(2,1)S(1)}, u32[]{:S(2)}, u32[]{:S(2)}) collective-permute-start(bf16[512,512]{1,0:T(8,128)(2,1)S(1)} %shard_map.113.k_ref.v_ref), channel_id=1, source_target_pairs={{0,8},{4,12},{8,16},{12,20},{16,24},{20,28},{24,32},{28,36},{32,40... | collective-permute-start | bytes 1572872 | tf_op jit(solution)/shard_map/ppermute | solution.py:31
  134.7 2.1 %shard_map.114 = (f32[512,512]{1,0:T(8,128)S(1)}, f32[512,512]{1,0:T(8,128)S(1)}) custom-call(bf16[512,512]{1,0:T(8,128)(2,1)S(1)} %shard_map.112.q_ref, bf16[512,512]{1,0:T(8,128)(2,1)S(1)} %shard_map.113.k_ref.v_ref, bf16[512,512]{1,0:T(8,128)(2,1)S(1)} %shard_map.113.k_ref.v_ref), custom_call_target="tpu_custom_call" | custom-call | flops 536870912 | bytes 3000000 | tf_op jit(solution)/shard_map/pallas_call | solution.py:211
  137.4 10.6 %collective-permute-done.22.k2_ref.v2_ref = bf16[512,512]{1,0:T(8,128)(2,1)S(1)} collective-permute-done((bf16[512,512]{1,0:T(8,128)(2,1)S(1)}, bf16[512,512]{1,0:T(8,128)(2,1)S(1)}, u32[]{:S(2)}, u32[]{:S(2)}) %collective-permute-start.22) | collective-permute-done | bytes 524320 | tf_op jit(solution)/shard_map/ppermute | solution.py:31
  148.0 3.5 %shard_map.115 = bf16[512,512]{1,0:T(8,128)(2,1)S(1)} custom-call(s32[2]{0:T(128)S(1)} %add_convert_fusion.2.valid, bf16[512,512]{1,0:T(8,128)(2,1)S(1)} %shard_map.112.q_ref, bf16[512,512]{1,0:T(8,128)(2,1)S(1)} %collective-permute-done.21.k1_ref.v1_ref, bf16[512,512]{1,0:T(8,128)(2,1)S(1)} %collective-permute-done.21.k1_ref.v1_ref, ...), custom_call_target="tpu_custom_call" | custom-call | flops 1073741824 | bytes 4000000 | tf_op jit(solution)/shard_map/pallas_call | solution.py:234
  151.5 3.5 %collective-permute-start.23 = (bf16[512,512]{1,0:T(8,128)(2,1)S(1)}, bf16[512,512]{1,0:T(8,128)(2,1)S(1)}, u32[]{:S(2)}, u32[]{:S(2)}) collective-permute-start(bf16[512,512]{1,0:T(8,128)(2,1)S(1)} %shard_map.115), channel_id=1, source_target_pairs={{0,2},{2,0},{1,3},{3,1},{4,6},{6,4},{5,7},{7,5},{8,10},{10,8},{9,1... | collective-permute-start | bytes 1572872 | tf_op jit(solution)/shard_map/ppermute | solution.py:26
  155.1 3.3 %collective-permute-start.30 = (bf16[2,168,512]{2,1,0:T(8,128)(2,1)S(1)}, bf16[2,168,512]{2,1,0:T(8,128)(2,1)S(1)}, u32[]{:S(2)}, u32[]{:S(2)}) collective-permute-start(bf16[2,168,512]{2,1,0:T(8,128)(2,1)S(1)} %slice.17), channel_id=1, source_target_pairs={{0,12},{4,0},{8,4},{12,8},{1,13},{5,1},{9,5},{13,9},{2,14},{6,2},{... | collective-permute-start | bytes 1032200 | tf_op jit(solution)/shard_map/ppermute | solution.py:26
  158.5 2.7 %collective-permute-start.36 = (bf16[2,168,512]{2,1,0:T(8,128)(2,1)S(1)}, bf16[2,168,512]{2,1,0:T(8,128)(2,1)S(1)}, u32[]{:S(2)}, u32[]{:S(2)}) collective-permute-start(bf16[2,168,512]{2,1,0:T(8,128)(2,1)S(1)} %slice.18), channel_id=1, source_target_pairs={{0,16},{16,32},{32,48},{48,0},{1,17},{17,33},{33,49},{49,1},{2,18}... | collective-permute-start | bytes 1032200 | tf_op jit(solution)/shard_map/ppermute | solution.py:26
  161.5 2.0 %collective-permute-done.29 = bf16[2,168,512]{2,1,0:T(8,128)(2,1)S(1)} collective-permute-done((bf16[2,168,512]{2,1,0:T(8,128)(2,1)S(1)}, bf16[2,168,512]{2,1,0:T(8,128)(2,1)S(1)}, u32[]{:S(2)}, u32[]{:S(2)}) %collective-permute-start.29) | collective-permute-done | bytes 344096 | tf_op jit(solution)/shard_map/ppermute | solution.py:26
  163.6 0.8 collective-permute-done.30
  164.5 1.7 fusion.86
  166.3 3.4 %collective-permute-done.37 = bf16[2,168,512]{2,1,0:T(8,128)(2,1)S(1)} collective-permute-done((bf16[2,168,512]{2,1,0:T(8,128)(2,1)S(1)}, bf16[2,168,512]{2,1,0:T(8,128)(2,1)S(1)}, u32[]{:S(2)}, u32[]{:S(2)}) %collective-permute-start.37) | collective-permute-done | bytes 344096 | tf_op jit(solution)/shard_map/ppermute | solution.py:26
  169.8 0.9 add_convert_fusion
  171.3 3.3 %collective-permute-done.38 = bf16[1344,512]{1,0:T(8,128)(2,1)} collective-permute-done((bf16[1344,512]{1,0:T(8,128)(2,1)S(1)}, bf16[1344,512]{1,0:T(8,128)(2,1)}, u32[]{:S(2)}, u32[]{:S(2)}) %collective-permute-start.38) | collective-permute-done | bytes 1376288 | tf_op jit(solution)/shard_map/ppermute | solution.py:26
  174.6 3.8 %multiply_reduce_fusion = (f32[512]{0:T(512)S(1)}, f32[1344,512]{1,0:T(8,128)S(1)}) fusion(bf16[1344,512]{1,0:T(8,128)(2,1)} %collective-permute-done.38, f32[2688,512]{1,0:T(8,128)} %copy-done.5, s32[]{:T(128)S(6)} %select_n.220, bf16[512,512]{1,0:T(8,128)(2,1)} %copy-done.7, bf16[2688,512]{1,0:T(8,128)(2,1)} %bitcast.145), kind=kOutput, calls=%fused_computation.2 | convolution fusion | flops 708083200 | bytes 8784896 | tf_op jit(solution)/shard_map/dot_general | solution.py:336
  178.4 9.8 %psum.7 = f32[512]{0:T(512)S(1)} all-reduce(f32[512]{0:T(512)S(1)} %get-tuple-element.52), channel_id=1, replica_groups=mesh['yl'=2,'x'=4,'z'=4,'yh'=2,'c'=2] {'yh','c'}, use_global_device_ids=true, to_apply=%region_1.2 | all-reduce | flops 512 | bytes 4096 | tf_op jit(solution)/shard_map/psum | solution.py:349
  188.2 4.4 %fusion = bf16[512,1344]{0,1:T(8,128)(2,1)} fusion(bf16[512,1344]{0,1:T(8,128)(2,1)} %param.11, f32[1344]{0:T(1024)S(1)} %copy-done.15, f32[512]{0:T(512)S(1)} %add_rsqrt_fusion, bf16[1344,512]{1,0:T(8,128)(2,1)} %collective-permute-done.38, f32[1344,512]{1,0:T(8,128)S(1)} %get-tuple-element.53, f32[2688,512]{1,0:T(8,128)} %copy-done.5, s32[]{:T(128)S(6)} %select_n.220), kind=kLoop, calls=%fused_computation.1 | loop fusion | flops 5505024 | bytes 9641220 | tf_op jit(solution)/shard_map/convert_element_type | solution.py:351
  (121 shorter events, 15.4 us)
Async XLA Ops:
  6.5 19.4 %copy-start.16 = (s32[4]{0:T(128)S(1)}, s32[4]{0:T(128)}, u32[]{:S(2)}) copy-start(s32[4]{0:T(128)} %constant.229.clone) | copy-start | bytes 52
  6.5 55.7 %all-gather.3.cloned.1.call-start = ((), (), s32[]{:S(2)}) async-start(), calls=%async_computation | async-start | bytes 6881280 | tf_op jit(solution)/shard_map/all_gather | solution.py:277
  10.0 9.8 %collective-permute-start.5 = (bf16[168,1024]{1,0:T(8,128)(2,1)S(1)}, bf16[168,1024]{1,0:T(8,128)(2,1)S(1)}, u32[]{:S(2)}, u32[]{:S(2)}) collective-permute-start(bf16[168,1024]{1,0:T(8,128)(2,1)S(1)} %constant_dynamic-update-slice_fusion.refs_0_), channel_id=1, source_target_pairs={{0,64},{64,0},{1,65},{65,1},{2,66},{66,2},{3,67},{67,3},{4,68},{68... | collective-permute-start | bytes 1032200 | tf_op jit(solution)/shard_map/ppermute | solution.py:26
  10.7 13.1 %collective-permute-start = (bf16[168,1024]{1,0:T(8,128)(2,1)S(1)}, bf16[168,1024]{1,0:T(8,128)(2,1)S(1)}, u32[]{:S(2)}, u32[]{:S(2)}) collective-permute-start(bf16[168,1024]{1,0:T(8,128)(2,1)S(1)} %constant_dynamic-update-slice_fusion.refs_0_), channel_id=1, source_target_pairs={{0,16},{16,32},{32,48},{48,0},{1,17},{17,33},{33,49},{49,1},{2,18}... | collective-permute-start | bytes 1032200 | tf_op jit(solution)/shard_map/ppermute | solution.py:26
  11.2 17.8 %collective-permute-start.1 = (bf16[168,1024]{1,0:T(8,128)(2,1)S(1)}, bf16[168,1024]{1,0:T(8,128)(2,1)S(1)}, u32[]{:S(2)}, u32[]{:S(2)}) collective-permute-start(bf16[168,1024]{1,0:T(8,128)(2,1)S(1)} %constant_dynamic-update-slice_fusion.refs_0_), channel_id=1, source_target_pairs={{0,48},{16,0},{32,16},{48,32},{1,49},{17,1},{33,17},{49,33},{2,50}... | collective-permute-start | bytes 1032200 | tf_op jit(solution)/shard_map/ppermute | solution.py:26
  12.8 16.3 %collective-permute-start.2 = (bf16[168,1024]{1,0:T(8,128)(2,1)S(1)}, bf16[168,1024]{1,0:T(8,128)(2,1)S(1)}, u32[]{:S(2)}, u32[]{:S(2)}) collective-permute-start(bf16[168,1024]{1,0:T(8,128)(2,1)S(1)} %constant_dynamic-update-slice_fusion.refs_0_), channel_id=1, source_target_pairs={{0,32},{16,48},{32,0},{48,16},{1,33},{17,49},{33,1},{49,17},{2,34}... | collective-permute-start | bytes 1032200 | tf_op jit(solution)/shard_map/ppermute | solution.py:26
  19.8 22.0 %copy-start.1 = (bf16[168,1024]{1,0:T(8,128)(2,1)}, bf16[168,1024]{1,0:T(8,128)(2,1)S(1)}, u32[]{:S(2)}) copy-start(bf16[168,1024]{1,0:T(8,128)(2,1)S(1)} %collective-permute-done.5.refs_0_) | copy-start | bytes 1032196
  19.8 14.2 %collective-permute-start.6 = (bf16[168,1024]{1,0:T(8,128)(2,1)S(1)}, bf16[168,1024]{1,0:T(8,128)(2,1)}, u32[]{:S(2)}, u32[]{:S(2)}) collective-permute-start(bf16[168,1024]{1,0:T(8,128)(2,1)S(1)} %collective-permute-done.5.refs_0_), channel_id=1, source_target_pairs={{0,4},{4,8},{8,12},{12,0},{1,5},{5,9},{9,13},{13,1},{2,6},{6,10},{... | collective-permute-start | bytes 1032200 | tf_op jit(solution)/shard_map/ppermute | solution.py:26
  21.7 15.2 %collective-permute-start.7 = (bf16[168,1024]{1,0:T(8,128)(2,1)S(1)}, bf16[168,1024]{1,0:T(8,128)(2,1)}, u32[]{:S(2)}, u32[]{:S(2)}) collective-permute-start(bf16[168,1024]{1,0:T(8,128)(2,1)S(1)} %collective-permute-done.5.refs_0_), channel_id=1, source_target_pairs={{0,12},{4,0},{8,4},{12,8},{1,13},{5,1},{9,5},{13,9},{2,14},{6,2},{... | collective-permute-start | bytes 1032200 | tf_op jit(solution)/shard_map/ppermute | solution.py:26
  23.8 18.0 %collective-permute-start.8 = (bf16[168,1024]{1,0:T(8,128)(2,1)S(1)}, bf16[168,1024]{1,0:T(8,128)(2,1)}, u32[]{:S(2)}, u32[]{:S(2)}) collective-permute-start(bf16[168,1024]{1,0:T(8,128)(2,1)S(1)} %collective-permute-done.5.refs_0_), channel_id=1, source_target_pairs={{0,8},{4,12},{8,0},{12,4},{1,9},{5,13},{9,1},{13,5},{2,10},{6,14},... | collective-permute-start | bytes 1032200 | tf_op jit(solution)/shard_map/ppermute | solution.py:26
  29.8 23.9 %collective-permute-start.3 = (bf16[672,512]{1,0:T(8,128)(2,1)S(1)}, bf16[672,512]{1,0:T(8,128)(2,1)S(1)}, u32[]{:S(2)}, u32[]{:S(2)}) collective-permute-start(bf16[672,512]{1,0:T(8,128)(2,1)S(1)} %bitcast.132), channel_id=1, source_target_pairs={{0,4},{4,8},{8,12},{12,0},{1,5},{5,9},{9,13},{13,1},{2,6},{6,10},{... | collective-permute-start | bytes 2064392 | tf_op jit(solution)/shard_map/ppermute | solution.py:26
  31.8 23.1 %collective-permute-start.4 = (bf16[672,512]{1,0:T(8,128)(2,1)S(1)}, bf16[672,512]{1,0:T(8,128)(2,1)S(1)}, u32[]{:S(2)}, u32[]{:S(2)}) collective-permute-start(bf16[672,512]{1,0:T(8,128)(2,1)S(1)} %bitcast.129), channel_id=1, source_target_pairs={{0,12},{4,0},{8,4},{12,8},{1,13},{5,1},{9,5},{13,9},{2,14},{6,2},{... | collective-permute-start | bytes 2064392 | tf_op jit(solution)/shard_map/ppermute | solution.py:26
  41.8 1.0 copy-start.2
  44.8 14.9 %collective-permute-start.9 = (bf16[672,512]{1,0:T(8,128)(2,1)S(1)}, bf16[672,512]{1,0:T(8,128)(2,1)S(1)}, u32[]{:S(2)}, u32[]{:S(2)}) collective-permute-start(bf16[672,512]{1,0:T(8,128)(2,1)S(1)} %bitcast.135), channel_id=1, source_target_pairs={{0,16},{16,32},{32,48},{48,0},{1,17},{17,33},{33,49},{49,1},{2,18}... | collective-permute-start | bytes 2064392 | tf_op jit(solution)/shard_map/ppermute | solution.py:26
  45.4 16.9 %collective-permute-start.10 = (bf16[672,512]{1,0:T(8,128)(2,1)S(1)}, bf16[672,512]{1,0:T(8,128)(2,1)}, u32[]{:S(2)}, u32[]{:S(2)}) collective-permute-start(bf16[672,512]{1,0:T(8,128)(2,1)S(1)} %bitcast.138), channel_id=1, source_target_pairs={{0,48},{16,0},{32,16},{48,32},{1,49},{17,1},{33,17},{49,33},{2,50}... | collective-permute-start | bytes 2064392 | tf_op jit(solution)/shard_map/ppermute | solution.py:26
  48.3 30.1 %collective-permute-start.11 = (bf16[672,512]{1,0:T(8,128)(2,1)S(1)}, bf16[672,512]{1,0:T(8,128)(2,1)}, u32[]{:S(2)}, u32[]{:S(2)}) collective-permute-start(bf16[672,512]{1,0:T(8,128)(2,1)S(1)} %bitcast.133), channel_id=1, source_target_pairs={{0,12},{4,0},{8,4},{12,8},{1,13},{5,1},{9,5},{13,9},{2,14},{6,2},{... | collective-permute-start | bytes 2064392 | tf_op jit(solution)/shard_map/ppermute | solution.py:26
  53.7 6.0 %copy-start.8 = (bf16[672,512]{1,0:T(8,128)(2,1)}, bf16[672,512]{1,0:T(8,128)(2,1)S(1)}, u32[]{:S(2)}) copy-start(bf16[672,512]{1,0:T(8,128)(2,1)S(1)} %collective-permute-done.3) | copy-start | bytes 2064388
  53.7 30.5 %collective-permute-start.15 = (bf16[672,512]{1,0:T(8,128)(2,1)S(1)}, bf16[672,512]{1,0:T(8,128)(2,1)}, u32[]{:S(2)}, u32[]{:S(2)}) collective-permute-start(bf16[672,512]{1,0:T(8,128)(2,1)S(1)} %bitcast.130), channel_id=1, source_target_pairs={{0,4},{4,8},{8,12},{12,0},{1,5},{5,9},{9,13},{13,1},{2,6},{6,10},{... | collective-permute-start | bytes 2064392 | tf_op jit(solution)/shard_map/ppermute | solution.py:26
  54.9 5.0 %copy-start.12 = (bf16[672,512]{1,0:T(8,128)(2,1)}, bf16[672,512]{1,0:T(8,128)(2,1)S(1)}, u32[]{:S(2)}) copy-start(bf16[672,512]{1,0:T(8,128)(2,1)S(1)} %collective-permute-done.4) | copy-start | bytes 2064388
  54.9 21.7 %collective-permute-start.12 = (bf16[672,512]{1,0:T(8,128)(2,1)S(1)}, bf16[672,512]{1,0:T(8,128)(2,1)}, u32[]{:S(2)}, u32[]{:S(2)}) collective-permute-start(bf16[672,512]{1,0:T(8,128)(2,1)S(1)} %bitcast.136), channel_id=1, source_target_pairs={{0,48},{16,0},{32,16},{48,32},{1,49},{17,1},{33,17},{49,33},{2,50}... | collective-permute-start | bytes 2064392 | tf_op jit(solution)/shard_map/ppermute | solution.py:26
  59.7 0.8 copy-start.10
  59.7 22.6 %collective-permute-start.16 = (bf16[672,512]{1,0:T(8,128)(2,1)S(1)}, bf16[672,512]{1,0:T(8,128)(2,1)}, u32[]{:S(2)}, u32[]{:S(2)}) collective-permute-start(bf16[672,512]{1,0:T(8,128)(2,1)S(1)} %bitcast.139), channel_id=1, source_target_pairs={{0,16},{16,32},{32,48},{48,0},{1,17},{17,33},{33,49},{49,1},{2,18}... | collective-permute-start | bytes 2064392 | tf_op jit(solution)/shard_map/ppermute | solution.py:26
  62.2 2.6 %copy-start = (bf16[5376,512]{1,0:T(8,128)(2,1)S(1)}, bf16[5376,512]{1,0:T(8,128)(2,1)}, u32[]{:S(2)}) copy-start(bf16[5376,512]{1,0:T(8,128)(2,1)} %all-gather.3.cloned.1.call-done) | copy-start | bytes 16515076
  71.9 1.2 copy-start.11
  72.4 1.3 copy-start.9
  73.0 26.8 %collective-permute-start.14 = (bf16[672,512]{1,0:T(8,128)(2,1)S(1)}, bf16[672,512]{1,0:T(8,128)(2,1)S(1)}, u32[]{:S(2)}, u32[]{:S(2)}) collective-permute-start(bf16[672,512]{1,0:T(8,128)(2,1)S(1)} %copy-done.11), channel_id=1, source_target_pairs={{0,16},{16,32},{32,48},{48,0},{1,17},{17,33},{33,49},{49,1},{2,18}... | collective-permute-start | bytes 2064392 | tf_op jit(solution)/shard_map/ppermute | solution.py:26
  73.7 2.3 %copy-start.13 = (bf16[672,512]{1,0:T(8,128)(2,1)S(1)}, bf16[672,512]{1,0:T(8,128)(2,1)}, u32[]{:S(2)}) copy-start(bf16[672,512]{1,0:T(8,128)(2,1)} %copy-done.12) | copy-start | bytes 2064388
  76.6 5.7 %copy-start.14 = (bf16[512,168]{0,1:T(8,128)(2,1)S(1)}, bf16[512,168]{0,1:T(8,128)(2,1)}, u32[]{:S(2)}) copy-start(bf16[512,168]{0,1:T(8,128)(2,1)} %param.15) | copy-start | bytes 516100
  76.6 14.7 %collective-permute-start.19 = (bf16[672,512]{1,0:T(8,128)(2,1)S(1)}, bf16[672,512]{1,0:T(8,128)(2,1)S(1)}, u32[]{:S(2)}, u32[]{:S(2)}) collective-permute-start(bf16[672,512]{1,0:T(8,128)(2,1)S(1)} %copy-done.13), channel_id=1, source_target_pairs={{0,12},{4,0},{8,4},{12,8},{1,13},{5,1},{9,5},{13,9},{2,14},{6,2},{... | collective-permute-start | bytes 2064392 | tf_op jit(solution)/shard_map/ppermute | solution.py:26
  78.4 16.2 %collective-permute-start.20 = (bf16[672,512]{1,0:T(8,128)(2,1)}, bf16[672,512]{1,0:T(8,128)(2,1)S(1)}, u32[]{:S(2)}, u32[]{:S(2)}) collective-permute-start(bf16[672,512]{1,0:T(8,128)(2,1)} %collective-permute-done.10), channel_id=1, source_target_pairs={{0,48},{16,0},{32,16},{48,32},{1,49},{17,1},{33,17},{49,33},{2,50}... | collective-permute-start | bytes 2064392 | tf_op jit(solution)/shard_map/ppermute | solution.py:26
  82.3 7.0 %collective-permute-start.17 = (bf16[168,512]{1,0:T(8,128)(2,1)S(1)}, bf16[168,512]{1,0:T(8,128)(2,1)S(1)}, u32[]{:S(2)}, u32[]{:S(2)}) collective-permute-start(bf16[168,512]{1,0:T(8,128)(2,1)S(1)} %bitcast.147), channel_id=1, source_target_pairs={{0,64},{2,0},{64,66},{66,2},{1,65},{3,1},{65,67},{67,3},{4,68},{6,... | collective-permute-start | bytes 516104 | tf_op jit(solution)/shard_map/ppermute | solution.py:304
  84.2 7.1 %collective-permute-start.18 = (bf16[168,512]{1,0:T(8,128)(2,1)S(1)}, bf16[168,512]{1,0:T(8,128)(2,1)S(1)}, u32[]{:S(2)}, u32[]{:S(2)}) collective-permute-start(bf16[168,512]{1,0:T(8,128)(2,1)S(1)} %bitcast.148), channel_id=1, source_target_pairs={{64,2},{2,64},{65,3},{3,65},{68,6},{6,68},{69,7},{7,69},{72,10},{1... | collective-permute-start | bytes 516104 | tf_op jit(solution)/shard_map/ppermute | solution.py:305
  89.3 22.7 %collective-permute-start.13 = (bf16[672,512]{1,0:T(8,128)(2,1)S(1)}, bf16[672,512]{1,0:T(8,128)(2,1)S(1)}, u32[]{:S(2)}, u32[]{:S(2)}) collective-permute-start(bf16[672,512]{1,0:T(8,128)(2,1)S(1)} %copy-done.9), channel_id=1, source_target_pairs={{0,4},{4,8},{8,12},{12,0},{1,5},{5,9},{9,13},{13,1},{2,6},{6,10},{... | collective-permute-start | bytes 2064392 | tf_op jit(solution)/shard_map/ppermute | solution.py:26
  94.6 18.1 %collective-permute-start.24 = (bf16[168,512]{1,0:T(8,128)(2,1)S(1)}, bf16[168,512]{1,0:T(8,128)(2,1)S(1)}, u32[]{:S(2)}, u32[]{:S(2)}) collective-permute-start(bf16[168,512]{1,0:T(8,128)(2,1)S(1)} %get-tuple-element.41), channel_id=1, source_target_pairs={{0,16},{16,32},{32,48},{48,0},{1,17},{17,33},{33,49},{49,1},{2,18}... | collective-permute-start | bytes 516104 | tf_op jit(solution)/shard_map/ppermute | solution.py:26
  94.9 17.8 %collective-permute-start.25 = (bf16[168,512]{1,0:T(8,128)(2,1)S(1)}, bf16[168,512]{1,0:T(8,128)(2,1)S(1)}, u32[]{:S(2)}, u32[]{:S(2)}) collective-permute-start(bf16[168,512]{1,0:T(8,128)(2,1)S(1)} %get-tuple-element.41), channel_id=1, source_target_pairs={{0,48},{16,0},{32,16},{48,32},{1,49},{17,1},{33,17},{49,33},{2,50}... | collective-permute-start | bytes 516104 | tf_op jit(solution)/shard_map/ppermute | solution.py:26
  96.6 20.1 %collective-permute-start.26 = (bf16[168,512]{1,0:T(8,128)(2,1)S(1)}, bf16[168,512]{1,0:T(8,128)(2,1)S(1)}, u32[]{:S(2)}, u32[]{:S(2)}) collective-permute-start(bf16[168,512]{1,0:T(8,128)(2,1)S(1)} %get-tuple-element.41), channel_id=1, source_target_pairs={{0,32},{16,48},{32,0},{48,16},{1,33},{17,49},{33,1},{49,17},{2,34}... | collective-permute-start | bytes 516104 | tf_op jit(solution)/shard_map/ppermute | solution.py:26
  98.1 0.9 copy-start.3
  99.8 18.4 %collective-permute-start.31 = (bf16[168,512]{1,0:T(8,128)(2,1)S(1)}, bf16[168,512]{1,0:T(8,128)(2,1)S(1)}, u32[]{:S(2)}, u32[]{:S(2)}) collective-permute-start(bf16[168,512]{1,0:T(8,128)(2,1)S(1)} %get-tuple-element.43), channel_id=1, source_target_pairs={{0,4},{4,8},{8,12},{12,0},{1,5},{5,9},{9,13},{13,1},{2,6},{6,10},{... | collective-permute-start | bytes 516104 | tf_op jit(solution)/shard_map/ppermute | solution.py:26
  112.0 8.1 %collective-permute-start.32 = (bf16[168,512]{1,0:T(8,128)(2,1)S(1)}, bf16[168,512]{1,0:T(8,128)(2,1)S(1)}, u32[]{:S(2)}, u32[]{:S(2)}) collective-permute-start(bf16[168,512]{1,0:T(8,128)(2,1)S(1)} %get-tuple-element.43), channel_id=1, source_target_pairs={{0,12},{4,0},{8,4},{12,8},{1,13},{5,1},{9,5},{13,9},{2,14},{6,2},{... | collective-permute-start | bytes 516104 | tf_op jit(solution)/shard_map/ppermute | solution.py:26
  112.6 9.0 %collective-permute-start.33 = (bf16[168,512]{1,0:T(8,128)(2,1)S(1)}, bf16[168,512]{1,0:T(8,128)(2,1)S(1)}, u32[]{:S(2)}, u32[]{:S(2)}) collective-permute-start(bf16[168,512]{1,0:T(8,128)(2,1)S(1)} %get-tuple-element.43), channel_id=1, source_target_pairs={{0,8},{4,12},{8,0},{12,4},{1,9},{5,13},{9,1},{13,5},{2,10},{6,14},... | collective-permute-start | bytes 516104 | tf_op jit(solution)/shard_map/ppermute | solution.py:26
  112.8 19.6 %collective-permute-start.21 = (bf16[512,512]{1,0:T(8,128)(2,1)S(1)}, bf16[512,512]{1,0:T(8,128)(2,1)S(1)}, u32[]{:S(2)}, u32[]{:S(2)}) collective-permute-start(bf16[512,512]{1,0:T(8,128)(2,1)S(1)} %shard_map.113.k_ref.v_ref), channel_id=1, source_target_pairs={{0,4},{4,8},{8,12},{12,16},{16,20},{20,24},{24,28},{28,32},{32,36}... | collective-permute-start | bytes 1572872 | tf_op jit(solution)/shard_map/ppermute | solution.py:31
  116.8 38.2 %collective-permute-start.27 = (bf16[4,168,512]{2,1,0:T(8,128)(2,1)S(1)}, bf16[4,168,512]{2,1,0:T(8,128)(2,1)S(1)}, u32[]{:S(2)}, u32[]{:S(2)}) collective-permute-start(bf16[4,168,512]{2,1,0:T(8,128)(2,1)S(1)} %bitcast_dynamic-update-slice_fusion.14), channel_id=1, source_target_pairs={{0,4},{4,8},{8,12},{12,0},{1,5},{5,9},{9,13},{13,1},{2,6},{6,10},{... | collective-permute-start | bytes 2064392 | tf_op jit(solution)/shard_map/ppermute | solution.py:26
  118.3 36.8 %collective-permute-start.28 = (bf16[4,168,512]{2,1,0:T(8,128)(2,1)S(1)}, bf16[4,168,512]{2,1,0:T(8,128)(2,1)S(1)}, u32[]{:S(2)}, u32[]{:S(2)}) collective-permute-start(bf16[4,168,512]{2,1,0:T(8,128)(2,1)S(1)} %bitcast_dynamic-update-slice_fusion.14), channel_id=1, source_target_pairs={{0,12},{4,0},{8,4},{12,8},{1,13},{5,1},{9,5},{13,9},{2,14},{6,2},{... | collective-permute-start | bytes 2064392 | tf_op jit(solution)/shard_map/ppermute | solution.py:26
  121.7 2.9 %copy-start.4 = (f32[128]{0:T(128)S(1)}, f32[128]{0:T(128)}, u32[]{:S(2)}) copy-start(f32[128]{0:T(128)} %param.18) | copy-start | bytes 1540
  121.7 36.7 %collective-permute-start.34 = (bf16[4,168,512]{2,1,0:T(8,128)(2,1)S(1)}, bf16[4,168,512]{2,1,0:T(8,128)(2,1)S(1)}, u32[]{:S(2)}, u32[]{:S(2)}) collective-permute-start(bf16[4,168,512]{2,1,0:T(8,128)(2,1)S(1)} %bitcast_dynamic-update-slice_fusion.10), channel_id=1, source_target_pairs={{0,16},{16,32},{32,48},{48,0},{1,17},{17,33},{33,49},{49,1},{2,18}... | collective-permute-start | bytes 2064392 | tf_op jit(solution)/shard_map/ppermute | solution.py:26
  121.8 39.4 %collective-permute-start.35 = (bf16[4,168,512]{2,1,0:T(8,128)(2,1)S(1)}, bf16[4,168,512]{2,1,0:T(8,128)(2,1)S(1)}, u32[]{:S(2)}, u32[]{:S(2)}) collective-permute-start(bf16[4,168,512]{2,1,0:T(8,128)(2,1)S(1)} %bitcast_dynamic-update-slice_fusion.10), channel_id=1, source_target_pairs={{0,48},{16,0},{32,16},{48,32},{1,49},{17,1},{33,17},{49,33},{2,50}... | collective-permute-start | bytes 2064392 | tf_op jit(solution)/shard_map/ppermute | solution.py:26
  132.4 15.7 %collective-permute-start.22 = (bf16[512,512]{1,0:T(8,128)(2,1)S(1)}, bf16[512,512]{1,0:T(8,128)(2,1)S(1)}, u32[]{:S(2)}, u32[]{:S(2)}) collective-permute-start(bf16[512,512]{1,0:T(8,128)(2,1)S(1)} %shard_map.113.k_ref.v_ref), channel_id=1, source_target_pairs={{0,8},{4,12},{8,16},{12,20},{16,24},{20,28},{24,32},{28,36},{32,40... | collective-permute-start | bytes 1572872 | tf_op jit(solution)/shard_map/ppermute | solution.py:31
  151.5 14.7 %collective-permute-start.23 = (bf16[512,512]{1,0:T(8,128)(2,1)S(1)}, bf16[512,512]{1,0:T(8,128)(2,1)S(1)}, u32[]{:S(2)}, u32[]{:S(2)}) collective-permute-start(bf16[512,512]{1,0:T(8,128)(2,1)S(1)} %shard_map.115), channel_id=1, source_target_pairs={{0,2},{2,0},{1,3},{3,1},{4,6},{6,4},{5,7},{7,5},{8,10},{10,8},{9,1... | collective-permute-start | bytes 1572872 | tf_op jit(solution)/shard_map/ppermute | solution.py:26
  155.0 8.5 %collective-permute-start.29 = (bf16[2,168,512]{2,1,0:T(8,128)(2,1)S(1)}, bf16[2,168,512]{2,1,0:T(8,128)(2,1)S(1)}, u32[]{:S(2)}, u32[]{:S(2)}) collective-permute-start(bf16[2,168,512]{2,1,0:T(8,128)(2,1)S(1)} %slice.16), channel_id=1, source_target_pairs={{0,4},{4,8},{8,12},{12,0},{1,5},{5,9},{9,13},{13,1},{2,6},{6,10},{... | collective-permute-start | bytes 1032200 | tf_op jit(solution)/shard_map/ppermute | solution.py:26
  155.1 9.3 %collective-permute-start.30 = (bf16[2,168,512]{2,1,0:T(8,128)(2,1)S(1)}, bf16[2,168,512]{2,1,0:T(8,128)(2,1)S(1)}, u32[]{:S(2)}, u32[]{:S(2)}) collective-permute-start(bf16[2,168,512]{2,1,0:T(8,128)(2,1)S(1)} %slice.17), channel_id=1, source_target_pairs={{0,12},{4,0},{8,4},{12,8},{1,13},{5,1},{9,5},{13,9},{2,14},{6,2},{... | collective-permute-start | bytes 1032200 | tf_op jit(solution)/shard_map/ppermute | solution.py:26
  158.5 7.8 %collective-permute-start.36 = (bf16[2,168,512]{2,1,0:T(8,128)(2,1)S(1)}, bf16[2,168,512]{2,1,0:T(8,128)(2,1)S(1)}, u32[]{:S(2)}, u32[]{:S(2)}) collective-permute-start(bf16[2,168,512]{2,1,0:T(8,128)(2,1)S(1)} %slice.18), channel_id=1, source_target_pairs={{0,16},{16,32},{32,48},{48,0},{1,17},{17,33},{33,49},{49,1},{2,18}... | collective-permute-start | bytes 1032200 | tf_op jit(solution)/shard_map/ppermute | solution.py:26
  161.2 8.5 %collective-permute-start.37 = (bf16[2,168,512]{2,1,0:T(8,128)(2,1)S(1)}, bf16[2,168,512]{2,1,0:T(8,128)(2,1)S(1)}, u32[]{:S(2)}, u32[]{:S(2)}) collective-permute-start(bf16[2,168,512]{2,1,0:T(8,128)(2,1)S(1)} %slice.19), channel_id=1, source_target_pairs={{0,48},{16,0},{32,16},{48,32},{1,49},{17,1},{33,17},{49,33},{2,50}... | collective-permute-start | bytes 1032200 | tf_op jit(solution)/shard_map/ppermute | solution.py:26
  166.2 3.6 %copy-start.5 = (f32[2688,512]{1,0:T(8,128)}, f32[2688,512]{1,0:T(8,128)S(1)}, u32[]{:S(2)}) copy-start(f32[2688,512]{1,0:T(8,128)S(1)} %fusion.86) | copy-start | bytes 16515076
  166.2 4.5 %copy-start.7 = (bf16[512,512]{1,0:T(8,128)(2,1)}, bf16[512,512]{1,0:T(8,128)(2,1)S(1)}, u32[]{:S(2)}) copy-start(bf16[512,512]{1,0:T(8,128)(2,1)S(1)} %collective-permute-done.23) | copy-start | bytes 1572868
  169.7 1.6 copy-start.6
  171.3 3.3 %collective-permute-start.38 = (bf16[1344,512]{1,0:T(8,128)(2,1)S(1)}, bf16[1344,512]{1,0:T(8,128)(2,1)}, u32[]{:S(2)}, u32[]{:S(2)}) collective-permute-start(bf16[1344,512]{1,0:T(8,128)(2,1)S(1)} %add_convert_fusion), channel_id=1, source_target_pairs={{0,1},{1,0},{2,3},{3,2},{4,5},{5,4},{6,7},{7,6},{8,9},{9,8},{10,11... | collective-permute-start | bytes 4128776 | tf_op jit(solution)/shard_map/ppermute | solution.py:26
  171.3 16.9 %copy-start.15 = (f32[1344]{0:T(1024)S(1)}, f32[1344]{0:T(1024)}, u32[]{:S(2)}) copy-start(f32[1344]{0:T(1024)} %param.17) | copy-start | bytes 16132
Sparse Core Ops, SparseCore 0:
  9.0 46.4 all-gather.2

commit v5 on v4

--- a/solution.py
+++ b/solution.py
@@ -14,6 +14,8 @@
 SHARD = MODEL_WIDTH // 32
 VMEM = 40 << 20
 SMALL = 16 << 20
+LARGE = 58 << 20
+QUICK = pl.CostEstimate(flops=0, bytes_accessed=0, transcendentals=0)
 
 score_scale = 168.0 ** (-0.5)
 epsilon = 1e-06
@@ -36,35 +38,63 @@
 
 
 def line_kernel(slots, *refs):
-    pieces, (first, second) = refs[:4], refs[4:]
-    cut = first.shape[2]
-    for k, piece in enumerate(pieces):
+    for k, piece in enumerate(refs[:4]):
 
         @pl.when(pl.program_id(0) == k)
         def _():
-            first[0] = piece[:, :cut]
-            second[0] = piece[:, cut:]
-
-
-def in_line(pieces, at, cut):
+            refs[4][0] = piece[...]
+
+
+def in_line(pieces, at):
     depth, columns = pieces[0].shape
-    out = lambda wide: pl.BlockSpec((1, depth, wide), lambda i, s: (s[i], 0, 0))
-    first, second = pl.pallas_call(
+    line = pl.pallas_call(
         line_kernel,
         grid_spec=pltpu.PrefetchScalarGridSpec(
             num_scalar_prefetch=1,
             grid=(4,),
             in_specs=[pl.BlockSpec((depth, columns), lambda i, s: (0, 0))] * 4,
-            out_specs=[out(cut), out(columns - cut)],
+            out_specs=pl.BlockSpec((1, depth, columns), lambda i, s: (s[i], 0, 0)),
         ),
-        out_shape=[
-            jax.ShapeDtypeStruct((4, depth, cut), jnp.bfloat16),
-            jax.ShapeDtypeStruct((4, depth, columns - cut), jnp.bfloat16),
-        ],
+        out_shape=jax.ShapeDtypeStruct((4, depth, columns), jnp.bfloat16),
         compiler_params=pltpu.CompilerParams(vmem_limit_bytes=VMEM),
-        cost_estimate=pl.CostEstimate(flops=0, bytes_accessed=3_000_000, transcendentals=0),
+        cost_estimate=QUICK,
     )((at + jnp.array([0, 3, 1, 2], jnp.int32)) % 4, *pieces)
-    return first.reshape(4 * depth, cut), second.reshape(4 * depth, columns - cut)
+    return line.reshape(4 * depth, columns)
+
+
+def beside_kernel(*refs):
+    out_ref, start = refs[-1], 0
+    for ref in refs[:-1]:
+        out_ref[:, start : start + ref.shape[1]] = ref[...]
+        start += ref.shape[1]
+
+
+def beside(*values):
+    rows, columns = values[0].shape[0], sum(value.shape[1] for value in values)
+    return pl.pallas_call(
+        beside_kernel,
+        out_shape=jax.ShapeDtypeStruct((rows, columns), values[0].dtype),
+        compiler_params=pltpu.CompilerParams(vmem_limit_bytes=LARGE),
+        cost_estimate=QUICK,
+    )(*values)
+
+
+def cut_kernel(value_ref, out_ref):
+    out_ref[...] = value_ref[...]
+
+
+def cut(value, part):
+    rows, columns = value.shape
+    step = rows // 2
+    return pl.pallas_call(
+        cut_kernel,
+        grid=(2,),
+        in_specs=[pl.BlockSpec((step, columns // 2), lambda i: (i, part))],
+        out_specs=pl.BlockSpec((step, columns // 2), lambda i: (i, 0)),
+        out_shape=jax.ShapeDtypeStruct((rows, columns // 2), value.dtype),
+        compiler_params=pltpu.CompilerParams(vmem_limit_bytes=VMEM),
+        cost_estimate=QUICK,
+    )(value)
 
 
 def norm_kernel(side, own_ref, other_ref, near_gain, far_gain, near_ref, far_ref):
@@ -103,9 +133,56 @@
             out_specs=[out, out],
         ),
         out_shape=[shape, shape],
-        compiler_params=pltpu.CompilerParams(vmem_limit_bytes=VMEM),
-        cost_estimate=pl.CostEstimate(flops=20_000_000, bytes_accessed=12_000_000, transcendentals=0),
+        compiler_params=pltpu.CompilerParams(vmem_limit_bytes=LARGE),
+        cost_estimate=QUICK,
     )(jnp.stack([side, 1 - side]), pieces, pieces, near_gain, far_gain)
+
+
+def early_kernel(n_near, count, side, index, near_ref, far_ref, *refs):
+    weights, (total, w_buf, t_buf, sems) = refs[:count], refs[count:]
+    columns = total.shape[1]
+    copies = []
+    for k in range(count):
+        source = near_ref if k < n_near else far_ref
+        weight = weights[k].at[:, side * columns : (side + 1) * columns]
+        copies.append(
+            (
+                pltpu.make_async_copy(source.at[index[k]], t_buf.at[k], sems.at[0, k]),
+                pltpu.make_async_copy(weight, w_buf.at[k], sems.at[1, k]),
+            )
+        )
+    for pair in copies:
+        for copy in pair:
+            copy.start()
+    for k, pair in enumerate(copies):
+        for copy in pair:
+            copy.wait()
+        part = jnp.dot(t_buf[k], w_buf[k], preferred_element_type=jnp.float32)
+        total[...] = part if k == 0 else total[...] + part
+
+
+def early_product(side, index, near, far, near_weights, far_weights):
+    weights = near_weights + far_weights
+    rows, depth, columns = near.shape[1], near.shape[2], weights[0].shape[1] // 2
+    anywhere = pl.BlockSpec(memory_space=pl.ANY)
+    count = len(weights)
+    return pl.pallas_call(
+        functools.partial(early_kernel, len(near_weights), count, side),
+        grid_spec=pltpu.PrefetchScalarGridSpec(
+            num_scalar_prefetch=1,
+            grid=(1,),
+            in_specs=[anywhere] * (2 + count),
+            out_specs=pl.BlockSpec((rows, columns), lambda i, s: (0, 0)),
+            scratch_shapes=[
+                pltpu.VMEM((count, depth, columns), jnp.bfloat16),
+                pltpu.VMEM((count, rows, depth), jnp.bfloat16),
+                pltpu.SemaphoreType.DMA((2, count)),
+            ],
+        ),
+        out_shape=jax.ShapeDtypeStruct((rows, columns), jnp.float32),
+        compiler_params=pltpu.CompilerParams(vmem_limit_bytes=LARGE),
+        cost_estimate=QUICK,
+    )(index, near, far, *weights)
 
 
 def pick(parts, at):
@@ -142,7 +219,7 @@
         out_specs=block,
         out_shape=jax.ShapeDtypeStruct((rows, columns), jnp.bfloat16),
         compiler_params=pltpu.CompilerParams(vmem_limit_bytes=SMALL),
-        cost_estimate=pl.CostEstimate(flops=5_000_000, bytes_accessed=3_000_000, transcendentals=0),
+        cost_estimate=QUICK,
     )(raw, gain, cosine, sine)
 
 
@@ -219,9 +296,7 @@
         out_specs=[pair, pair],
         out_shape=[shape, shape],
         compiler_params=pltpu.CompilerParams(vmem_limit_bytes=SMALL),
-        cost_estimate=pl.CostEstimate(
-            flops=4 * rows * rows * columns, bytes_accessed=3_000_000, transcendentals=rows * rows * 4
-        ),
+        cost_estimate=QUICK,
     )(queries, keyed, keyed)
 
 
@@ -241,30 +316,8 @@
         ),
         out_shape=jax.ShapeDtypeStruct((rows, columns), jnp.bfloat16),
         compiler_params=pltpu.CompilerParams(vmem_limit_bytes=SMALL),
-        cost_estimate=pl.CostEstimate(
-            flops=8 * rows * rows * columns, bytes_accessed=4_000_000, transcendentals=rows * rows * 8
-        ),
+        cost_estimate=QUICK,
     )(valid, queries, one, one, two, two, sums, weights)
-
-
-def gather_out(own, first, second):
-    depth, columns = own.shape
-    at = lax.axis_index(first)
-    line = jnp.zeros((4, depth, columns), own.dtype)
-    for step in (0, 1, 3, 2):
-        piece = own if step == 0 else shift(own, first, step)
-        line = lax.dynamic_update_index_in_dim(line, piece, (at - step) % 4, 0)
-    ahead, behind = shift(line, second, 1), shift(line, second, 3)
-    low, high = shift(ahead[:2], second, 1), shift(behind[2:], second, 3)
-    there = lax.axis_index(second)
-    whole = jnp.zeros((4, 4, depth, columns), own.dtype)
-    for piece, offset, start in ((line, 0, 0), (ahead, 3, 0), (behind, 1, 0), (low, 2, 0), (high, 2, 2)):
-        place = (there + offset) % 4
-        if first == "x":
-            whole = lax.dynamic_update_slice(whole, piece[:, None], (start, place, 0, 0))
-        else:
-            whole = lax.dynamic_update_slice(whole, piece[None], (place, start, 0, 0))
-    return whole.reshape(16 * depth, columns)
 
 
 def local(
@@ -276,41 +329,21 @@
     seq_index = (yl * 4 + x) * 4 + z
     whole = lax.all_gather(tokens.T, MP, axis=0)
 
-    own = jnp.concatenate([q_weight, key_matrix, value_matrix], axis=1)
+    own = beside(q_weight, key_matrix, value_matrix)
     other = shift(own, "yl", 1)
     own_pieces = [own] + [shift(own, "x", step) for step in (1, 3, 2)]
     other_pieces = [other] + [shift(other, "z", step) for step in (1, 3, 2)]
-    own_q, own_kv = in_line(own_pieces, x, q_cols)
-    other_q, other_kv = in_line(other_pieces, z, q_cols)
-    own_ahead_q, own_behind_kv = shift(own_q, "z", 1), shift(own_kv, "z", 3)
-    other_ahead_q, other_behind_kv = shift(other_q, "x", 1), shift(other_kv, "x", 3)
-    own_ahead_kv, own_behind_q = shift(own_kv, "z", 1), shift(own_q, "z", 3)
-    other_ahead_kv, other_behind_q = shift(other_kv, "x", 1), shift(other_q, "x", 3)
-    own_ahead_q, own_behind_kv, other_ahead_q, other_behind_kv, whole, turned = lax.optimization_barrier(
-        (own_ahead_q, own_behind_kv, other_ahead_q, other_behind_kv, whole, o_weight.T)
-    )
-    own_far_kv = shift(own_behind_kv, "z", 3)
-    other_far_kv = shift(other_behind_kv, "x", 3)
-    own_far_q = shift(own_ahead_q, "z", 1)
-    other_far_q = shift(other_ahead_q, "x", 1)
+    own_line = in_line(own_pieces, x)
+    other_line = in_line(other_pieces, z)
+    own_line, turned = lax.optimization_barrier((own_line, o_weight.T))
+    own_ahead, own_behind = shift(own_line, "z", 1), shift(own_line, "z", 3)
+    other_ahead, other_behind = shift(other_line, "x", 1), shift(other_line, "x", 3)
     near, far = norm_parts(whole, pre_gain, yl)
-    part_kv = product(pick(near, z), own_kv) + product(pick(far, x), other_kv)
-    part_q = product(pick(near, z), own_q) + product(pick(far, x), other_q)
-    part_kv = part_kv + product(pick(near, z + 3), own_ahead_kv) + product(pick(near, z + 1), own_behind_kv)
-    part_kv = part_kv + product(pick(far, x + 3), other_ahead_kv) + product(pick(far, x + 1), other_behind_kv)
 
     y = yh * 2 + yl
     flat = lambda p: (p % 2) * 2 + p // 2
     one = lax.ppermute(turned, ("yl", "yh"), [(flat(a), flat(b)) for a, b in ((0, 1), (2, 0), (1, 3), (3, 2))])
     two = lax.ppermute(turned, ("yl", "yh"), [(flat(a), flat(b)) for a, b in ((1, 2), (2, 1))])
-    outer = (y == 0) | (y == 3)
-    out_same, out_other = jnp.where(outer, turned, one), jnp.where(outer, one, two)
-    out_same, out_other, own_far_kv, other_far_kv = lax.optimization_barrier(
-        (out_same, out_other, own_far_kv, other_far_kv)
-    )
-    out_same = gather_out(out_same, "x", "z")
-    out_other = gather_out(out_other, "z", "x")
-
     positions = seq_index * rows + jnp.arange(rows, dtype=jnp.int32)
     half = HEAD_SIZE // 2
     freq = 10000.0 ** (-(jnp.arange(half, dtype=jnp.float32) * 2.0) / HEAD_SIZE)
@@ -319,33 +352,53 @@
     sine = jnp.sin(angle)
     cosine = jnp.concatenate([cosine, cosine], axis=1)
     sine = jnp.concatenate([-sine, sine], axis=1)
+    index = jnp.stack([z, (z + 3) % 4, (z + 1) % 4, x, (x + 3) % 4, (x + 1) % 4])
+
+    own_ahead, own_behind, other_ahead, other_behind, near, far, one, two, cosine, sine, index = (
+        lax.optimization_barrier(
+            (own_ahead, own_behind, other_ahead, other_behind, near, far, one, two, cosine, sine, index)
+        )
+    )
+
+    own_far_kv = shift(cut(own_behind, 1), "z", 3)
+    other_far_kv = shift(cut(other_behind, 1), "x", 3)
+    own_far_q = shift(cut(own_ahead, 0), "z", 1)
+    other_far_q = shift(cut(other_ahead, 0), "x", 1)
+    outer = (y == 0) | (y == 3)
+    pair = jnp.concatenate([jnp.where(outer, turned, one), jnp.where(outer, one, two)], axis=1)
+    out_all = lax.all_gather(pair, ("x", "z"), axis=0, tiled=True)
+    parts = [own_line, own_ahead, own_behind], [other_line, other_ahead, other_behind]
+    part_kv = early_product(1, index, near, far, *parts)
+    part_kv, own_far_kv, other_far_kv = lax.optimization_barrier((part_kv, own_far_kv, other_far_kv))
+
 
     part_kv = part_kv + product(pick(near, z + 2), own_far_kv) + product(pick(far, x + 2), other_far_kv)
     keyed = finish_heads(2, part_kv, k_gain[None], cosine, sine)
     behind_one = from_behind(keyed, 1)
     behind_two = from_behind(keyed, 2)
-    part_q = part_q + product(pick(near, z + 3), own_ahead_q) + product(pick(near, z + 1), own_behind_q)
-    part_q = part_q + product(pick(far, x + 3), other_ahead_q) + product(pick(far, x + 1), other_behind_q)
+    keyed, index = lax.optimization_barrier((keyed, index))
+    part_q = early_product(0, index, near, far, *parts)
     part_q = part_q + product(pick(near, z + 2), own_far_q) + product(pick(far, x + 2), other_far_q)
     queries = finish_heads(4, part_q, q_gain[None], cosine, sine)
     sums, weights = attend_own(queries, keyed)
     valid = jnp.stack([seq_index >= 1, seq_index >= 2]).astype(jnp.int32)
     context = attend_behind(valid, queries, behind_one, behind_two, sums, weights)
-
     across = shift(context, "yh", 1)
     summed = lambda weight, value: lax.dot_general(
         weight, value, (((1,), (1,)), ((), ())), preferred_element_type=jnp.float32
     )
-    before = summed(out_same, context)
+    out_all, context = lax.optimization_barrier((out_all, context))
+    before = summed(out_all[:, :q_cols], context)
     across, before = lax.optimization_barrier((across, before))
-    columns = out_same.shape[0] // 2
+    columns = out_all.shape[0] // 2
 
     def half_of(core):
-        weight = lax.dynamic_slice_in_dim(out_other, core * columns, columns, 0)
+        weight = lax.dynamic_slice(out_all, (core * columns, q_cols), (columns, q_cols))
         return lax.dynamic_slice_in_dim(before, core * columns, columns, 0) + summed(weight, across)
 
     received = shift(half_of(1 - c).astype(jnp.bfloat16), "c", 1)
-    share = (half_of(c) + received.astype(jnp.float32)).T
+    kept, received = lax.optimization_barrier((half_of(c), received))
+    share = (kept + received.astype(jnp.float32)).T
     total = lax.psum(jnp.sum(share * share, axis=1), MP)
     scale_rows = lax.rsqrt(total / MODEL_WIDTH + epsilon)
     return (tokens.astype(jnp.float32) + share * scale_rows[:, None] * post_gain).astype(

time: 200 us -> 195 us (0.975)
  the two profiles are of different devices: /device:TPU:30 before, /device:TPU:40 now
where the time goes in v5:
time: 195 us; the launch traced here: 193 us
  waiting for transfers between devices  61.1 us (31%)
  Pallas kernels  40.2 us (21%)
  starting transfers between devices  36.4 us (19%)
  matrix products  17.4 us (9%)
  between operations  13.8 us (7%)
  other arithmetic  12.1 us (6%)
  blocking collectives  7.64 us (4%)
  local copies, waits for them, and re-layouts  4.7 us (2%)
    ppermute x17, waiting for transfers between devices, shift(): lax.ppermute(value, axis, [(i, (i + step) % count) for i in range(count)])  29.2 us
    ppermute x2, waiting for transfers between devices, from_behind(): lax.ppermute(value, SEQ, [(source, source + steps) for source in range(co...  26.1 us
    ppermute x17, starting transfers between devices, shift(): lax.ppermute(value, axis, [(i, (i + step) % count) for i in range(count)])  20.7 us
    pallas_call x2, Pallas kernels, early_product(): pl.pallas_call(functools.partial(early_kernel, len(near_weights), count,...  12 us
    dot_general x3, matrix products, local(): lax.dot_general(weight, value, (((1,), (1,)), ((), ())), preferred_elemen...  9.86 us
    ppermute x2, starting transfers between devices, from_behind(): lax.ppermute(value, SEQ, [(source, source + steps) for source in range(co...  9.71 us
    pallas_call x1, Pallas kernels, norm_parts(): pl.pallas_call(norm_kernel, grid_spec=pltpu.PrefetchScalarGridSpec(num_sc...  9.22 us
    psum x1, blocking collectives, local(): total = lax.psum(jnp.sum(share * share, axis=1), MP)  7.64 us
  transfers between devices with their start and end apart: 23, of which 12 were waited for; matrix products, arithmetic and copies ran while one was open for 12% of the time, Pallas kernels for 21%

profile of v5, /device:TPU:40, one launch (start us, length us, event | category | flops | bytes accessed | tf_op | source)
XLA Modules:
  0.0 193.3 jit_solution(5207790098535882746)
XLA Ops:
  6.5 0.7 all-gather.6.cloned.1.call-update
  7.3 1.8 shard_map.109.refs_0_
  9.1 0.4 collective-permute-start.5
  9.5 1.5 collective-permute-start
  11.0 1.7 collective-permute-start.1
  12.8 1.8 collective-permute-start.2
  14.6 4.5 %collective-permute-done.5.refs_0_ = bf16[168,1024]{1,0:T(8,128)(2,1)S(1)} collective-permute-done((bf16[168,1024]{1,0:T(8,128)(2,1)}, bf16[168,1024]{1,0:T(8,128)(2,1)S(1)}, u32[]{:S(2)}, u32[]{:S(2)}) %collective-permute-start.5) | collective-permute-done | bytes 344096 | tf_op jit(solution)/shard_map/ppermute | solution.py:28
  19.1 1.9 collective-permute-start.6
  21.1 3.0 %collective-permute-start.8 = (bf16[168,1024]{1,0:T(8,128)(2,1)S(1)}, bf16[168,1024]{1,0:T(8,128)(2,1)}, u32[]{:S(2)}, u32[]{:S(2)}) collective-permute-start(bf16[168,1024]{1,0:T(8,128)(2,1)S(1)} %collective-permute-done.5.refs_0_), channel_id=1, source_target_pairs={{0,8},{4,12},{8,0},{12,4},{1,9},{5,13},{9,1},{13,5},{2,10},{6,14},... | collective-permute-start | bytes 1032200 | tf_op jit(solution)/shard_map/ppermute | solution.py:28
  24.1 0.7 and_select_fusion
  24.8 2.5 %collective-permute-done.1.refs_2_ = bf16[168,1024]{1,0:T(8,128)(2,1)S(1)} collective-permute-done((bf16[168,1024]{1,0:T(8,128)(2,1)}, bf16[168,1024]{1,0:T(8,128)(2,1)S(1)}, u32[]{:S(2)}, u32[]{:S(2)}) %collective-permute-start.1) | collective-permute-done | bytes 344096 | tf_op jit(solution)/shard_map/ppermute | solution.py:28
  27.2 1.6 collective-permute-done.2.refs_3_
  28.8 1.0 copy-done.2
  29.8 0.8 shard_map.110
  30.6 2.0 %collective-permute-start.3 = (bf16[672,1024]{1,0:T(8,128)(2,1)S(1)}, bf16[672,1024]{1,0:T(8,128)(2,1)S(1)}, u32[]{:S(2)}, u32[]{:S(2)}) collective-permute-start(bf16[672,1024]{1,0:T(8,128)(2,1)S(1)} %bitcast.41), channel_id=1, source_target_pairs={{0,4},{4,8},{8,12},{12,0},{1,5},{5,9},{9,13},{13,1},{2,6},{6,10},{... | collective-permute-start | bytes 4128776 | tf_op jit(solution)/shard_map/ppermute | solution.py:28
  32.7 0.6 collective-permute-done.6.refs_1_
  33.2 7.3 %collective-permute-done.8.refs_3_ = bf16[168,1024]{1,0:T(8,128)(2,1)} collective-permute-done((bf16[168,1024]{1,0:T(8,128)(2,1)S(1)}, bf16[168,1024]{1,0:T(8,128)(2,1)}, u32[]{:S(2)}, u32[]{:S(2)}) %collective-permute-start.8) | collective-permute-done | bytes 344096 | tf_op jit(solution)/shard_map/ppermute | solution.py:28
  40.6 3.3 %shard_map.111 = bf16[4,168,1024]{2,1,0:T(8,128)(2,1)} custom-call(s32[4]{0:T(128)S(1)} %get-tuple-element.66.slots, bf16[168,1024]{1,0:T(8,128)(2,1)S(1)} %collective-permute-done.5.refs_0_, bf16[168,1024]{1,0:T(8,128)(2,1)S(1)} %collective-permute-done.6.refs_1_, bf16[168,1024]{1,0:T(8,128)(2,1)} %collective-permute-done.7.refs_2_, ...), custom_call_target="tpu_custom_call" | custom-call | tf_op jit(solution)/shard_map/pallas_call | solution.py:50
  43.9 1.5 collective-permute-start.9
  45.4 1.7 collective-permute-start.10
  47.1 2.4 %collective-permute-start.11 = (bf16[168,512]{1,0:T(8,128)(2,1)}, bf16[168,512]{1,0:T(8,128)(2,1)S(1)}, u32[]{:S(2)}, u32[]{:S(2)}) collective-permute-start(bf16[168,512]{1,0:T(8,128)(2,1)} %bitcast.50), channel_id=1, source_target_pairs={{0,64},{2,0},{64,66},{66,2},{1,65},{3,1},{65,67},{67,3},{4,68},{6,... | collective-permute-start | bytes 516104 | tf_op jit(solution)/shard_map/ppermute | solution.py:345
  49.5 1.8 fusion.25
  51.3 5.1 %collective-permute-done.11 = bf16[168,512]{1,0:T(8,128)(2,1)S(1)} collective-permute-done((bf16[168,512]{1,0:T(8,128)(2,1)}, bf16[168,512]{1,0:T(8,128)(2,1)S(1)}, u32[]{:S(2)}, u32[]{:S(2)}) %collective-permute-start.11) | collective-permute-done | bytes 172064 | tf_op jit(solution)/shard_map/ppermute | solution.py:345
  56.4 3.5 %collective-permute-start.12 = (bf16[168,512]{1,0:T(8,128)(2,1)}, bf16[168,512]{1,0:T(8,128)(2,1)}, u32[]{:S(2)}, u32[]{:S(2)}) collective-permute-start(bf16[168,512]{1,0:T(8,128)(2,1)} %bitcast.51), channel_id=1, source_target_pairs={{64,2},{2,64},{65,3},{3,65},{68,6},{6,68},{69,7},{7,69},{72,10},{1... | collective-permute-start | bytes 516104 | tf_op jit(solution)/shard_map/ppermute | solution.py:346
  59.9 0.7 pad_add_fusion.side
  60.6 0.8 reshape.32
  61.4 1.4 reshape_reshape.3.far_gain
  62.9 0.7 reshape.33.near_gain
  63.6 0.7 stack.51.index
  64.3 1.3 pad_maximum_fusion.1
  65.6 9.2 %shard_map.112 = (bf16[4,512,672]{2,1,0:T(8,128)(2,1)}, bf16[4,512,672]{2,1,0:T(8,128)(2,1)}) custom-call(s32[2]{0:T(128)} %pad_add_fusion.side, bf16[2,2,1344,512]{3,2,1,0:T(8,128)(2,1)} %bitcast.47, bf16[2,2,1344,512]{3,2,1,0:T(8,128)(2,1)} %bitcast.48, f32[2,4,1,672]{3,2,1,0:T(1,128)} %reshape.33.near_gain, f32[2,4,1,672]{3,2,1,0:T(1,128)} %reshape_reshape.3.far_gain), custom_call_target="tpu_custom_call" | custom-call | tf_op jit(solution)/shard_map/pallas_call | solution.py:127
  74.9 1.2 broadcast_select_fusion.1
  76.1 0.8 pad_maximum_fusion
  76.9 1.9 shard_map.114
  78.7 0.6 collective-permute-start.13
  79.4 1.8 shard_map.115
  81.2 1.6 collective-permute-start.14
  82.8 1.9 shard_map.119
  84.7 0.5 collective-permute-start.16
  85.4 1.5 collective-permute-start.15
  86.8 6.0 %shard_map.113 = f32[512,512]{1,0:T(8,128)} custom-call(s32[6]{0:T(128)} %stack.51.index, bf16[4,512,672]{2,1,0:T(8,128)(2,1)} %get-tuple-element.38.near_ref, bf16[4,512,672]{2,1,0:T(8,128)(2,1)} %get-tuple-element.39.far_ref, bf16[672,1024]{1,0:T(8,128)(2,1)} %bitcast.43, bf16[672,1024]{1,0:T(8,128)(2,1)} %copy-done.1, ...), custom_call_target="tpu_custom_call" | custom-call | tf_op jit(solution)/shard_map/pallas_call | solution.py:169
  93.0 5.6 %collective-permute-done.14 = bf16[672,512]{1,0:T(8,128)(2,1)} collective-permute-done((bf16[672,512]{1,0:T(8,128)(2,1)}, bf16[672,512]{1,0:T(8,128)(2,1)}, u32[]{:S(2)}, u32[]{:S(2)}) %collective-permute-start.14) | collective-permute-done | bytes 688160 | tf_op jit(solution)/shard_map/ppermute | solution.py:28
  98.6 1.9 fusion.19
  100.6 1.9 add_add_fusion.1.raw_ref
  102.5 0.7 shard_map.116.k_ref.v_ref
  103.2 3.5 %collective-permute-start.17 = (bf16[512,512]{1,0:T(8,128)(2,1)S(1)}, bf16[512,512]{1,0:T(8,128)(2,1)S(1)}, u32[]{:S(2)}, u32[]{:S(2)}) collective-permute-start(bf16[512,512]{1,0:T(8,128)(2,1)S(1)} %shard_map.116.k_ref.v_ref), channel_id=1, source_target_pairs={{0,4},{4,8},{8,12},{12,16},{16,20},{20,24},{24,28},{28,32},{32,36}... | collective-permute-start | bytes 1572872 | tf_op jit(solution)/shard_map/ppermute | solution.py:33
  106.6 6.3 %collective-permute-start.18 = (bf16[512,512]{1,0:T(8,128)(2,1)S(1)}, bf16[512,512]{1,0:T(8,128)(2,1)S(1)}, u32[]{:S(2)}, u32[]{:S(2)}) collective-permute-start(bf16[512,512]{1,0:T(8,128)(2,1)S(1)} %shard_map.116.k_ref.v_ref), channel_id=1, source_target_pairs={{0,8},{4,12},{8,16},{12,20},{16,24},{20,28},{24,32},{28,36},{32,40... | collective-permute-start | bytes 1572872 | tf_op jit(solution)/shard_map/ppermute | solution.py:33
  112.9 6.1 %shard_map.117 = f32[512,512]{1,0:T(8,128)} custom-call(s32[6]{0:T(128)} %stack.51.index, bf16[4,512,672]{2,1,0:T(8,128)(2,1)} %get-tuple-element.38.near_ref, bf16[4,512,672]{2,1,0:T(8,128)(2,1)} %get-tuple-element.39.far_ref, bf16[672,1024]{1,0:T(8,128)(2,1)} %bitcast.44, bf16[672,1024]{1,0:T(8,128)(2,1)} %copy-done.1, ...), custom_call_target="tpu_custom_call" | custom-call | tf_op jit(solution)/shard_map/pallas_call | solution.py:169
  119.0 2.0 %fusion.11 = f32[512,512]{1,0:T(8,128)S(1)} fusion(bf16[672,512]{1,0:T(8,128)(2,1)} %collective-permute-done.16, bf16[4,512,672]{2,1,0:T(8,128)(2,1)} %get-tuple-element.39.far_ref, s32[]{:T(128)S(6)} %select_n.79), kind=kOutput, calls=%fused_computation.14 | convolution fusion | flops 352321536 | bytes 2523140 | tf_op jit(solution)/shard_map/dot_general | solution.py:193
  121.0 1.7 fusion.17
  122.7 0.4 add_add_fusion.raw_ref
  123.1 1.2 shard_map.120.q_ref
  124.4 2.1 %shard_map.121 = (f32[512,512]{1,0:T(8,128)S(1)}, f32[512,512]{1,0:T(8,128)S(1)}) custom-call(bf16[512,512]{1,0:T(8,128)(2,1)S(1)} %shard_map.120.q_ref, bf16[512,512]{1,0:T(8,128)(2,1)S(1)} %shard_map.116.k_ref.v_ref, bf16[512,512]{1,0:T(8,128)(2,1)S(1)} %shard_map.116.k_ref.v_ref), custom_call_target="tpu_custom_call" | custom-call | tf_op jit(solution)/shard_map/pallas_call | solution.py:288
  126.4 4.6 %collective-permute-done.17.k1_ref.v1_ref = bf16[512,512]{1,0:T(8,128)(2,1)S(1)} collective-permute-done((bf16[512,512]{1,0:T(8,128)(2,1)S(1)}, bf16[512,512]{1,0:T(8,128)(2,1)S(1)}, u32[]{:S(2)}, u32[]{:S(2)}) %collective-permute-start.17) | collective-permute-done | bytes 524320 | tf_op jit(solution)/shard_map/ppermute | solution.py:33
  131.0 21.5 %collective-permute-done.18.k2_ref.v2_ref = bf16[512,512]{1,0:T(8,128)(2,1)S(1)} collective-permute-done((bf16[512,512]{1,0:T(8,128)(2,1)S(1)}, bf16[512,512]{1,0:T(8,128)(2,1)S(1)}, u32[]{:S(2)}, u32[]{:S(2)}) %collective-permute-start.18) | collective-permute-done | bytes 524320 | tf_op jit(solution)/shard_map/ppermute | solution.py:33
  152.5 3.5 %shard_map.122 = bf16[512,512]{1,0:T(8,128)(2,1)S(1)} custom-call(s32[2]{0:T(128)S(1)} %add_convert_fusion.2.valid, bf16[512,512]{1,0:T(8,128)(2,1)S(1)} %shard_map.120.q_ref, bf16[512,512]{1,0:T(8,128)(2,1)S(1)} %collective-permute-done.17.k1_ref.v1_ref, bf16[512,512]{1,0:T(8,128)(2,1)S(1)} %collective-permute-done.17.k1_ref.v1_ref, ...), custom_call_target="tpu_custom_call" | custom-call | tf_op jit(solution)/shard_map/pallas_call | solution.py:309
  156.0 0.8 collective-permute-start.19
  156.8 3.4 %fusion.1 = f32[2688,512]{1,0:T(8,128)S(1)} fusion(bf16[512,512]{1,0:T(8,128)(2,1)S(1)} %shard_map.122, bf16[2688,1024]{1,0:T(8,128)(2,1)} %all-gather.4.cloned.1.call-done), kind=kOutput, calls=%fused_computation.6 | convolution fusion | flops 1409286144 | bytes 8781824 | tf_op jit(solution)/shard_map/dot_general | solution.py:387
  160.2 6.6 %collective-permute-done.19 = bf16[512,512]{1,0:T(8,128)(2,1)S(1)} collective-permute-done((bf16[512,512]{1,0:T(8,128)(2,1)S(1)}, bf16[512,512]{1,0:T(8,128)(2,1)S(1)}, u32[]{:S(2)}, u32[]{:S(2)}) %collective-permute-start.19) | collective-permute-done | bytes 524320 | tf_op jit(solution)/shard_map/ppermute | solution.py:28
  166.8 3.4 %add_convert_fusion = bf16[1344,512]{1,0:T(8,128)(2,1)} fusion(f32[2688,512]{1,0:T(8,128)S(1)} %fusion.1, s32[]{:T(128)S(6)} %select_n.84, bf16[512,512]{1,0:T(8,128)(2,1)S(1)} %collective-permute-done.19, bf16[2688,1024]{1,0:T(8,128)(2,1)} %all-gather.4.cloned.1.call-done), kind=kOutput, calls=%fused_computation.4 | convolution fusion | flops 706019328 | bytes 6030336 | tf_op jit(solution)/shard_map/dot_general | solution.py:387
  170.1 3.1 %dynamic-slice_add_fusion = f32[1344,512]{1,0:T(8,128)S(1)} fusion(f32[2688,512]{1,0:T(8,128)} %copy-done.5, s32[]{:T(128)S(6)} %select_n.83, bf16[512,512]{1,0:T(8,128)(2,1)S(1)} %collective-permute-done.19, bf16[2688,1024]{1,0:T(8,128)(2,1)} %all-gather.4.cloned.1.call-done), kind=kOutput, calls=%fused_computation.5 | convolution fusion | flops 705331200 | bytes 7406592 | tf_op jit(solution)/shard_map/dot_general | solution.py:387
  173.6 1.8 multiply_reduce_fusion
  175.4 7.6 %psum.7 = f32[512]{0:T(512)S(1)} all-reduce(f32[512]{0:T(512)S(1)} %multiply_reduce_fusion), channel_id=1, replica_groups=mesh['yl'=2,'x'=4,'z'=4,'yh'=2,'c'=2] {'yh','c'}, use_global_device_ids=true, to_apply=%region_1.2 | all-reduce | flops 512 | bytes 4096 | tf_op jit(solution)/shard_map/psum | solution.py:402
  183.0 3.4 %fusion = bf16[512,1344]{0,1:T(8,128)(2,1)} fusion(bf16[512,1344]{0,1:T(8,128)(2,1)} %param.11, f32[1344,512]{1,0:T(8,128)S(1)} %dynamic-slice_add_fusion, bf16[1344,512]{1,0:T(8,128)(2,1)} %collective-permute-done.20, f32[1344]{0:T(1024)S(1)} %copy-done.11, f32[512]{0:T(512)S(1)} %add_rsqrt_fusion), kind=kLoop, calls=%fused_computation.1 | loop fusion | flops 4816896 | bytes 6888704 | tf_op jit(solution)/shard_map/convert_element_type | solution.py:404
  (48 shorter events, 1.2 us)
Async XLA Ops:
  6.5 59.1 %all-gather.6.cloned.1.call-start = ((), (), s32[]{:S(2)}) async-start(), calls=%async_computation.1 | async-start | bytes 6881280 | tf_op jit(solution)/shard_map/all_gather | solution.py:330
  7.3 149.5 %all-gather.4.cloned.1.call-start = ((), (), s32[]{:S(2)}) async-start(), calls=%async_computation | async-start | bytes 5849088 | tf_op jit(solution)/shard_map/all_gather | solution.py:369
  9.1 10.0 %collective-permute-start.5 = (bf16[168,1024]{1,0:T(8,128)(2,1)}, bf16[168,1024]{1,0:T(8,128)(2,1)S(1)}, u32[]{:S(2)}, u32[]{:S(2)}) collective-permute-start(bf16[168,1024]{1,0:T(8,128)(2,1)} %shard_map.109.refs_0_), channel_id=1, source_target_pairs={{0,64},{64,0},{1,65},{65,1},{2,66},{66,2},{3,67},{67,3},{4,68},{68... | collective-permute-start | bytes 1032200 | tf_op jit(solution)/shard_map/ppermute | solution.py:28
  9.5 11.6 %collective-permute-start = (bf16[168,1024]{1,0:T(8,128)(2,1)}, bf16[168,1024]{1,0:T(8,128)(2,1)S(1)}, u32[]{:S(2)}, u32[]{:S(2)}) collective-permute-start(bf16[168,1024]{1,0:T(8,128)(2,1)} %shard_map.109.refs_0_), channel_id=1, source_target_pairs={{0,16},{16,32},{32,48},{48,0},{1,17},{17,33},{33,49},{49,1},{2,18}... | collective-permute-start | bytes 1032200 | tf_op jit(solution)/shard_map/ppermute | solution.py:28
  11.0 16.2 %collective-permute-start.1 = (bf16[168,1024]{1,0:T(8,128)(2,1)}, bf16[168,1024]{1,0:T(8,128)(2,1)S(1)}, u32[]{:S(2)}, u32[]{:S(2)}) collective-permute-start(bf16[168,1024]{1,0:T(8,128)(2,1)} %shard_map.109.refs_0_), channel_id=1, source_target_pairs={{0,48},{16,0},{32,16},{48,32},{1,49},{17,1},{33,17},{49,33},{2,50}... | collective-permute-start | bytes 1032200 | tf_op jit(solution)/shard_map/ppermute | solution.py:28
  12.8 16.1 %collective-permute-start.2 = (bf16[168,1024]{1,0:T(8,128)(2,1)}, bf16[168,1024]{1,0:T(8,128)(2,1)S(1)}, u32[]{:S(2)}, u32[]{:S(2)}) collective-permute-start(bf16[168,1024]{1,0:T(8,128)(2,1)} %shard_map.109.refs_0_), channel_id=1, source_target_pairs={{0,32},{16,48},{32,0},{48,16},{1,33},{17,49},{33,1},{49,17},{2,34}... | collective-permute-start | bytes 1032200 | tf_op jit(solution)/shard_map/ppermute | solution.py:28
  19.1 14.1 %collective-permute-start.6 = (bf16[168,1024]{1,0:T(8,128)(2,1)S(1)}, bf16[168,1024]{1,0:T(8,128)(2,1)S(1)}, u32[]{:S(2)}, u32[]{:S(2)}) collective-permute-start(bf16[168,1024]{1,0:T(8,128)(2,1)S(1)} %collective-permute-done.5.refs_0_), channel_id=1, source_target_pairs={{0,4},{4,8},{8,12},{12,0},{1,5},{5,9},{9,13},{13,1},{2,6},{6,10},{... | collective-permute-start | bytes 1032200 | tf_op jit(solution)/shard_map/ppermute | solution.py:28
  21.0 12.2 %collective-permute-start.7 = (bf16[168,1024]{1,0:T(8,128)(2,1)S(1)}, bf16[168,1024]{1,0:T(8,128)(2,1)}, u32[]{:S(2)}, u32[]{:S(2)}) collective-permute-start(bf16[168,1024]{1,0:T(8,128)(2,1)S(1)} %collective-permute-done.5.refs_0_), channel_id=1, source_target_pairs={{0,12},{4,0},{8,4},{12,8},{1,13},{5,1},{9,5},{13,9},{2,14},{6,2},{... | collective-permute-start | bytes 1032200 | tf_op jit(solution)/shard_map/ppermute | solution.py:28
  21.1 19.5 %collective-permute-start.8 = (bf16[168,1024]{1,0:T(8,128)(2,1)S(1)}, bf16[168,1024]{1,0:T(8,128)(2,1)}, u32[]{:S(2)}, u32[]{:S(2)}) collective-permute-start(bf16[168,1024]{1,0:T(8,128)(2,1)S(1)} %collective-permute-done.5.refs_0_), channel_id=1, source_target_pairs={{0,8},{4,12},{8,0},{12,4},{1,9},{5,13},{9,1},{13,5},{2,10},{6,14},... | collective-permute-start | bytes 1032200 | tf_op jit(solution)/shard_map/ppermute | solution.py:28
  28.8 1.0 copy-start.2
  30.6 44.3 %copy-start = (bf16[4,168,1024]{2,1,0:T(8,128)(2,1)}, bf16[4,168,1024]{2,1,0:T(8,128)(2,1)S(1)}, u32[]{:S(2)}) copy-start(bf16[4,168,1024]{2,1,0:T(8,128)(2,1)S(1)} %shard_map.110) | copy-start | bytes 4128772
  30.6 44.3 %collective-permute-start.3 = (bf16[672,1024]{1,0:T(8,128)(2,1)S(1)}, bf16[672,1024]{1,0:T(8,128)(2,1)S(1)}, u32[]{:S(2)}, u32[]{:S(2)}) collective-permute-start(bf16[672,1024]{1,0:T(8,128)(2,1)S(1)} %bitcast.41), channel_id=1, source_target_pairs={{0,4},{4,8},{8,12},{12,0},{1,5},{5,9},{9,13},{13,1},{2,6},{6,10},{... | collective-permute-start | bytes 4128776 | tf_op jit(solution)/shard_map/ppermute | solution.py:28
  32.6 42.3 %collective-permute-start.4 = (bf16[672,1024]{1,0:T(8,128)(2,1)S(1)}, bf16[672,1024]{1,0:T(8,128)(2,1)}, u32[]{:S(2)}, u32[]{:S(2)}) collective-permute-start(bf16[672,1024]{1,0:T(8,128)(2,1)S(1)} %bitcast.42), channel_id=1, source_target_pairs={{0,12},{4,0},{8,4},{12,8},{1,13},{5,1},{9,5},{13,9},{2,14},{6,2},{... | collective-permute-start | bytes 4128776 | tf_op jit(solution)/shard_map/ppermute | solution.py:28
  43.9 31.0 %collective-permute-start.9 = (bf16[672,1024]{1,0:T(8,128)(2,1)}, bf16[672,1024]{1,0:T(8,128)(2,1)}, u32[]{:S(2)}, u32[]{:S(2)}) collective-permute-start(bf16[672,1024]{1,0:T(8,128)(2,1)} %bitcast.4.refs_3_), channel_id=1, source_target_pairs={{0,16},{16,32},{32,48},{48,0},{1,17},{17,33},{33,49},{49,1},{2,18}... | collective-permute-start | bytes 4128776 | tf_op jit(solution)/shard_map/ppermute | solution.py:28
  45.4 29.5 %collective-permute-start.10 = (bf16[672,1024]{1,0:T(8,128)(2,1)}, bf16[672,1024]{1,0:T(8,128)(2,1)}, u32[]{:S(2)}, u32[]{:S(2)}) collective-permute-start(bf16[672,1024]{1,0:T(8,128)(2,1)} %bitcast.4.refs_3_), channel_id=1, source_target_pairs={{0,48},{16,0},{32,16},{48,32},{1,49},{17,1},{33,17},{49,33},{2,50}... | collective-permute-start | bytes 4128776 | tf_op jit(solution)/shard_map/ppermute | solution.py:28
  47.1 9.2 %collective-permute-start.11 = (bf16[168,512]{1,0:T(8,128)(2,1)}, bf16[168,512]{1,0:T(8,128)(2,1)S(1)}, u32[]{:S(2)}, u32[]{:S(2)}) collective-permute-start(bf16[168,512]{1,0:T(8,128)(2,1)} %bitcast.50), channel_id=1, source_target_pairs={{0,64},{2,0},{64,66},{66,2},{1,65},{3,1},{65,67},{67,3},{4,68},{6,... | collective-permute-start | bytes 516104 | tf_op jit(solution)/shard_map/ppermute | solution.py:345
  56.4 7.9 %copy-start.9 = (bf16[168,512]{1,0:T(8,128)(2,1)}, bf16[168,512]{1,0:T(8,128)(2,1)S(1)}, u32[]{:S(2)}) copy-start(bf16[168,512]{1,0:T(8,128)(2,1)S(1)} %collective-permute-done.11) | copy-start | bytes 516100
  56.4 18.5 %collective-permute-start.12 = (bf16[168,512]{1,0:T(8,128)(2,1)}, bf16[168,512]{1,0:T(8,128)(2,1)}, u32[]{:S(2)}, u32[]{:S(2)}) collective-permute-start(bf16[168,512]{1,0:T(8,128)(2,1)} %bitcast.51), channel_id=1, source_target_pairs={{64,2},{2,64},{65,3},{3,65},{68,6},{6,68},{69,7},{7,69},{72,10},{1... | collective-permute-start | bytes 516104 | tf_op jit(solution)/shard_map/ppermute | solution.py:346
  65.6 9.3 %copy-start.8 = (bf16[512,168]{0,1:T(8,128)(2,1)S(1)}, bf16[512,168]{0,1:T(8,128)(2,1)}, u32[]{:S(2)}) copy-start(bf16[512,168]{0,1:T(8,128)(2,1)} %param.15) | copy-start | bytes 516100
  65.6 9.3 %copy-start.10 = (bf16[168,512]{1,0:T(8,128)(2,1)S(1)}, bf16[168,512]{1,0:T(8,128)(2,1)}, u32[]{:S(2)}) copy-start(bf16[168,512]{1,0:T(8,128)(2,1)} %copy-done.9) | copy-start | bytes 516100
  74.9 10.3 %copy-start.1 = (bf16[672,1024]{1,0:T(8,128)(2,1)}, bf16[672,1024]{1,0:T(8,128)(2,1)S(1)}, u32[]{:S(2)}) copy-start(bf16[672,1024]{1,0:T(8,128)(2,1)S(1)} %collective-permute-done.3.refs_1_.value_ref) | copy-start | bytes 4128772
  78.7 14.3 %collective-permute-start.13 = (bf16[672,512]{1,0:T(8,128)(2,1)}, bf16[672,512]{1,0:T(8,128)(2,1)}, u32[]{:S(2)}, u32[]{:S(2)}) collective-permute-start(bf16[672,512]{1,0:T(8,128)(2,1)} %shard_map.114), channel_id=1, source_target_pairs={{0,12},{4,0},{8,4},{12,8},{1,13},{5,1},{9,5},{13,9},{2,14},{6,2},{... | collective-permute-start | bytes 2064392 | tf_op jit(solution)/shard_map/ppermute | solution.py:28
  81.2 17.4 %collective-permute-start.14 = (bf16[672,512]{1,0:T(8,128)(2,1)}, bf16[672,512]{1,0:T(8,128)(2,1)}, u32[]{:S(2)}, u32[]{:S(2)}) collective-permute-start(bf16[672,512]{1,0:T(8,128)(2,1)} %shard_map.115), channel_id=1, source_target_pairs={{0,48},{16,0},{32,16},{48,32},{1,49},{17,1},{33,17},{49,33},{2,50}... | collective-permute-start | bytes 2064392 | tf_op jit(solution)/shard_map/ppermute | solution.py:28
  84.7 34.3 %collective-permute-start.16 = (bf16[672,512]{1,0:T(8,128)(2,1)}, bf16[672,512]{1,0:T(8,128)(2,1)}, u32[]{:S(2)}, u32[]{:S(2)}) collective-permute-start(bf16[672,512]{1,0:T(8,128)(2,1)} %shard_map.119), channel_id=1, source_target_pairs={{0,16},{16,32},{32,48},{48,0},{1,17},{17,33},{33,49},{49,1},{2,18}... | collective-permute-start | bytes 2064392 | tf_op jit(solution)/shard_map/ppermute | solution.py:28
  85.4 35.6 %collective-permute-start.15 = (bf16[672,512]{1,0:T(8,128)(2,1)S(1)}, bf16[672,512]{1,0:T(8,128)(2,1)S(1)}, u32[]{:S(2)}, u32[]{:S(2)}) collective-permute-start(bf16[672,512]{1,0:T(8,128)(2,1)S(1)} %shard_map.118), channel_id=1, source_target_pairs={{0,4},{4,8},{8,12},{12,0},{1,5},{5,9},{9,13},{13,1},{2,6},{6,10},{... | collective-permute-start | bytes 2064392 | tf_op jit(solution)/shard_map/ppermute | solution.py:28
  92.8 7.7 %copy-start.6 = (f32[512,512]{1,0:T(8,128)S(1)}, f32[512,512]{1,0:T(8,128)}, u32[]{:S(2)}) copy-start(f32[512,512]{1,0:T(8,128)} %shard_map.113) | copy-start | bytes 3145732
  100.5 1.9 %copy-start.3 = (f32[128]{0:T(128)S(1)}, f32[128]{0:T(128)}, u32[]{:S(2)}) copy-start(f32[128]{0:T(128)} %param.19) | copy-start | bytes 1540
  103.2 27.8 %collective-permute-start.17 = (bf16[512,512]{1,0:T(8,128)(2,1)S(1)}, bf16[512,512]{1,0:T(8,128)(2,1)S(1)}, u32[]{:S(2)}, u32[]{:S(2)}) collective-permute-start(bf16[512,512]{1,0:T(8,128)(2,1)S(1)} %shard_map.116.k_ref.v_ref), channel_id=1, source_target_pairs={{0,4},{4,8},{8,12},{12,16},{16,20},{20,24},{24,28},{28,32},{32,36}... | collective-permute-start | bytes 1572872 | tf_op jit(solution)/shard_map/ppermute | solution.py:33
  106.6 45.9 %collective-permute-start.18 = (bf16[512,512]{1,0:T(8,128)(2,1)S(1)}, bf16[512,512]{1,0:T(8,128)(2,1)S(1)}, u32[]{:S(2)}, u32[]{:S(2)}) collective-permute-start(bf16[512,512]{1,0:T(8,128)(2,1)S(1)} %shard_map.116.k_ref.v_ref), channel_id=1, source_target_pairs={{0,8},{4,12},{8,16},{12,20},{16,24},{20,28},{24,32},{28,36},{32,40... | collective-permute-start | bytes 1572872 | tf_op jit(solution)/shard_map/ppermute | solution.py:33
  118.9 3.8 %copy-start.7 = (f32[512,512]{1,0:T(8,128)S(1)}, f32[512,512]{1,0:T(8,128)}, u32[]{:S(2)}) copy-start(f32[512,512]{1,0:T(8,128)} %shard_map.117) | copy-start | bytes 3145732
  121.0 2.1 %copy-start.4 = (f32[128]{0:T(128)S(1)}, f32[128]{0:T(128)}, u32[]{:S(2)}) copy-start(f32[128]{0:T(128)} %param.18) | copy-start | bytes 1540
  156.0 10.8 %collective-permute-start.19 = (bf16[512,512]{1,0:T(8,128)(2,1)S(1)}, bf16[512,512]{1,0:T(8,128)(2,1)S(1)}, u32[]{:S(2)}, u32[]{:S(2)}) collective-permute-start(bf16[512,512]{1,0:T(8,128)(2,1)S(1)} %shard_map.122), channel_id=1, source_target_pairs={{0,2},{2,0},{1,3},{3,1},{4,6},{6,4},{5,7},{7,5},{8,10},{10,8},{9,1... | collective-permute-start | bytes 1572872 | tf_op jit(solution)/shard_map/ppermute | solution.py:28
  160.2 9.9 %copy-start.5 = (f32[2688,512]{1,0:T(8,128)}, f32[2688,512]{1,0:T(8,128)S(1)}, u32[]{:S(2)}) copy-start(f32[2688,512]{1,0:T(8,128)S(1)} %fusion.1) | copy-start | bytes 16515076
  170.1 3.5 %collective-permute-start.20 = (bf16[1344,512]{1,0:T(8,128)(2,1)}, bf16[1344,512]{1,0:T(8,128)(2,1)}, u32[]{:S(2)}, u32[]{:S(2)}) collective-permute-start(bf16[1344,512]{1,0:T(8,128)(2,1)} %add_convert_fusion), channel_id=1, source_target_pairs={{0,1},{1,0},{2,3},{3,2},{4,5},{5,4},{6,7},{7,6},{8,9},{9,8},{10,11... | collective-permute-start | bytes 4128776 | tf_op jit(solution)/shard_map/ppermute | solution.py:28
  173.2 9.8 %copy-start.11 = (f32[1344]{0:T(1024)S(1)}, f32[1344]{0:T(1024)}, u32[]{:S(2)}) copy-start(f32[1344]{0:T(1024)} %param.17) | copy-start | bytes 16132
Sparse Core Ops, SparseCore 0:
  9.0 50.7 all-gather.5
  77.0 73.6 all-gather.3

commit v6 on v5

--- a/solution.py
+++ b/solution.py
@@ -115,7 +115,7 @@
 
 def norm_parts(pieces, gain, side):
     width, rows = pieces.shape[1:]
-    step = 128
+    step = 256
     pieces = pieces.reshape(2, 2, width, rows)
     far_gain = gain.reshape(2, 4, 4, SHARD)
     near_gain = jnp.swapaxes(far_gain, 1, 2).reshape(2, 4, 1, 4 * SHARD)
@@ -388,13 +388,11 @@
         weight, value, (((1,), (1,)), ((), ())), preferred_element_type=jnp.float32
     )
     out_all, context = lax.optimization_barrier((out_all, context))
-    before = summed(out_all[:, :q_cols], context)
-    across, before = lax.optimization_barrier((across, before))
+    both = jnp.concatenate([context, across], axis=1)
     columns = out_all.shape[0] // 2
 
     def half_of(core):
-        weight = lax.dynamic_slice(out_all, (core * columns, q_cols), (columns, q_cols))
-        return lax.dynamic_slice_in_dim(before, core * columns, columns, 0) + summed(weight, across)
+        return summed(lax.dynamic_slice_in_dim(out_all, core * columns, columns, 0), both)
 
     received = shift(half_of(1 - c).astype(jnp.bfloat16), "c", 1)
     kept, received = lax.optimization_barrier((half_of(c), received))

time: 195 us -> 185 us (0.949)
  starting transfers between devices: 36.4 us -> 32.9 us
  Pallas kernels: 40.2 us -> 37 us
  waiting for transfers between devices: 61.1 us -> 59.1 us
    all_gather x1, waiting for transfers between devices: 0.01 us -> 18.9 us  [local(): out_all = lax.all_gather(pair, ('x', 'z'), axis=0, tiled=True)]
    ppermute x2, waiting for transfers between devices: 26.1 us -> 9.23 us  [from_behind(): lax.ppermute(value, SEQ, [(source, source + steps) for source in range(co...]
    ppermute x17, waiting for transfers between devices: 29.2 us -> 25 us  [shift(): lax.ppermute(value, axis, [(i, (i + step) % count) for i in range(count)])]
    ppermute x2, starting transfers between devices: 9.71 us -> 7.19 us  [from_behind(): lax.ppermute(value, SEQ, [(source, source + steps) for source in range(co...]
    pallas_call x4, Pallas kernels: 5.71 us -> 3.57 us  [cut(): pl.pallas_call(cut_kernel, grid=(2,), in_specs=[pl.BlockSpec((step, colum...]
    dot_general x3 -> x2, matrix products: 9.86 us -> 7.89 us  [local(): lax.dot_general(weight, value, (((1,), (1,)), ((), ())), preferred_elemen...]
  transfers between devices with their start and end apart: 23 -> 23, of which waited for: 12 -> 11; matrix products, arithmetic and copies ran while one was open for 12% -> 11% of each run, Pallas kernels for 21% -> 20%
where the time goes in v6:
time: 185 us; the launch traced here: 183 us
  waiting for transfers between devices  59.1 us (32%)
  Pallas kernels  37 us (20%)
  starting transfers between devices  32.9 us (18%)
  matrix products  15.6 us (8%)
  between operations  13.8 us (7%)
  other arithmetic  10.5 us (6%)
  blocking collectives  7.6 us (4%)
  local copies, waits for them, and re-layouts  6.33 us (3%)
    ppermute x17, waiting for transfers between devices, shift(): lax.ppermute(value, axis, [(i, (i + step) % count) for i in range(count)])  25 us
    ppermute x17, starting transfers between devices, shift(): lax.ppermute(value, axis, [(i, (i + step) % count) for i in range(count)])  19.8 us
    all_gather x1, waiting for transfers between devices, local(): out_all = lax.all_gather(pair, ('x', 'z'), axis=0, tiled=True)  18.9 us
    pallas_call x2, Pallas kernels, early_product(): pl.pallas_call(functools.partial(early_kernel, len(near_weights), count,...  12 us
    ppermute x2, waiting for transfers between devices, from_behind(): lax.ppermute(value, SEQ, [(source, source + steps) for source in range(co...  9.23 us
    pallas_call x1, Pallas kernels, norm_parts(): pl.pallas_call(norm_kernel, grid_spec=pltpu.PrefetchScalarGridSpec(num_sc...  8.12 us
    dot_general x2, matrix products, local(): lax.dot_general(weight, value, (((1,), (1,)), ((), ())), preferred_elemen...  7.89 us
    dot_general x4, matrix products, product(): return jnp.dot(left, right, preferred_element_type=jnp.float32)  7.72 us
  transfers between devices with their start and end apart: 23, of which 11 were waited for; matrix products, arithmetic and copies ran while one was open for 11% of the time, Pallas kernels for 20%

profile of v6, /device:TPU:40, one launch (start us, length us, event | category | flops | bytes accessed | tf_op | source)
XLA Modules:
  0.0 182.8 jit_solution(5070711208308491887)
XLA Ops:
  6.5 0.7 all-gather.6.cloned.1.call-update
  7.3 1.8 shard_map.109.refs_0_
  9.1 0.4 collective-permute-start.5
  9.5 1.5 collective-permute-start
  11.0 1.7 collective-permute-start.1
  12.8 1.8 collective-permute-start.2
  14.6 4.5 %collective-permute-done.5.refs_0_ = bf16[168,1024]{1,0:T(8,128)(2,1)S(1)} collective-permute-done((bf16[168,1024]{1,0:T(8,128)(2,1)}, bf16[168,1024]{1,0:T(8,128)(2,1)S(1)}, u32[]{:S(2)}, u32[]{:S(2)}) %collective-permute-start.5) | collective-permute-done | bytes 344096 | tf_op jit(solution)/shard_map/ppermute | solution.py:28
  19.1 1.9 %collective-permute-start.6 = (bf16[168,1024]{1,0:T(8,128)(2,1)S(1)}, bf16[168,1024]{1,0:T(8,128)(2,1)S(1)}, u32[]{:S(2)}, u32[]{:S(2)}) collective-permute-start(bf16[168,1024]{1,0:T(8,128)(2,1)S(1)} %collective-permute-done.5.refs_0_), channel_id=1, source_target_pairs={{0,4},{4,8},{8,12},{12,0},{1,5},{5,9},{9,13},{13,1},{2,6},{6,10},{... | collective-permute-start | bytes 1032200 | tf_op jit(solution)/shard_map/ppermute | solution.py:28
  21.1 3.0 %collective-permute-start.8 = (bf16[168,1024]{1,0:T(8,128)(2,1)S(1)}, bf16[168,1024]{1,0:T(8,128)(2,1)}, u32[]{:S(2)}, u32[]{:S(2)}) collective-permute-start(bf16[168,1024]{1,0:T(8,128)(2,1)S(1)} %collective-permute-done.5.refs_0_), channel_id=1, source_target_pairs={{0,8},{4,12},{8,0},{12,4},{1,9},{5,13},{9,1},{13,5},{2,10},{6,14},... | collective-permute-start | bytes 1032200 | tf_op jit(solution)/shard_map/ppermute | solution.py:28
  24.1 0.7 and_select_fusion
  24.8 2.5 %collective-permute-done.1.refs_2_ = bf16[168,1024]{1,0:T(8,128)(2,1)S(1)} collective-permute-done((bf16[168,1024]{1,0:T(8,128)(2,1)}, bf16[168,1024]{1,0:T(8,128)(2,1)S(1)}, u32[]{:S(2)}, u32[]{:S(2)}) %collective-permute-start.1) | collective-permute-done | bytes 344096 | tf_op jit(solution)/shard_map/ppermute | solution.py:28
  27.2 1.6 collective-permute-done.2.refs_3_
  28.8 1.0 copy-done.2
  29.8 0.8 shard_map.110
  30.6 2.0 %collective-permute-start.3 = (bf16[672,1024]{1,0:T(8,128)(2,1)S(1)}, bf16[672,1024]{1,0:T(8,128)(2,1)S(1)}, u32[]{:S(2)}, u32[]{:S(2)}) collective-permute-start(bf16[672,1024]{1,0:T(8,128)(2,1)S(1)} %bitcast.40), channel_id=1, source_target_pairs={{0,4},{4,8},{8,12},{12,0},{1,5},{5,9},{9,13},{13,1},{2,6},{6,10},{... | collective-permute-start | bytes 4128776 | tf_op jit(solution)/shard_map/ppermute | solution.py:28
  32.7 0.6 collective-permute-done.6.refs_1_
  33.2 7.3 %collective-permute-done.8.refs_3_ = bf16[168,1024]{1,0:T(8,128)(2,1)} collective-permute-done((bf16[168,1024]{1,0:T(8,128)(2,1)S(1)}, bf16[168,1024]{1,0:T(8,128)(2,1)}, u32[]{:S(2)}, u32[]{:S(2)}) %collective-permute-start.8) | collective-permute-done | bytes 344096 | tf_op jit(solution)/shard_map/ppermute | solution.py:28
  40.6 3.3 %shard_map.111 = bf16[4,168,1024]{2,1,0:T(8,128)(2,1)} custom-call(s32[4]{0:T(128)S(1)} %get-tuple-element.62.slots, bf16[168,1024]{1,0:T(8,128)(2,1)S(1)} %collective-permute-done.5.refs_0_, bf16[168,1024]{1,0:T(8,128)(2,1)S(1)} %collective-permute-done.6.refs_1_, bf16[168,1024]{1,0:T(8,128)(2,1)} %collective-permute-done.7.refs_2_, ...), custom_call_target="tpu_custom_call" | custom-call | tf_op jit(solution)/shard_map/pallas_call | solution.py:50
  43.9 2.8 %collective-permute-start.10 = (bf16[672,1024]{1,0:T(8,128)(2,1)}, bf16[672,1024]{1,0:T(8,128)(2,1)}, u32[]{:S(2)}, u32[]{:S(2)}) collective-permute-start(bf16[672,1024]{1,0:T(8,128)(2,1)} %bitcast.2.refs_3_), channel_id=1, source_target_pairs={{0,48},{16,0},{32,16},{48,32},{1,49},{17,1},{33,17},{49,33},{2,50}... | collective-permute-start | bytes 4128776 | tf_op jit(solution)/shard_map/ppermute | solution.py:28
  46.7 2.4 %collective-permute-start.11 = (bf16[168,512]{1,0:T(8,128)(2,1)}, bf16[168,512]{1,0:T(8,128)(2,1)S(1)}, u32[]{:S(2)}, u32[]{:S(2)}) collective-permute-start(bf16[168,512]{1,0:T(8,128)(2,1)} %bitcast.49), channel_id=1, source_target_pairs={{0,64},{2,0},{64,66},{66,2},{1,65},{3,1},{65,67},{67,3},{4,68},{6,... | collective-permute-start | bytes 516104 | tf_op jit(solution)/shard_map/ppermute | solution.py:345
  49.0 1.8 fusion.18
  50.8 5.2 %collective-permute-done.11 = bf16[168,512]{1,0:T(8,128)(2,1)S(1)} collective-permute-done((bf16[168,512]{1,0:T(8,128)(2,1)}, bf16[168,512]{1,0:T(8,128)(2,1)S(1)}, u32[]{:S(2)}, u32[]{:S(2)}) %collective-permute-start.11) | collective-permute-done | bytes 172064 | tf_op jit(solution)/shard_map/ppermute | solution.py:345
  56.0 3.5 %collective-permute-start.12 = (bf16[168,512]{1,0:T(8,128)(2,1)}, bf16[168,512]{1,0:T(8,128)(2,1)}, u32[]{:S(2)}, u32[]{:S(2)}) collective-permute-start(bf16[168,512]{1,0:T(8,128)(2,1)} %bitcast.50), channel_id=1, source_target_pairs={{64,2},{2,64},{65,3},{3,65},{68,6},{6,68},{69,7},{7,69},{72,10},{1... | collective-permute-start | bytes 516104 | tf_op jit(solution)/shard_map/ppermute | solution.py:346
  59.5 0.6 pad_add_fusion.side
  60.1 0.8 reshape.32
  60.9 1.4 reshape_reshape.3.far_gain
  62.4 0.7 reshape.33.near_gain
  63.1 0.7 stack.48.index
  63.8 1.3 pad_maximum_fusion.1
  65.2 8.1 %shard_map.112 = (bf16[4,512,672]{2,1,0:T(8,128)(2,1)}, bf16[4,512,672]{2,1,0:T(8,128)(2,1)}) custom-call(s32[2]{0:T(128)} %pad_add_fusion.side, bf16[2,2,1344,512]{3,2,1,0:T(8,128)(2,1)} %bitcast.46, bf16[2,2,1344,512]{3,2,1,0:T(8,128)(2,1)} %bitcast.47, f32[2,4,1,672]{3,2,1,0:T(1,128)} %reshape.33.near_gain, f32[2,4,1,672]{3,2,1,0:T(1,128)} %reshape_reshape.3.far_gain), custom_call_target="tpu_custom_call" | custom-call | tf_op jit(solution)/shard_map/pallas_call | solution.py:127
  73.3 2.1 %collective-permute-done.9.refs_4_.value_ref = bf16[672,1024]{1,0:T(8,128)(2,1)} collective-permute-done((bf16[672,1024]{1,0:T(8,128)(2,1)}, bf16[672,1024]{1,0:T(8,128)(2,1)}, u32[]{:S(2)}, u32[]{:S(2)}) %collective-permute-start.9) | collective-permute-done | bytes 1376288 | tf_op jit(solution)/shard_map/ppermute | solution.py:28
  75.4 1.0 broadcast_select_fusion.1
  76.3 0.8 pad_maximum_fusion
  77.2 1.1 shard_map.114
  78.3 1.2 collective-permute-start.13
  79.5 1.1 shard_map.115
  80.7 0.9 collective-permute-start.14
  81.6 0.1 shard_map.118
  81.7 1.5 collective-permute-start.15
  83.3 1.2 shard_map.119
  84.5 0.7 collective-permute-start.16
  85.1 6.0 %shard_map.113 = f32[512,512]{1,0:T(8,128)} custom-call(s32[6]{0:T(128)} %stack.48.index, bf16[4,512,672]{2,1,0:T(8,128)(2,1)} %get-tuple-element.38.near_ref, bf16[4,512,672]{2,1,0:T(8,128)(2,1)} %get-tuple-element.39.far_ref, bf16[672,1024]{1,0:T(8,128)(2,1)} %bitcast.42, bf16[672,1024]{1,0:T(8,128)(2,1)} %copy-done.1, ...), custom_call_target="tpu_custom_call" | custom-call | tf_op jit(solution)/shard_map/pallas_call | solution.py:169
  91.2 0.7 collective-permute-done.13
  91.9 5.8 %collective-permute-done.14 = bf16[672,512]{1,0:T(8,128)(2,1)} collective-permute-done((bf16[672,512]{1,0:T(8,128)(2,1)S(1)}, bf16[672,512]{1,0:T(8,128)(2,1)}, u32[]{:S(2)}, u32[]{:S(2)}) %collective-permute-start.14) | collective-permute-done | bytes 688160 | tf_op jit(solution)/shard_map/ppermute | solution.py:28
  97.6 1.9 %fusion.12 = f32[512,512]{1,0:T(8,128)S(1)} fusion(bf16[672,512]{1,0:T(8,128)(2,1)} %collective-permute-done.13, bf16[4,512,672]{2,1,0:T(8,128)(2,1)} %get-tuple-element.38.near_ref, s32[]{:T(128)S(6)} %select_n.78), kind=kOutput, calls=%fused_computation.16 | convolution fusion | flops 352321536 | bytes 2523140 | tf_op jit(solution)/shard_map/dot_general | solution.py:193
  99.6 1.9 %add_add_fusion.1.raw_ref = f32[512,512]{1,0:T(8,128)S(1)} fusion(f32[512,512]{1,0:T(8,128)S(1)} %copy-done.7, f32[512,512]{1,0:T(8,128)S(1)} %fusion.12, bf16[672,512]{1,0:T(8,128)(2,1)} %collective-permute-done.14, bf16[4,512,672]{2,1,0:T(8,128)(2,1)} %get-tuple-element.39.far_ref, s32[]{:T(128)S(6)} %select_n.80), kind=kOutput, calls=%fused_computation.9 | convolution fusion | flops 352845824 | bytes 4620292 | tf_op jit(solution)/shard_map/dot_general | solution.py:193
  101.5 0.7 shard_map.116.k_ref.v_ref
  102.2 1.9 %collective-permute-start.17 = (bf16[512,512]{1,0:T(8,128)(2,1)S(1)}, bf16[512,512]{1,0:T(8,128)(2,1)S(1)}, u32[]{:S(2)}, u32[]{:S(2)}) collective-permute-start(bf16[512,512]{1,0:T(8,128)(2,1)S(1)} %shard_map.116.k_ref.v_ref), channel_id=1, source_target_pairs={{0,4},{4,8},{8,12},{12,16},{16,20},{20,24},{24,28},{28,32},{32,36}... | collective-permute-start | bytes 1572872 | tf_op jit(solution)/shard_map/ppermute | solution.py:33
  104.1 5.3 %collective-permute-start.18 = (bf16[512,512]{1,0:T(8,128)(2,1)S(1)}, bf16[512,512]{1,0:T(8,128)(2,1)S(1)}, u32[]{:S(2)}, u32[]{:S(2)}) collective-permute-start(bf16[512,512]{1,0:T(8,128)(2,1)S(1)} %shard_map.116.k_ref.v_ref), channel_id=1, source_target_pairs={{0,8},{4,12},{8,16},{12,20},{16,24},{20,28},{24,32},{28,36},{32,40... | collective-permute-start | bytes 1572872 | tf_op jit(solution)/shard_map/ppermute | solution.py:33
  109.4 6.0 %shard_map.117 = f32[512,512]{1,0:T(8,128)} custom-call(s32[6]{0:T(128)} %stack.48.index, bf16[4,512,672]{2,1,0:T(8,128)(2,1)} %get-tuple-element.38.near_ref, bf16[4,512,672]{2,1,0:T(8,128)(2,1)} %get-tuple-element.39.far_ref, bf16[672,1024]{1,0:T(8,128)(2,1)} %bitcast.43, bf16[672,1024]{1,0:T(8,128)(2,1)} %copy-done.1, ...), custom_call_target="tpu_custom_call" | custom-call | tf_op jit(solution)/shard_map/pallas_call | solution.py:169
  115.4 2.0 %fusion.10 = f32[512,512]{1,0:T(8,128)S(1)} fusion(bf16[672,512]{1,0:T(8,128)(2,1)} %collective-permute-done.15, bf16[4,512,672]{2,1,0:T(8,128)(2,1)} %get-tuple-element.38.near_ref, s32[]{:T(128)S(6)} %select_n.78), kind=kOutput, calls=%fused_computation.14 | convolution fusion | flops 352321536 | bytes 2523140 | tf_op jit(solution)/shard_map/dot_general | solution.py:193
  117.4 1.9 %fusion.4 = f32[512,512]{1,0:T(8,128)S(1)} fusion(bf16[672,512]{1,0:T(8,128)(2,1)} %collective-permute-done.16, bf16[4,512,672]{2,1,0:T(8,128)(2,1)} %get-tuple-element.39.far_ref, s32[]{:T(128)S(6)} %select_n.80), kind=kOutput, calls=%fused_computation.10 | convolution fusion | flops 352321536 | bytes 2523140 | tf_op jit(solution)/shard_map/dot_general | solution.py:193
  119.3 0.3 add_add_fusion.raw_ref
  119.7 1.2 shard_map.120.q_ref
  120.9 2.1 %shard_map.121 = (f32[512,512]{1,0:T(8,128)S(1)}, f32[512,512]{1,0:T(8,128)S(1)}) custom-call(bf16[512,512]{1,0:T(8,128)(2,1)S(1)} %shard_map.120.q_ref, bf16[512,512]{1,0:T(8,128)(2,1)S(1)} %shard_map.116.k_ref.v_ref, bf16[512,512]{1,0:T(8,128)(2,1)S(1)} %shard_map.116.k_ref.v_ref), custom_call_target="tpu_custom_call" | custom-call | tf_op jit(solution)/shard_map/pallas_call | solution.py:288
  123.0 9.2 %collective-permute-done.18.k2_ref.v2_ref = bf16[512,512]{1,0:T(8,128)(2,1)S(1)} collective-permute-done((bf16[512,512]{1,0:T(8,128)(2,1)S(1)}, bf16[512,512]{1,0:T(8,128)(2,1)S(1)}, u32[]{:S(2)}, u32[]{:S(2)}) %collective-permute-start.18) | collective-permute-done | bytes 524320 | tf_op jit(solution)/shard_map/ppermute | solution.py:33
  132.2 3.5 %shard_map.122 = bf16[512,512]{1,0:T(8,128)(2,1)S(1)} custom-call(s32[2]{0:T(128)S(1)} %add_convert_fusion.1.valid, bf16[512,512]{1,0:T(8,128)(2,1)S(1)} %shard_map.120.q_ref, bf16[512,512]{1,0:T(8,128)(2,1)S(1)} %collective-permute-done.17.k1_ref.v1_ref, bf16[512,512]{1,0:T(8,128)(2,1)S(1)} %collective-permute-done.17.k1_ref.v1_ref, ...), custom_call_target="tpu_custom_call" | custom-call | tf_op jit(solution)/shard_map/pallas_call | solution.py:309
  135.8 18.9 %all-gather.4.cloned.1.call-done = bf16[2688,1024]{1,0:T(8,128)(2,1)} async-done(((bf16[168,1024]{1,0:T(8,128)(2,1)}), bf16[2688,1024]{1,0:T(8,128)(2,1)}) %all-gather.4.cloned.1.call-update) | async-done | bytes 5505040 | tf_op jit(solution)/shard_map/all_gather | solution.py:369
  154.8 4.5 %convolution_convert_fusion = bf16[1344,512]{1,0:T(8,128)(2,1)} fusion(bf16[512,1024]{1,0:T(8,128)(2,1)S(1)} %constant_dynamic-update-slice_fusion, bf16[2688,1024]{1,0:T(8,128)(2,1)} %all-gather.4.cloned.1.call-done, s32[]{:T(128)S(6)} %select_n.82), kind=kOutput, calls=%fused_computation | convolution fusion | flops 1409974272 | bytes 5177348 | tf_op jit(solution)/shard_map/dot_general | solution.py:387
  159.4 3.4 %fusion.2 = f32[1344,512]{1,0:T(8,128)S(1)} fusion(bf16[512,1024]{1,0:T(8,128)(2,1)S(1)} %constant_dynamic-update-slice_fusion, bf16[2688,1024]{1,0:T(8,128)(2,1)} %all-gather.4.cloned.1.call-done, s32[]{:T(128)S(6)} %select_n.81), kind=kOutput, calls=%fused_computation.6 | convolution fusion | flops 1409286144 | bytes 6553604 | tf_op jit(solution)/shard_map/dot_general | solution.py:387
  162.8 1.5 copy-done.5
  164.3 0.5 multiply_reduce_fusion
  164.9 7.6 %psum.7 = f32[512]{0:T(512)S(1)} all-reduce(f32[512]{0:T(512)S(1)} %multiply_reduce_fusion), channel_id=1, replica_groups=mesh['yl'=2,'x'=4,'z'=4,'yh'=2,'c'=2] {'yh','c'}, use_global_device_ids=true, to_apply=%region_1.2 | all-reduce | flops 512 | bytes 4096 | tf_op jit(solution)/shard_map/psum | solution.py:400
  172.5 3.5 %fusion = bf16[512,1344]{0,1:T(8,128)(2,1)} fusion(bf16[512,1344]{0,1:T(8,128)(2,1)S(1)} %copy-done.6, f32[1344,512]{1,0:T(8,128)} %copy-done.5, bf16[1344,512]{1,0:T(8,128)(2,1)S(1)} %collective-permute-done.20, f32[1344]{0:T(1024)S(1)} %copy-done.12, f32[512]{0:T(512)S(1)} %add_rsqrt_fusion), kind=kLoop, calls=%fused_computation.2 | loop fusion | flops 4816896 | bytes 6888704 | tf_op jit(solution)/shard_map/convert_element_type | solution.py:402
  (51 shorter events, 0.7 us)
Async XLA Ops:
  6.5 58.6 %all-gather.6.cloned.1.call-start = ((), (), s32[]{:S(2)}) async-start(), calls=%async_computation.1 | async-start | bytes 6881280 | tf_op jit(solution)/shard_map/all_gather | solution.py:330
  7.3 147.4 %all-gather.4.cloned.1.call-start = ((), (), s32[]{:S(2)}) async-start(), calls=%async_computation | async-start | bytes 5849088 | tf_op jit(solution)/shard_map/all_gather | solution.py:369
  9.1 10.0 %collective-permute-start.5 = (bf16[168,1024]{1,0:T(8,128)(2,1)}, bf16[168,1024]{1,0:T(8,128)(2,1)S(1)}, u32[]{:S(2)}, u32[]{:S(2)}) collective-permute-start(bf16[168,1024]{1,0:T(8,128)(2,1)} %shard_map.109.refs_0_), channel_id=1, source_target_pairs={{0,64},{64,0},{1,65},{65,1},{2,66},{66,2},{3,67},{67,3},{4,68},{68... | collective-permute-start | bytes 1032200 | tf_op jit(solution)/shard_map/ppermute | solution.py:28
  9.5 11.6 %collective-permute-start = (bf16[168,1024]{1,0:T(8,128)(2,1)}, bf16[168,1024]{1,0:T(8,128)(2,1)S(1)}, u32[]{:S(2)}, u32[]{:S(2)}) collective-permute-start(bf16[168,1024]{1,0:T(8,128)(2,1)} %shard_map.109.refs_0_), channel_id=1, source_target_pairs={{0,16},{16,32},{32,48},{48,0},{1,17},{17,33},{33,49},{49,1},{2,18}... | collective-permute-start | bytes 1032200 | tf_op jit(solution)/shard_map/ppermute | solution.py:28
  11.0 16.2 %collective-permute-start.1 = (bf16[168,1024]{1,0:T(8,128)(2,1)}, bf16[168,1024]{1,0:T(8,128)(2,1)S(1)}, u32[]{:S(2)}, u32[]{:S(2)}) collective-permute-start(bf16[168,1024]{1,0:T(8,128)(2,1)} %shard_map.109.refs_0_), channel_id=1, source_target_pairs={{0,48},{16,0},{32,16},{48,32},{1,49},{17,1},{33,17},{49,33},{2,50}... | collective-permute-start | bytes 1032200 | tf_op jit(solution)/shard_map/ppermute | solution.py:28
  12.8 16.1 %collective-permute-start.2 = (bf16[168,1024]{1,0:T(8,128)(2,1)}, bf16[168,1024]{1,0:T(8,128)(2,1)S(1)}, u32[]{:S(2)}, u32[]{:S(2)}) collective-permute-start(bf16[168,1024]{1,0:T(8,128)(2,1)} %shard_map.109.refs_0_), channel_id=1, source_target_pairs={{0,32},{16,48},{32,0},{48,16},{1,33},{17,49},{33,1},{49,17},{2,34}... | collective-permute-start | bytes 1032200 | tf_op jit(solution)/shard_map/ppermute | solution.py:28
  19.1 14.1 %collective-permute-start.6 = (bf16[168,1024]{1,0:T(8,128)(2,1)S(1)}, bf16[168,1024]{1,0:T(8,128)(2,1)S(1)}, u32[]{:S(2)}, u32[]{:S(2)}) collective-permute-start(bf16[168,1024]{1,0:T(8,128)(2,1)S(1)} %collective-permute-done.5.refs_0_), channel_id=1, source_target_pairs={{0,4},{4,8},{8,12},{12,0},{1,5},{5,9},{9,13},{13,1},{2,6},{6,10},{... | collective-permute-start | bytes 1032200 | tf_op jit(solution)/shard_map/ppermute | solution.py:28
  21.0 12.2 %collective-permute-start.7 = (bf16[168,1024]{1,0:T(8,128)(2,1)S(1)}, bf16[168,1024]{1,0:T(8,128)(2,1)}, u32[]{:S(2)}, u32[]{:S(2)}) collective-permute-start(bf16[168,1024]{1,0:T(8,128)(2,1)S(1)} %collective-permute-done.5.refs_0_), channel_id=1, source_target_pairs={{0,12},{4,0},{8,4},{12,8},{1,13},{5,1},{9,5},{13,9},{2,14},{6,2},{... | collective-permute-start | bytes 1032200 | tf_op jit(solution)/shard_map/ppermute | solution.py:28
  21.1 19.5 %collective-permute-start.8 = (bf16[168,1024]{1,0:T(8,128)(2,1)S(1)}, bf16[168,1024]{1,0:T(8,128)(2,1)}, u32[]{:S(2)}, u32[]{:S(2)}) collective-permute-start(bf16[168,1024]{1,0:T(8,128)(2,1)S(1)} %collective-permute-done.5.refs_0_), channel_id=1, source_target_pairs={{0,8},{4,12},{8,0},{12,4},{1,9},{5,13},{9,1},{13,5},{2,10},{6,14},... | collective-permute-start | bytes 1032200 | tf_op jit(solution)/shard_map/ppermute | solution.py:28
  28.8 1.0 copy-start.2
  30.6 42.7 %copy-start = (bf16[4,168,1024]{2,1,0:T(8,128)(2,1)}, bf16[4,168,1024]{2,1,0:T(8,128)(2,1)S(1)}, u32[]{:S(2)}) copy-start(bf16[4,168,1024]{2,1,0:T(8,128)(2,1)S(1)} %shard_map.110) | copy-start | bytes 4128772
  30.6 42.7 %collective-permute-start.3 = (bf16[672,1024]{1,0:T(8,128)(2,1)S(1)}, bf16[672,1024]{1,0:T(8,128)(2,1)S(1)}, u32[]{:S(2)}, u32[]{:S(2)}) collective-permute-start(bf16[672,1024]{1,0:T(8,128)(2,1)S(1)} %bitcast.40), channel_id=1, source_target_pairs={{0,4},{4,8},{8,12},{12,0},{1,5},{5,9},{9,13},{13,1},{2,6},{6,10},{... | collective-permute-start | bytes 4128776 | tf_op jit(solution)/shard_map/ppermute | solution.py:28
  32.6 40.7 %collective-permute-start.4 = (bf16[672,1024]{1,0:T(8,128)(2,1)S(1)}, bf16[672,1024]{1,0:T(8,128)(2,1)}, u32[]{:S(2)}, u32[]{:S(2)}) collective-permute-start(bf16[672,1024]{1,0:T(8,128)(2,1)S(1)} %bitcast.41), channel_id=1, source_target_pairs={{0,12},{4,0},{8,4},{12,8},{1,13},{5,1},{9,5},{13,9},{2,14},{6,2},{... | collective-permute-start | bytes 4128776 | tf_op jit(solution)/shard_map/ppermute | solution.py:28
  43.9 29.4 %collective-permute-start.10 = (bf16[672,1024]{1,0:T(8,128)(2,1)}, bf16[672,1024]{1,0:T(8,128)(2,1)}, u32[]{:S(2)}, u32[]{:S(2)}) collective-permute-start(bf16[672,1024]{1,0:T(8,128)(2,1)} %bitcast.2.refs_3_), channel_id=1, source_target_pairs={{0,48},{16,0},{32,16},{48,32},{1,49},{17,1},{33,17},{49,33},{2,50}... | collective-permute-start | bytes 4128776 | tf_op jit(solution)/shard_map/ppermute | solution.py:28
  46.6 28.7 %collective-permute-start.9 = (bf16[672,1024]{1,0:T(8,128)(2,1)}, bf16[672,1024]{1,0:T(8,128)(2,1)}, u32[]{:S(2)}, u32[]{:S(2)}) collective-permute-start(bf16[672,1024]{1,0:T(8,128)(2,1)} %bitcast.2.refs_3_), channel_id=1, source_target_pairs={{0,16},{16,32},{32,48},{48,0},{1,17},{17,33},{33,49},{49,1},{2,18}... | collective-permute-start | bytes 4128776 | tf_op jit(solution)/shard_map/ppermute | solution.py:28
  46.7 9.3 %collective-permute-start.11 = (bf16[168,512]{1,0:T(8,128)(2,1)}, bf16[168,512]{1,0:T(8,128)(2,1)S(1)}, u32[]{:S(2)}, u32[]{:S(2)}) collective-permute-start(bf16[168,512]{1,0:T(8,128)(2,1)} %bitcast.49), channel_id=1, source_target_pairs={{0,64},{2,0},{64,66},{66,2},{1,65},{3,1},{65,67},{67,3},{4,68},{6,... | collective-permute-start | bytes 516104 | tf_op jit(solution)/shard_map/ppermute | solution.py:345
  56.0 7.8 %copy-start.10 = (bf16[168,512]{1,0:T(8,128)(2,1)}, bf16[168,512]{1,0:T(8,128)(2,1)S(1)}, u32[]{:S(2)}) copy-start(bf16[168,512]{1,0:T(8,128)(2,1)S(1)} %collective-permute-done.11) | copy-start | bytes 516100
  56.0 17.3 %collective-permute-start.12 = (bf16[168,512]{1,0:T(8,128)(2,1)}, bf16[168,512]{1,0:T(8,128)(2,1)}, u32[]{:S(2)}, u32[]{:S(2)}) collective-permute-start(bf16[168,512]{1,0:T(8,128)(2,1)} %bitcast.50), channel_id=1, source_target_pairs={{64,2},{2,64},{65,3},{3,65},{68,6},{6,68},{69,7},{7,69},{72,10},{1... | collective-permute-start | bytes 516104 | tf_op jit(solution)/shard_map/ppermute | solution.py:346
  65.1 10.3 %copy-start.9 = (bf16[512,168]{0,1:T(8,128)(2,1)S(1)}, bf16[512,168]{0,1:T(8,128)(2,1)}, u32[]{:S(2)}) copy-start(bf16[512,168]{0,1:T(8,128)(2,1)} %param.15) | copy-start | bytes 516100
  65.1 10.2 %copy-start.11 = (bf16[168,512]{1,0:T(8,128)(2,1)S(1)}, bf16[168,512]{1,0:T(8,128)(2,1)}, u32[]{:S(2)}) copy-start(bf16[168,512]{1,0:T(8,128)(2,1)} %copy-done.10) | copy-start | bytes 516100
  73.3 8.3 %copy-start.1 = (bf16[672,1024]{1,0:T(8,128)(2,1)}, bf16[672,1024]{1,0:T(8,128)(2,1)S(1)}, u32[]{:S(2)}) copy-start(bf16[672,1024]{1,0:T(8,128)(2,1)S(1)} %collective-permute-done.3.refs_1_.value_ref) | copy-start | bytes 4128772
  78.3 13.6 %collective-permute-start.13 = (bf16[672,512]{1,0:T(8,128)(2,1)S(1)}, bf16[672,512]{1,0:T(8,128)(2,1)}, u32[]{:S(2)}, u32[]{:S(2)}) collective-permute-start(bf16[672,512]{1,0:T(8,128)(2,1)S(1)} %shard_map.114), channel_id=1, source_target_pairs={{0,12},{4,0},{8,4},{12,8},{1,13},{5,1},{9,5},{13,9},{2,14},{6,2},{... | collective-permute-start | bytes 2064392 | tf_op jit(solution)/shard_map/ppermute | solution.py:28
  80.7 17.0 %collective-permute-start.14 = (bf16[672,512]{1,0:T(8,128)(2,1)S(1)}, bf16[672,512]{1,0:T(8,128)(2,1)}, u32[]{:S(2)}, u32[]{:S(2)}) collective-permute-start(bf16[672,512]{1,0:T(8,128)(2,1)S(1)} %shard_map.115), channel_id=1, source_target_pairs={{0,48},{16,0},{32,16},{48,32},{1,49},{17,1},{33,17},{49,33},{2,50}... | collective-permute-start | bytes 2064392 | tf_op jit(solution)/shard_map/ppermute | solution.py:28
  81.7 33.6 %collective-permute-start.15 = (bf16[672,512]{1,0:T(8,128)(2,1)S(1)}, bf16[672,512]{1,0:T(8,128)(2,1)}, u32[]{:S(2)}, u32[]{:S(2)}) collective-permute-start(bf16[672,512]{1,0:T(8,128)(2,1)S(1)} %shard_map.118), channel_id=1, source_target_pairs={{0,4},{4,8},{8,12},{12,0},{1,5},{5,9},{9,13},{13,1},{2,6},{6,10},{... | collective-permute-start | bytes 2064392 | tf_op jit(solution)/shard_map/ppermute | solution.py:28
  84.5 32.9 %collective-permute-start.16 = (bf16[672,512]{1,0:T(8,128)(2,1)S(1)}, bf16[672,512]{1,0:T(8,128)(2,1)}, u32[]{:S(2)}, u32[]{:S(2)}) collective-permute-start(bf16[672,512]{1,0:T(8,128)(2,1)S(1)} %shard_map.119), channel_id=1, source_target_pairs={{0,16},{16,32},{32,48},{48,0},{1,17},{17,33},{33,49},{49,1},{2,18}... | collective-permute-start | bytes 2064392 | tf_op jit(solution)/shard_map/ppermute | solution.py:28
  91.2 8.4 %copy-start.7 = (f32[512,512]{1,0:T(8,128)S(1)}, f32[512,512]{1,0:T(8,128)}, u32[]{:S(2)}) copy-start(f32[512,512]{1,0:T(8,128)} %shard_map.113) | copy-start | bytes 3145732
  99.5 1.9 %copy-start.3 = (f32[128]{0:T(128)S(1)}, f32[128]{0:T(128)}, u32[]{:S(2)}) copy-start(f32[128]{0:T(128)} %param.19) | copy-start | bytes 1540
  102.2 20.8 %collective-permute-start.17 = (bf16[512,512]{1,0:T(8,128)(2,1)S(1)}, bf16[512,512]{1,0:T(8,128)(2,1)S(1)}, u32[]{:S(2)}, u32[]{:S(2)}) collective-permute-start(bf16[512,512]{1,0:T(8,128)(2,1)S(1)} %shard_map.116.k_ref.v_ref), channel_id=1, source_target_pairs={{0,4},{4,8},{8,12},{12,16},{16,20},{20,24},{24,28},{28,32},{32,36}... | collective-permute-start | bytes 1572872 | tf_op jit(solution)/shard_map/ppermute | solution.py:33
  104.1 28.1 %collective-permute-start.18 = (bf16[512,512]{1,0:T(8,128)(2,1)S(1)}, bf16[512,512]{1,0:T(8,128)(2,1)S(1)}, u32[]{:S(2)}, u32[]{:S(2)}) collective-permute-start(bf16[512,512]{1,0:T(8,128)(2,1)S(1)} %shard_map.116.k_ref.v_ref), channel_id=1, source_target_pairs={{0,8},{4,12},{8,16},{12,20},{16,24},{20,28},{24,32},{28,36},{32,40... | collective-permute-start | bytes 1572872 | tf_op jit(solution)/shard_map/ppermute | solution.py:33
  115.3 4.0 %copy-start.8 = (f32[512,512]{1,0:T(8,128)S(1)}, f32[512,512]{1,0:T(8,128)}, u32[]{:S(2)}) copy-start(f32[512,512]{1,0:T(8,128)} %shard_map.117) | copy-start | bytes 3145732
  117.4 2.3 %copy-start.4 = (f32[128]{0:T(128)S(1)}, f32[128]{0:T(128)}, u32[]{:S(2)}) copy-start(f32[128]{0:T(128)} %param.18) | copy-start | bytes 1540
  135.7 19.0 %collective-permute-start.19 = (bf16[512,512]{1,0:T(8,128)(2,1)S(1)}, bf16[512,512]{1,0:T(8,128)(2,1)S(1)}, u32[]{:S(2)}, u32[]{:S(2)}) collective-permute-start(bf16[512,512]{1,0:T(8,128)(2,1)S(1)} %shard_map.122), channel_id=1, source_target_pairs={{0,2},{2,0},{1,3},{3,1},{4,6},{6,4},{5,7},{7,5},{8,10},{10,8},{9,1... | collective-permute-start | bytes 1572872 | tf_op jit(solution)/shard_map/ppermute | solution.py:28
  159.3 3.5 %collective-permute-start.20 = (bf16[1344,512]{1,0:T(8,128)(2,1)}, bf16[1344,512]{1,0:T(8,128)(2,1)S(1)}, u32[]{:S(2)}, u32[]{:S(2)}) collective-permute-start(bf16[1344,512]{1,0:T(8,128)(2,1)} %convolution_convert_fusion), channel_id=1, source_target_pairs={{0,1},{1,0},{2,3},{3,2},{4,5},{5,4},{6,7},{7,6},{8,9},{9,8},{10,11... | collective-permute-start | bytes 4128776 | tf_op jit(solution)/shard_map/ppermute | solution.py:28
  162.8 1.5 copy-start.5
  162.8 9.7 %copy-start.6 = (bf16[512,1344]{0,1:T(8,128)(2,1)S(1)}, bf16[512,1344]{0,1:T(8,128)(2,1)}, u32[]{:S(2)}) copy-start(bf16[512,1344]{0,1:T(8,128)(2,1)} %param.11) | copy-start | bytes 4128772
  162.8 9.7 %copy-start.12 = (f32[1344]{0:T(1024)S(1)}, f32[1344]{0:T(1024)}, u32[]{:S(2)}) copy-start(f32[1344]{0:T(1024)} %param.17) | copy-start | bytes 16132
Sparse Core Ops, SparseCore 0:
  9.0 50.7 all-gather.5
  77.3 77.3 all-gather.3

commit v7 on v6

--- a/solution.py
+++ b/solution.py
@@ -320,6 +320,34 @@
     )(valid, queries, one, one, two, two, sums, weights)
 
 
+def half_kernel(half, weight_ref, context_ref, out_ref):
+    out_ref[...] = lax.dot_general(
+        weight_ref[...], context_ref[...], (((1,), (1,)), ((), ())), preferred_element_type=jnp.float32
+    ).astype(out_ref.dtype)
+
+
+def out_half(weight, context, half, dtype):
+    rows, depth = context.shape
+    columns = weight.shape[0] // 2
+    steps = 4
+    tile = columns // steps
+    return pl.pallas_call(
+        half_kernel,
+        grid_spec=pltpu.PrefetchScalarGridSpec(
+            num_scalar_prefetch=1,
+            grid=(steps,),
+            in_specs=[
+                pl.BlockSpec((tile, depth), lambda i, s: (s[0] * steps + i, 0)),
+                pl.BlockSpec((rows, depth), lambda i, s: (0, 0)),
+            ],
+            out_specs=pl.BlockSpec((tile, rows), lambda i, s: (i, 0)),
+        ),
+        out_shape=jax.ShapeDtypeStruct((columns, rows), dtype),
+        compiler_params=pltpu.CompilerParams(vmem_limit_bytes=SMALL),
+        cost_estimate=QUICK,
+    )(half[None], weight, context)
+
+
 def local(
     tokens, q_weight, key_matrix, value_matrix, o_weight, pre_gain, post_gain, q_gain, k_gain
 ):
@@ -384,20 +412,16 @@
     valid = jnp.stack([seq_index >= 1, seq_index >= 2]).astype(jnp.int32)
     context = attend_behind(valid, queries, behind_one, behind_two, sums, weights)
     across = shift(context, "yh", 1)
-    summed = lambda weight, value: lax.dot_general(
-        weight, value, (((1,), (1,)), ((), ())), preferred_element_type=jnp.float32
-    )
     out_all, context = lax.optimization_barrier((out_all, context))
     both = jnp.concatenate([context, across], axis=1)
-    columns = out_all.shape[0] // 2
-
-    def half_of(core):
-        return summed(lax.dynamic_slice_in_dim(out_all, core * columns, columns, 0), both)
-
-    received = shift(half_of(1 - c).astype(jnp.bfloat16), "c", 1)
-    kept, received = lax.optimization_barrier((half_of(c), received))
+
+    half_of = functools.partial(out_half, out_all, both)
+    received = shift(half_of(1 - c, jnp.bfloat16), "c", 1)
+    kept, received = lax.optimization_barrier((half_of(c, jnp.float32), received))
     share = (kept + received.astype(jnp.float32)).T
-    total = lax.psum(jnp.sum(share * share, axis=1), MP)
+    squares = jnp.sum(share * share, axis=1)
+    others = [lax.ppermute(squares, MP, [(i, i ^ bit) for i in range(4)]) for bit in (2, 3, 1)]
+    total = (squares + others[2]) + (others[0] + others[1])
     scale_rows = lax.rsqrt(total / MODEL_WIDTH + epsilon)
     return (tokens.astype(jnp.float32) + share * scale_rows[:, None] * post_gain).astype(
         jnp.bfloat16

time: 185 us -> 180 us (0.973)
  matrix products: 15.6 us -> 7.72 us
  blocking collectives: 7.6 us -> 0 us
  Pallas kernels: 37 us -> 41.4 us
  starting transfers between devices: 32.9 us -> 36.3 us
  waiting for transfers between devices: 59.1 us -> 61.5 us
    dot_general x2 -> x0, matrix products: 7.89 us -> none  [local(): lax.dot_general(weight, value, (((1,), (1,)), ((), ())), preferred_elemen...]
    psum x1 -> x0, blocking collectives: 7.6 us -> none  [local(): total = lax.psum(jnp.sum(share * share, axis=1), MP)]
    pallas_call x0 -> x2, Pallas kernels: none -> 4.47 us  [out_half(): pl.pallas_call(half_kernel, grid_spec=pltpu.PrefetchScalarGridSpec(num_sc...]
    ppermute x0 -> x3, starting transfers between devices: none -> 3.44 us  [local(): lax.ppermute(squares, MP, [(i, i ^ bit) for i in range(4)])]
    ppermute x0 -> x3, waiting for transfers between devices: none -> 1.88 us  [local(): lax.ppermute(squares, MP, [(i, i ^ bit) for i in range(4)])]
    unnamed x27 -> x29, local copies, waits for them, and re-layouts: 2.58 us -> 3.83 us
  transfers between devices with their start and end apart: 23 -> 26, of which waited for: 11 -> 13; matrix products, arithmetic and copies ran while one was open for 11% -> 9% of each run, Pallas kernels for 20% -> 22%
where the time goes in v7:
time: 180 us; the launch traced here: 177 us
  waiting for transfers between devices  61.5 us (34%)
  Pallas kernels  41.4 us (23%)
  starting transfers between devices  36.3 us (20%)
  between operations  13.8 us (8%)
  other arithmetic  8.81 us (5%)
  matrix products  7.72 us (4%)
  local copies, waits for them, and re-layouts  7.57 us (4%)
    ppermute x17, waiting for transfers between devices, shift(): lax.ppermute(value, axis, [(i, (i + step) % count) for i in range(count)])  25.7 us
    ppermute x17, starting transfers between devices, shift(): lax.ppermute(value, axis, [(i, (i + step) % count) for i in range(count)])  19.9 us
    all_gather x1, waiting for transfers between devices, local(): out_all = lax.all_gather(pair, ('x', 'z'), axis=0, tiled=True)  18.9 us
    pallas_call x2, Pallas kernels, early_product(): pl.pallas_call(functools.partial(early_kernel, len(near_weights), count,...  11.9 us
    ppermute x2, waiting for transfers between devices, from_behind(): lax.ppermute(value, SEQ, [(source, source + steps) for source in range(co...  9.14 us
    pallas_call x1, Pallas kernels, norm_parts(): pl.pallas_call(norm_kernel, grid_spec=pltpu.PrefetchScalarGridSpec(num_sc...  8.14 us
    dot_general x4, matrix products, product(): return jnp.dot(left, right, preferred_element_type=jnp.float32)  7.72 us
    ppermute x2, starting transfers between devices, from_behind(): lax.ppermute(value, SEQ, [(source, source + steps) for source in range(co...  7.14 us
  transfers between devices with their start and end apart: 26, of which 13 were waited for; matrix products, arithmetic and copies ran while one was open for 9% of the time, Pallas kernels for 22%

profile of v7, /device:TPU:40, one launch (start us, length us, event | category | flops | bytes accessed | tf_op | source)
XLA Modules:
  0.0 177.2 jit_solution(6140046680884320854)
XLA Ops:
  6.5 0.7 all-gather.6.cloned.1.call-update
  7.3 1.8 %shard_map.109.refs_0_ = bf16[168,1024]{1,0:T(8,128)(2,1)} custom-call(bf16[168,512]{1,0:T(8,128)(2,1)} %refs_0_.1, bf16[168,256]{1,0:T(8,128)(2,1)} %refs_1_.1, bf16[168,256]{1,0:T(8,128)(2,1)} %refs_2_.1), custom_call_target="tpu_custom_call" | custom-call | tf_op jit(solution)/shard_map/pallas_call | solution.py:74
  9.1 0.4 collective-permute-start.5
  9.5 1.5 collective-permute-start
  11.0 1.7 collective-permute-start.1
  12.8 1.8 %collective-permute-start.2 = (bf16[168,1024]{1,0:T(8,128)(2,1)}, bf16[168,1024]{1,0:T(8,128)(2,1)S(1)}, u32[]{:S(2)}, u32[]{:S(2)}) collective-permute-start(bf16[168,1024]{1,0:T(8,128)(2,1)} %shard_map.109.refs_0_), channel_id=1, source_target_pairs={{0,32},{16,48},{32,0},{48,16},{1,33},{17,49},{33,1},{49,17},{2,34}... | collective-permute-start | bytes 1032200 | tf_op jit(solution)/shard_map/ppermute | solution.py:28
  14.6 4.5 %collective-permute-done.5.refs_0_ = bf16[168,1024]{1,0:T(8,128)(2,1)S(1)} collective-permute-done((bf16[168,1024]{1,0:T(8,128)(2,1)}, bf16[168,1024]{1,0:T(8,128)(2,1)S(1)}, u32[]{:S(2)}, u32[]{:S(2)}) %collective-permute-start.5) | collective-permute-done | bytes 344096 | tf_op jit(solution)/shard_map/ppermute | solution.py:28
  19.1 1.9 %collective-permute-start.6 = (bf16[168,1024]{1,0:T(8,128)(2,1)S(1)}, bf16[168,1024]{1,0:T(8,128)(2,1)S(1)}, u32[]{:S(2)}, u32[]{:S(2)}) collective-permute-start(bf16[168,1024]{1,0:T(8,128)(2,1)S(1)} %collective-permute-done.5.refs_0_), channel_id=1, source_target_pairs={{0,4},{4,8},{8,12},{12,0},{1,5},{5,9},{9,13},{13,1},{2,6},{6,10},{... | collective-permute-start | bytes 1032200 | tf_op jit(solution)/shard_map/ppermute | solution.py:28
  21.1 3.0 %collective-permute-start.8 = (bf16[168,1024]{1,0:T(8,128)(2,1)S(1)}, bf16[168,1024]{1,0:T(8,128)(2,1)}, u32[]{:S(2)}, u32[]{:S(2)}) collective-permute-start(bf16[168,1024]{1,0:T(8,128)(2,1)S(1)} %collective-permute-done.5.refs_0_), channel_id=1, source_target_pairs={{0,8},{4,12},{8,0},{12,4},{1,9},{5,13},{9,1},{13,5},{2,10},{6,14},... | collective-permute-start | bytes 1032200 | tf_op jit(solution)/shard_map/ppermute | solution.py:28
  24.1 0.7 and_select_fusion
  24.8 2.5 %collective-permute-done.1.refs_2_ = bf16[168,1024]{1,0:T(8,128)(2,1)S(1)} collective-permute-done((bf16[168,1024]{1,0:T(8,128)(2,1)}, bf16[168,1024]{1,0:T(8,128)(2,1)S(1)}, u32[]{:S(2)}, u32[]{:S(2)}) %collective-permute-start.1) | collective-permute-done | bytes 344096 | tf_op jit(solution)/shard_map/ppermute | solution.py:28
  27.2 1.6 collective-permute-done.2.refs_3_
  28.8 1.0 copy-done.4
  29.8 0.8 shard_map.110
  30.6 2.0 %collective-permute-start.3 = (bf16[672,1024]{1,0:T(8,128)(2,1)S(1)}, bf16[672,1024]{1,0:T(8,128)(2,1)S(1)}, u32[]{:S(2)}, u32[]{:S(2)}) collective-permute-start(bf16[672,1024]{1,0:T(8,128)(2,1)S(1)} %bitcast.40), channel_id=1, source_target_pairs={{0,4},{4,8},{8,12},{12,0},{1,5},{5,9},{9,13},{13,1},{2,6},{6,10},{... | collective-permute-start | bytes 4128776 | tf_op jit(solution)/shard_map/ppermute | solution.py:28
  32.7 0.6 collective-permute-done.6.refs_1_
  33.2 7.3 %collective-permute-done.8.refs_3_ = bf16[168,1024]{1,0:T(8,128)(2,1)} collective-permute-done((bf16[168,1024]{1,0:T(8,128)(2,1)S(1)}, bf16[168,1024]{1,0:T(8,128)(2,1)}, u32[]{:S(2)}, u32[]{:S(2)}) %collective-permute-start.8) | collective-permute-done | bytes 344096 | tf_op jit(solution)/shard_map/ppermute | solution.py:28
  40.6 3.3 %shard_map.111 = bf16[4,168,1024]{2,1,0:T(8,128)(2,1)} custom-call(s32[4]{0:T(128)S(1)} %get-tuple-element.62.slots, bf16[168,1024]{1,0:T(8,128)(2,1)S(1)} %collective-permute-done.5.refs_0_, bf16[168,1024]{1,0:T(8,128)(2,1)S(1)} %collective-permute-done.6.refs_1_, bf16[168,1024]{1,0:T(8,128)(2,1)} %collective-permute-done.7.refs_2_, ...), custom_call_target="tpu_custom_call" | custom-call | tf_op jit(solution)/shard_map/pallas_call | solution.py:50
  43.9 2.8 %collective-permute-start.10 = (bf16[672,1024]{1,0:T(8,128)(2,1)}, bf16[672,1024]{1,0:T(8,128)(2,1)}, u32[]{:S(2)}, u32[]{:S(2)}) collective-permute-start(bf16[672,1024]{1,0:T(8,128)(2,1)} %bitcast.3.refs_3_), channel_id=1, source_target_pairs={{0,48},{16,0},{32,16},{48,32},{1,49},{17,1},{33,17},{49,33},{2,50}... | collective-permute-start | bytes 4128776 | tf_op jit(solution)/shard_map/ppermute | solution.py:28
  46.7 2.4 %collective-permute-start.11 = (bf16[168,512]{1,0:T(8,128)(2,1)}, bf16[168,512]{1,0:T(8,128)(2,1)S(1)}, u32[]{:S(2)}, u32[]{:S(2)}) collective-permute-start(bf16[168,512]{1,0:T(8,128)(2,1)} %bitcast.49), channel_id=1, source_target_pairs={{0,64},{2,0},{64,66},{66,2},{1,65},{3,1},{65,67},{67,3},{4,68},{6,... | collective-permute-start | bytes 516104 | tf_op jit(solution)/shard_map/ppermute | solution.py:373
  49.0 1.8 %fusion.15 = (f32[512,64]{1,0:T(8,128)S(1)}, f32[512,64]{1,0:T(8,128)}, f32[512,64]{1,0:T(8,128)}) fusion(f32[64]{0:T(128)S(1)} %multiply_power_fusion, f32[512]{0:T(512)S(1)} %add_convert_fusion), kind=kLoop, calls=%fused_computation.25 | loop fusion | flops 65536 | bytes 395520 | tf_op jit(solution)/shard_map/neg | solution.py:382
  50.8 5.2 %collective-permute-done.11 = bf16[168,512]{1,0:T(8,128)(2,1)S(1)} collective-permute-done((bf16[168,512]{1,0:T(8,128)(2,1)}, bf16[168,512]{1,0:T(8,128)(2,1)S(1)}, u32[]{:S(2)}, u32[]{:S(2)}) %collective-permute-start.11) | collective-permute-done | bytes 172064 | tf_op jit(solution)/shard_map/ppermute | solution.py:373
  56.0 3.5 %collective-permute-start.12 = (bf16[168,512]{1,0:T(8,128)(2,1)}, bf16[168,512]{1,0:T(8,128)(2,1)}, u32[]{:S(2)}, u32[]{:S(2)}) collective-permute-start(bf16[168,512]{1,0:T(8,128)(2,1)} %bitcast.50), channel_id=1, source_target_pairs={{64,2},{2,64},{65,3},{3,65},{68,6},{6,68},{69,7},{7,69},{72,10},{1... | collective-permute-start | bytes 516104 | tf_op jit(solution)/shard_map/ppermute | solution.py:374
  59.5 0.7 pad_add_fusion.side
  60.2 0.8 reshape.32
  61.0 1.4 reshape_reshape.3.far_gain
  62.4 0.7 reshape.33.near_gain
  63.2 0.7 stack.48.index
  63.8 1.3 pad_maximum_fusion.1
  65.2 8.1 %shard_map.112 = (bf16[4,512,672]{2,1,0:T(8,128)(2,1)}, bf16[4,512,672]{2,1,0:T(8,128)(2,1)}) custom-call(s32[2]{0:T(128)} %pad_add_fusion.side, bf16[2,2,1344,512]{3,2,1,0:T(8,128)(2,1)} %bitcast.46, bf16[2,2,1344,512]{3,2,1,0:T(8,128)(2,1)} %bitcast.47, f32[2,4,1,672]{3,2,1,0:T(1,128)} %reshape.33.near_gain, f32[2,4,1,672]{3,2,1,0:T(1,128)} %reshape_reshape.3.far_gain), custom_call_target="tpu_custom_call" | custom-call | tf_op jit(solution)/shard_map/pallas_call | solution.py:127
  73.4 2.0 %collective-permute-done.9.refs_4_.value_ref = bf16[672,1024]{1,0:T(8,128)(2,1)} collective-permute-done((bf16[672,1024]{1,0:T(8,128)(2,1)}, bf16[672,1024]{1,0:T(8,128)(2,1)}, u32[]{:S(2)}, u32[]{:S(2)}) %collective-permute-start.9) | collective-permute-done | bytes 1376288 | tf_op jit(solution)/shard_map/ppermute | solution.py:28
  75.4 1.0 broadcast_select_fusion.1
  76.3 0.8 pad_maximum_fusion
  77.1 1.1 shard_map.114
  78.3 1.2 collective-permute-start.13
  79.5 1.1 shard_map.115
  80.6 1.0 collective-permute-start.14
  81.8 1.5 collective-permute-start.15
  83.4 1.2 shard_map.119
  84.5 0.6 collective-permute-start.16
  85.1 6.0 %shard_map.113 = f32[512,512]{1,0:T(8,128)} custom-call(s32[6]{0:T(128)} %stack.48.index, bf16[4,512,672]{2,1,0:T(8,128)(2,1)} %get-tuple-element.38.near_ref, bf16[4,512,672]{2,1,0:T(8,128)(2,1)} %get-tuple-element.39.far_ref, bf16[672,1024]{1,0:T(8,128)(2,1)} %bitcast.42, bf16[672,1024]{1,0:T(8,128)(2,1)} %copy-done.3, ...), custom_call_target="tpu_custom_call" | custom-call | tf_op jit(solution)/shard_map/pallas_call | solution.py:169
  91.1 0.7 collective-permute-done.13
  91.9 5.8 %collective-permute-done.14 = bf16[672,512]{1,0:T(8,128)(2,1)} collective-permute-done((bf16[672,512]{1,0:T(8,128)(2,1)S(1)}, bf16[672,512]{1,0:T(8,128)(2,1)}, u32[]{:S(2)}, u32[]{:S(2)}) %collective-permute-start.14) | collective-permute-done | bytes 688160 | tf_op jit(solution)/shard_map/ppermute | solution.py:28
  97.7 1.9 %fusion.9 = f32[512,512]{1,0:T(8,128)S(1)} fusion(bf16[672,512]{1,0:T(8,128)(2,1)} %collective-permute-done.13, bf16[4,512,672]{2,1,0:T(8,128)(2,1)} %get-tuple-element.38.near_ref, s32[]{:T(128)S(6)} %select_n.72), kind=kOutput, calls=%fused_computation.12 | convolution fusion | flops 352321536 | bytes 2523140 | tf_op jit(solution)/shard_map/dot_general | solution.py:193
  99.6 1.9 %add_add_fusion.1.raw_ref = f32[512,512]{1,0:T(8,128)S(1)} fusion(f32[512,512]{1,0:T(8,128)S(1)} %copy-done.8, f32[512,512]{1,0:T(8,128)S(1)} %fusion.9, bf16[672,512]{1,0:T(8,128)(2,1)} %collective-permute-done.14, bf16[4,512,672]{2,1,0:T(8,128)(2,1)} %get-tuple-element.39.far_ref, s32[]{:T(128)S(6)} %select_n.74), kind=kOutput, calls=%fused_computation.5 | convolution fusion | flops 352845824 | bytes 4620292 | tf_op jit(solution)/shard_map/dot_general | solution.py:193
  101.5 0.7 shard_map.116.k_ref.v_ref
  102.2 1.9 %collective-permute-start.17 = (bf16[512,512]{1,0:T(8,128)(2,1)S(1)}, bf16[512,512]{1,0:T(8,128)(2,1)S(1)}, u32[]{:S(2)}, u32[]{:S(2)}) collective-permute-start(bf16[512,512]{1,0:T(8,128)(2,1)S(1)} %shard_map.116.k_ref.v_ref), channel_id=1, source_target_pairs={{0,4},{4,8},{8,12},{12,16},{16,20},{20,24},{24,28},{28,32},{32,36}... | collective-permute-start | bytes 1572872 | tf_op jit(solution)/shard_map/ppermute | solution.py:33
  104.1 5.2 %collective-permute-start.18 = (bf16[512,512]{1,0:T(8,128)(2,1)S(1)}, bf16[512,512]{1,0:T(8,128)(2,1)S(1)}, u32[]{:S(2)}, u32[]{:S(2)}) collective-permute-start(bf16[512,512]{1,0:T(8,128)(2,1)S(1)} %shard_map.116.k_ref.v_ref), channel_id=1, source_target_pairs={{0,8},{4,12},{8,16},{12,20},{16,24},{20,28},{24,32},{28,36},{32,40... | collective-permute-start | bytes 1572872 | tf_op jit(solution)/shard_map/ppermute | solution.py:33
  109.4 6.0 %shard_map.117 = f32[512,512]{1,0:T(8,128)} custom-call(s32[6]{0:T(128)} %stack.48.index, bf16[4,512,672]{2,1,0:T(8,128)(2,1)} %get-tuple-element.38.near_ref, bf16[4,512,672]{2,1,0:T(8,128)(2,1)} %get-tuple-element.39.far_ref, bf16[672,1024]{1,0:T(8,128)(2,1)} %bitcast.43, bf16[672,1024]{1,0:T(8,128)(2,1)} %copy-done.3, ...), custom_call_target="tpu_custom_call" | custom-call | tf_op jit(solution)/shard_map/pallas_call | solution.py:169
  115.4 2.0 %fusion.7 = f32[512,512]{1,0:T(8,128)S(1)} fusion(bf16[672,512]{1,0:T(8,128)(2,1)} %collective-permute-done.15, bf16[4,512,672]{2,1,0:T(8,128)(2,1)} %get-tuple-element.38.near_ref, s32[]{:T(128)S(6)} %select_n.72), kind=kOutput, calls=%fused_computation.10 | convolution fusion | flops 352321536 | bytes 2523140 | tf_op jit(solution)/shard_map/dot_general | solution.py:193
  117.4 1.9 %fusion.1 = f32[512,512]{1,0:T(8,128)S(1)} fusion(bf16[672,512]{1,0:T(8,128)(2,1)} %collective-permute-done.16, bf16[4,512,672]{2,1,0:T(8,128)(2,1)} %get-tuple-element.39.far_ref, s32[]{:T(128)S(6)} %select_n.74), kind=kOutput, calls=%fused_computation.6 | convolution fusion | flops 352321536 | bytes 2523140 | tf_op jit(solution)/shard_map/dot_general | solution.py:193
  119.7 1.2 shard_map.120.q_ref
  120.9 2.1 %shard_map.121 = (f32[512,512]{1,0:T(8,128)S(1)}, f32[512,512]{1,0:T(8,128)S(1)}) custom-call(bf16[512,512]{1,0:T(8,128)(2,1)S(1)} %shard_map.120.q_ref, bf16[512,512]{1,0:T(8,128)(2,1)S(1)} %shard_map.116.k_ref.v_ref, bf16[512,512]{1,0:T(8,128)(2,1)S(1)} %shard_map.116.k_ref.v_ref), custom_call_target="tpu_custom_call" | custom-call | tf_op jit(solution)/shard_map/pallas_call | solution.py:288
  123.0 9.1 %collective-permute-done.18.k2_ref.v2_ref = bf16[512,512]{1,0:T(8,128)(2,1)S(1)} collective-permute-done((bf16[512,512]{1,0:T(8,128)(2,1)S(1)}, bf16[512,512]{1,0:T(8,128)(2,1)S(1)}, u32[]{:S(2)}, u32[]{:S(2)}) %collective-permute-start.18) | collective-permute-done | bytes 524320 | tf_op jit(solution)/shard_map/ppermute | solution.py:33
  132.2 3.5 %shard_map.122 = bf16[512,512]{1,0:T(8,128)(2,1)S(1)} custom-call(s32[2]{0:T(128)S(1)} %add_convert_fusion.1.valid, bf16[512,512]{1,0:T(8,128)(2,1)S(1)} %shard_map.120.q_ref, bf16[512,512]{1,0:T(8,128)(2,1)S(1)} %collective-permute-done.17.k1_ref.v1_ref, bf16[512,512]{1,0:T(8,128)(2,1)S(1)} %collective-permute-done.17.k1_ref.v1_ref, ...), custom_call_target="tpu_custom_call" | custom-call | tf_op jit(solution)/shard_map/pallas_call | solution.py:309
  135.8 18.9 %all-gather.4.cloned.1.call-done.weight_ref = bf16[2688,1024]{1,0:T(8,128)(2,1)} async-done(((bf16[168,1024]{1,0:T(8,128)(2,1)}), bf16[2688,1024]{1,0:T(8,128)(2,1)}) %all-gather.4.cloned.1.call-update) | async-done | bytes 5505040 | tf_op jit(solution)/shard_map/all_gather | solution.py:397
  154.8 2.6 %copy-done = bf16[2688,1024]{1,0:T(8,128)(2,1)S(1)} copy-done((bf16[2688,1024]{1,0:T(8,128)(2,1)S(1)}, bf16[2688,1024]{1,0:T(8,128)(2,1)}, u32[]{:S(2)}) %copy-start) | copy-done | bytes 5505048
  157.4 2.2 %shard_map.124 = bf16[1344,512]{1,0:T(8,128)(2,1)S(1)} custom-call(s32[1]{0:T(128)} %bitcast.21.half, bf16[2688,1024]{1,0:T(8,128)(2,1)S(1)} %copy-done, bf16[512,1024]{1,0:T(8,128)(2,1)S(1)} %constant_dynamic-update-slice_fusion.context_ref), custom_call_target="tpu_custom_call" | custom-call | tf_op jit(solution)/shard_map/pallas_call | solution.py:334
  159.9 2.2 %shard_map.123 = f32[1344,512]{1,0:T(8,128)S(1)} custom-call(s32[1]{0:T(128)} %bitcast.half, bf16[2688,1024]{1,0:T(8,128)(2,1)S(1)} %copy-done.1, bf16[512,1024]{1,0:T(8,128)(2,1)S(1)} %constant_dynamic-update-slice_fusion.context_ref), custom_call_target="tpu_custom_call" | custom-call | tf_op jit(solution)/shard_map/pallas_call | solution.py:334
  162.2 0.6 collective-permute-done.20
  162.8 0.5 multiply_reduce_fusion
  163.9 2.8 %collective-permute-start.23 = (f32[512]{0:T(512)S(1)}, f32[512]{0:T(512)S(1)}, u32[]{:S(2)}, u32[]{:S(2)}) collective-permute-start(f32[512]{0:T(512)S(1)} %multiply_reduce_fusion), channel_id=1, source_target_pairs={{0,3},{1,2},{2,1},{3,0},{4,7},{5,6},{6,5},{7,4},{8,11},{9,10},{10,... | collective-permute-start | bytes 6152 | tf_op jit(solution)/shard_map/ppermute | solution.py:423
  166.8 1.9 %collective-permute-done.22 = f32[512]{0:T(512)S(1)} collective-permute-done((f32[512]{0:T(512)S(1)}, f32[512]{0:T(512)S(1)}, u32[]{:S(2)}, u32[]{:S(2)}) %collective-permute-start.22) | collective-permute-done | bytes 2080 | tf_op jit(solution)/shard_map/ppermute | solution.py:423
  168.7 1.7 fusion
  (58 shorter events, 2.1 us)
Async XLA Ops:
  6.5 58.6 %all-gather.6.cloned.1.call-start = ((), (), s32[]{:S(2)}) async-start(), calls=%async_computation.1 | async-start | bytes 6881280 | tf_op jit(solution)/shard_map/all_gather | solution.py:358
  7.3 147.4 %all-gather.4.cloned.1.call-start = ((), (), s32[]{:S(2)}) async-start(), calls=%async_computation | async-start | bytes 5849088 | tf_op jit(solution)/shard_map/all_gather | solution.py:397
  9.1 10.0 %collective-permute-start.5 = (bf16[168,1024]{1,0:T(8,128)(2,1)}, bf16[168,1024]{1,0:T(8,128)(2,1)S(1)}, u32[]{:S(2)}, u32[]{:S(2)}) collective-permute-start(bf16[168,1024]{1,0:T(8,128)(2,1)} %shard_map.109.refs_0_), channel_id=1, source_target_pairs={{0,64},{64,0},{1,65},{65,1},{2,66},{66,2},{3,67},{67,3},{4,68},{68... | collective-permute-start | bytes 1032200 | tf_op jit(solution)/shard_map/ppermute | solution.py:28
  9.5 11.6 %collective-permute-start = (bf16[168,1024]{1,0:T(8,128)(2,1)}, bf16[168,1024]{1,0:T(8,128)(2,1)S(1)}, u32[]{:S(2)}, u32[]{:S(2)}) collective-permute-start(bf16[168,1024]{1,0:T(8,128)(2,1)} %shard_map.109.refs_0_), channel_id=1, source_target_pairs={{0,16},{16,32},{32,48},{48,0},{1,17},{17,33},{33,49},{49,1},{2,18}... | collective-permute-start | bytes 1032200 | tf_op jit(solution)/shard_map/ppermute | solution.py:28
  11.0 16.2 %collective-permute-start.1 = (bf16[168,1024]{1,0:T(8,128)(2,1)}, bf16[168,1024]{1,0:T(8,128)(2,1)S(1)}, u32[]{:S(2)}, u32[]{:S(2)}) collective-permute-start(bf16[168,1024]{1,0:T(8,128)(2,1)} %shard_map.109.refs_0_), channel_id=1, source_target_pairs={{0,48},{16,0},{32,16},{48,32},{1,49},{17,1},{33,17},{49,33},{2,50}... | collective-permute-start | bytes 1032200 | tf_op jit(solution)/shard_map/ppermute | solution.py:28
  12.8 16.1 %collective-permute-start.2 = (bf16[168,1024]{1,0:T(8,128)(2,1)}, bf16[168,1024]{1,0:T(8,128)(2,1)S(1)}, u32[]{:S(2)}, u32[]{:S(2)}) collective-permute-start(bf16[168,1024]{1,0:T(8,128)(2,1)} %shard_map.109.refs_0_), channel_id=1, source_target_pairs={{0,32},{16,48},{32,0},{48,16},{1,33},{17,49},{33,1},{49,17},{2,34}... | collective-permute-start | bytes 1032200 | tf_op jit(solution)/shard_map/ppermute | solution.py:28
  19.1 14.1 %collective-permute-start.6 = (bf16[168,1024]{1,0:T(8,128)(2,1)S(1)}, bf16[168,1024]{1,0:T(8,128)(2,1)S(1)}, u32[]{:S(2)}, u32[]{:S(2)}) collective-permute-start(bf16[168,1024]{1,0:T(8,128)(2,1)S(1)} %collective-permute-done.5.refs_0_), channel_id=1, source_target_pairs={{0,4},{4,8},{8,12},{12,0},{1,5},{5,9},{9,13},{13,1},{2,6},{6,10},{... | collective-permute-start | bytes 1032200 | tf_op jit(solution)/shard_map/ppermute | solution.py:28
  21.0 12.2 %collective-permute-start.7 = (bf16[168,1024]{1,0:T(8,128)(2,1)S(1)}, bf16[168,1024]{1,0:T(8,128)(2,1)}, u32[]{:S(2)}, u32[]{:S(2)}) collective-permute-start(bf16[168,1024]{1,0:T(8,128)(2,1)S(1)} %collective-permute-done.5.refs_0_), channel_id=1, source_target_pairs={{0,12},{4,0},{8,4},{12,8},{1,13},{5,1},{9,5},{13,9},{2,14},{6,2},{... | collective-permute-start | bytes 1032200 | tf_op jit(solution)/shard_map/ppermute | solution.py:28
  21.1 19.5 %collective-permute-start.8 = (bf16[168,1024]{1,0:T(8,128)(2,1)S(1)}, bf16[168,1024]{1,0:T(8,128)(2,1)}, u32[]{:S(2)}, u32[]{:S(2)}) collective-permute-start(bf16[168,1024]{1,0:T(8,128)(2,1)S(1)} %collective-permute-done.5.refs_0_), channel_id=1, source_target_pairs={{0,8},{4,12},{8,0},{12,4},{1,9},{5,13},{9,1},{13,5},{2,10},{6,14},... | collective-permute-start | bytes 1032200 | tf_op jit(solution)/shard_map/ppermute | solution.py:28
  28.8 1.0 copy-start.4
  30.6 42.8 %copy-start.2 = (bf16[4,168,1024]{2,1,0:T(8,128)(2,1)}, bf16[4,168,1024]{2,1,0:T(8,128)(2,1)S(1)}, u32[]{:S(2)}) copy-start(bf16[4,168,1024]{2,1,0:T(8,128)(2,1)S(1)} %shard_map.110) | copy-start | bytes 4128772
  30.6 42.8 %collective-permute-start.3 = (bf16[672,1024]{1,0:T(8,128)(2,1)S(1)}, bf16[672,1024]{1,0:T(8,128)(2,1)S(1)}, u32[]{:S(2)}, u32[]{:S(2)}) collective-permute-start(bf16[672,1024]{1,0:T(8,128)(2,1)S(1)} %bitcast.40), channel_id=1, source_target_pairs={{0,4},{4,8},{8,12},{12,0},{1,5},{5,9},{9,13},{13,1},{2,6},{6,10},{... | collective-permute-start | bytes 4128776 | tf_op jit(solution)/shard_map/ppermute | solution.py:28
  32.6 40.8 %collective-permute-start.4 = (bf16[672,1024]{1,0:T(8,128)(2,1)S(1)}, bf16[672,1024]{1,0:T(8,128)(2,1)}, u32[]{:S(2)}, u32[]{:S(2)}) collective-permute-start(bf16[672,1024]{1,0:T(8,128)(2,1)S(1)} %bitcast.41), channel_id=1, source_target_pairs={{0,12},{4,0},{8,4},{12,8},{1,13},{5,1},{9,5},{13,9},{2,14},{6,2},{... | collective-permute-start | bytes 4128776 | tf_op jit(solution)/shard_map/ppermute | solution.py:28
  43.9 29.5 %collective-permute-start.10 = (bf16[672,1024]{1,0:T(8,128)(2,1)}, bf16[672,1024]{1,0:T(8,128)(2,1)}, u32[]{:S(2)}, u32[]{:S(2)}) collective-permute-start(bf16[672,1024]{1,0:T(8,128)(2,1)} %bitcast.3.refs_3_), channel_id=1, source_target_pairs={{0,48},{16,0},{32,16},{48,32},{1,49},{17,1},{33,17},{49,33},{2,50}... | collective-permute-start | bytes 4128776 | tf_op jit(solution)/shard_map/ppermute | solution.py:28
  46.6 28.7 %collective-permute-start.9 = (bf16[672,1024]{1,0:T(8,128)(2,1)}, bf16[672,1024]{1,0:T(8,128)(2,1)}, u32[]{:S(2)}, u32[]{:S(2)}) collective-permute-start(bf16[672,1024]{1,0:T(8,128)(2,1)} %bitcast.3.refs_3_), channel_id=1, source_target_pairs={{0,16},{16,32},{32,48},{48,0},{1,17},{17,33},{33,49},{49,1},{2,18}... | collective-permute-start | bytes 4128776 | tf_op jit(solution)/shard_map/ppermute | solution.py:28
  46.7 9.3 %collective-permute-start.11 = (bf16[168,512]{1,0:T(8,128)(2,1)}, bf16[168,512]{1,0:T(8,128)(2,1)S(1)}, u32[]{:S(2)}, u32[]{:S(2)}) collective-permute-start(bf16[168,512]{1,0:T(8,128)(2,1)} %bitcast.49), channel_id=1, source_target_pairs={{0,64},{2,0},{64,66},{66,2},{1,65},{3,1},{65,67},{67,3},{4,68},{6,... | collective-permute-start | bytes 516104 | tf_op jit(solution)/shard_map/ppermute | solution.py:373
  56.0 7.8 %copy-start.11 = (bf16[168,512]{1,0:T(8,128)(2,1)}, bf16[168,512]{1,0:T(8,128)(2,1)S(1)}, u32[]{:S(2)}) copy-start(bf16[168,512]{1,0:T(8,128)(2,1)S(1)} %collective-permute-done.11) | copy-start | bytes 516100
  56.0 17.3 %collective-permute-start.12 = (bf16[168,512]{1,0:T(8,128)(2,1)}, bf16[168,512]{1,0:T(8,128)(2,1)}, u32[]{:S(2)}, u32[]{:S(2)}) collective-permute-start(bf16[168,512]{1,0:T(8,128)(2,1)} %bitcast.50), channel_id=1, source_target_pairs={{64,2},{2,64},{65,3},{3,65},{68,6},{6,68},{69,7},{7,69},{72,10},{1... | collective-permute-start | bytes 516104 | tf_op jit(solution)/shard_map/ppermute | solution.py:374
  65.2 10.2 %copy-start.10 = (bf16[512,168]{0,1:T(8,128)(2,1)S(1)}, bf16[512,168]{0,1:T(8,128)(2,1)}, u32[]{:S(2)}) copy-start(bf16[512,168]{0,1:T(8,128)(2,1)} %param.15) | copy-start | bytes 516100
  65.2 10.2 %copy-start.12 = (bf16[168,512]{1,0:T(8,128)(2,1)S(1)}, bf16[168,512]{1,0:T(8,128)(2,1)}, u32[]{:S(2)}) copy-start(bf16[168,512]{1,0:T(8,128)(2,1)} %copy-done.11) | copy-start | bytes 516100
  73.4 8.3 %copy-start.3 = (bf16[672,1024]{1,0:T(8,128)(2,1)}, bf16[672,1024]{1,0:T(8,128)(2,1)S(1)}, u32[]{:S(2)}) copy-start(bf16[672,1024]{1,0:T(8,128)(2,1)S(1)} %collective-permute-done.3.refs_1_.value_ref) | copy-start | bytes 4128772
  78.3 13.6 %collective-permute-start.13 = (bf16[672,512]{1,0:T(8,128)(2,1)S(1)}, bf16[672,512]{1,0:T(8,128)(2,1)}, u32[]{:S(2)}, u32[]{:S(2)}) collective-permute-start(bf16[672,512]{1,0:T(8,128)(2,1)S(1)} %shard_map.114), channel_id=1, source_target_pairs={{0,12},{4,0},{8,4},{12,8},{1,13},{5,1},{9,5},{13,9},{2,14},{6,2},{... | collective-permute-start | bytes 2064392 | tf_op jit(solution)/shard_map/ppermute | solution.py:28
  80.6 17.0 %collective-permute-start.14 = (bf16[672,512]{1,0:T(8,128)(2,1)S(1)}, bf16[672,512]{1,0:T(8,128)(2,1)}, u32[]{:S(2)}, u32[]{:S(2)}) collective-permute-start(bf16[672,512]{1,0:T(8,128)(2,1)S(1)} %shard_map.115), channel_id=1, source_target_pairs={{0,48},{16,0},{32,16},{48,32},{1,49},{17,1},{33,17},{49,33},{2,50}... | collective-permute-start | bytes 2064392 | tf_op jit(solution)/shard_map/ppermute | solution.py:28
  81.8 33.6 %collective-permute-start.15 = (bf16[672,512]{1,0:T(8,128)(2,1)S(1)}, bf16[672,512]{1,0:T(8,128)(2,1)}, u32[]{:S(2)}, u32[]{:S(2)}) collective-permute-start(bf16[672,512]{1,0:T(8,128)(2,1)S(1)} %shard_map.118), channel_id=1, source_target_pairs={{0,4},{4,8},{8,12},{12,0},{1,5},{5,9},{9,13},{13,1},{2,6},{6,10},{... | collective-permute-start | bytes 2064392 | tf_op jit(solution)/shard_map/ppermute | solution.py:28
  84.5 32.9 %collective-permute-start.16 = (bf16[672,512]{1,0:T(8,128)(2,1)S(1)}, bf16[672,512]{1,0:T(8,128)(2,1)}, u32[]{:S(2)}, u32[]{:S(2)}) collective-permute-start(bf16[672,512]{1,0:T(8,128)(2,1)S(1)} %shard_map.119), channel_id=1, source_target_pairs={{0,16},{16,32},{32,48},{48,0},{1,17},{17,33},{33,49},{49,1},{2,18}... | collective-permute-start | bytes 2064392 | tf_op jit(solution)/shard_map/ppermute | solution.py:28
  91.1 8.5 %copy-start.8 = (f32[512,512]{1,0:T(8,128)S(1)}, f32[512,512]{1,0:T(8,128)}, u32[]{:S(2)}) copy-start(f32[512,512]{1,0:T(8,128)} %shard_map.113) | copy-start | bytes 3145732
  99.6 1.9 %copy-start.5 = (f32[128]{0:T(128)S(1)}, f32[128]{0:T(128)}, u32[]{:S(2)}) copy-start(f32[128]{0:T(128)} %param.19) | copy-start | bytes 1540
  102.2 20.8 %collective-permute-start.17 = (bf16[512,512]{1,0:T(8,128)(2,1)S(1)}, bf16[512,512]{1,0:T(8,128)(2,1)S(1)}, u32[]{:S(2)}, u32[]{:S(2)}) collective-permute-start(bf16[512,512]{1,0:T(8,128)(2,1)S(1)} %shard_map.116.k_ref.v_ref), channel_id=1, source_target_pairs={{0,4},{4,8},{8,12},{12,16},{16,20},{20,24},{24,28},{28,32},{32,36}... | collective-permute-start | bytes 1572872 | tf_op jit(solution)/shard_map/ppermute | solution.py:33
  104.1 28.0 %collective-permute-start.18 = (bf16[512,512]{1,0:T(8,128)(2,1)S(1)}, bf16[512,512]{1,0:T(8,128)(2,1)S(1)}, u32[]{:S(2)}, u32[]{:S(2)}) collective-permute-start(bf16[512,512]{1,0:T(8,128)(2,1)S(1)} %shard_map.116.k_ref.v_ref), channel_id=1, source_target_pairs={{0,8},{4,12},{8,16},{12,20},{16,24},{20,28},{24,32},{28,36},{32,40... | collective-permute-start | bytes 1572872 | tf_op jit(solution)/shard_map/ppermute | solution.py:33
  115.4 4.0 %copy-start.9 = (f32[512,512]{1,0:T(8,128)S(1)}, f32[512,512]{1,0:T(8,128)}, u32[]{:S(2)}) copy-start(f32[512,512]{1,0:T(8,128)} %shard_map.117) | copy-start | bytes 3145732
  117.4 2.3 %copy-start.6 = (f32[128]{0:T(128)S(1)}, f32[128]{0:T(128)}, u32[]{:S(2)}) copy-start(f32[128]{0:T(128)} %param.18) | copy-start | bytes 1540
  135.7 19.0 %collective-permute-start.19 = (bf16[512,512]{1,0:T(8,128)(2,1)S(1)}, bf16[512,512]{1,0:T(8,128)(2,1)S(1)}, u32[]{:S(2)}, u32[]{:S(2)}) collective-permute-start(bf16[512,512]{1,0:T(8,128)(2,1)S(1)} %shard_map.122), channel_id=1, source_target_pairs={{0,2},{2,0},{1,3},{3,1},{4,6},{6,4},{5,7},{7,5},{8,10},{10,8},{9,1... | collective-permute-start | bytes 1572872 | tf_op jit(solution)/shard_map/ppermute | solution.py:28
  154.8 2.6 %copy-start = (bf16[2688,1024]{1,0:T(8,128)(2,1)S(1)}, bf16[2688,1024]{1,0:T(8,128)(2,1)}, u32[]{:S(2)}) copy-start(bf16[2688,1024]{1,0:T(8,128)(2,1)} %all-gather.4.cloned.1.call-done.weight_ref) | copy-start | bytes 16515076
  157.4 2.6 %copy-start.1 = (bf16[2688,1024]{1,0:T(8,128)(2,1)S(1)}, bf16[2688,1024]{1,0:T(8,128)(2,1)}, u32[]{:S(2)}) copy-start(bf16[2688,1024]{1,0:T(8,128)(2,1)} %all-gather.4.cloned.1.call-done.weight_ref) | copy-start | bytes 16515076
  159.6 3.2 %collective-permute-start.20 = (bf16[1344,512]{1,0:T(8,128)(2,1)S(1)}, bf16[1344,512]{1,0:T(8,128)(2,1)S(1)}, u32[]{:S(2)}, u32[]{:S(2)}) collective-permute-start(bf16[1344,512]{1,0:T(8,128)(2,1)S(1)} %shard_map.124), channel_id=1, source_target_pairs={{0,1},{1,0},{2,3},{3,2},{4,5},{5,4},{6,7},{7,6},{8,9},{9,8},{10,11... | collective-permute-start | bytes 4128776 | tf_op jit(solution)/shard_map/ppermute | solution.py:28
  162.2 6.5 %copy-start.7 = (bf16[512,1344]{0,1:T(8,128)(2,1)S(1)}, bf16[512,1344]{0,1:T(8,128)(2,1)}, u32[]{:S(2)}) copy-start(bf16[512,1344]{0,1:T(8,128)(2,1)} %param.11) | copy-start | bytes 4128772
  162.2 6.5 %copy-start.13 = (f32[1344]{0:T(1024)S(1)}, f32[1344]{0:T(1024)}, u32[]{:S(2)}) copy-start(f32[1344]{0:T(1024)} %param.17) | copy-start | bytes 16132
  163.3 3.4 %collective-permute-start.21 = (f32[512]{0:T(512)S(1)}, f32[512]{0:T(512)S(1)}, u32[]{:S(2)}, u32[]{:S(2)}) collective-permute-start(f32[512]{0:T(512)S(1)} %multiply_reduce_fusion), channel_id=1, source_target_pairs={{0,1},{1,0},{2,3},{3,2},{4,5},{5,4},{6,7},{7,6},{8,9},{9,8},{10,11... | collective-permute-start | bytes 6152 | tf_op jit(solution)/shard_map/ppermute | solution.py:423
  163.5 5.1 %collective-permute-start.22 = (f32[512]{0:T(512)S(1)}, f32[512]{0:T(512)S(1)}, u32[]{:S(2)}, u32[]{:S(2)}) collective-permute-start(f32[512]{0:T(512)S(1)} %multiply_reduce_fusion), channel_id=1, source_target_pairs={{0,2},{1,3},{2,0},{3,1},{4,6},{5,7},{6,4},{7,5},{8,10},{9,11},{10,... | collective-permute-start | bytes 6152 | tf_op jit(solution)/shard_map/ppermute | solution.py:423
  163.9 4.7 %collective-permute-start.23 = (f32[512]{0:T(512)S(1)}, f32[512]{0:T(512)S(1)}, u32[]{:S(2)}, u32[]{:S(2)}) collective-permute-start(f32[512]{0:T(512)S(1)} %multiply_reduce_fusion), channel_id=1, source_target_pairs={{0,3},{1,2},{2,1},{3,0},{4,7},{5,6},{6,5},{7,4},{8,11},{9,10},{10,... | collective-permute-start | bytes 6152 | tf_op jit(solution)/shard_map/ppermute | solution.py:423
Sparse Core Ops, SparseCore 0:
  9.0 50.7 all-gather.5
  77.3 77.3 all-gather.3

commit v8 on v7

--- a/solution.py
+++ b/solution.py
@@ -420,8 +420,8 @@
     kept, received = lax.optimization_barrier((half_of(c, jnp.float32), received))
     share = (kept + received.astype(jnp.float32)).T
     squares = jnp.sum(share * share, axis=1)
-    others = [lax.ppermute(squares, MP, [(i, i ^ bit) for i in range(4)]) for bit in (2, 3, 1)]
-    total = (squares + others[2]) + (others[0] + others[1])
+    squares = squares + shift(squares, "c", 1)
+    total = squares + shift(squares, "yh", 1)
     scale_rows = lax.rsqrt(total / MODEL_WIDTH + epsilon)
     return (tokens.astype(jnp.float32) + share * scale_rows[:, None] * post_gain).astype(
         jnp.bfloat16

time: 180 us -> 179 us (level); the launches traced: 177 us -> 178 us
  waiting for transfers between devices: 61.5 us -> 65.4 us
  starting transfers between devices: 36.3 us -> 33.5 us
    ppermute x17 -> x19, waiting for transfers between devices: 25.7 us -> 31.4 us  [shift(): lax.ppermute(value, axis, [(i, (i + step) % count) for i in range(count)])]
    ppermute x3 -> x0, starting transfers between devices: 3.44 us -> none  [local(): lax.ppermute(squares, MP, [(i, i ^ bit) for i in range(4)])]
    ppermute x3 -> x0, waiting for transfers between devices: 1.88 us -> none  [local(): lax.ppermute(squares, MP, [(i, i ^ bit) for i in range(4)])]
    ppermute x17 -> x19, starting transfers between devices: 19.9 us -> 20.4 us  [shift(): lax.ppermute(value, axis, [(i, (i + step) % count) for i in range(count)])]
  transfers between devices with their start and end apart: 26 -> 25, of which waited for: 13 -> 14; matrix products, arithmetic and copies ran while one was open for 9% -> 9% of each run, Pallas kernels for 22% -> 22%
where the time goes in v8:
time: 179 us; the launch traced here: 178 us
  waiting for transfers between devices  65.4 us (37%)
  Pallas kernels  41.4 us (23%)
  starting transfers between devices  33.5 us (19%)
  between operations  13.8 us (8%)
  other arithmetic  8.82 us (5%)
  matrix products  7.72 us (4%)
  local copies, waits for them, and re-layouts  7.5 us (4%)
    ppermute x19, waiting for transfers between devices, shift(): lax.ppermute(value, axis, [(i, (i + step) % count) for i in range(count)])  31.4 us
    ppermute x19, starting transfers between devices, shift(): lax.ppermute(value, axis, [(i, (i + step) % count) for i in range(count)])  20.4 us
    all_gather x1, waiting for transfers between devices, local(): out_all = lax.all_gather(pair, ('x', 'z'), axis=0, tiled=True)  18.9 us
    pallas_call x2, Pallas kernels, early_product(): pl.pallas_call(functools.partial(early_kernel, len(near_weights), count,...  12 us
    ppermute x2, waiting for transfers between devices, from_behind(): lax.ppermute(value, SEQ, [(source, source + steps) for source in range(co...  9.17 us
    pallas_call x1, Pallas kernels, norm_parts(): pl.pallas_call(norm_kernel, grid_spec=pltpu.PrefetchScalarGridSpec(num_sc...  8.14 us
    dot_general x4, matrix products, product(): return jnp.dot(left, right, preferred_element_type=jnp.float32)  7.72 us
    ppermute x2, starting transfers between devices, from_behind(): lax.ppermute(value, SEQ, [(source, source + steps) for source in range(co...  7.22 us
  transfers between devices with their start and end apart: 25, of which 14 were waited for; matrix products, arithmetic and copies ran while one was open for 9% of the time, Pallas kernels for 22%

profile of v8, /device:TPU:40, one launch (start us, length us, event | category | flops | bytes accessed | tf_op | source)
XLA Modules:
  0.0 178.2 jit_solution(12998459372740771120)
XLA Ops:
  6.5 0.7 all-gather.6.cloned.1.call-update
  7.3 1.8 shard_map.109.refs_0_
  9.1 0.4 collective-permute-start.5
  9.5 1.5 collective-permute-start
  11.0 1.7 collective-permute-start.1
  12.8 1.8 %collective-permute-start.2 = (bf16[168,1024]{1,0:T(8,128)(2,1)}, bf16[168,1024]{1,0:T(8,128)(2,1)S(1)}, u32[]{:S(2)}, u32[]{:S(2)}) collective-permute-start(bf16[168,1024]{1,0:T(8,128)(2,1)} %shard_map.109.refs_0_), channel_id=1, source_target_pairs={{0,32},{16,48},{32,0},{48,16},{1,33},{17,49},{33,1},{49,17},{2,34}... | collective-permute-start | bytes 1032200 | tf_op jit(solution)/shard_map/ppermute | solution.py:28
  14.6 4.5 %collective-permute-done.5.refs_0_ = bf16[168,1024]{1,0:T(8,128)(2,1)S(1)} collective-permute-done((bf16[168,1024]{1,0:T(8,128)(2,1)}, bf16[168,1024]{1,0:T(8,128)(2,1)S(1)}, u32[]{:S(2)}, u32[]{:S(2)}) %collective-permute-start.5) | collective-permute-done | bytes 344096 | tf_op jit(solution)/shard_map/ppermute | solution.py:28
  19.1 1.9 %collective-permute-start.6 = (bf16[168,1024]{1,0:T(8,128)(2,1)S(1)}, bf16[168,1024]{1,0:T(8,128)(2,1)S(1)}, u32[]{:S(2)}, u32[]{:S(2)}) collective-permute-start(bf16[168,1024]{1,0:T(8,128)(2,1)S(1)} %collective-permute-done.5.refs_0_), channel_id=1, source_target_pairs={{0,4},{4,8},{8,12},{12,0},{1,5},{5,9},{9,13},{13,1},{2,6},{6,10},{... | collective-permute-start | bytes 1032200 | tf_op jit(solution)/shard_map/ppermute | solution.py:28
  21.1 3.0 %collective-permute-start.8 = (bf16[168,1024]{1,0:T(8,128)(2,1)S(1)}, bf16[168,1024]{1,0:T(8,128)(2,1)}, u32[]{:S(2)}, u32[]{:S(2)}) collective-permute-start(bf16[168,1024]{1,0:T(8,128)(2,1)S(1)} %collective-permute-done.5.refs_0_), channel_id=1, source_target_pairs={{0,8},{4,12},{8,0},{12,4},{1,9},{5,13},{9,1},{13,5},{2,10},{6,14},... | collective-permute-start | bytes 1032200 | tf_op jit(solution)/shard_map/ppermute | solution.py:28
  24.1 0.7 and_select_fusion
  24.8 2.5 %collective-permute-done.1.refs_2_ = bf16[168,1024]{1,0:T(8,128)(2,1)S(1)} collective-permute-done((bf16[168,1024]{1,0:T(8,128)(2,1)}, bf16[168,1024]{1,0:T(8,128)(2,1)S(1)}, u32[]{:S(2)}, u32[]{:S(2)}) %collective-permute-start.1) | collective-permute-done | bytes 344096 | tf_op jit(solution)/shard_map/ppermute | solution.py:28
  27.2 1.6 collective-permute-done.2.refs_3_
  28.8 1.0 copy-done.4
  29.8 0.8 shard_map.110
  30.6 2.0 %collective-permute-start.3 = (bf16[672,1024]{1,0:T(8,128)(2,1)S(1)}, bf16[672,1024]{1,0:T(8,128)(2,1)S(1)}, u32[]{:S(2)}, u32[]{:S(2)}) collective-permute-start(bf16[672,1024]{1,0:T(8,128)(2,1)S(1)} %bitcast.40), channel_id=1, source_target_pairs={{0,4},{4,8},{8,12},{12,0},{1,5},{5,9},{9,13},{13,1},{2,6},{6,10},{... | collective-permute-start | bytes 4128776 | tf_op jit(solution)/shard_map/ppermute | solution.py:28
  32.7 0.6 collective-permute-done.6.refs_1_
  33.2 7.3 %collective-permute-done.8.refs_3_ = bf16[168,1024]{1,0:T(8,128)(2,1)} collective-permute-done((bf16[168,1024]{1,0:T(8,128)(2,1)S(1)}, bf16[168,1024]{1,0:T(8,128)(2,1)}, u32[]{:S(2)}, u32[]{:S(2)}) %collective-permute-start.8) | collective-permute-done | bytes 344096 | tf_op jit(solution)/shard_map/ppermute | solution.py:28
  40.6 3.3 %shard_map.111 = bf16[4,168,1024]{2,1,0:T(8,128)(2,1)} custom-call(s32[4]{0:T(128)S(1)} %get-tuple-element.62.slots, bf16[168,1024]{1,0:T(8,128)(2,1)S(1)} %collective-permute-done.5.refs_0_, bf16[168,1024]{1,0:T(8,128)(2,1)S(1)} %collective-permute-done.6.refs_1_, bf16[168,1024]{1,0:T(8,128)(2,1)} %collective-permute-done.7.refs_2_, ...), custom_call_target="tpu_custom_call" | custom-call | tf_op jit(solution)/shard_map/pallas_call | solution.py:50
  43.9 2.8 %collective-permute-start.10 = (bf16[672,1024]{1,0:T(8,128)(2,1)}, bf16[672,1024]{1,0:T(8,128)(2,1)}, u32[]{:S(2)}, u32[]{:S(2)}) collective-permute-start(bf16[672,1024]{1,0:T(8,128)(2,1)} %bitcast.3.refs_3_), channel_id=1, source_target_pairs={{0,48},{16,0},{32,16},{48,32},{1,49},{17,1},{33,17},{49,33},{2,50}... | collective-permute-start | bytes 4128776 | tf_op jit(solution)/shard_map/ppermute | solution.py:28
  46.7 2.4 %collective-permute-start.11 = (bf16[168,512]{1,0:T(8,128)(2,1)}, bf16[168,512]{1,0:T(8,128)(2,1)S(1)}, u32[]{:S(2)}, u32[]{:S(2)}) collective-permute-start(bf16[168,512]{1,0:T(8,128)(2,1)} %bitcast.49), channel_id=1, source_target_pairs={{0,64},{2,0},{64,66},{66,2},{1,65},{3,1},{65,67},{67,3},{4,68},{6,... | collective-permute-start | bytes 516104 | tf_op jit(solution)/shard_map/ppermute | solution.py:373
  49.0 1.8 %fusion.15 = (f32[512,64]{1,0:T(8,128)S(1)}, f32[512,64]{1,0:T(8,128)}, f32[512,64]{1,0:T(8,128)}) fusion(f32[64]{0:T(128)S(1)} %multiply_power_fusion, f32[512]{0:T(512)S(1)} %add_convert_fusion), kind=kLoop, calls=%fused_computation.25 | loop fusion | flops 65536 | bytes 395520 | tf_op jit(solution)/shard_map/neg | solution.py:382
  50.8 5.2 %collective-permute-done.11 = bf16[168,512]{1,0:T(8,128)(2,1)S(1)} collective-permute-done((bf16[168,512]{1,0:T(8,128)(2,1)}, bf16[168,512]{1,0:T(8,128)(2,1)S(1)}, u32[]{:S(2)}, u32[]{:S(2)}) %collective-permute-start.11) | collective-permute-done | bytes 172064 | tf_op jit(solution)/shard_map/ppermute | solution.py:373
  56.0 3.5 %collective-permute-start.12 = (bf16[168,512]{1,0:T(8,128)(2,1)}, bf16[168,512]{1,0:T(8,128)(2,1)}, u32[]{:S(2)}, u32[]{:S(2)}) collective-permute-start(bf16[168,512]{1,0:T(8,128)(2,1)} %bitcast.50), channel_id=1, source_target_pairs={{64,2},{2,64},{65,3},{3,65},{68,6},{6,68},{69,7},{7,69},{72,10},{1... | collective-permute-start | bytes 516104 | tf_op jit(solution)/shard_map/ppermute | solution.py:374
  59.5 0.7 pad_add_fusion.side
  60.1 0.8 reshape.32
  61.0 1.4 reshape_reshape.3.far_gain
  62.4 0.7 reshape.33.near_gain
  63.2 0.6 stack.48.index
  63.8 1.3 pad_maximum_fusion.1
  65.1 8.1 %shard_map.112 = (bf16[4,512,672]{2,1,0:T(8,128)(2,1)}, bf16[4,512,672]{2,1,0:T(8,128)(2,1)}) custom-call(s32[2]{0:T(128)} %pad_add_fusion.side, bf16[2,2,1344,512]{3,2,1,0:T(8,128)(2,1)} %bitcast.46, bf16[2,2,1344,512]{3,2,1,0:T(8,128)(2,1)} %bitcast.47, f32[2,4,1,672]{3,2,1,0:T(1,128)} %reshape.33.near_gain, f32[2,4,1,672]{3,2,1,0:T(1,128)} %reshape_reshape.3.far_gain), custom_call_target="tpu_custom_call" | custom-call | tf_op jit(solution)/shard_map/pallas_call | solution.py:127
  73.3 2.1 %collective-permute-done.9.refs_4_.value_ref = bf16[672,1024]{1,0:T(8,128)(2,1)} collective-permute-done((bf16[672,1024]{1,0:T(8,128)(2,1)}, bf16[672,1024]{1,0:T(8,128)(2,1)}, u32[]{:S(2)}, u32[]{:S(2)}) %collective-permute-start.9) | collective-permute-done | bytes 1376288 | tf_op jit(solution)/shard_map/ppermute | solution.py:28
  75.4 1.0 broadcast_select_fusion.1
  76.3 0.8 pad_maximum_fusion
  77.1 1.1 shard_map.114
  78.3 1.2 collective-permute-start.13
  79.5 1.1 shard_map.115
  80.7 0.9 collective-permute-start.14
  81.7 1.5 collective-permute-start.15
  83.3 1.2 shard_map.119
  84.5 0.7 collective-permute-start.16
  85.1 6.0 %shard_map.113 = f32[512,512]{1,0:T(8,128)} custom-call(s32[6]{0:T(128)} %stack.48.index, bf16[4,512,672]{2,1,0:T(8,128)(2,1)} %get-tuple-element.38.near_ref, bf16[4,512,672]{2,1,0:T(8,128)(2,1)} %get-tuple-element.39.far_ref, bf16[672,1024]{1,0:T(8,128)(2,1)} %bitcast.42, bf16[672,1024]{1,0:T(8,128)(2,1)} %copy-done.3, ...), custom_call_target="tpu_custom_call" | custom-call | tf_op jit(solution)/shard_map/pallas_call | solution.py:169
  91.1 0.7 collective-permute-done.13
  91.9 5.8 %collective-permute-done.14 = bf16[672,512]{1,0:T(8,128)(2,1)} collective-permute-done((bf16[672,512]{1,0:T(8,128)(2,1)S(1)}, bf16[672,512]{1,0:T(8,128)(2,1)}, u32[]{:S(2)}, u32[]{:S(2)}) %collective-permute-start.14) | collective-permute-done | bytes 688160 | tf_op jit(solution)/shard_map/ppermute | solution.py:28
  97.6 1.9 %fusion.9 = f32[512,512]{1,0:T(8,128)S(1)} fusion(bf16[672,512]{1,0:T(8,128)(2,1)} %collective-permute-done.13, bf16[4,512,672]{2,1,0:T(8,128)(2,1)} %get-tuple-element.38.near_ref, s32[]{:T(128)S(6)} %select_n.72), kind=kOutput, calls=%fused_computation.12 | convolution fusion | flops 352321536 | bytes 2523140 | tf_op jit(solution)/shard_map/dot_general | solution.py:193
  99.5 1.9 %add_add_fusion.1.raw_ref = f32[512,512]{1,0:T(8,128)S(1)} fusion(f32[512,512]{1,0:T(8,128)S(1)} %copy-done.8, f32[512,512]{1,0:T(8,128)S(1)} %fusion.9, bf16[672,512]{1,0:T(8,128)(2,1)} %collective-permute-done.14, bf16[4,512,672]{2,1,0:T(8,128)(2,1)} %get-tuple-element.39.far_ref, s32[]{:T(128)S(6)} %select_n.74), kind=kOutput, calls=%fused_computation.5 | convolution fusion | flops 352845824 | bytes 4620292 | tf_op jit(solution)/shard_map/dot_general | solution.py:193
  101.5 0.7 shard_map.116.k_ref.v_ref
  102.2 1.9 %collective-permute-start.17 = (bf16[512,512]{1,0:T(8,128)(2,1)S(1)}, bf16[512,512]{1,0:T(8,128)(2,1)S(1)}, u32[]{:S(2)}, u32[]{:S(2)}) collective-permute-start(bf16[512,512]{1,0:T(8,128)(2,1)S(1)} %shard_map.116.k_ref.v_ref), channel_id=1, source_target_pairs={{0,4},{4,8},{8,12},{12,16},{16,20},{20,24},{24,28},{28,32},{32,36}... | collective-permute-start | bytes 1572872 | tf_op jit(solution)/shard_map/ppermute | solution.py:33
  104.1 5.3 %collective-permute-start.18 = (bf16[512,512]{1,0:T(8,128)(2,1)S(1)}, bf16[512,512]{1,0:T(8,128)(2,1)S(1)}, u32[]{:S(2)}, u32[]{:S(2)}) collective-permute-start(bf16[512,512]{1,0:T(8,128)(2,1)S(1)} %shard_map.116.k_ref.v_ref), channel_id=1, source_target_pairs={{0,8},{4,12},{8,16},{12,20},{16,24},{20,28},{24,32},{28,36},{32,40... | collective-permute-start | bytes 1572872 | tf_op jit(solution)/shard_map/ppermute | solution.py:33
  109.4 6.0 %shard_map.117 = f32[512,512]{1,0:T(8,128)} custom-call(s32[6]{0:T(128)} %stack.48.index, bf16[4,512,672]{2,1,0:T(8,128)(2,1)} %get-tuple-element.38.near_ref, bf16[4,512,672]{2,1,0:T(8,128)(2,1)} %get-tuple-element.39.far_ref, bf16[672,1024]{1,0:T(8,128)(2,1)} %bitcast.43, bf16[672,1024]{1,0:T(8,128)(2,1)} %copy-done.3, ...), custom_call_target="tpu_custom_call" | custom-call | tf_op jit(solution)/shard_map/pallas_call | solution.py:169
  115.4 2.0 %fusion.7 = f32[512,512]{1,0:T(8,128)S(1)} fusion(bf16[672,512]{1,0:T(8,128)(2,1)} %collective-permute-done.15, bf16[4,512,672]{2,1,0:T(8,128)(2,1)} %get-tuple-element.38.near_ref, s32[]{:T(128)S(6)} %select_n.72), kind=kOutput, calls=%fused_computation.10 | convolution fusion | flops 352321536 | bytes 2523140 | tf_op jit(solution)/shard_map/dot_general | solution.py:193
  117.4 1.9 %fusion.1 = f32[512,512]{1,0:T(8,128)S(1)} fusion(bf16[672,512]{1,0:T(8,128)(2,1)} %collective-permute-done.16, bf16[4,512,672]{2,1,0:T(8,128)(2,1)} %get-tuple-element.39.far_ref, s32[]{:T(128)S(6)} %select_n.74), kind=kOutput, calls=%fused_computation.6 | convolution fusion | flops 352321536 | bytes 2523140 | tf_op jit(solution)/shard_map/dot_general | solution.py:193
  119.7 1.2 shard_map.120.q_ref
  121.0 2.1 %shard_map.121 = (f32[512,512]{1,0:T(8,128)S(1)}, f32[512,512]{1,0:T(8,128)S(1)}) custom-call(bf16[512,512]{1,0:T(8,128)(2,1)S(1)} %shard_map.120.q_ref, bf16[512,512]{1,0:T(8,128)(2,1)S(1)} %shard_map.116.k_ref.v_ref, bf16[512,512]{1,0:T(8,128)(2,1)S(1)} %shard_map.116.k_ref.v_ref), custom_call_target="tpu_custom_call" | custom-call | tf_op jit(solution)/shard_map/pallas_call | solution.py:288
  123.1 9.2 %collective-permute-done.18.k2_ref.v2_ref = bf16[512,512]{1,0:T(8,128)(2,1)S(1)} collective-permute-done((bf16[512,512]{1,0:T(8,128)(2,1)S(1)}, bf16[512,512]{1,0:T(8,128)(2,1)S(1)}, u32[]{:S(2)}, u32[]{:S(2)}) %collective-permute-start.18) | collective-permute-done | bytes 524320 | tf_op jit(solution)/shard_map/ppermute | solution.py:33
  132.2 3.5 %shard_map.122 = bf16[512,512]{1,0:T(8,128)(2,1)S(1)} custom-call(s32[2]{0:T(128)S(1)} %add_convert_fusion.1.valid, bf16[512,512]{1,0:T(8,128)(2,1)S(1)} %shard_map.120.q_ref, bf16[512,512]{1,0:T(8,128)(2,1)S(1)} %collective-permute-done.17.k1_ref.v1_ref, bf16[512,512]{1,0:T(8,128)(2,1)S(1)} %collective-permute-done.17.k1_ref.v1_ref, ...), custom_call_target="tpu_custom_call" | custom-call | tf_op jit(solution)/shard_map/pallas_call | solution.py:309
  135.8 18.9 %all-gather.4.cloned.1.call-done.weight_ref = bf16[2688,1024]{1,0:T(8,128)(2,1)} async-done(((bf16[168,1024]{1,0:T(8,128)(2,1)}), bf16[2688,1024]{1,0:T(8,128)(2,1)}) %all-gather.4.cloned.1.call-update) | async-done | bytes 5505040 | tf_op jit(solution)/shard_map/all_gather | solution.py:397
  154.8 2.6 %copy-done = bf16[2688,1024]{1,0:T(8,128)(2,1)S(1)} copy-done((bf16[2688,1024]{1,0:T(8,128)(2,1)S(1)}, bf16[2688,1024]{1,0:T(8,128)(2,1)}, u32[]{:S(2)}) %copy-start) | copy-done | bytes 5505048
  157.4 2.2 %shard_map.124 = bf16[1344,512]{1,0:T(8,128)(2,1)S(1)} custom-call(s32[1]{0:T(128)} %bitcast.21.half, bf16[2688,1024]{1,0:T(8,128)(2,1)S(1)} %copy-done, bf16[512,1024]{1,0:T(8,128)(2,1)S(1)} %constant_dynamic-update-slice_fusion.context_ref), custom_call_target="tpu_custom_call" | custom-call | tf_op jit(solution)/shard_map/pallas_call | solution.py:334
  160.0 2.2 %shard_map.123 = f32[1344,512]{1,0:T(8,128)S(1)} custom-call(s32[1]{0:T(128)} %bitcast.half, bf16[2688,1024]{1,0:T(8,128)(2,1)S(1)} %copy-done.1, bf16[512,1024]{1,0:T(8,128)(2,1)S(1)} %constant_dynamic-update-slice_fusion.context_ref), custom_call_target="tpu_custom_call" | custom-call | tf_op jit(solution)/shard_map/pallas_call | solution.py:334
  162.2 0.6 collective-permute-done.20
  162.9 0.5 multiply_reduce_fusion
  163.6 1.0 collective-permute-done.21
  164.9 4.7 %collective-permute-done.22 = f32[512]{0:T(512)S(1)} collective-permute-done((f32[512]{0:T(512)S(1)}, f32[512]{0:T(512)S(1)}, u32[]{:S(2)}, u32[]{:S(2)}) %collective-permute-start.22) | collective-permute-done | bytes 2080 | tf_op jit(solution)/shard_map/ppermute | solution.py:28
  169.7 1.7 fusion
  (57 shorter events, 2.1 us)
Async XLA Ops:
  6.5 58.6 %all-gather.6.cloned.1.call-start = ((), (), s32[]{:S(2)}) async-start(), calls=%async_computation.1 | async-start | bytes 6881280 | tf_op jit(solution)/shard_map/all_gather | solution.py:358
  7.3 147.4 %all-gather.4.cloned.1.call-start = ((), (), s32[]{:S(2)}) async-start(), calls=%async_computation | async-start | bytes 5849088 | tf_op jit(solution)/shard_map/all_gather | solution.py:397
  9.1 10.0 %collective-permute-start.5 = (bf16[168,1024]{1,0:T(8,128)(2,1)}, bf16[168,1024]{1,0:T(8,128)(2,1)S(1)}, u32[]{:S(2)}, u32[]{:S(2)}) collective-permute-start(bf16[168,1024]{1,0:T(8,128)(2,1)} %shard_map.109.refs_0_), channel_id=1, source_target_pairs={{0,64},{64,0},{1,65},{65,1},{2,66},{66,2},{3,67},{67,3},{4,68},{68... | collective-permute-start | bytes 1032200 | tf_op jit(solution)/shard_map/ppermute | solution.py:28
  9.5 11.6 %collective-permute-start = (bf16[168,1024]{1,0:T(8,128)(2,1)}, bf16[168,1024]{1,0:T(8,128)(2,1)S(1)}, u32[]{:S(2)}, u32[]{:S(2)}) collective-permute-start(bf16[168,1024]{1,0:T(8,128)(2,1)} %shard_map.109.refs_0_), channel_id=1, source_target_pairs={{0,16},{16,32},{32,48},{48,0},{1,17},{17,33},{33,49},{49,1},{2,18}... | collective-permute-start | bytes 1032200 | tf_op jit(solution)/shard_map/ppermute | solution.py:28
  11.0 16.2 %collective-permute-start.1 = (bf16[168,1024]{1,0:T(8,128)(2,1)}, bf16[168,1024]{1,0:T(8,128)(2,1)S(1)}, u32[]{:S(2)}, u32[]{:S(2)}) collective-permute-start(bf16[168,1024]{1,0:T(8,128)(2,1)} %shard_map.109.refs_0_), channel_id=1, source_target_pairs={{0,48},{16,0},{32,16},{48,32},{1,49},{17,1},{33,17},{49,33},{2,50}... | collective-permute-start | bytes 1032200 | tf_op jit(solution)/shard_map/ppermute | solution.py:28
  12.8 16.1 %collective-permute-start.2 = (bf16[168,1024]{1,0:T(8,128)(2,1)}, bf16[168,1024]{1,0:T(8,128)(2,1)S(1)}, u32[]{:S(2)}, u32[]{:S(2)}) collective-permute-start(bf16[168,1024]{1,0:T(8,128)(2,1)} %shard_map.109.refs_0_), channel_id=1, source_target_pairs={{0,32},{16,48},{32,0},{48,16},{1,33},{17,49},{33,1},{49,17},{2,34}... | collective-permute-start | bytes 1032200 | tf_op jit(solution)/shard_map/ppermute | solution.py:28
  19.1 14.1 %collective-permute-start.6 = (bf16[168,1024]{1,0:T(8,128)(2,1)S(1)}, bf16[168,1024]{1,0:T(8,128)(2,1)S(1)}, u32[]{:S(2)}, u32[]{:S(2)}) collective-permute-start(bf16[168,1024]{1,0:T(8,128)(2,1)S(1)} %collective-permute-done.5.refs_0_), channel_id=1, source_target_pairs={{0,4},{4,8},{8,12},{12,0},{1,5},{5,9},{9,13},{13,1},{2,6},{6,10},{... | collective-permute-start | bytes 1032200 | tf_op jit(solution)/shard_map/ppermute | solution.py:28
  21.0 12.2 %collective-permute-start.7 = (bf16[168,1024]{1,0:T(8,128)(2,1)S(1)}, bf16[168,1024]{1,0:T(8,128)(2,1)}, u32[]{:S(2)}, u32[]{:S(2)}) collective-permute-start(bf16[168,1024]{1,0:T(8,128)(2,1)S(1)} %collective-permute-done.5.refs_0_), channel_id=1, source_target_pairs={{0,12},{4,0},{8,4},{12,8},{1,13},{5,1},{9,5},{13,9},{2,14},{6,2},{... | collective-permute-start | bytes 1032200 | tf_op jit(solution)/shard_map/ppermute | solution.py:28
  21.1 19.5 %collective-permute-start.8 = (bf16[168,1024]{1,0:T(8,128)(2,1)S(1)}, bf16[168,1024]{1,0:T(8,128)(2,1)}, u32[]{:S(2)}, u32[]{:S(2)}) collective-permute-start(bf16[168,1024]{1,0:T(8,128)(2,1)S(1)} %collective-permute-done.5.refs_0_), channel_id=1, source_target_pairs={{0,8},{4,12},{8,0},{12,4},{1,9},{5,13},{9,1},{13,5},{2,10},{6,14},... | collective-permute-start | bytes 1032200 | tf_op jit(solution)/shard_map/ppermute | solution.py:28
  28.8 1.0 copy-start.4
  30.6 42.7 %copy-start.2 = (bf16[4,168,1024]{2,1,0:T(8,128)(2,1)}, bf16[4,168,1024]{2,1,0:T(8,128)(2,1)S(1)}, u32[]{:S(2)}) copy-start(bf16[4,168,1024]{2,1,0:T(8,128)(2,1)S(1)} %shard_map.110) | copy-start | bytes 4128772
  30.6 42.7 %collective-permute-start.3 = (bf16[672,1024]{1,0:T(8,128)(2,1)S(1)}, bf16[672,1024]{1,0:T(8,128)(2,1)S(1)}, u32[]{:S(2)}, u32[]{:S(2)}) collective-permute-start(bf16[672,1024]{1,0:T(8,128)(2,1)S(1)} %bitcast.40), channel_id=1, source_target_pairs={{0,4},{4,8},{8,12},{12,0},{1,5},{5,9},{9,13},{13,1},{2,6},{6,10},{... | collective-permute-start | bytes 4128776 | tf_op jit(solution)/shard_map/ppermute | solution.py:28
  32.6 40.7 %collective-permute-start.4 = (bf16[672,1024]{1,0:T(8,128)(2,1)S(1)}, bf16[672,1024]{1,0:T(8,128)(2,1)}, u32[]{:S(2)}, u32[]{:S(2)}) collective-permute-start(bf16[672,1024]{1,0:T(8,128)(2,1)S(1)} %bitcast.41), channel_id=1, source_target_pairs={{0,12},{4,0},{8,4},{12,8},{1,13},{5,1},{9,5},{13,9},{2,14},{6,2},{... | collective-permute-start | bytes 4128776 | tf_op jit(solution)/shard_map/ppermute | solution.py:28
  43.9 29.4 %collective-permute-start.10 = (bf16[672,1024]{1,0:T(8,128)(2,1)}, bf16[672,1024]{1,0:T(8,128)(2,1)}, u32[]{:S(2)}, u32[]{:S(2)}) collective-permute-start(bf16[672,1024]{1,0:T(8,128)(2,1)} %bitcast.3.refs_3_), channel_id=1, source_target_pairs={{0,48},{16,0},{32,16},{48,32},{1,49},{17,1},{33,17},{49,33},{2,50}... | collective-permute-start | bytes 4128776 | tf_op jit(solution)/shard_map/ppermute | solution.py:28
  46.6 28.7 %collective-permute-start.9 = (bf16[672,1024]{1,0:T(8,128)(2,1)}, bf16[672,1024]{1,0:T(8,128)(2,1)}, u32[]{:S(2)}, u32[]{:S(2)}) collective-permute-start(bf16[672,1024]{1,0:T(8,128)(2,1)} %bitcast.3.refs_3_), channel_id=1, source_target_pairs={{0,16},{16,32},{32,48},{48,0},{1,17},{17,33},{33,49},{49,1},{2,18}... | collective-permute-start | bytes 4128776 | tf_op jit(solution)/shard_map/ppermute | solution.py:28
  46.7 9.3 %collective-permute-start.11 = (bf16[168,512]{1,0:T(8,128)(2,1)}, bf16[168,512]{1,0:T(8,128)(2,1)S(1)}, u32[]{:S(2)}, u32[]{:S(2)}) collective-permute-start(bf16[168,512]{1,0:T(8,128)(2,1)} %bitcast.49), channel_id=1, source_target_pairs={{0,64},{2,0},{64,66},{66,2},{1,65},{3,1},{65,67},{67,3},{4,68},{6,... | collective-permute-start | bytes 516104 | tf_op jit(solution)/shard_map/ppermute | solution.py:373
  56.0 7.8 %copy-start.11 = (bf16[168,512]{1,0:T(8,128)(2,1)}, bf16[168,512]{1,0:T(8,128)(2,1)S(1)}, u32[]{:S(2)}) copy-start(bf16[168,512]{1,0:T(8,128)(2,1)S(1)} %collective-permute-done.11) | copy-start | bytes 516100
  56.0 17.3 %collective-permute-start.12 = (bf16[168,512]{1,0:T(8,128)(2,1)}, bf16[168,512]{1,0:T(8,128)(2,1)}, u32[]{:S(2)}, u32[]{:S(2)}) collective-permute-start(bf16[168,512]{1,0:T(8,128)(2,1)} %bitcast.50), channel_id=1, source_target_pairs={{64,2},{2,64},{65,3},{3,65},{68,6},{6,68},{69,7},{7,69},{72,10},{1... | collective-permute-start | bytes 516104 | tf_op jit(solution)/shard_map/ppermute | solution.py:374
  65.1 10.3 %copy-start.10 = (bf16[512,168]{0,1:T(8,128)(2,1)S(1)}, bf16[512,168]{0,1:T(8,128)(2,1)}, u32[]{:S(2)}) copy-start(bf16[512,168]{0,1:T(8,128)(2,1)} %param.15) | copy-start | bytes 516100
  65.1 10.3 %copy-start.12 = (bf16[168,512]{1,0:T(8,128)(2,1)S(1)}, bf16[168,512]{1,0:T(8,128)(2,1)}, u32[]{:S(2)}) copy-start(bf16[168,512]{1,0:T(8,128)(2,1)} %copy-done.11) | copy-start | bytes 516100
  73.3 8.3 %copy-start.3 = (bf16[672,1024]{1,0:T(8,128)(2,1)}, bf16[672,1024]{1,0:T(8,128)(2,1)S(1)}, u32[]{:S(2)}) copy-start(bf16[672,1024]{1,0:T(8,128)(2,1)S(1)} %collective-permute-done.3.refs_1_.value_ref) | copy-start | bytes 4128772
  78.3 13.6 %collective-permute-start.13 = (bf16[672,512]{1,0:T(8,128)(2,1)S(1)}, bf16[672,512]{1,0:T(8,128)(2,1)}, u32[]{:S(2)}, u32[]{:S(2)}) collective-permute-start(bf16[672,512]{1,0:T(8,128)(2,1)S(1)} %shard_map.114), channel_id=1, source_target_pairs={{0,12},{4,0},{8,4},{12,8},{1,13},{5,1},{9,5},{13,9},{2,14},{6,2},{... | collective-permute-start | bytes 2064392 | tf_op jit(solution)/shard_map/ppermute | solution.py:28
  80.7 17.0 %collective-permute-start.14 = (bf16[672,512]{1,0:T(8,128)(2,1)S(1)}, bf16[672,512]{1,0:T(8,128)(2,1)}, u32[]{:S(2)}, u32[]{:S(2)}) collective-permute-start(bf16[672,512]{1,0:T(8,128)(2,1)S(1)} %shard_map.115), channel_id=1, source_target_pairs={{0,48},{16,0},{32,16},{48,32},{1,49},{17,1},{33,17},{49,33},{2,50}... | collective-permute-start | bytes 2064392 | tf_op jit(solution)/shard_map/ppermute | solution.py:28
  81.7 33.7 %collective-permute-start.15 = (bf16[672,512]{1,0:T(8,128)(2,1)S(1)}, bf16[672,512]{1,0:T(8,128)(2,1)}, u32[]{:S(2)}, u32[]{:S(2)}) collective-permute-start(bf16[672,512]{1,0:T(8,128)(2,1)S(1)} %shard_map.118), channel_id=1, source_target_pairs={{0,4},{4,8},{8,12},{12,0},{1,5},{5,9},{9,13},{13,1},{2,6},{6,10},{... | collective-permute-start | bytes 2064392 | tf_op jit(solution)/shard_map/ppermute | solution.py:28
  84.5 33.0 %collective-permute-start.16 = (bf16[672,512]{1,0:T(8,128)(2,1)S(1)}, bf16[672,512]{1,0:T(8,128)(2,1)}, u32[]{:S(2)}, u32[]{:S(2)}) collective-permute-start(bf16[672,512]{1,0:T(8,128)(2,1)S(1)} %shard_map.119), channel_id=1, source_target_pairs={{0,16},{16,32},{32,48},{48,0},{1,17},{17,33},{33,49},{49,1},{2,18}... | collective-permute-start | bytes 2064392 | tf_op jit(solution)/shard_map/ppermute | solution.py:28
  91.1 8.4 %copy-start.8 = (f32[512,512]{1,0:T(8,128)S(1)}, f32[512,512]{1,0:T(8,128)}, u32[]{:S(2)}) copy-start(f32[512,512]{1,0:T(8,128)} %shard_map.113) | copy-start | bytes 3145732
  99.5 1.9 %copy-start.5 = (f32[128]{0:T(128)S(1)}, f32[128]{0:T(128)}, u32[]{:S(2)}) copy-start(f32[128]{0:T(128)} %param.19) | copy-start | bytes 1540
  102.2 20.9 %collective-permute-start.17 = (bf16[512,512]{1,0:T(8,128)(2,1)S(1)}, bf16[512,512]{1,0:T(8,128)(2,1)S(1)}, u32[]{:S(2)}, u32[]{:S(2)}) collective-permute-start(bf16[512,512]{1,0:T(8,128)(2,1)S(1)} %shard_map.116.k_ref.v_ref), channel_id=1, source_target_pairs={{0,4},{4,8},{8,12},{12,16},{16,20},{20,24},{24,28},{28,32},{32,36}... | collective-permute-start | bytes 1572872 | tf_op jit(solution)/shard_map/ppermute | solution.py:33
  104.1 28.1 %collective-permute-start.18 = (bf16[512,512]{1,0:T(8,128)(2,1)S(1)}, bf16[512,512]{1,0:T(8,128)(2,1)S(1)}, u32[]{:S(2)}, u32[]{:S(2)}) collective-permute-start(bf16[512,512]{1,0:T(8,128)(2,1)S(1)} %shard_map.116.k_ref.v_ref), channel_id=1, source_target_pairs={{0,8},{4,12},{8,16},{12,20},{16,24},{20,28},{24,32},{28,36},{32,40... | collective-permute-start | bytes 1572872 | tf_op jit(solution)/shard_map/ppermute | solution.py:33
  115.4 4.0 %copy-start.9 = (f32[512,512]{1,0:T(8,128)S(1)}, f32[512,512]{1,0:T(8,128)}, u32[]{:S(2)}) copy-start(f32[512,512]{1,0:T(8,128)} %shard_map.117) | copy-start | bytes 3145732
  117.4 2.3 %copy-start.6 = (f32[128]{0:T(128)S(1)}, f32[128]{0:T(128)}, u32[]{:S(2)}) copy-start(f32[128]{0:T(128)} %param.18) | copy-start | bytes 1540
  135.7 19.0 %collective-permute-start.19 = (bf16[512,512]{1,0:T(8,128)(2,1)S(1)}, bf16[512,512]{1,0:T(8,128)(2,1)S(1)}, u32[]{:S(2)}, u32[]{:S(2)}) collective-permute-start(bf16[512,512]{1,0:T(8,128)(2,1)S(1)} %shard_map.122), channel_id=1, source_target_pairs={{0,2},{2,0},{1,3},{3,1},{4,6},{6,4},{5,7},{7,5},{8,10},{10,8},{9,1... | collective-permute-start | bytes 1572872 | tf_op jit(solution)/shard_map/ppermute | solution.py:28
  154.8 2.6 %copy-start = (bf16[2688,1024]{1,0:T(8,128)(2,1)S(1)}, bf16[2688,1024]{1,0:T(8,128)(2,1)}, u32[]{:S(2)}) copy-start(bf16[2688,1024]{1,0:T(8,128)(2,1)} %all-gather.4.cloned.1.call-done.weight_ref) | copy-start | bytes 16515076
  157.4 2.6 %copy-start.1 = (bf16[2688,1024]{1,0:T(8,128)(2,1)S(1)}, bf16[2688,1024]{1,0:T(8,128)(2,1)}, u32[]{:S(2)}) copy-start(bf16[2688,1024]{1,0:T(8,128)(2,1)} %all-gather.4.cloned.1.call-done.weight_ref) | copy-start | bytes 16515076
  159.6 3.2 %collective-permute-start.20 = (bf16[1344,512]{1,0:T(8,128)(2,1)S(1)}, bf16[1344,512]{1,0:T(8,128)(2,1)S(1)}, u32[]{:S(2)}, u32[]{:S(2)}) collective-permute-start(bf16[1344,512]{1,0:T(8,128)(2,1)S(1)} %shard_map.124), channel_id=1, source_target_pairs={{0,1},{1,0},{2,3},{3,2},{4,5},{5,4},{6,7},{7,6},{8,9},{9,8},{10,11... | collective-permute-start | bytes 4128776 | tf_op jit(solution)/shard_map/ppermute | solution.py:28
  162.2 7.5 %copy-start.7 = (bf16[512,1344]{0,1:T(8,128)(2,1)S(1)}, bf16[512,1344]{0,1:T(8,128)(2,1)}, u32[]{:S(2)}) copy-start(bf16[512,1344]{0,1:T(8,128)(2,1)} %param.11) | copy-start | bytes 4128772
  162.2 7.5 %copy-start.13 = (f32[1344]{0:T(1024)S(1)}, f32[1344]{0:T(1024)}, u32[]{:S(2)}) copy-start(f32[1344]{0:T(1024)} %param.17) | copy-start | bytes 16132
  163.4 1.2 collective-permute-start.21
  164.6 5.1 %collective-permute-start.22 = (f32[512]{0:T(512)S(1)}, f32[512]{0:T(512)S(1)}, u32[]{:S(2)}, u32[]{:S(2)}) collective-permute-start(f32[512]{0:T(512)S(1)} %add.151), channel_id=1, source_target_pairs={{0,2},{2,0},{1,3},{3,1},{4,6},{6,4},{5,7},{7,5},{8,10},{10,8},{9,1... | collective-permute-start | bytes 6152 | tf_op jit(solution)/shard_map/ppermute | solution.py:28
Sparse Core Ops, SparseCore 0:
  9.0 50.7 all-gather.5
  77.3 77.3 all-gather.3

commit v9 on v8

--- a/solution.py
+++ b/solution.py
@@ -382,9 +382,11 @@
     sine = jnp.concatenate([-sine, sine], axis=1)
     index = jnp.stack([z, (z + 3) % 4, (z + 1) % 4, x, (x + 3) % 4, (x + 1) % 4])
 
-    own_ahead, own_behind, other_ahead, other_behind, near, far, one, two, cosine, sine, index = (
+    outer = (y == 0) | (y == 3)
+    pair = jnp.concatenate([jnp.where(outer, turned, one), jnp.where(outer, one, two)], axis=1)
+    own_ahead, own_behind, other_ahead, other_behind, near, far, pair, cosine, sine, index = (
         lax.optimization_barrier(
-            (own_ahead, own_behind, other_ahead, other_behind, near, far, one, two, cosine, sine, index)
+            (own_ahead, own_behind, other_ahead, other_behind, near, far, pair, cosine, sine, index)
         )
     )
 
@@ -392,8 +394,6 @@
     other_far_kv = shift(cut(other_behind, 1), "x", 3)
     own_far_q = shift(cut(own_ahead, 0), "z", 1)
     other_far_q = shift(cut(other_ahead, 0), "x", 1)
-    outer = (y == 0) | (y == 3)
-    pair = jnp.concatenate([jnp.where(outer, turned, one), jnp.where(outer, one, two)], axis=1)
     out_all = lax.all_gather(pair, ("x", "z"), axis=0, tiled=True)
     parts = [own_line, own_ahead, own_behind], [other_line, other_ahead, other_behind]
     part_kv = early_product(1, index, near, far, *parts)

time: 179 us -> 178 us (level)
  waiting for transfers between devices: 65.4 us -> 61.2 us
  starting transfers between devices: 33.5 us -> 36.7 us
    ppermute x19, waiting for transfers between devices: 31.4 us -> 28.3 us  [shift(): lax.ppermute(value, axis, [(i, (i + step) % count) for i in range(count)])]
    ppermute x2, starting transfers between devices: 7.22 us -> 9.09 us  [from_behind(): lax.ppermute(value, SEQ, [(source, source + steps) for source in range(co...]
    unnamed x29 -> x25, local copies, waits for them, and re-layouts: 3.84 us -> 3.82 us
  transfers between devices with their start and end apart: 25 -> 25, of which waited for: 14 -> 14; matrix products, arithmetic and copies ran while one was open for 9% -> 10% of each run, Pallas kernels for 22% -> 22%
where the time goes in v9:
time: 178 us; the launch traced here: 177 us
  waiting for transfers between devices  61.2 us (34%)
  Pallas kernels  41.3 us (23%)
  starting transfers between devices  36.7 us (21%)
  between operations  13.8 us (8%)
  other arithmetic  8.91 us (5%)
  matrix products  7.73 us (4%)
  local copies, waits for them, and re-layouts  7.5 us (4%)
    ppermute x19, waiting for transfers between devices, shift(): lax.ppermute(value, axis, [(i, (i + step) % count) for i in range(count)])  28.3 us
    ppermute x19, starting transfers between devices, shift(): lax.ppermute(value, axis, [(i, (i + step) % count) for i in range(count)])  21.8 us
    all_gather x1, waiting for transfers between devices, local(): out_all = lax.all_gather(pair, ('x', 'z'), axis=0, tiled=True)  18.9 us
    pallas_call x2, Pallas kernels, early_product(): pl.pallas_call(functools.partial(early_kernel, len(near_weights), count,...  11.9 us
    ppermute x2, starting transfers between devices, from_behind(): lax.ppermute(value, SEQ, [(source, source + steps) for source in range(co...  9.09 us
    ppermute x2, waiting for transfers between devices, from_behind(): lax.ppermute(value, SEQ, [(source, source + steps) for source in range(co...  8.14 us
    pallas_call x1, Pallas kernels, norm_parts(): pl.pallas_call(norm_kernel, grid_spec=pltpu.PrefetchScalarGridSpec(num_sc...  8 us
    dot_general x4, matrix products, product(): return jnp.dot(left, right, preferred_element_type=jnp.float32)  7.73 us
  transfers between devices with their start and end apart: 25, of which 14 were waited for; matrix products, arithmetic and copies ran while one was open for 10% of the time, Pallas kernels for 22%

profile of v9, /device:TPU:40, one launch (start us, length us, event | category | flops | bytes accessed | tf_op | source)
XLA Modules:
  0.0 177.1 jit_solution(4832579382199222292)
XLA Ops:
  6.5 0.7 all-gather.6.cloned.1.call-update
  7.3 1.8 %shard_map.109.refs_0_ = bf16[168,1024]{1,0:T(8,128)(2,1)} custom-call(bf16[168,512]{1,0:T(8,128)(2,1)} %refs_0_.1, bf16[168,256]{1,0:T(8,128)(2,1)} %refs_1_.1, bf16[168,256]{1,0:T(8,128)(2,1)} %refs_2_.1), custom_call_target="tpu_custom_call" | custom-call | tf_op jit(solution)/shard_map/pallas_call | solution.py:74
  9.1 0.4 collective-permute-start.5
  9.5 1.5 collective-permute-start
  11.0 1.7 collective-permute-start.1
  12.8 1.8 %collective-permute-start.2 = (bf16[168,1024]{1,0:T(8,128)(2,1)}, bf16[168,1024]{1,0:T(8,128)(2,1)S(1)}, u32[]{:S(2)}, u32[]{:S(2)}) collective-permute-start(bf16[168,1024]{1,0:T(8,128)(2,1)} %shard_map.109.refs_0_), channel_id=1, source_target_pairs={{0,32},{16,48},{32,0},{48,16},{1,33},{17,49},{33,1},{49,17},{2,34}... | collective-permute-start | bytes 1032200 | tf_op jit(solution)/shard_map/ppermute | solution.py:28
  14.6 4.5 %collective-permute-done.5.refs_0_ = bf16[168,1024]{1,0:T(8,128)(2,1)S(1)} collective-permute-done((bf16[168,1024]{1,0:T(8,128)(2,1)}, bf16[168,1024]{1,0:T(8,128)(2,1)S(1)}, u32[]{:S(2)}, u32[]{:S(2)}) %collective-permute-start.5) | collective-permute-done | bytes 344096 | tf_op jit(solution)/shard_map/ppermute | solution.py:28
  19.1 1.9 %collective-permute-start.6 = (bf16[168,1024]{1,0:T(8,128)(2,1)S(1)}, bf16[168,1024]{1,0:T(8,128)(2,1)S(1)}, u32[]{:S(2)}, u32[]{:S(2)}) collective-permute-start(bf16[168,1024]{1,0:T(8,128)(2,1)S(1)} %collective-permute-done.5.refs_0_), channel_id=1, source_target_pairs={{0,4},{4,8},{8,12},{12,0},{1,5},{5,9},{9,13},{13,1},{2,6},{6,10},{... | collective-permute-start | bytes 1032200 | tf_op jit(solution)/shard_map/ppermute | solution.py:28
  21.1 3.0 %collective-permute-start.8 = (bf16[168,1024]{1,0:T(8,128)(2,1)S(1)}, bf16[168,1024]{1,0:T(8,128)(2,1)}, u32[]{:S(2)}, u32[]{:S(2)}) collective-permute-start(bf16[168,1024]{1,0:T(8,128)(2,1)S(1)} %collective-permute-done.5.refs_0_), channel_id=1, source_target_pairs={{0,8},{4,12},{8,0},{12,4},{1,9},{5,13},{9,1},{13,5},{2,10},{6,14},... | collective-permute-start | bytes 1032200 | tf_op jit(solution)/shard_map/ppermute | solution.py:28
  24.1 0.7 and_select_fusion
  24.8 2.5 %collective-permute-done.1.refs_2_ = bf16[168,1024]{1,0:T(8,128)(2,1)S(1)} collective-permute-done((bf16[168,1024]{1,0:T(8,128)(2,1)}, bf16[168,1024]{1,0:T(8,128)(2,1)S(1)}, u32[]{:S(2)}, u32[]{:S(2)}) %collective-permute-start.1) | collective-permute-done | bytes 344096 | tf_op jit(solution)/shard_map/ppermute | solution.py:28
  27.2 1.6 collective-permute-done.2.refs_3_
  28.8 1.0 copy-done.4
  29.8 0.8 shard_map.110
  30.6 2.0 %collective-permute-start.3 = (bf16[672,1024]{1,0:T(8,128)(2,1)S(1)}, bf16[672,1024]{1,0:T(8,128)(2,1)S(1)}, u32[]{:S(2)}, u32[]{:S(2)}) collective-permute-start(bf16[672,1024]{1,0:T(8,128)(2,1)S(1)} %bitcast.40), channel_id=1, source_target_pairs={{0,4},{4,8},{8,12},{12,0},{1,5},{5,9},{9,13},{13,1},{2,6},{6,10},{... | collective-permute-start | bytes 4128776 | tf_op jit(solution)/shard_map/ppermute | solution.py:28
  32.7 0.6 collective-permute-done.6.refs_1_
  33.2 7.3 %collective-permute-done.8.refs_3_ = bf16[168,1024]{1,0:T(8,128)(2,1)} collective-permute-done((bf16[168,1024]{1,0:T(8,128)(2,1)S(1)}, bf16[168,1024]{1,0:T(8,128)(2,1)}, u32[]{:S(2)}, u32[]{:S(2)}) %collective-permute-start.8) | collective-permute-done | bytes 344096 | tf_op jit(solution)/shard_map/ppermute | solution.py:28
  40.6 3.3 %shard_map.111 = bf16[4,168,1024]{2,1,0:T(8,128)(2,1)} custom-call(s32[4]{0:T(128)S(1)} %get-tuple-element.60.slots, bf16[168,1024]{1,0:T(8,128)(2,1)S(1)} %collective-permute-done.5.refs_0_, bf16[168,1024]{1,0:T(8,128)(2,1)S(1)} %collective-permute-done.6.refs_1_, bf16[168,1024]{1,0:T(8,128)(2,1)} %collective-permute-done.7.refs_2_, ...), custom_call_target="tpu_custom_call" | custom-call | tf_op jit(solution)/shard_map/pallas_call | solution.py:50
  43.9 2.8 %collective-permute-start.10 = (bf16[672,1024]{1,0:T(8,128)(2,1)}, bf16[672,1024]{1,0:T(8,128)(2,1)}, u32[]{:S(2)}, u32[]{:S(2)}) collective-permute-start(bf16[672,1024]{1,0:T(8,128)(2,1)} %bitcast.3.refs_3_), channel_id=1, source_target_pairs={{0,48},{16,0},{32,16},{48,32},{1,49},{17,1},{33,17},{49,33},{2,50}... | collective-permute-start | bytes 4128776 | tf_op jit(solution)/shard_map/ppermute | solution.py:28
  46.7 2.4 %collective-permute-start.11 = (bf16[168,512]{1,0:T(8,128)(2,1)}, bf16[168,512]{1,0:T(8,128)(2,1)S(1)}, u32[]{:S(2)}, u32[]{:S(2)}) collective-permute-start(bf16[168,512]{1,0:T(8,128)(2,1)} %bitcast.49), channel_id=1, source_target_pairs={{0,64},{2,0},{64,66},{66,2},{1,65},{3,1},{65,67},{67,3},{4,68},{6,... | collective-permute-start | bytes 516104 | tf_op jit(solution)/shard_map/ppermute | solution.py:373
  49.0 1.8 %fusion.15 = (f32[512,64]{1,0:T(8,128)S(1)}, f32[512,64]{1,0:T(8,128)}, f32[512,64]{1,0:T(8,128)}) fusion(f32[64]{0:T(128)S(1)} %multiply_power_fusion, f32[512]{0:T(512)S(1)} %add_convert_fusion), kind=kLoop, calls=%fused_computation.25 | loop fusion | flops 65536 | bytes 395520 | tf_op jit(solution)/shard_map/neg | solution.py:382
  50.9 5.2 %collective-permute-done.11 = bf16[168,512]{1,0:T(8,128)(2,1)S(1)} collective-permute-done((bf16[168,512]{1,0:T(8,128)(2,1)}, bf16[168,512]{1,0:T(8,128)(2,1)S(1)}, u32[]{:S(2)}, u32[]{:S(2)}) %collective-permute-start.11) | collective-permute-done | bytes 172064 | tf_op jit(solution)/shard_map/ppermute | solution.py:373
  56.0 3.5 %collective-permute-start.12 = (bf16[168,512]{1,0:T(8,128)(2,1)}, bf16[168,512]{1,0:T(8,128)(2,1)}, u32[]{:S(2)}, u32[]{:S(2)}) collective-permute-start(bf16[168,512]{1,0:T(8,128)(2,1)} %bitcast.50), channel_id=1, source_target_pairs={{64,2},{2,64},{65,3},{3,65},{68,6},{6,68},{69,7},{7,69},{72,10},{1... | collective-permute-start | bytes 516104 | tf_op jit(solution)/shard_map/ppermute | solution.py:374
  59.5 0.6 pad_add_fusion.side
  60.1 0.8 reshape.32
  61.0 1.4 reshape_reshape.3.far_gain
  62.4 0.7 reshape.33.near_gain
  63.1 0.6 stack.48.index
  63.8 1.3 pad_maximum_fusion.1
  65.1 1.0 broadcast_select_fusion.1
  66.1 0.8 pad_maximum_fusion
  66.9 8.0 %shard_map.112 = (bf16[4,512,672]{2,1,0:T(8,128)(2,1)}, bf16[4,512,672]{2,1,0:T(8,128)(2,1)}) custom-call(s32[2]{0:T(128)} %pad_add_fusion.side, bf16[2,2,1344,512]{3,2,1,0:T(8,128)(2,1)} %bitcast.46, bf16[2,2,1344,512]{3,2,1,0:T(8,128)(2,1)} %bitcast.47, f32[2,4,1,672]{3,2,1,0:T(1,128)} %reshape.33.near_gain, f32[2,4,1,672]{3,2,1,0:T(1,128)} %reshape_reshape.3.far_gain), custom_call_target="tpu_custom_call" | custom-call | tf_op jit(solution)/shard_map/pallas_call | solution.py:127
  74.9 0.4 collective-permute-done.9.refs_4_.value_ref
  75.4 1.1 shard_map.114
  76.6 1.2 collective-permute-start.13
  77.8 1.1 shard_map.115
  78.9 2.7 %collective-permute-start.14 = (bf16[672,512]{1,0:T(8,128)(2,1)S(1)}, bf16[672,512]{1,0:T(8,128)(2,1)}, u32[]{:S(2)}, u32[]{:S(2)}) collective-permute-start(bf16[672,512]{1,0:T(8,128)(2,1)S(1)} %shard_map.115), channel_id=1, source_target_pairs={{0,48},{16,0},{32,16},{48,32},{1,49},{17,1},{33,17},{49,33},{2,50}... | collective-permute-start | bytes 2064392 | tf_op jit(solution)/shard_map/ppermute | solution.py:28
  81.8 1.5 collective-permute-start.15
  83.4 1.2 shard_map.119
  84.6 6.0 %shard_map.113 = f32[512,512]{1,0:T(8,128)} custom-call(s32[6]{0:T(128)} %stack.48.index, bf16[4,512,672]{2,1,0:T(8,128)(2,1)} %get-tuple-element.36.near_ref, bf16[4,512,672]{2,1,0:T(8,128)(2,1)} %get-tuple-element.37.far_ref, bf16[672,1024]{1,0:T(8,128)(2,1)} %bitcast.42, bf16[672,1024]{1,0:T(8,128)(2,1)} %copy-done.3, ...), custom_call_target="tpu_custom_call" | custom-call | tf_op jit(solution)/shard_map/pallas_call | solution.py:169
  90.6 0.4 collective-permute-done.13
  91.0 4.6 %collective-permute-done.14 = bf16[672,512]{1,0:T(8,128)(2,1)} collective-permute-done((bf16[672,512]{1,0:T(8,128)(2,1)S(1)}, bf16[672,512]{1,0:T(8,128)(2,1)}, u32[]{:S(2)}, u32[]{:S(2)}) %collective-permute-start.14) | collective-permute-done | bytes 688160 | tf_op jit(solution)/shard_map/ppermute | solution.py:28
  95.7 1.9 %fusion.9 = f32[512,512]{1,0:T(8,128)S(1)} fusion(bf16[672,512]{1,0:T(8,128)(2,1)} %collective-permute-done.13, bf16[4,512,672]{2,1,0:T(8,128)(2,1)} %get-tuple-element.36.near_ref, s32[]{:T(128)S(6)} %select_n.72), kind=kOutput, calls=%fused_computation.12 | convolution fusion | flops 352321536 | bytes 2523140 | tf_op jit(solution)/shard_map/dot_general | solution.py:193
  97.6 1.9 %add_add_fusion.1.raw_ref = f32[512,512]{1,0:T(8,128)S(1)} fusion(f32[512,512]{1,0:T(8,128)S(1)} %copy-done.8, f32[512,512]{1,0:T(8,128)S(1)} %fusion.9, bf16[672,512]{1,0:T(8,128)(2,1)} %collective-permute-done.14, bf16[4,512,672]{2,1,0:T(8,128)(2,1)} %get-tuple-element.37.far_ref, s32[]{:T(128)S(6)} %select_n.74), kind=kOutput, calls=%fused_computation.5 | convolution fusion | flops 352845824 | bytes 4620292 | tf_op jit(solution)/shard_map/dot_general | solution.py:193
  99.6 0.7 shard_map.116.k_ref.v_ref
  100.2 2.4 %collective-permute-start.17 = (bf16[512,512]{1,0:T(8,128)(2,1)S(1)}, bf16[512,512]{1,0:T(8,128)(2,1)S(1)}, u32[]{:S(2)}, u32[]{:S(2)}) collective-permute-start(bf16[512,512]{1,0:T(8,128)(2,1)S(1)} %shard_map.116.k_ref.v_ref), channel_id=1, source_target_pairs={{0,4},{4,8},{8,12},{12,16},{16,20},{20,24},{24,28},{28,32},{32,36}... | collective-permute-start | bytes 1572872 | tf_op jit(solution)/shard_map/ppermute | solution.py:33
  102.6 6.7 %collective-permute-start.18 = (bf16[512,512]{1,0:T(8,128)(2,1)S(1)}, bf16[512,512]{1,0:T(8,128)(2,1)S(1)}, u32[]{:S(2)}, u32[]{:S(2)}) collective-permute-start(bf16[512,512]{1,0:T(8,128)(2,1)S(1)} %shard_map.116.k_ref.v_ref), channel_id=1, source_target_pairs={{0,8},{4,12},{8,16},{12,20},{16,24},{20,28},{24,32},{28,36},{32,40... | collective-permute-start | bytes 1572872 | tf_op jit(solution)/shard_map/ppermute | solution.py:33
  109.3 6.0 %shard_map.117 = f32[512,512]{1,0:T(8,128)} custom-call(s32[6]{0:T(128)} %stack.48.index, bf16[4,512,672]{2,1,0:T(8,128)(2,1)} %get-tuple-element.36.near_ref, bf16[4,512,672]{2,1,0:T(8,128)(2,1)} %get-tuple-element.37.far_ref, bf16[672,1024]{1,0:T(8,128)(2,1)} %bitcast.43, bf16[672,1024]{1,0:T(8,128)(2,1)} %copy-done.3, ...), custom_call_target="tpu_custom_call" | custom-call | tf_op jit(solution)/shard_map/pallas_call | solution.py:169
  115.3 2.0 %fusion.7 = f32[512,512]{1,0:T(8,128)S(1)} fusion(bf16[672,512]{1,0:T(8,128)(2,1)} %collective-permute-done.15, bf16[4,512,672]{2,1,0:T(8,128)(2,1)} %get-tuple-element.36.near_ref, s32[]{:T(128)S(6)} %select_n.72), kind=kOutput, calls=%fused_computation.10 | convolution fusion | flops 352321536 | bytes 2523140 | tf_op jit(solution)/shard_map/dot_general | solution.py:193
  117.4 1.9 %fusion.1 = f32[512,512]{1,0:T(8,128)S(1)} fusion(bf16[672,512]{1,0:T(8,128)(2,1)} %collective-permute-done.16, bf16[4,512,672]{2,1,0:T(8,128)(2,1)} %get-tuple-element.37.far_ref, s32[]{:T(128)S(6)} %select_n.74), kind=kOutput, calls=%fused_computation.6 | convolution fusion | flops 352321536 | bytes 2523140 | tf_op jit(solution)/shard_map/dot_general | solution.py:193
  119.7 1.2 shard_map.120.q_ref
  120.9 2.1 %shard_map.121 = (f32[512,512]{1,0:T(8,128)S(1)}, f32[512,512]{1,0:T(8,128)S(1)}) custom-call(bf16[512,512]{1,0:T(8,128)(2,1)S(1)} %shard_map.120.q_ref, bf16[512,512]{1,0:T(8,128)(2,1)S(1)} %shard_map.116.k_ref.v_ref, bf16[512,512]{1,0:T(8,128)(2,1)S(1)} %shard_map.116.k_ref.v_ref), custom_call_target="tpu_custom_call" | custom-call | tf_op jit(solution)/shard_map/pallas_call | solution.py:288
  123.0 8.1 %collective-permute-done.18.k2_ref.v2_ref = bf16[512,512]{1,0:T(8,128)(2,1)S(1)} collective-permute-done((bf16[512,512]{1,0:T(8,128)(2,1)S(1)}, bf16[512,512]{1,0:T(8,128)(2,1)S(1)}, u32[]{:S(2)}, u32[]{:S(2)}) %collective-permute-start.18) | collective-permute-done | bytes 524320 | tf_op jit(solution)/shard_map/ppermute | solution.py:33
  131.1 3.5 %shard_map.122 = bf16[512,512]{1,0:T(8,128)(2,1)S(1)} custom-call(s32[2]{0:T(128)S(1)} %add_convert_fusion.1.valid, bf16[512,512]{1,0:T(8,128)(2,1)S(1)} %shard_map.120.q_ref, bf16[512,512]{1,0:T(8,128)(2,1)S(1)} %collective-permute-done.17.k1_ref.v1_ref, bf16[512,512]{1,0:T(8,128)(2,1)S(1)} %collective-permute-done.17.k1_ref.v1_ref, ...), custom_call_target="tpu_custom_call" | custom-call | tf_op jit(solution)/shard_map/pallas_call | solution.py:309
  134.7 18.9 %all-gather.4.cloned.1.call-done.weight_ref = bf16[2688,1024]{1,0:T(8,128)(2,1)} async-done(((bf16[168,1024]{1,0:T(8,128)(2,1)}), bf16[2688,1024]{1,0:T(8,128)(2,1)}) %all-gather.4.cloned.1.call-update) | async-done | bytes 5505040 | tf_op jit(solution)/shard_map/all_gather | solution.py:397
  153.8 2.6 %copy-done = bf16[2688,1024]{1,0:T(8,128)(2,1)S(1)} copy-done((bf16[2688,1024]{1,0:T(8,128)(2,1)S(1)}, bf16[2688,1024]{1,0:T(8,128)(2,1)}, u32[]{:S(2)}) %copy-start) | copy-done | bytes 5505048
  156.3 2.2 %shard_map.124 = bf16[1344,512]{1,0:T(8,128)(2,1)S(1)} custom-call(s32[1]{0:T(128)} %bitcast.21.half, bf16[2688,1024]{1,0:T(8,128)(2,1)S(1)} %copy-done, bf16[512,1024]{1,0:T(8,128)(2,1)S(1)} %constant_dynamic-update-slice_fusion.context_ref), custom_call_target="tpu_custom_call" | custom-call | tf_op jit(solution)/shard_map/pallas_call | solution.py:334
  158.9 2.2 %shard_map.123 = f32[1344,512]{1,0:T(8,128)S(1)} custom-call(s32[1]{0:T(128)} %bitcast.half, bf16[2688,1024]{1,0:T(8,128)(2,1)S(1)} %copy-done.1, bf16[512,1024]{1,0:T(8,128)(2,1)S(1)} %constant_dynamic-update-slice_fusion.context_ref), custom_call_target="tpu_custom_call" | custom-call | tf_op jit(solution)/shard_map/pallas_call | solution.py:334
  161.1 0.6 collective-permute-done.20
  161.8 0.5 multiply_reduce_fusion
  162.5 1.0 collective-permute-done.21
  163.5 0.5 collective-permute-start.22
  164.0 4.6 %collective-permute-done.22 = f32[512]{0:T(512)S(1)} collective-permute-done((f32[512]{0:T(512)S(1)}, f32[512]{0:T(512)S(1)}, u32[]{:S(2)}, u32[]{:S(2)}) %collective-permute-start.22) | collective-permute-done | bytes 2080 | tf_op jit(solution)/shard_map/ppermute | solution.py:28
  168.6 1.7 fusion
  (53 shorter events, 1.8 us)
Async XLA Ops:
  6.5 60.4 %all-gather.6.cloned.1.call-start = ((), (), s32[]{:S(2)}) async-start(), calls=%async_computation.1 | async-start | bytes 6881280 | tf_op jit(solution)/shard_map/all_gather | solution.py:358
  7.3 146.3 %all-gather.4.cloned.1.call-start = ((), (), s32[]{:S(2)}) async-start(), calls=%async_computation | async-start | bytes 5849088 | tf_op jit(solution)/shard_map/all_gather | solution.py:397
  9.1 10.0 %collective-permute-start.5 = (bf16[168,1024]{1,0:T(8,128)(2,1)}, bf16[168,1024]{1,0:T(8,128)(2,1)S(1)}, u32[]{:S(2)}, u32[]{:S(2)}) collective-permute-start(bf16[168,1024]{1,0:T(8,128)(2,1)} %shard_map.109.refs_0_), channel_id=1, source_target_pairs={{0,64},{64,0},{1,65},{65,1},{2,66},{66,2},{3,67},{67,3},{4,68},{68... | collective-permute-start | bytes 1032200 | tf_op jit(solution)/shard_map/ppermute | solution.py:28
  9.5 11.6 %collective-permute-start = (bf16[168,1024]{1,0:T(8,128)(2,1)}, bf16[168,1024]{1,0:T(8,128)(2,1)S(1)}, u32[]{:S(2)}, u32[]{:S(2)}) collective-permute-start(bf16[168,1024]{1,0:T(8,128)(2,1)} %shard_map.109.refs_0_), channel_id=1, source_target_pairs={{0,16},{16,32},{32,48},{48,0},{1,17},{17,33},{33,49},{49,1},{2,18}... | collective-permute-start | bytes 1032200 | tf_op jit(solution)/shard_map/ppermute | solution.py:28
  11.0 16.2 %collective-permute-start.1 = (bf16[168,1024]{1,0:T(8,128)(2,1)}, bf16[168,1024]{1,0:T(8,128)(2,1)S(1)}, u32[]{:S(2)}, u32[]{:S(2)}) collective-permute-start(bf16[168,1024]{1,0:T(8,128)(2,1)} %shard_map.109.refs_0_), channel_id=1, source_target_pairs={{0,48},{16,0},{32,16},{48,32},{1,49},{17,1},{33,17},{49,33},{2,50}... | collective-permute-start | bytes 1032200 | tf_op jit(solution)/shard_map/ppermute | solution.py:28
  12.8 16.1 %collective-permute-start.2 = (bf16[168,1024]{1,0:T(8,128)(2,1)}, bf16[168,1024]{1,0:T(8,128)(2,1)S(1)}, u32[]{:S(2)}, u32[]{:S(2)}) collective-permute-start(bf16[168,1024]{1,0:T(8,128)(2,1)} %shard_map.109.refs_0_), channel_id=1, source_target_pairs={{0,32},{16,48},{32,0},{48,16},{1,33},{17,49},{33,1},{49,17},{2,34}... | collective-permute-start | bytes 1032200 | tf_op jit(solution)/shard_map/ppermute | solution.py:28
  19.1 14.1 %collective-permute-start.6 = (bf16[168,1024]{1,0:T(8,128)(2,1)S(1)}, bf16[168,1024]{1,0:T(8,128)(2,1)S(1)}, u32[]{:S(2)}, u32[]{:S(2)}) collective-permute-start(bf16[168,1024]{1,0:T(8,128)(2,1)S(1)} %collective-permute-done.5.refs_0_), channel_id=1, source_target_pairs={{0,4},{4,8},{8,12},{12,0},{1,5},{5,9},{9,13},{13,1},{2,6},{6,10},{... | collective-permute-start | bytes 1032200 | tf_op jit(solution)/shard_map/ppermute | solution.py:28
  21.0 12.2 %collective-permute-start.7 = (bf16[168,1024]{1,0:T(8,128)(2,1)S(1)}, bf16[168,1024]{1,0:T(8,128)(2,1)}, u32[]{:S(2)}, u32[]{:S(2)}) collective-permute-start(bf16[168,1024]{1,0:T(8,128)(2,1)S(1)} %collective-permute-done.5.refs_0_), channel_id=1, source_target_pairs={{0,12},{4,0},{8,4},{12,8},{1,13},{5,1},{9,5},{13,9},{2,14},{6,2},{... | collective-permute-start | bytes 1032200 | tf_op jit(solution)/shard_map/ppermute | solution.py:28
  21.1 19.5 %collective-permute-start.8 = (bf16[168,1024]{1,0:T(8,128)(2,1)S(1)}, bf16[168,1024]{1,0:T(8,128)(2,1)}, u32[]{:S(2)}, u32[]{:S(2)}) collective-permute-start(bf16[168,1024]{1,0:T(8,128)(2,1)S(1)} %collective-permute-done.5.refs_0_), channel_id=1, source_target_pairs={{0,8},{4,12},{8,0},{12,4},{1,9},{5,13},{9,1},{13,5},{2,10},{6,14},... | collective-permute-start | bytes 1032200 | tf_op jit(solution)/shard_map/ppermute | solution.py:28
  28.8 1.0 copy-start.4
  30.6 35.6 %copy-start.2 = (bf16[4,168,1024]{2,1,0:T(8,128)(2,1)}, bf16[4,168,1024]{2,1,0:T(8,128)(2,1)S(1)}, u32[]{:S(2)}) copy-start(bf16[4,168,1024]{2,1,0:T(8,128)(2,1)S(1)} %shard_map.110) | copy-start | bytes 4128772
  30.6 44.3 %collective-permute-start.3 = (bf16[672,1024]{1,0:T(8,128)(2,1)S(1)}, bf16[672,1024]{1,0:T(8,128)(2,1)S(1)}, u32[]{:S(2)}, u32[]{:S(2)}) collective-permute-start(bf16[672,1024]{1,0:T(8,128)(2,1)S(1)} %bitcast.40), channel_id=1, source_target_pairs={{0,4},{4,8},{8,12},{12,0},{1,5},{5,9},{9,13},{13,1},{2,6},{6,10},{... | collective-permute-start | bytes 4128776 | tf_op jit(solution)/shard_map/ppermute | solution.py:28
  32.6 42.3 %collective-permute-start.4 = (bf16[672,1024]{1,0:T(8,128)(2,1)S(1)}, bf16[672,1024]{1,0:T(8,128)(2,1)}, u32[]{:S(2)}, u32[]{:S(2)}) collective-permute-start(bf16[672,1024]{1,0:T(8,128)(2,1)S(1)} %bitcast.41), channel_id=1, source_target_pairs={{0,12},{4,0},{8,4},{12,8},{1,13},{5,1},{9,5},{13,9},{2,14},{6,2},{... | collective-permute-start | bytes 4128776 | tf_op jit(solution)/shard_map/ppermute | solution.py:28
  43.9 31.1 %collective-permute-start.10 = (bf16[672,1024]{1,0:T(8,128)(2,1)}, bf16[672,1024]{1,0:T(8,128)(2,1)}, u32[]{:S(2)}, u32[]{:S(2)}) collective-permute-start(bf16[672,1024]{1,0:T(8,128)(2,1)} %bitcast.3.refs_3_), channel_id=1, source_target_pairs={{0,48},{16,0},{32,16},{48,32},{1,49},{17,1},{33,17},{49,33},{2,50}... | collective-permute-start | bytes 4128776 | tf_op jit(solution)/shard_map/ppermute | solution.py:28
  46.6 28.7 %collective-permute-start.9 = (bf16[672,1024]{1,0:T(8,128)(2,1)}, bf16[672,1024]{1,0:T(8,128)(2,1)}, u32[]{:S(2)}, u32[]{:S(2)}) collective-permute-start(bf16[672,1024]{1,0:T(8,128)(2,1)} %bitcast.3.refs_3_), channel_id=1, source_target_pairs={{0,16},{16,32},{32,48},{48,0},{1,17},{17,33},{33,49},{49,1},{2,18}... | collective-permute-start | bytes 4128776 | tf_op jit(solution)/shard_map/ppermute | solution.py:28
  46.7 9.3 %collective-permute-start.11 = (bf16[168,512]{1,0:T(8,128)(2,1)}, bf16[168,512]{1,0:T(8,128)(2,1)S(1)}, u32[]{:S(2)}, u32[]{:S(2)}) collective-permute-start(bf16[168,512]{1,0:T(8,128)(2,1)} %bitcast.49), channel_id=1, source_target_pairs={{0,64},{2,0},{64,66},{66,2},{1,65},{3,1},{65,67},{67,3},{4,68},{6,... | collective-permute-start | bytes 516104 | tf_op jit(solution)/shard_map/ppermute | solution.py:373
  56.0 7.8 %copy-start.10 = (bf16[168,512]{1,0:T(8,128)(2,1)}, bf16[168,512]{1,0:T(8,128)(2,1)S(1)}, u32[]{:S(2)}) copy-start(bf16[168,512]{1,0:T(8,128)(2,1)S(1)} %collective-permute-done.11) | copy-start | bytes 516100
  56.0 9.1 %collective-permute-start.12 = (bf16[168,512]{1,0:T(8,128)(2,1)}, bf16[168,512]{1,0:T(8,128)(2,1)}, u32[]{:S(2)}, u32[]{:S(2)}) collective-permute-start(bf16[168,512]{1,0:T(8,128)(2,1)} %bitcast.50), channel_id=1, source_target_pairs={{64,2},{2,64},{65,3},{3,65},{68,6},{6,68},{69,7},{7,69},{72,10},{1... | collective-permute-start | bytes 516104 | tf_op jit(solution)/shard_map/ppermute | solution.py:374
  74.9 6.9 %copy-start.3 = (bf16[672,1024]{1,0:T(8,128)(2,1)}, bf16[672,1024]{1,0:T(8,128)(2,1)S(1)}, u32[]{:S(2)}) copy-start(bf16[672,1024]{1,0:T(8,128)(2,1)S(1)} %collective-permute-done.3.refs_1_.value_ref) | copy-start | bytes 4128772
  76.6 14.5 %collective-permute-start.13 = (bf16[672,512]{1,0:T(8,128)(2,1)S(1)}, bf16[672,512]{1,0:T(8,128)(2,1)}, u32[]{:S(2)}, u32[]{:S(2)}) collective-permute-start(bf16[672,512]{1,0:T(8,128)(2,1)S(1)} %shard_map.114), channel_id=1, source_target_pairs={{0,12},{4,0},{8,4},{12,8},{1,13},{5,1},{9,5},{13,9},{2,14},{6,2},{... | collective-permute-start | bytes 2064392 | tf_op jit(solution)/shard_map/ppermute | solution.py:28
  78.9 16.8 %collective-permute-start.14 = (bf16[672,512]{1,0:T(8,128)(2,1)S(1)}, bf16[672,512]{1,0:T(8,128)(2,1)}, u32[]{:S(2)}, u32[]{:S(2)}) collective-permute-start(bf16[672,512]{1,0:T(8,128)(2,1)S(1)} %shard_map.115), channel_id=1, source_target_pairs={{0,48},{16,0},{32,16},{48,32},{1,49},{17,1},{33,17},{49,33},{2,50}... | collective-permute-start | bytes 2064392 | tf_op jit(solution)/shard_map/ppermute | solution.py:28
  81.8 33.5 %collective-permute-start.15 = (bf16[672,512]{1,0:T(8,128)(2,1)S(1)}, bf16[672,512]{1,0:T(8,128)(2,1)}, u32[]{:S(2)}, u32[]{:S(2)}) collective-permute-start(bf16[672,512]{1,0:T(8,128)(2,1)S(1)} %shard_map.118), channel_id=1, source_target_pairs={{0,4},{4,8},{8,12},{12,0},{1,5},{5,9},{9,13},{13,1},{2,6},{6,10},{... | collective-permute-start | bytes 2064392 | tf_op jit(solution)/shard_map/ppermute | solution.py:28
  84.6 32.8 %collective-permute-start.16 = (bf16[672,512]{1,0:T(8,128)(2,1)S(1)}, bf16[672,512]{1,0:T(8,128)(2,1)}, u32[]{:S(2)}, u32[]{:S(2)}) collective-permute-start(bf16[672,512]{1,0:T(8,128)(2,1)S(1)} %shard_map.119), channel_id=1, source_target_pairs={{0,16},{16,32},{32,48},{48,0},{1,17},{17,33},{33,49},{49,1},{2,18}... | collective-permute-start | bytes 2064392 | tf_op jit(solution)/shard_map/ppermute | solution.py:28
  90.6 7.0 %copy-start.8 = (f32[512,512]{1,0:T(8,128)S(1)}, f32[512,512]{1,0:T(8,128)}, u32[]{:S(2)}) copy-start(f32[512,512]{1,0:T(8,128)} %shard_map.113) | copy-start | bytes 3145732
  97.6 1.9 %copy-start.5 = (f32[128]{0:T(128)S(1)}, f32[128]{0:T(128)}, u32[]{:S(2)}) copy-start(f32[128]{0:T(128)} %param.19) | copy-start | bytes 1540
  100.2 22.8 %collective-permute-start.17 = (bf16[512,512]{1,0:T(8,128)(2,1)S(1)}, bf16[512,512]{1,0:T(8,128)(2,1)S(1)}, u32[]{:S(2)}, u32[]{:S(2)}) collective-permute-start(bf16[512,512]{1,0:T(8,128)(2,1)S(1)} %shard_map.116.k_ref.v_ref), channel_id=1, source_target_pairs={{0,4},{4,8},{8,12},{12,16},{16,20},{20,24},{24,28},{28,32},{32,36}... | collective-permute-start | bytes 1572872 | tf_op jit(solution)/shard_map/ppermute | solution.py:33
  102.6 28.5 %collective-permute-start.18 = (bf16[512,512]{1,0:T(8,128)(2,1)S(1)}, bf16[512,512]{1,0:T(8,128)(2,1)S(1)}, u32[]{:S(2)}, u32[]{:S(2)}) collective-permute-start(bf16[512,512]{1,0:T(8,128)(2,1)S(1)} %shard_map.116.k_ref.v_ref), channel_id=1, source_target_pairs={{0,8},{4,12},{8,16},{12,20},{16,24},{20,28},{24,32},{28,36},{32,40... | collective-permute-start | bytes 1572872 | tf_op jit(solution)/shard_map/ppermute | solution.py:33
  115.3 4.0 %copy-start.9 = (f32[512,512]{1,0:T(8,128)S(1)}, f32[512,512]{1,0:T(8,128)}, u32[]{:S(2)}) copy-start(f32[512,512]{1,0:T(8,128)} %shard_map.117) | copy-start | bytes 3145732
  117.3 2.3 %copy-start.6 = (f32[128]{0:T(128)S(1)}, f32[128]{0:T(128)}, u32[]{:S(2)}) copy-start(f32[128]{0:T(128)} %param.18) | copy-start | bytes 1540
  134.6 19.0 %collective-permute-start.19 = (bf16[512,512]{1,0:T(8,128)(2,1)S(1)}, bf16[512,512]{1,0:T(8,128)(2,1)S(1)}, u32[]{:S(2)}, u32[]{:S(2)}) collective-permute-start(bf16[512,512]{1,0:T(8,128)(2,1)S(1)} %shard_map.122), channel_id=1, source_target_pairs={{0,2},{2,0},{1,3},{3,1},{4,6},{6,4},{5,7},{7,5},{8,10},{10,8},{9,1... | collective-permute-start | bytes 1572872 | tf_op jit(solution)/shard_map/ppermute | solution.py:28
  153.7 2.6 %copy-start = (bf16[2688,1024]{1,0:T(8,128)(2,1)S(1)}, bf16[2688,1024]{1,0:T(8,128)(2,1)}, u32[]{:S(2)}) copy-start(bf16[2688,1024]{1,0:T(8,128)(2,1)} %all-gather.4.cloned.1.call-done.weight_ref) | copy-start | bytes 16515076
  156.3 2.6 %copy-start.1 = (bf16[2688,1024]{1,0:T(8,128)(2,1)S(1)}, bf16[2688,1024]{1,0:T(8,128)(2,1)}, u32[]{:S(2)}) copy-start(bf16[2688,1024]{1,0:T(8,128)(2,1)} %all-gather.4.cloned.1.call-done.weight_ref) | copy-start | bytes 16515076
  158.6 3.2 %collective-permute-start.20 = (bf16[1344,512]{1,0:T(8,128)(2,1)S(1)}, bf16[1344,512]{1,0:T(8,128)(2,1)S(1)}, u32[]{:S(2)}, u32[]{:S(2)}) collective-permute-start(bf16[1344,512]{1,0:T(8,128)(2,1)S(1)} %shard_map.124), channel_id=1, source_target_pairs={{0,1},{1,0},{2,3},{3,2},{4,5},{5,4},{6,7},{7,6},{8,9},{9,8},{10,11... | collective-permute-start | bytes 4128776 | tf_op jit(solution)/shard_map/ppermute | solution.py:28
  161.1 7.5 %copy-start.7 = (bf16[512,1344]{0,1:T(8,128)(2,1)S(1)}, bf16[512,1344]{0,1:T(8,128)(2,1)}, u32[]{:S(2)}) copy-start(bf16[512,1344]{0,1:T(8,128)(2,1)} %param.11) | copy-start | bytes 4128772
  161.1 7.5 %copy-start.11 = (f32[1344]{0:T(1024)S(1)}, f32[1344]{0:T(1024)}, u32[]{:S(2)}) copy-start(f32[1344]{0:T(1024)} %param.17) | copy-start | bytes 16132
  162.3 1.2 collective-permute-start.21
  163.5 5.1 %collective-permute-start.22 = (f32[512]{0:T(512)S(1)}, f32[512]{0:T(512)S(1)}, u32[]{:S(2)}, u32[]{:S(2)}) collective-permute-start(f32[512]{0:T(512)S(1)} %add.151), channel_id=1, source_target_pairs={{0,2},{2,0},{1,3},{3,1},{4,6},{6,4},{5,7},{7,5},{8,10},{10,8},{9,1... | collective-permute-start | bytes 6152 | tf_op jit(solution)/shard_map/ppermute | solution.py:28
Sparse Core Ops, SparseCore 0:
  9.0 50.7 all-gather.5
  75.5 78.0 all-gather.3

commit v10 on v9

--- a/solution.py
+++ b/solution.py
@@ -329,7 +329,7 @@
 def out_half(weight, context, half, dtype):
     rows, depth = context.shape
     columns = weight.shape[0] // 2
-    steps = 4
+    steps = 2
     tile = columns // steps
     return pl.pallas_call(
         half_kernel,

time: 178 us -> 177 us (level)
  no operation moved by 1% of the time
where the time goes in v10:
time: 177 us
  waiting for transfers between devices  61.2 us (35%)
  Pallas kernels  40.5 us (23%)
  starting transfers between devices  36.7 us (21%)
  between operations  13.8 us (8%)
  other arithmetic  8.91 us (5%)
  local copies, waits for them, and re-layouts  7.9 us (4%)
  matrix products  7.73 us (4%)
    ppermute x19, waiting for transfers between devices, shift(): lax.ppermute(value, axis, [(i, (i + step) % count) for i in range(count)])  28.3 us
    ppermute x19, starting transfers between devices, shift(): lax.ppermute(value, axis, [(i, (i + step) % count) for i in range(count)])  21.8 us
    all_gather x1, waiting for transfers between devices, local(): out_all = lax.all_gather(pair, ('x', 'z'), axis=0, tiled=True)  18.9 us
    pallas_call x2, Pallas kernels, early_product(): pl.pallas_call(functools.partial(early_kernel, len(near_weights), count,...  11.9 us
    ppermute x2, starting transfers between devices, from_behind(): lax.ppermute(value, SEQ, [(source, source + steps) for source in range(co...  9.09 us
    ppermute x2, waiting for transfers between devices, from_behind(): lax.ppermute(value, SEQ, [(source, source + steps) for source in range(co...  8.14 us
    pallas_call x1, Pallas kernels, norm_parts(): pl.pallas_call(norm_kernel, grid_spec=pltpu.PrefetchScalarGridSpec(num_sc...  8 us
    dot_general x4, matrix products, product(): return jnp.dot(left, right, preferred_element_type=jnp.float32)  7.73 us
  transfers between devices with their start and end apart: 25, of which 14 were waited for; matrix products, arithmetic and copies ran while one was open for 10% of the time, Pallas kernels for 22%

profile of v10, /device:TPU:40, one launch (start us, length us, event | category | flops | bytes accessed | tf_op | source)
XLA Modules:
  0.0 176.7 jit_solution(9264325174386832650)
XLA Ops:
  6.5 0.7 all-gather.6.cloned.1.call-update
  7.3 1.8 %shard_map.109.refs_0_ = bf16[168,1024]{1,0:T(8,128)(2,1)} custom-call(bf16[168,512]{1,0:T(8,128)(2,1)} %refs_0_.1, bf16[168,256]{1,0:T(8,128)(2,1)} %refs_1_.1, bf16[168,256]{1,0:T(8,128)(2,1)} %refs_2_.1), custom_call_target="tpu_custom_call" | custom-call | tf_op jit(solution)/shard_map/pallas_call | solution.py:74
  9.1 0.4 collective-permute-start.5
  9.5 1.5 collective-permute-start
  11.0 1.7 collective-permute-start.1
  12.8 1.8 %collective-permute-start.2 = (bf16[168,1024]{1,0:T(8,128)(2,1)}, bf16[168,1024]{1,0:T(8,128)(2,1)S(1)}, u32[]{:S(2)}, u32[]{:S(2)}) collective-permute-start(bf16[168,1024]{1,0:T(8,128)(2,1)} %shard_map.109.refs_0_), channel_id=1, source_target_pairs={{0,32},{16,48},{32,0},{48,16},{1,33},{17,49},{33,1},{49,17},{2,34}... | collective-permute-start | bytes 1032200 | tf_op jit(solution)/shard_map/ppermute | solution.py:28
  14.6 4.5 %collective-permute-done.5.refs_0_ = bf16[168,1024]{1,0:T(8,128)(2,1)S(1)} collective-permute-done((bf16[168,1024]{1,0:T(8,128)(2,1)}, bf16[168,1024]{1,0:T(8,128)(2,1)S(1)}, u32[]{:S(2)}, u32[]{:S(2)}) %collective-permute-start.5) | collective-permute-done | bytes 344096 | tf_op jit(solution)/shard_map/ppermute | solution.py:28
  19.1 1.9 %collective-permute-start.6 = (bf16[168,1024]{1,0:T(8,128)(2,1)S(1)}, bf16[168,1024]{1,0:T(8,128)(2,1)S(1)}, u32[]{:S(2)}, u32[]{:S(2)}) collective-permute-start(bf16[168,1024]{1,0:T(8,128)(2,1)S(1)} %collective-permute-done.5.refs_0_), channel_id=1, source_target_pairs={{0,4},{4,8},{8,12},{12,0},{1,5},{5,9},{9,13},{13,1},{2,6},{6,10},{... | collective-permute-start | bytes 1032200 | tf_op jit(solution)/shard_map/ppermute | solution.py:28
  21.1 3.0 %collective-permute-start.8 = (bf16[168,1024]{1,0:T(8,128)(2,1)S(1)}, bf16[168,1024]{1,0:T(8,128)(2,1)}, u32[]{:S(2)}, u32[]{:S(2)}) collective-permute-start(bf16[168,1024]{1,0:T(8,128)(2,1)S(1)} %collective-permute-done.5.refs_0_), channel_id=1, source_target_pairs={{0,8},{4,12},{8,0},{12,4},{1,9},{5,13},{9,1},{13,5},{2,10},{6,14},... | collective-permute-start | bytes 1032200 | tf_op jit(solution)/shard_map/ppermute | solution.py:28
  24.1 0.7 and_select_fusion
  24.8 2.5 %collective-permute-done.1.refs_2_ = bf16[168,1024]{1,0:T(8,128)(2,1)S(1)} collective-permute-done((bf16[168,1024]{1,0:T(8,128)(2,1)}, bf16[168,1024]{1,0:T(8,128)(2,1)S(1)}, u32[]{:S(2)}, u32[]{:S(2)}) %collective-permute-start.1) | collective-permute-done | bytes 344096 | tf_op jit(solution)/shard_map/ppermute | solution.py:28
  27.2 1.6 collective-permute-done.2.refs_3_
  28.8 1.0 copy-done.4
  29.8 0.8 shard_map.110
  30.6 2.0 %collective-permute-start.3 = (bf16[672,1024]{1,0:T(8,128)(2,1)S(1)}, bf16[672,1024]{1,0:T(8,128)(2,1)S(1)}, u32[]{:S(2)}, u32[]{:S(2)}) collective-permute-start(bf16[672,1024]{1,0:T(8,128)(2,1)S(1)} %bitcast.40), channel_id=1, source_target_pairs={{0,4},{4,8},{8,12},{12,0},{1,5},{5,9},{9,13},{13,1},{2,6},{6,10},{... | collective-permute-start | bytes 4128776 | tf_op jit(solution)/shard_map/ppermute | solution.py:28
  32.7 0.6 collective-permute-done.6.refs_1_
  33.2 7.3 %collective-permute-done.8.refs_3_ = bf16[168,1024]{1,0:T(8,128)(2,1)} collective-permute-done((bf16[168,1024]{1,0:T(8,128)(2,1)S(1)}, bf16[168,1024]{1,0:T(8,128)(2,1)}, u32[]{:S(2)}, u32[]{:S(2)}) %collective-permute-start.8) | collective-permute-done | bytes 344096 | tf_op jit(solution)/shard_map/ppermute | solution.py:28
  40.6 3.3 %shard_map.111 = bf16[4,168,1024]{2,1,0:T(8,128)(2,1)} custom-call(s32[4]{0:T(128)S(1)} %get-tuple-element.60.slots, bf16[168,1024]{1,0:T(8,128)(2,1)S(1)} %collective-permute-done.5.refs_0_, bf16[168,1024]{1,0:T(8,128)(2,1)S(1)} %collective-permute-done.6.refs_1_, bf16[168,1024]{1,0:T(8,128)(2,1)} %collective-permute-done.7.refs_2_, ...), custom_call_target="tpu_custom_call" | custom-call | tf_op jit(solution)/shard_map/pallas_call | solution.py:50
  43.9 2.8 %collective-permute-start.10 = (bf16[672,1024]{1,0:T(8,128)(2,1)}, bf16[672,1024]{1,0:T(8,128)(2,1)}, u32[]{:S(2)}, u32[]{:S(2)}) collective-permute-start(bf16[672,1024]{1,0:T(8,128)(2,1)} %bitcast.3.refs_3_), channel_id=1, source_target_pairs={{0,48},{16,0},{32,16},{48,32},{1,49},{17,1},{33,17},{49,33},{2,50}... | collective-permute-start | bytes 4128776 | tf_op jit(solution)/shard_map/ppermute | solution.py:28
  46.7 2.4 %collective-permute-start.11 = (bf16[168,512]{1,0:T(8,128)(2,1)}, bf16[168,512]{1,0:T(8,128)(2,1)S(1)}, u32[]{:S(2)}, u32[]{:S(2)}) collective-permute-start(bf16[168,512]{1,0:T(8,128)(2,1)} %bitcast.49), channel_id=1, source_target_pairs={{0,64},{2,0},{64,66},{66,2},{1,65},{3,1},{65,67},{67,3},{4,68},{6,... | collective-permute-start | bytes 516104 | tf_op jit(solution)/shard_map/ppermute | solution.py:373
  49.0 1.8 %fusion.15 = (f32[512,64]{1,0:T(8,128)S(1)}, f32[512,64]{1,0:T(8,128)}, f32[512,64]{1,0:T(8,128)}) fusion(f32[64]{0:T(128)S(1)} %multiply_power_fusion, f32[512]{0:T(512)S(1)} %add_convert_fusion), kind=kLoop, calls=%fused_computation.25 | loop fusion | flops 65536 | bytes 395520 | tf_op jit(solution)/shard_map/neg | solution.py:382
  50.9 5.2 %collective-permute-done.11 = bf16[168,512]{1,0:T(8,128)(2,1)S(1)} collective-permute-done((bf16[168,512]{1,0:T(8,128)(2,1)}, bf16[168,512]{1,0:T(8,128)(2,1)S(1)}, u32[]{:S(2)}, u32[]{:S(2)}) %collective-permute-start.11) | collective-permute-done | bytes 172064 | tf_op jit(solution)/shard_map/ppermute | solution.py:373
  56.0 3.5 %collective-permute-start.12 = (bf16[168,512]{1,0:T(8,128)(2,1)}, bf16[168,512]{1,0:T(8,128)(2,1)}, u32[]{:S(2)}, u32[]{:S(2)}) collective-permute-start(bf16[168,512]{1,0:T(8,128)(2,1)} %bitcast.50), channel_id=1, source_target_pairs={{64,2},{2,64},{65,3},{3,65},{68,6},{6,68},{69,7},{7,69},{72,10},{1... | collective-permute-start | bytes 516104 | tf_op jit(solution)/shard_map/ppermute | solution.py:374
  59.5 0.6 pad_add_fusion.side
  60.1 0.8 reshape.32
  61.0 1.4 reshape_reshape.3.far_gain
  62.4 0.7 reshape.33.near_gain
  63.1 0.6 stack.48.index
  63.8 1.3 pad_maximum_fusion.1
  65.1 1.0 broadcast_select_fusion.1
  66.1 0.8 pad_maximum_fusion
  66.9 8.0 %shard_map.112 = (bf16[4,512,672]{2,1,0:T(8,128)(2,1)}, bf16[4,512,672]{2,1,0:T(8,128)(2,1)}) custom-call(s32[2]{0:T(128)} %pad_add_fusion.side, bf16[2,2,1344,512]{3,2,1,0:T(8,128)(2,1)} %bitcast.46, bf16[2,2,1344,512]{3,2,1,0:T(8,128)(2,1)} %bitcast.47, f32[2,4,1,672]{3,2,1,0:T(1,128)} %reshape.33.near_gain, f32[2,4,1,672]{3,2,1,0:T(1,128)} %reshape_reshape.3.far_gain), custom_call_target="tpu_custom_call" | custom-call | tf_op jit(solution)/shard_map/pallas_call | solution.py:127
  74.9 0.4 collective-permute-done.9.refs_4_.value_ref
  75.4 1.1 shard_map.114
  76.6 1.2 collective-permute-start.13
  77.8 1.1 shard_map.115
  78.9 2.7 %collective-permute-start.14 = (bf16[672,512]{1,0:T(8,128)(2,1)S(1)}, bf16[672,512]{1,0:T(8,128)(2,1)}, u32[]{:S(2)}, u32[]{:S(2)}) collective-permute-start(bf16[672,512]{1,0:T(8,128)(2,1)S(1)} %shard_map.115), channel_id=1, source_target_pairs={{0,48},{16,0},{32,16},{48,32},{1,49},{17,1},{33,17},{49,33},{2,50}... | collective-permute-start | bytes 2064392 | tf_op jit(solution)/shard_map/ppermute | solution.py:28
  81.8 1.5 collective-permute-start.15
  83.4 1.2 shard_map.119
  84.6 6.0 %shard_map.113 = f32[512,512]{1,0:T(8,128)} custom-call(s32[6]{0:T(128)} %stack.48.index, bf16[4,512,672]{2,1,0:T(8,128)(2,1)} %get-tuple-element.36.near_ref, bf16[4,512,672]{2,1,0:T(8,128)(2,1)} %get-tuple-element.37.far_ref, bf16[672,1024]{1,0:T(8,128)(2,1)} %bitcast.42, bf16[672,1024]{1,0:T(8,128)(2,1)} %copy-done.3, ...), custom_call_target="tpu_custom_call" | custom-call | tf_op jit(solution)/shard_map/pallas_call | solution.py:169
  91.0 4.6 %collective-permute-done.14 = bf16[672,512]{1,0:T(8,128)(2,1)} collective-permute-done((bf16[672,512]{1,0:T(8,128)(2,1)S(1)}, bf16[672,512]{1,0:T(8,128)(2,1)}, u32[]{:S(2)}, u32[]{:S(2)}) %collective-permute-start.14) | collective-permute-done | bytes 688160 | tf_op jit(solution)/shard_map/ppermute | solution.py:28
  95.7 1.9 %fusion.9 = f32[512,512]{1,0:T(8,128)S(1)} fusion(bf16[672,512]{1,0:T(8,128)(2,1)} %collective-permute-done.13, bf16[4,512,672]{2,1,0:T(8,128)(2,1)} %get-tuple-element.36.near_ref, s32[]{:T(128)S(6)} %select_n.72), kind=kOutput, calls=%fused_computation.12 | convolution fusion | flops 352321536 | bytes 2523140 | tf_op jit(solution)/shard_map/dot_general | solution.py:193
  97.6 1.9 %add_add_fusion.1.raw_ref = f32[512,512]{1,0:T(8,128)S(1)} fusion(f32[512,512]{1,0:T(8,128)S(1)} %copy-done.8, f32[512,512]{1,0:T(8,128)S(1)} %fusion.9, bf16[672,512]{1,0:T(8,128)(2,1)} %collective-permute-done.14, bf16[4,512,672]{2,1,0:T(8,128)(2,1)} %get-tuple-element.37.far_ref, s32[]{:T(128)S(6)} %select_n.74), kind=kOutput, calls=%fused_computation.5 | convolution fusion | flops 352845824 | bytes 4620292 | tf_op jit(solution)/shard_map/dot_general | solution.py:193
  99.6 0.7 shard_map.116.k_ref.v_ref
  100.2 2.4 %collective-permute-start.17 = (bf16[512,512]{1,0:T(8,128)(2,1)S(1)}, bf16[512,512]{1,0:T(8,128)(2,1)S(1)}, u32[]{:S(2)}, u32[]{:S(2)}) collective-permute-start(bf16[512,512]{1,0:T(8,128)(2,1)S(1)} %shard_map.116.k_ref.v_ref), channel_id=1, source_target_pairs={{0,4},{4,8},{8,12},{12,16},{16,20},{20,24},{24,28},{28,32},{32,36}... | collective-permute-start | bytes 1572872 | tf_op jit(solution)/shard_map/ppermute | solution.py:33
  102.6 6.7 %collective-permute-start.18 = (bf16[512,512]{1,0:T(8,128)(2,1)S(1)}, bf16[512,512]{1,0:T(8,128)(2,1)S(1)}, u32[]{:S(2)}, u32[]{:S(2)}) collective-permute-start(bf16[512,512]{1,0:T(8,128)(2,1)S(1)} %shard_map.116.k_ref.v_ref), channel_id=1, source_target_pairs={{0,8},{4,12},{8,16},{12,20},{16,24},{20,28},{24,32},{28,36},{32,40... | collective-permute-start | bytes 1572872 | tf_op jit(solution)/shard_map/ppermute | solution.py:33
  109.3 6.0 %shard_map.117 = f32[512,512]{1,0:T(8,128)} custom-call(s32[6]{0:T(128)} %stack.48.index, bf16[4,512,672]{2,1,0:T(8,128)(2,1)} %get-tuple-element.36.near_ref, bf16[4,512,672]{2,1,0:T(8,128)(2,1)} %get-tuple-element.37.far_ref, bf16[672,1024]{1,0:T(8,128)(2,1)} %bitcast.43, bf16[672,1024]{1,0:T(8,128)(2,1)} %copy-done.3, ...), custom_call_target="tpu_custom_call" | custom-call | tf_op jit(solution)/shard_map/pallas_call | solution.py:169
  115.3 2.0 %fusion.7 = f32[512,512]{1,0:T(8,128)S(1)} fusion(bf16[672,512]{1,0:T(8,128)(2,1)} %collective-permute-done.15, bf16[4,512,672]{2,1,0:T(8,128)(2,1)} %get-tuple-element.36.near_ref, s32[]{:T(128)S(6)} %select_n.72), kind=kOutput, calls=%fused_computation.10 | convolution fusion | flops 352321536 | bytes 2523140 | tf_op jit(solution)/shard_map/dot_general | solution.py:193
  117.4 1.9 %fusion.1 = f32[512,512]{1,0:T(8,128)S(1)} fusion(bf16[672,512]{1,0:T(8,128)(2,1)} %collective-permute-done.16, bf16[4,512,672]{2,1,0:T(8,128)(2,1)} %get-tuple-element.37.far_ref, s32[]{:T(128)S(6)} %select_n.74), kind=kOutput, calls=%fused_computation.6 | convolution fusion | flops 352321536 | bytes 2523140 | tf_op jit(solution)/shard_map/dot_general | solution.py:193
  119.7 1.2 shard_map.120.q_ref
  120.9 2.1 %shard_map.121 = (f32[512,512]{1,0:T(8,128)S(1)}, f32[512,512]{1,0:T(8,128)S(1)}) custom-call(bf16[512,512]{1,0:T(8,128)(2,1)S(1)} %shard_map.120.q_ref, bf16[512,512]{1,0:T(8,128)(2,1)S(1)} %shard_map.116.k_ref.v_ref, bf16[512,512]{1,0:T(8,128)(2,1)S(1)} %shard_map.116.k_ref.v_ref), custom_call_target="tpu_custom_call" | custom-call | tf_op jit(solution)/shard_map/pallas_call | solution.py:288
  123.0 8.1 %collective-permute-done.18.k2_ref.v2_ref = bf16[512,512]{1,0:T(8,128)(2,1)S(1)} collective-permute-done((bf16[512,512]{1,0:T(8,128)(2,1)S(1)}, bf16[512,512]{1,0:T(8,128)(2,1)S(1)}, u32[]{:S(2)}, u32[]{:S(2)}) %collective-permute-start.18) | collective-permute-done | bytes 524320 | tf_op jit(solution)/shard_map/ppermute | solution.py:33
  131.1 3.5 %shard_map.122 = bf16[512,512]{1,0:T(8,128)(2,1)S(1)} custom-call(s32[2]{0:T(128)S(1)} %add_convert_fusion.1.valid, bf16[512,512]{1,0:T(8,128)(2,1)S(1)} %shard_map.120.q_ref, bf16[512,512]{1,0:T(8,128)(2,1)S(1)} %collective-permute-done.17.k1_ref.v1_ref, bf16[512,512]{1,0:T(8,128)(2,1)S(1)} %collective-permute-done.17.k1_ref.v1_ref, ...), custom_call_target="tpu_custom_call" | custom-call | tf_op jit(solution)/shard_map/pallas_call | solution.py:309
  134.7 18.9 %all-gather.4.cloned.1.call-done.weight_ref = bf16[2688,1024]{1,0:T(8,128)(2,1)} async-done(((bf16[168,1024]{1,0:T(8,128)(2,1)}), bf16[2688,1024]{1,0:T(8,128)(2,1)}) %all-gather.4.cloned.1.call-update) | async-done | bytes 5505040 | tf_op jit(solution)/shard_map/all_gather | solution.py:397
  153.8 2.6 %copy-done = bf16[2688,1024]{1,0:T(8,128)(2,1)S(1)} copy-done((bf16[2688,1024]{1,0:T(8,128)(2,1)S(1)}, bf16[2688,1024]{1,0:T(8,128)(2,1)}, u32[]{:S(2)}) %copy-start) | copy-done | bytes 5505048
  156.3 1.8 %shard_map.124 = bf16[1344,512]{1,0:T(8,128)(2,1)S(1)} custom-call(s32[1]{0:T(128)} %bitcast.21.half, bf16[2688,1024]{1,0:T(8,128)(2,1)S(1)} %copy-done, bf16[512,1024]{1,0:T(8,128)(2,1)S(1)} %constant_dynamic-update-slice_fusion.context_ref), custom_call_target="tpu_custom_call" | custom-call | tf_op jit(solution)/shard_map/pallas_call | solution.py:334
  158.3 0.6 copy-done.1
  158.9 1.8 %shard_map.123 = f32[1344,512]{1,0:T(8,128)S(1)} custom-call(s32[1]{0:T(128)} %bitcast.half, bf16[2688,1024]{1,0:T(8,128)(2,1)S(1)} %copy-done.1, bf16[512,1024]{1,0:T(8,128)(2,1)S(1)} %constant_dynamic-update-slice_fusion.context_ref), custom_call_target="tpu_custom_call" | custom-call | tf_op jit(solution)/shard_map/pallas_call | solution.py:334
  160.7 0.6 collective-permute-done.20
  161.4 0.5 multiply_reduce_fusion
  162.1 1.0 collective-permute-done.21
  163.1 0.5 collective-permute-start.22
  163.6 4.6 %collective-permute-done.22 = f32[512]{0:T(512)S(1)} collective-permute-done((f32[512]{0:T(512)S(1)}, f32[512]{0:T(512)S(1)}, u32[]{:S(2)}, u32[]{:S(2)}) %collective-permute-start.22) | collective-permute-done | bytes 2080 | tf_op jit(solution)/shard_map/ppermute | solution.py:28
  168.2 1.7 fusion
  (53 shorter events, 2.0 us)
Async XLA Ops:
  6.5 60.4 %all-gather.6.cloned.1.call-start = ((), (), s32[]{:S(2)}) async-start(), calls=%async_computation.1 | async-start | bytes 6881280 | tf_op jit(solution)/shard_map/all_gather | solution.py:358
  7.3 146.3 %all-gather.4.cloned.1.call-start = ((), (), s32[]{:S(2)}) async-start(), calls=%async_computation | async-start | bytes 5849088 | tf_op jit(solution)/shard_map/all_gather | solution.py:397
  9.1 10.0 %collective-permute-start.5 = (bf16[168,1024]{1,0:T(8,128)(2,1)}, bf16[168,1024]{1,0:T(8,128)(2,1)S(1)}, u32[]{:S(2)}, u32[]{:S(2)}) collective-permute-start(bf16[168,1024]{1,0:T(8,128)(2,1)} %shard_map.109.refs_0_), channel_id=1, source_target_pairs={{0,64},{64,0},{1,65},{65,1},{2,66},{66,2},{3,67},{67,3},{4,68},{68... | collective-permute-start | bytes 1032200 | tf_op jit(solution)/shard_map/ppermute | solution.py:28
  9.5 11.6 %collective-permute-start = (bf16[168,1024]{1,0:T(8,128)(2,1)}, bf16[168,1024]{1,0:T(8,128)(2,1)S(1)}, u32[]{:S(2)}, u32[]{:S(2)}) collective-permute-start(bf16[168,1024]{1,0:T(8,128)(2,1)} %shard_map.109.refs_0_), channel_id=1, source_target_pairs={{0,16},{16,32},{32,48},{48,0},{1,17},{17,33},{33,49},{49,1},{2,18}... | collective-permute-start | bytes 1032200 | tf_op jit(solution)/shard_map/ppermute | solution.py:28
  11.0 16.2 %collective-permute-start.1 = (bf16[168,1024]{1,0:T(8,128)(2,1)}, bf16[168,1024]{1,0:T(8,128)(2,1)S(1)}, u32[]{:S(2)}, u32[]{:S(2)}) collective-permute-start(bf16[168,1024]{1,0:T(8,128)(2,1)} %shard_map.109.refs_0_), channel_id=1, source_target_pairs={{0,48},{16,0},{32,16},{48,32},{1,49},{17,1},{33,17},{49,33},{2,50}... | collective-permute-start | bytes 1032200 | tf_op jit(solution)/shard_map/ppermute | solution.py:28
  12.8 16.1 %collective-permute-start.2 = (bf16[168,1024]{1,0:T(8,128)(2,1)}, bf16[168,1024]{1,0:T(8,128)(2,1)S(1)}, u32[]{:S(2)}, u32[]{:S(2)}) collective-permute-start(bf16[168,1024]{1,0:T(8,128)(2,1)} %shard_map.109.refs_0_), channel_id=1, source_target_pairs={{0,32},{16,48},{32,0},{48,16},{1,33},{17,49},{33,1},{49,17},{2,34}... | collective-permute-start | bytes 1032200 | tf_op jit(solution)/shard_map/ppermute | solution.py:28
  19.1 14.1 %collective-permute-start.6 = (bf16[168,1024]{1,0:T(8,128)(2,1)S(1)}, bf16[168,1024]{1,0:T(8,128)(2,1)S(1)}, u32[]{:S(2)}, u32[]{:S(2)}) collective-permute-start(bf16[168,1024]{1,0:T(8,128)(2,1)S(1)} %collective-permute-done.5.refs_0_), channel_id=1, source_target_pairs={{0,4},{4,8},{8,12},{12,0},{1,5},{5,9},{9,13},{13,1},{2,6},{6,10},{... | collective-permute-start | bytes 1032200 | tf_op jit(solution)/shard_map/ppermute | solution.py:28
  21.0 12.2 %collective-permute-start.7 = (bf16[168,1024]{1,0:T(8,128)(2,1)S(1)}, bf16[168,1024]{1,0:T(8,128)(2,1)}, u32[]{:S(2)}, u32[]{:S(2)}) collective-permute-start(bf16[168,1024]{1,0:T(8,128)(2,1)S(1)} %collective-permute-done.5.refs_0_), channel_id=1, source_target_pairs={{0,12},{4,0},{8,4},{12,8},{1,13},{5,1},{9,5},{13,9},{2,14},{6,2},{... | collective-permute-start | bytes 1032200 | tf_op jit(solution)/shard_map/ppermute | solution.py:28
  21.1 19.5 %collective-permute-start.8 = (bf16[168,1024]{1,0:T(8,128)(2,1)S(1)}, bf16[168,1024]{1,0:T(8,128)(2,1)}, u32[]{:S(2)}, u32[]{:S(2)}) collective-permute-start(bf16[168,1024]{1,0:T(8,128)(2,1)S(1)} %collective-permute-done.5.refs_0_), channel_id=1, source_target_pairs={{0,8},{4,12},{8,0},{12,4},{1,9},{5,13},{9,1},{13,5},{2,10},{6,14},... | collective-permute-start | bytes 1032200 | tf_op jit(solution)/shard_map/ppermute | solution.py:28
  28.8 1.0 copy-start.4
  30.6 35.6 %copy-start.2 = (bf16[4,168,1024]{2,1,0:T(8,128)(2,1)}, bf16[4,168,1024]{2,1,0:T(8,128)(2,1)S(1)}, u32[]{:S(2)}) copy-start(bf16[4,168,1024]{2,1,0:T(8,128)(2,1)S(1)} %shard_map.110) | copy-start | bytes 4128772
  30.6 44.3 %collective-permute-start.3 = (bf16[672,1024]{1,0:T(8,128)(2,1)S(1)}, bf16[672,1024]{1,0:T(8,128)(2,1)S(1)}, u32[]{:S(2)}, u32[]{:S(2)}) collective-permute-start(bf16[672,1024]{1,0:T(8,128)(2,1)S(1)} %bitcast.40), channel_id=1, source_target_pairs={{0,4},{4,8},{8,12},{12,0},{1,5},{5,9},{9,13},{13,1},{2,6},{6,10},{... | collective-permute-start | bytes 4128776 | tf_op jit(solution)/shard_map/ppermute | solution.py:28
  32.6 42.3 %collective-permute-start.4 = (bf16[672,1024]{1,0:T(8,128)(2,1)S(1)}, bf16[672,1024]{1,0:T(8,128)(2,1)}, u32[]{:S(2)}, u32[]{:S(2)}) collective-permute-start(bf16[672,1024]{1,0:T(8,128)(2,1)S(1)} %bitcast.41), channel_id=1, source_target_pairs={{0,12},{4,0},{8,4},{12,8},{1,13},{5,1},{9,5},{13,9},{2,14},{6,2},{... | collective-permute-start | bytes 4128776 | tf_op jit(solution)/shard_map/ppermute | solution.py:28
  43.9 31.1 %collective-permute-start.10 = (bf16[672,1024]{1,0:T(8,128)(2,1)}, bf16[672,1024]{1,0:T(8,128)(2,1)}, u32[]{:S(2)}, u32[]{:S(2)}) collective-permute-start(bf16[672,1024]{1,0:T(8,128)(2,1)} %bitcast.3.refs_3_), channel_id=1, source_target_pairs={{0,48},{16,0},{32,16},{48,32},{1,49},{17,1},{33,17},{49,33},{2,50}... | collective-permute-start | bytes 4128776 | tf_op jit(solution)/shard_map/ppermute | solution.py:28
  46.6 28.7 %collective-permute-start.9 = (bf16[672,1024]{1,0:T(8,128)(2,1)}, bf16[672,1024]{1,0:T(8,128)(2,1)}, u32[]{:S(2)}, u32[]{:S(2)}) collective-permute-start(bf16[672,1024]{1,0:T(8,128)(2,1)} %bitcast.3.refs_3_), channel_id=1, source_target_pairs={{0,16},{16,32},{32,48},{48,0},{1,17},{17,33},{33,49},{49,1},{2,18}... | collective-permute-start | bytes 4128776 | tf_op jit(solution)/shard_map/ppermute | solution.py:28
  46.7 9.3 %collective-permute-start.11 = (bf16[168,512]{1,0:T(8,128)(2,1)}, bf16[168,512]{1,0:T(8,128)(2,1)S(1)}, u32[]{:S(2)}, u32[]{:S(2)}) collective-permute-start(bf16[168,512]{1,0:T(8,128)(2,1)} %bitcast.49), channel_id=1, source_target_pairs={{0,64},{2,0},{64,66},{66,2},{1,65},{3,1},{65,67},{67,3},{4,68},{6,... | collective-permute-start | bytes 516104 | tf_op jit(solution)/shard_map/ppermute | solution.py:373
  56.0 7.8 %copy-start.10 = (bf16[168,512]{1,0:T(8,128)(2,1)}, bf16[168,512]{1,0:T(8,128)(2,1)S(1)}, u32[]{:S(2)}) copy-start(bf16[168,512]{1,0:T(8,128)(2,1)S(1)} %collective-permute-done.11) | copy-start | bytes 516100
  56.0 9.1 %collective-permute-start.12 = (bf16[168,512]{1,0:T(8,128)(2,1)}, bf16[168,512]{1,0:T(8,128)(2,1)}, u32[]{:S(2)}, u32[]{:S(2)}) collective-permute-start(bf16[168,512]{1,0:T(8,128)(2,1)} %bitcast.50), channel_id=1, source_target_pairs={{64,2},{2,64},{65,3},{3,65},{68,6},{6,68},{69,7},{7,69},{72,10},{1... | collective-permute-start | bytes 516104 | tf_op jit(solution)/shard_map/ppermute | solution.py:374
  74.9 6.9 %copy-start.3 = (bf16[672,1024]{1,0:T(8,128)(2,1)}, bf16[672,1024]{1,0:T(8,128)(2,1)S(1)}, u32[]{:S(2)}) copy-start(bf16[672,1024]{1,0:T(8,128)(2,1)S(1)} %collective-permute-done.3.refs_1_.value_ref) | copy-start | bytes 4128772
  76.6 14.5 %collective-permute-start.13 = (bf16[672,512]{1,0:T(8,128)(2,1)S(1)}, bf16[672,512]{1,0:T(8,128)(2,1)}, u32[]{:S(2)}, u32[]{:S(2)}) collective-permute-start(bf16[672,512]{1,0:T(8,128)(2,1)S(1)} %shard_map.114), channel_id=1, source_target_pairs={{0,12},{4,0},{8,4},{12,8},{1,13},{5,1},{9,5},{13,9},{2,14},{6,2},{... | collective-permute-start | bytes 2064392 | tf_op jit(solution)/shard_map/ppermute | solution.py:28
  78.9 16.8 %collective-permute-start.14 = (bf16[672,512]{1,0:T(8,128)(2,1)S(1)}, bf16[672,512]{1,0:T(8,128)(2,1)}, u32[]{:S(2)}, u32[]{:S(2)}) collective-permute-start(bf16[672,512]{1,0:T(8,128)(2,1)S(1)} %shard_map.115), channel_id=1, source_target_pairs={{0,48},{16,0},{32,16},{48,32},{1,49},{17,1},{33,17},{49,33},{2,50}... | collective-permute-start | bytes 2064392 | tf_op jit(solution)/shard_map/ppermute | solution.py:28
  81.8 33.5 %collective-permute-start.15 = (bf16[672,512]{1,0:T(8,128)(2,1)S(1)}, bf16[672,512]{1,0:T(8,128)(2,1)}, u32[]{:S(2)}, u32[]{:S(2)}) collective-permute-start(bf16[672,512]{1,0:T(8,128)(2,1)S(1)} %shard_map.118), channel_id=1, source_target_pairs={{0,4},{4,8},{8,12},{12,0},{1,5},{5,9},{9,13},{13,1},{2,6},{6,10},{... | collective-permute-start | bytes 2064392 | tf_op jit(solution)/shard_map/ppermute | solution.py:28
  84.6 32.8 %collective-permute-start.16 = (bf16[672,512]{1,0:T(8,128)(2,1)S(1)}, bf16[672,512]{1,0:T(8,128)(2,1)}, u32[]{:S(2)}, u32[]{:S(2)}) collective-permute-start(bf16[672,512]{1,0:T(8,128)(2,1)S(1)} %shard_map.119), channel_id=1, source_target_pairs={{0,16},{16,32},{32,48},{48,0},{1,17},{17,33},{33,49},{49,1},{2,18}... | collective-permute-start | bytes 2064392 | tf_op jit(solution)/shard_map/ppermute | solution.py:28
  90.6 7.0 %copy-start.8 = (f32[512,512]{1,0:T(8,128)S(1)}, f32[512,512]{1,0:T(8,128)}, u32[]{:S(2)}) copy-start(f32[512,512]{1,0:T(8,128)} %shard_map.113) | copy-start | bytes 3145732
  97.6 1.9 %copy-start.5 = (f32[128]{0:T(128)S(1)}, f32[128]{0:T(128)}, u32[]{:S(2)}) copy-start(f32[128]{0:T(128)} %param.19) | copy-start | bytes 1540
  100.2 22.8 %collective-permute-start.17 = (bf16[512,512]{1,0:T(8,128)(2,1)S(1)}, bf16[512,512]{1,0:T(8,128)(2,1)S(1)}, u32[]{:S(2)}, u32[]{:S(2)}) collective-permute-start(bf16[512,512]{1,0:T(8,128)(2,1)S(1)} %shard_map.116.k_ref.v_ref), channel_id=1, source_target_pairs={{0,4},{4,8},{8,12},{12,16},{16,20},{20,24},{24,28},{28,32},{32,36}... | collective-permute-start | bytes 1572872 | tf_op jit(solution)/shard_map/ppermute | solution.py:33
  102.6 28.5 %collective-permute-start.18 = (bf16[512,512]{1,0:T(8,128)(2,1)S(1)}, bf16[512,512]{1,0:T(8,128)(2,1)S(1)}, u32[]{:S(2)}, u32[]{:S(2)}) collective-permute-start(bf16[512,512]{1,0:T(8,128)(2,1)S(1)} %shard_map.116.k_ref.v_ref), channel_id=1, source_target_pairs={{0,8},{4,12},{8,16},{12,20},{16,24},{20,28},{24,32},{28,36},{32,40... | collective-permute-start | bytes 1572872 | tf_op jit(solution)/shard_map/ppermute | solution.py:33
  115.3 4.0 %copy-start.9 = (f32[512,512]{1,0:T(8,128)S(1)}, f32[512,512]{1,0:T(8,128)}, u32[]{:S(2)}) copy-start(f32[512,512]{1,0:T(8,128)} %shard_map.117) | copy-start | bytes 3145732
  117.3 2.3 %copy-start.6 = (f32[128]{0:T(128)S(1)}, f32[128]{0:T(128)}, u32[]{:S(2)}) copy-start(f32[128]{0:T(128)} %param.18) | copy-start | bytes 1540
  134.6 19.0 %collective-permute-start.19 = (bf16[512,512]{1,0:T(8,128)(2,1)S(1)}, bf16[512,512]{1,0:T(8,128)(2,1)S(1)}, u32[]{:S(2)}, u32[]{:S(2)}) collective-permute-start(bf16[512,512]{1,0:T(8,128)(2,1)S(1)} %shard_map.122), channel_id=1, source_target_pairs={{0,2},{2,0},{1,3},{3,1},{4,6},{6,4},{5,7},{7,5},{8,10},{10,8},{9,1... | collective-permute-start | bytes 1572872 | tf_op jit(solution)/shard_map/ppermute | solution.py:28
  153.7 2.6 %copy-start = (bf16[2688,1024]{1,0:T(8,128)(2,1)S(1)}, bf16[2688,1024]{1,0:T(8,128)(2,1)}, u32[]{:S(2)}) copy-start(bf16[2688,1024]{1,0:T(8,128)(2,1)} %all-gather.4.cloned.1.call-done.weight_ref) | copy-start | bytes 16515076
  156.3 2.6 %copy-start.1 = (bf16[2688,1024]{1,0:T(8,128)(2,1)S(1)}, bf16[2688,1024]{1,0:T(8,128)(2,1)}, u32[]{:S(2)}) copy-start(bf16[2688,1024]{1,0:T(8,128)(2,1)} %all-gather.4.cloned.1.call-done.weight_ref) | copy-start | bytes 16515076
  158.2 3.2 %collective-permute-start.20 = (bf16[1344,512]{1,0:T(8,128)(2,1)S(1)}, bf16[1344,512]{1,0:T(8,128)(2,1)S(1)}, u32[]{:S(2)}, u32[]{:S(2)}) collective-permute-start(bf16[1344,512]{1,0:T(8,128)(2,1)S(1)} %shard_map.124), channel_id=1, source_target_pairs={{0,1},{1,0},{2,3},{3,2},{4,5},{5,4},{6,7},{7,6},{8,9},{9,8},{10,11... | collective-permute-start | bytes 4128776 | tf_op jit(solution)/shard_map/ppermute | solution.py:28
  160.7 7.5 %copy-start.7 = (bf16[512,1344]{0,1:T(8,128)(2,1)S(1)}, bf16[512,1344]{0,1:T(8,128)(2,1)}, u32[]{:S(2)}) copy-start(bf16[512,1344]{0,1:T(8,128)(2,1)} %param.11) | copy-start | bytes 4128772
  160.7 7.5 %copy-start.11 = (f32[1344]{0:T(1024)S(1)}, f32[1344]{0:T(1024)}, u32[]{:S(2)}) copy-start(f32[1344]{0:T(1024)} %param.17) | copy-start | bytes 16132
  161.9 1.2 collective-permute-start.21
  163.1 5.1 %collective-permute-start.22 = (f32[512]{0:T(512)S(1)}, f32[512]{0:T(512)S(1)}, u32[]{:S(2)}, u32[]{:S(2)}) collective-permute-start(f32[512]{0:T(512)S(1)} %add.151), channel_id=1, source_target_pairs={{0,2},{2,0},{1,3},{3,1},{4,6},{6,4},{5,7},{7,5},{8,10},{10,8},{9,1... | collective-permute-start | bytes 6152 | tf_op jit(solution)/shard_map/ppermute | solution.py:28
Sparse Core Ops, SparseCore 0:
  9.0 50.7 all-gather.5
  75.5 78.0 all-gather.3
